TPU v7x, 32 devices: a whole 2x2x4 slice. The times are simulated.
32 devices in a mesh: row: 16 (over z, y, x), col: 2 (over core).
Axes of the slice: x: 2, y: 2, z: 4, core: 2. Of those that a mesh axis runs over, the one named last changes fastest.
Arguments:
- eigvecs: float32 [16384, 4096], P('row', 'col'), may hold values from -6 to 6
- reflectors: float32 [4, 16384, 256], P(None, 'row', 'col'), may hold values from -0.09375 to 0.09375
- factors: float32 [4, 256, 256], P(None, 'col'), may hold values from -2 to 2, as said below
Outputs:
- slab_out: float32 [16384, 4096], P('row', 'col')
Inputs may be any that keep to these rules, and one draw needn't show every extreme that they name: Each factors[p] is upper triangular with diagonal between 0.5 and 1.5.
All inputs are finite; a program needn't handle non-finite values.
Results may differ from a plain program's by a relative error of at most 0.00024.
Values sent between devices are 32-bit elements; how exact they have to be, the bound alone decides.
No kernel may reach another device: no remote copies, remote signals or barrier semaphores. Data moves between devices by JAX's collectives and lax.ppermute only.
A program may use at most 128 MiB of HBM per device.

v0:
```python
import jax
import jax.numpy as jnp
from jax import lax
from jax.sharding import PartitionSpec as P


def project(left, right):
    return lax.dot_general(
        left,
        right,
        (((0,), (0,)), ((), ())),
        precision=lax.Precision.HIGHEST,
        preferred_element_type=jnp.float32,
    )


def matmul(left, right):
    return jnp.dot(left, right, precision=lax.Precision.HIGHEST, preferred_element_type=jnp.float32)


def body(eigvecs, reflectors, factors):
    blocks, tables = (
        lax.all_gather(reflectors, "col", axis=2, tiled=True),
        lax.all_gather(factors, "col", axis=1, tiled=True),
    )
    panel_count = blocks.shape[0]
    slab = eigvecs
    for position in range(panel_count):
        reflect_block = blocks[position]
        factor_block = tables[position]
        partial_proj = project(reflect_block, slab)
        totals = lax.psum(partial_proj, "row")
        weights = matmul(factor_block, totals)
        slab = slab - matmul(reflect_block, weights)
    return slab


def solution(mesh):
    in_specs = (P("row", "col"), P(None, "row", "col"), P(None, "col", None))
    out_specs = P("row", "col")
    return jax.shard_map(body, mesh=mesh, in_specs=in_specs, out_specs=out_specs, check_vma=False)
```

profile of v0, /device:TPU:0, one launch (start us, length us, event | category | flops | bytes accessed | tf_op | source)
XLA Modules:
  0.0 666.1 jit_solution(17062957670361325182)
XLA Ops:
  6.5 0.7 all-gather.3.cloned.1.call-update
  7.3 0.0 all-gather.5.cloned.1.call-start
  7.3 0.7 all-gather.5.cloned.1.call-update
  8.0 0.0 all-reduce.5.cloned.1.call-start
  8.1 16.6 %all-gather.3.cloned.1.call-done = f32[4,1024,256]{2,1,0:T(8,128)} async-done(((f32[4,1024,128]{2,1,0:T(8,128)}), f32[4,1024,256]{2,1,0:T(8,128)}) %all-gather.3.cloned.1.call-update) | async-done | bytes 4194320 | tf_op jit(solution)/shard_map/all_gather | solution.py:23
  24.6 10.7 %fusion = f32[256,2048]{1,0:T(8,128)} fusion(f32[1024,2048]{1,0:T(8,128)} %param.3, f32[4,1024,256]{2,1,0:T(8,128)} %all-gather.3.cloned.1.call-done), kind=kOutput, calls=%fused_computation.11 | convolution fusion | flops 6442450944 | bytes 11534336 | tf_op jit(solution)/shard_map/dot_general | solution.py:8
  35.4 0.0 all-reduce.7.cloned.1.call-start
  35.4 9.3 %copy.4 = f32[1024,2048]{0,1:T(8,128)} copy(f32[1024,2048]{1,0:T(8,128)} %param.3) | data formatting | bytes 16777216 | tf_op args[0]
  44.7 124.4 %all-reduce.5.cloned.1.call-done = f32[256,2048]{1,0:T(8,128)} async-done(((f32[256,2048]{1,0:T(8,128)}), f32[256,2048]{1,0:T(8,128)}) %all-reduce.5.cloned.1.call-update) | async-done | bytes 2097168 | tf_op jit(solution)/shard_map/psum | solution.py:32
  169.0 5.3 fusion.4
  174.4 10.2 %bitcast_subtract_fusion.3 = f32[1024,2048]{0,1:T(8,128)S(1)} fusion(f32[1024,2048]{0,1:T(8,128)} %copy.4, f32[2048,256]{1,0:T(8,128)S(1)} %fusion.4, f32[4,1024,256]{2,1,0:T(8,128)S(1)} %copy-done.3), kind=kOutput, calls=%fused_computation.3 | convolution fusion | flops 6444548096 | bytes 19922944 | tf_op jit(solution)/shard_map/dot_general | solution.py:18
  184.6 3.4 copy-done
  188.0 8.3 %convolution_bitcast_fusion.2 = f32[256,2048]{0,1:T(8,128)} fusion(f32[1024,2048]{0,1:T(8,128)S(1)} %bitcast_subtract_fusion.3, f32[4,1024,256]{2,1,0:T(8,128)S(1)} %copy-done.3), kind=kOutput, calls=%fused_computation.6 | convolution fusion | flops 6442450944 | bytes 11534336 | tf_op jit(solution)/shard_map/dot_general | solution.py:8
  196.2 0.0 all-reduce.7.cloned.1.call-update
  196.2 0.0 all-reduce.9.cloned.1.call-start
  196.3 125.4 %all-reduce.7.cloned.1.call-done = f32[256,2048]{0,1:T(8,128)} async-done(((f32[256,2048]{0,1:T(8,128)}), f32[256,2048]{0,1:T(8,128)}) %all-reduce.7.cloned.1.call-update) | async-done | bytes 2097168 | tf_op jit(solution)/shard_map/psum | solution.py:32
  321.7 3.7 fusion.3
  325.4 21.4 %bitcast_subtract_fusion.2 = f32[1024,2048]{0,1:T(8,128)S(1)} fusion(f32[1024,2048]{0,1:T(8,128)} %copy-done, f32[2048,256]{1,0:T(8,128)S(1)} %fusion.3, f32[4,1024,256]{2,1,0:T(8,128)S(1)} %copy-done.4), kind=kOutput, calls=%fused_computation.2 | convolution fusion | flops 6444548096 | bytes 19922944 | tf_op jit(solution)/shard_map/dot_general | solution.py:18
  346.8 3.4 copy-done.1
  350.2 8.3 %convolution_bitcast_fusion.1 = f32[256,2048]{0,1:T(8,128)} fusion(f32[1024,2048]{0,1:T(8,128)S(1)} %bitcast_subtract_fusion.2, f32[4,1024,256]{2,1,0:T(8,128)S(1)} %copy-done.4), kind=kOutput, calls=%fused_computation.5 | convolution fusion | flops 6442450944 | bytes 11534336 | tf_op jit(solution)/shard_map/dot_general | solution.py:8
  358.4 0.0 all-reduce.9.cloned.1.call-update
  358.4 0.0 all-reduce.11.cloned.1.call-start
  358.5 125.4 %all-reduce.9.cloned.1.call-done = f32[256,2048]{0,1:T(8,128)} async-done(((f32[256,2048]{0,1:T(8,128)}), f32[256,2048]{0,1:T(8,128)}) %all-reduce.9.cloned.1.call-update) | async-done | bytes 2097168 | tf_op jit(solution)/shard_map/psum | solution.py:32
  483.9 3.7 fusion.2
  487.6 10.1 %bitcast_subtract_fusion.1 = f32[1024,2048]{0,1:T(8,128)S(1)} fusion(f32[1024,2048]{0,1:T(8,128)} %copy-done.1, f32[2048,256]{1,0:T(8,128)S(1)} %fusion.2, f32[4,1024,256]{2,1,0:T(8,128)S(1)} %copy-done.5), kind=kOutput, calls=%fused_computation.1 | convolution fusion | flops 6444548096 | bytes 19922944 | tf_op jit(solution)/shard_map/dot_general | solution.py:18
  497.8 3.4 copy-done.2
  501.1 8.3 %convolution_bitcast_fusion = f32[256,2048]{0,1:T(8,128)} fusion(f32[1024,2048]{0,1:T(8,128)S(1)} %bitcast_subtract_fusion.1, f32[4,1024,256]{2,1,0:T(8,128)S(1)} %copy-done.5), kind=kOutput, calls=%fused_computation.4 | convolution fusion | flops 6442450944 | bytes 11534336 | tf_op jit(solution)/shard_map/dot_general | solution.py:8
  509.4 0.0 all-reduce.11.cloned.1.call-update
  509.4 125.5 %all-reduce.11.cloned.1.call-done = f32[256,2048]{0,1:T(8,128)} async-done(((f32[256,2048]{0,1:T(8,128)}), f32[256,2048]{0,1:T(8,128)}) %all-reduce.11.cloned.1.call-update) | async-done | bytes 2097168 | tf_op jit(solution)/shard_map/psum | solution.py:32
  634.9 3.5 fusion.1
  638.4 11.3 %bitcast_subtract_fusion = f32[1024,2048]{0,1:T(8,128)} fusion(f32[1024,2048]{0,1:T(8,128)} %copy-done.2, f32[2048,256]{1,0:T(8,128)S(1)} %fusion.1, f32[4,1024,256]{2,1,0:T(8,128)} %all-gather.3.cloned.1.call-done), kind=kOutput, calls=%fused_computation | convolution fusion | flops 6444548096 | bytes 19922944 | tf_op jit(solution)/shard_map/dot_general | solution.py:18
  649.7 9.1 %copy.5 = f32[1024,2048]{1,0:T(8,128)} copy(f32[1024,2048]{0,1:T(8,128)} %bitcast_subtract_fusion) | data formatting | bytes 16777216 | tf_op jit(solution)/shard_map/sub | solution.py:34
  (14 shorter events, 0.0 us)
Async XLA Ops:
  6.5 18.1 %all-gather.3.cloned.1.call-start = ((), (), s32[]{:S(2)}) async-start(), calls=%async_computation | async-start | bytes 6291456 | tf_op jit(solution)/shard_map/all_gather | solution.py:23
  7.3 37.4 %all-gather.5.cloned.1.call-start = ((), (), s32[]{:S(2)}) async-start(), calls=%async_computation.2 | async-start | bytes 1572864 | tf_op jit(solution)/shard_map/all_gather | solution.py:24
  8.0 161.0 %all-reduce.5.cloned.1.call-start = ((), (), s32[]{:S(2)}) async-start(), calls=%async_computation.1 | async-start | bytes 4194304 | tf_op jit(solution)/shard_map/psum | solution.py:32
  35.4 286.4 %all-reduce.7.cloned.1.call-start = ((), (), s32[]{:S(2)}) async-start(), calls=%async_computation.3 | async-start | bytes 4194304 | tf_op jit(solution)/shard_map/psum | solution.py:32
  169.0 5.3 copy-start.3
  184.6 3.4 copy-start
  188.0 133.8 %copy-start.6 = (f32[4,256,256]{2,1,0:T(8,128)S(1)}, f32[4,256,256]{2,1,0:T(8,128)}, u32[]{:S(2)}) copy-start(f32[4,256,256]{2,1,0:T(8,128)} %all-gather.5.cloned.1.call-done) | copy-start | bytes 3145732
  196.2 287.7 %all-reduce.9.cloned.1.call-start = ((), (), s32[]{:S(2)}) async-start(), calls=%async_computation.4 | async-start | bytes 4194304 | tf_op jit(solution)/shard_map/psum | solution.py:32
  321.7 3.7 copy-start.4
  346.8 3.4 copy-start.1
  358.4 276.5 %all-reduce.11.cloned.1.call-start = ((), (), s32[]{:S(2)}) async-start(), calls=%async_computation.5 | async-start | bytes 4194304 | tf_op jit(solution)/shard_map/psum | solution.py:32
  483.9 3.7 copy-start.5
  497.7 3.4 copy-start.2
Sparse Core Ops, SparseCore 0:
  8.9 15.6 all-gather.2
  26.1 10.2 all-gather.4
  41.9 127.0 all-reduce.4
  196.4 125.3 all-reduce.6
  358.6 125.3 all-reduce.8
  509.5 125.3 all-reduce.10
where the time goes:
time: 675 us; the launch traced here: 666 us
  waiting for transfers between devices  519 us (77%)
  matrix products  105 us (16%)
  local copies, waits for them, and re-layouts  28.6 us (4%)
  between operations  14 us (2%)
    psum x4, waiting for transfers between devices, body(): totals = lax.psum(partial_proj, 'row')  501 us
    dot_general x8, matrix products, matmul(): jnp.dot(left, right, precision=lax.Precision.HIGHEST, preferred_element_t...  69.1 us
    dot_general x4, matrix products, project(): lax.dot_general(left, right, (((0,), (0,)), ((), ())), precision=lax.Prec...  35.5 us
    unnamed x15, local copies, waits for them, and re-layouts  19.4 us
    all_gather x1, waiting for transfers between devices, body(): lax.all_gather(reflectors, 'col', axis=2, tiled=True)  16.6 us
  transfers between devices with their start and end apart: 6, of which 5 were waited for; matrix products, arithmetic and copies ran while one was open for 3% of the time, Pallas kernels for 0%

commit v1 on v0

v1 whole, which is shorter than its diff:
```python
import functools

import jax
import jax.numpy as jnp
from jax import lax
from jax.experimental import pallas as pl
from jax.experimental.pallas import tpu as pltpu
from jax.sharding import PartitionSpec as P

LANES = 128
VMEM_LIMIT = 48 * 1024 * 1024


def halves(value):
    high = value.astype(jnp.bfloat16)
    low = (value - high.astype(jnp.float32)).astype(jnp.bfloat16)
    return high, low


def dot(left, right):
    return jnp.dot(left, right, preferred_element_type=jnp.float32)


def dot3(left_high, left_low, right):
    high, low = halves(right)
    return dot(left_high, high) + (dot(left_high, low) + dot(left_low, high))


def exact(left, right):
    return jnp.dot(left, right, precision=lax.Precision.HIGHEST, preferred_element_type=jnp.float32)


def reversed_bits(value, count):
    return sum(((value >> bit) & 1) << (count - 1 - bit) for bit in range(count))


def params(vmem=VMEM_LIMIT):
    return pltpu.CompilerParams(vmem_limit_bytes=vmem)


def pair_table(slots):
    me = lax.axis_index("row") % slots
    half = slots // 2
    count = half.bit_length() - 1
    table = [(me >> 1) ^ reversed_bits(step, count) for step in range(half)]
    return jnp.stack(table + [me & 1]).astype(jnp.int32)


def project_kernel(half, table, blocks_ref, slab_ref, keep0, send0, keep1, send1, high_ref, low_ref):
    step = pl.program_id(0)

    @pl.when(step == 0)
    def _():
        for position in range(2):
            high, low = halves(blocks_ref[position].T)
            high_ref[pl.ds(position * LANES, LANES)] = high
            low_ref[pl.ds(position * LANES, LANES)] = low

    proj = dot3(high_ref[...], low_ref[...], slab_ref[...])
    odd = table[half] == 1
    left, right = proj[:, :LANES], proj[:, LANES:]
    near = jnp.where(odd, right, left)
    far = jnp.where(odd, left, right)
    keep0[0] = near[:LANES]
    send0[0] = far[:LANES]

    @pl.when(step < half // 2)
    def _():
        keep1[0, 0] = near[LANES:]
        keep1[1, 0] = far[LANES:]

    @pl.when(step >= half // 2)
    def _():
        send1[0, 0] = near[LANES:]
        send1[1, 0] = far[LANES:]


def project(table, blocks, first, slab, slots, name):
    rows, columns = slab.shape
    half, quarter = slots // 2, slots // 4
    kind0 = jax.ShapeDtypeStruct((half, LANES, LANES), jnp.float32)
    kind1 = jax.ShapeDtypeStruct((2, quarter, LANES, LANES), jnp.float32)
    spec0 = pl.BlockSpec((1, LANES, LANES), lambda j, t: (j, 0, 0))
    keep1 = pl.BlockSpec((2, 1, LANES, LANES), lambda j, t: (0, jnp.minimum(j, quarter - 1), 0, 0))
    send1 = pl.BlockSpec((2, 1, LANES, LANES), lambda j, t: (0, jnp.maximum(j - quarter, 0), 0, 0))
    out = pl.pallas_call(
        functools.partial(project_kernel, half),
        grid_spec=pltpu.PrefetchScalarGridSpec(
            num_scalar_prefetch=1,
            grid=(half,),
            in_specs=[
                pl.BlockSpec((2, rows, LANES), lambda j, t: (first // 2, 0, 0)),
                pl.BlockSpec((rows, 2 * LANES), lambda j, t: (0, t[j])),
            ],
            out_specs=[spec0, spec0, keep1, send1],
            scratch_shapes=[pltpu.VMEM((2 * LANES, rows), jnp.bfloat16)] * 2,
        ),
        out_shape=[kind0, kind0, kind1, kind1],
        compiler_params=params(),
        cost_estimate=pl.CostEstimate(
            flops=3 * 2 * 2 * LANES * rows * columns, bytes_accessed=4 * rows * columns, transcendentals=0
        ),
        name=name,
    )(table, blocks, slab)
    flat = lambda x: x.reshape(half, LANES, LANES)
    return (out[0], out[1]), (flat(out[2]), flat(out[3]))


def swap(value, bit):
    count = lax.axis_size("row")
    return lax.ppermute(value, "row", [(source, source ^ (1 << bit)) for source in range(count)])


def bits_of(kind, slots):
    order = list(range(slots.bit_length() - 1))
    if kind:
        order[0], order[1] = order[1], order[0]
    return order


def reduce_scatter(pair, kind, slots):
    keep, send = pair
    order = bits_of(kind, slots)
    for bit in order[:-1]:
        got = swap(send, bit)
        half = keep.shape[0] // 2
        keep, send = keep[:half] + got[:half], keep[half:] + got[half:]
    total = keep + swap(send, order[-1])
    for bit in range(len(order), lax.axis_size("row").bit_length() - 1):
        total = total + swap(total, bit)
    return total


def all_gather(block, kind, slots):
    for bit in reversed(bits_of(kind, slots)):
        block = jnp.concatenate([block, swap(block, bit)])
    return block


def solve_kernel(panel, *refs):
    proj0, proj1, factor, gram = refs[:4]
    before, (out0, out1) = refs[4 : 4 + 2 * panel], refs[4 + 2 * panel :]
    proj = jnp.concatenate([proj0[0], proj1[0]])
    if panel:
        proj = proj - exact(gram[...], jnp.concatenate([ref[0] for ref in before]))
    weights = exact(factor[0], proj)
    out0[0] = weights[:LANES]
    out1[0] = weights[LANES:]


def solve(panel, proj, factors, gram, before):
    size = factors.shape[-1]
    block = pl.BlockSpec((1, LANES, LANES), lambda j: (0, 0, 0))
    width = max(panel, 1) * size
    at = panel * (panel - 1) // 2 * size
    return pl.pallas_call(
        functools.partial(solve_kernel, panel),
        grid=(1,),
        in_specs=[
            block,
            block,
            pl.BlockSpec((1, size, size), lambda j: (panel, 0, 0)),
            pl.BlockSpec((size, width), lambda j: (0, 0)),
        ]
        + [block] * len(before),
        out_specs=[block, block],
        out_shape=[jax.ShapeDtypeStruct((1, LANES, LANES), jnp.float32)] * 2,
        compiler_params=params(),
        name=f"solve_panel{panel}",
    )(*proj, factors, gram[:, at : at + width], *before)


def update_kernel(half, kinds, table, blocks0, blocks1, slab_ref, *rest):
    weights, (out_ref, high_ref, low_ref) = rest[:4], rest[4:]

    @pl.when(pl.program_id(0) == 0)
    def _():
        for position, block in enumerate([blocks0[0], blocks0[1], blocks1[0], blocks1[1]]):
            high, low = halves(block)
            high_ref[:, pl.ds(position * LANES, LANES)] = high
            low_ref[:, pl.ds(position * LANES, LANES)] = low

    odd = table[half] == 1
    near = jnp.concatenate([ref[0, 0] if kind == 0 else ref[0, 0, 0] for ref, kind in zip(weights, kinds)])
    far = jnp.concatenate([ref[1, 0] if kind == 0 else ref[0, 1, 0] for ref, kind in zip(weights, kinds)])
    both = jnp.concatenate([jnp.where(odd, far, near), jnp.where(odd, near, far)], axis=1)
    out_ref[...] = slab_ref[...] - dot3(high_ref[...], low_ref[...], both)


def update(table, blocks0, blocks1, first, slab, weights, kinds, slots, name):
    rows, columns = slab.shape
    half, quarter = slots // 2, slots // 4
    column = pl.BlockSpec((rows, 2 * LANES), lambda j, t: (0, t[j]))
    blocks = pl.BlockSpec((2, rows, LANES), lambda j, t: (first // 2, 0, 0))
    specs = [
        pl.BlockSpec((2, 1, LANES, LANES), lambda j, t: (0, j, 0, 0)),
        pl.BlockSpec((1, 2, 1, LANES, LANES), lambda j, t: (j // quarter, 0, j % quarter, 0, 0)),
    ]
    shapes = [(2, half, LANES, LANES), (2, 2, quarter, LANES, LANES)]
    return pl.pallas_call(
        functools.partial(update_kernel, half, kinds),
        grid_spec=pltpu.PrefetchScalarGridSpec(
            num_scalar_prefetch=1,
            grid=(half,),
            in_specs=[blocks, blocks, column] + [specs[kind] for kind in kinds],
            out_specs=column,
            scratch_shapes=[pltpu.VMEM((rows, 4 * LANES), jnp.bfloat16)] * 2,
        ),
        out_shape=jax.ShapeDtypeStruct((rows, columns), jnp.float32),
        compiler_params=params(),
        cost_estimate=pl.CostEstimate(
            flops=3 * 2 * 4 * LANES * rows * columns, bytes_accessed=8 * rows * columns, transcendentals=0
        ),
        name=name,
    )(table, blocks0, blocks1, slab, *[value.reshape(shapes[kind]) for value, kind in zip(weights, kinds)])


def shift(value, step):
    count = lax.axis_size("col")
    return lax.ppermute(value, "col", [((target + step) % count, target) for target in range(count)])


def rotated_gram(own_blocks, blocks):
    parts = []
    for panel in range(1, len(blocks)):
        for other in range(panel):
            parts.append(
                lax.dot_general(
                    own_blocks[panel], blocks[other], (((0,), (0,)), ((), ())),
                    precision=lax.Precision.HIGH, preferred_element_type=jnp.float32,
                )
            )
    return lax.psum(jnp.concatenate(parts, axis=1), "row")


def body(eigvecs, reflectors, factors):
    panels, _, width = reflectors.shape
    size = factors.shape[-1]
    others = size // width
    slots = min(lax.axis_size("row"), eigvecs.shape[1] // LANES)
    table = pair_table(slots)

    pieces = [reflectors] + [shift(reflectors, step) for step in range(1, others)]
    per = others // 2
    join = lambda parts: parts[0] if len(parts) == 1 else jnp.concatenate(parts, axis=2)
    sides = [join(pieces[:per]), join(pieces[per:])]
    factor_rows = jnp.concatenate([factors] + [shift(factors, step) for step in range(1, others)], axis=1)
    start = lax.axis_index("col") * width
    factors = lax.dynamic_slice_in_dim(jnp.concatenate([factor_rows, factor_rows], axis=2), start, size, axis=2)

    chunks = {}
    for first in range(0, panels, 2):
        for side in range(2):
            made = project(table, sides[side], first, eigvecs, slots, f"project_side{side}_panels{first}")
            for kind in range(2):
                chunks[first + kind, side] = (made[kind], kind)

    blocks = [jnp.concatenate([sides[0][panel], sides[1][panel]], axis=1) for panel in range(panels)]
    own = rotated_gram([reflectors[panel] for panel in range(panels)], blocks)
    groups = own.shape[1] // size
    rows = [own]
    for step in range(1, others):
        part = shift(own, step).reshape(width, groups, size)
        rows.append(jnp.roll(part, step * width, axis=2).reshape(width, groups * size))
    gram = jnp.concatenate(rows)

    sums = {at: reduce_scatter(pair, kind, slots) for at, (pair, kind) in chunks.items()}
    before, slab = [], eigvecs
    gathered = {}
    for panel in range(panels):
        weights = solve(panel, [sums[panel, 0], sums[panel, 1]], factors, gram, before)
        before = before + list(weights)
        for side in range(2):
            kind = chunks[panel, side][1]
            gathered[panel, side] = all_gather(weights[side], kind, slots)
    for first in range(0, panels, 2):
        at = [(first, 0), (first + 1, 0), (first, 1), (first + 1, 1)]
        slab = update(
            table, sides[0], sides[1], first, slab, [gathered[key] for key in at], [chunks[key][1] for key in at],
            slots, f"update_panels{first}",
        )
    return slab


def solution(mesh):
    in_specs = (P("row", "col"), P(None, "row", "col"), P(None, "col", None))
    out_specs = P("row", "col")
    return jax.shard_map(body, mesh=mesh, in_specs=in_specs, out_specs=out_specs, check_vma=False)
```

time: 675 us -> 400 us (0.59); the launches traced: 666 us -> 398 us
  waiting for transfers between devices: 519 us -> 207 us
  matrix products: 105 us -> 7.54 us
  starting transfers between devices: 0.2 us -> 77.8 us
  Pallas kernels: 0 us -> 72.3 us
  local copies, waits for them, and re-layouts: 28.6 us -> 8.33 us
  other arithmetic: 0 us -> 11.1 us
    psum x4 -> x1, waiting for transfers between devices: 501 us -> 84.7 us  [rotated_gram(): return lax.psum(jnp.concatenate(parts, axis=1), 'row')]
    ppermute x0 -> x67, waiting for transfers between devices: none -> 122 us  [the longest x64 122 us: swap(): lax.ppermute(value, 'row', [(source, source ^ 1 << bit) for source in ran...]
    dot_general x12 -> x6, matrix products: 105 us -> 7.54 us  [rotated_gram(): lax.dot_general(own_blocks[panel], blocks[other], (((0,), (0,)), ((), ())...]
    ppermute x0 -> x67, starting transfers between devices: none -> 77.8 us  [the longest x64 77.3 us: swap(): lax.ppermute(value, 'row', [(source, source ^ 1 << bit) for source in ran...]
    pallas_call x0 -> x10, Pallas kernels: none -> 72.3 us  [the longest x4 39.5 us: project(): pl.pallas_call(functools.partial(project_kernel, half), grid_spec=pltpu.P...]
    all_gather x2 -> x0, waiting for transfers between devices: 16.6 us -> none  [the longest x1 16.6 us: body(): lax.all_gather(reflectors, 'col', axis=2, tiled=True)]
    unnamed x15 -> x50, local copies, waits for them, and re-layouts: 19.4 us -> 3.58 us
    sub x1 -> x0, local copies, waits for them, and re-layouts: 9.12 us -> none  [body(): slab = slab - matmul(reflect_block, weights)]
  transfers between devices with their start and end apart: 6 -> 68, of which waited for: 5 -> 33; matrix products, arithmetic and copies ran while one was open for 3% -> 4% of each run, Pallas kernels for 0% -> 8%
where the time goes in v1:
time: 400 us; the launch traced here: 398 us
  waiting for transfers between devices  207 us (52%)
  starting transfers between devices  77.8 us (19%)
  Pallas kernels  72.3 us (18%)
  between operations  14.2 us (4%)
  other arithmetic  11.1 us (3%)
  local copies, waits for them, and re-layouts  8.33 us (2%)
  matrix products  7.54 us (2%)
    ppermute x64, waiting for transfers between devices, swap(): lax.ppermute(value, 'row', [(source, source ^ 1 << bit) for source in ran...  122 us
    psum x1, waiting for transfers between devices, rotated_gram(): return lax.psum(jnp.concatenate(parts, axis=1), 'row')  84.7 us
    ppermute x64, starting transfers between devices, swap(): lax.ppermute(value, 'row', [(source, source ^ 1 << bit) for source in ran...  77.3 us
    pallas_call x4, Pallas kernels, project(): pl.pallas_call(functools.partial(project_kernel, half), grid_spec=pltpu.P...  39.5 us
    pallas_call x2, Pallas kernels, update(): pl.pallas_call(functools.partial(update_kernel, half, kinds), grid_spec=p...  28.5 us
    add x24, other arithmetic, reduce_scatter(): keep, send = (keep[:half] + got[:half], keep[half:] + got[half:])  8.07 us
  transfers between devices with their start and end apart: 68, of which 33 were waited for; matrix products, arithmetic and copies ran while one was open for 4% of the time, Pallas kernels for 8%

profile of v1, /device:TPU:0, one launch (start us, length us, event | category | flops | bytes accessed | tf_op | source)
XLA Modules:
  0.0 398.1 jit_solution(13732231638745603474)
XLA Ops:
  8.7 9.9 %project_side0_panels0.1 = (f32[8,128,128]{2,1,0:T(8,128)S(1)}, f32[8,128,128]{2,1,0:T(8,128)}, f32[2,4,128,128]{3,2,1,0:T(8,128)S(1)}, f32[2,4,128,128]{3,2,1,0:T(8,128)}) custom-call(s32[9]{0:T(128)S(1)} %stack.39.table, f32[4,1024,128]{2,1,0:T(8,128)S(1)} %copy-done, f32[1024,2048]{1,0:T(8,128)} %slab_ref.9), custom_call_target="tpu_custom_call" | custom-call | flops 3221225472 | bytes 8388608 | tf_op jit(solution)/shard_map/project_side0_panels0/pallas_call | solution.py:86
  18.6 2.9 collective-permute-start.1
  23.1 9.2 %project_side0_panels2.1 = (f32[8,128,128]{2,1,0:T(8,128)S(1)}, f32[8,128,128]{2,1,0:T(8,128)S(1)}, f32[2,4,128,128]{3,2,1,0:T(8,128)S(1)}, f32[2,4,128,128]{3,2,1,0:T(8,128)S(1)}) custom-call(s32[9]{0:T(128)S(1)} %stack.39.table, f32[4,1024,128]{2,1,0:T(8,128)S(1)} %copy-done, f32[1024,2048]{1,0:T(8,128)} %slab_ref.9), custom_call_target="tpu_custom_call" | custom-call | flops 3221225472 | bytes 8388608 | tf_op jit(solution)/shard_map/project_side0_panels2/pallas_call | solution.py:86
  34.1 2.3 collective-permute-start.47
  38.9 6.9 %collective-permute-done.35 = f32[8,128,128]{2,1,0:T(8,128)} collective-permute-done((f32[8,128,128]{2,1,0:T(8,128)S(1)}, f32[8,128,128]{2,1,0:T(8,128)}, u32[]{:S(2)}, u32[]{:S(2)}) %collective-permute-start.35) | collective-permute-done | bytes 524320 | tf_op jit(solution)/shard_map/ppermute | solution.py:111
  60.8 2.6 collective-permute-start.4
  64.2 2.6 collective-permute-start.18
  71.8 3.5 collective-permute-done.38
  80.1 10.3 %project_side1_panels2.1 = (f32[8,128,128]{2,1,0:T(8,128)S(1)}, f32[8,128,128]{2,1,0:T(8,128)}, f32[2,4,128,128]{3,2,1,0:T(8,128)S(1)}, f32[2,4,128,128]{3,2,1,0:T(8,128)}) custom-call(s32[9]{0:T(128)S(1)} %stack.39.table, f32[4,1024,128]{2,1,0:T(8,128)} %collective-permute-done.blocks_ref.blocks1, f32[1024,2048]{1,0:T(8,128)} %slab_ref.9), custom_call_target="tpu_custom_call" | custom-call | flops 3221225472 | bytes 8388608 | tf_op jit(solution)/shard_map/project_side1_panels2/pallas_call | solution.py:86
  94.4 10.2 %project_side1_panels0.1 = (f32[8,128,128]{2,1,0:T(8,128)S(1)}, f32[8,128,128]{2,1,0:T(8,128)}, f32[2,4,128,128]{3,2,1,0:T(8,128)S(1)}, f32[2,4,128,128]{3,2,1,0:T(8,128)S(1)}) custom-call(s32[9]{0:T(128)S(1)} %stack.39.table, f32[4,1024,128]{2,1,0:T(8,128)} %collective-permute-done.blocks_ref.blocks1, f32[1024,2048]{1,0:T(8,128)} %slab_ref.9), custom_call_target="tpu_custom_call" | custom-call | flops 3221225472 | bytes 8388608 | tf_op jit(solution)/shard_map/project_side1_panels0/pallas_call | solution.py:86
  116.5 8.4 %collective-permute-done.5 = f32[8,128,128]{2,1,0:T(8,128)} collective-permute-done((f32[8,128,128]{2,1,0:T(8,128)}, f32[8,128,128]{2,1,0:T(8,128)}, u32[]{:S(2)}, u32[]{:S(2)}) %collective-permute-start.5) | collective-permute-done | bytes 524320 | tf_op jit(solution)/shard_map/ppermute | solution.py:111
  129.1 3.3 collective-permute-done.40
  135.9 2.1 collective-permute-start.21
  138.0 84.7 %all-reduce.2.cloned.1.call-done = f32[128,1536]{1,0:T(8,128)} async-done(((f32[128,1536]{1,0:T(8,128)}), f32[128,1536]{1,0:T(8,128)}) %all-reduce.2.cloned.1.call-update) | async-done | bytes 786448 | tf_op jit(solution)/shard_map/psum | solution.py:233
  228.8 5.1 %collective-permute-done.42 = f32[1,128,128]{2,1,0:T(8,128)S(1)} collective-permute-done((f32[1,128,128]{2,1,0:T(8,128)S(1)}, f32[1,128,128]{2,1,0:T(8,128)S(1)}, u32[]{:S(2)}, u32[]{:S(2)}) %collective-permute-start.42) | collective-permute-done | bytes 65568 | tf_op jit(solution)/shard_map/ppermute | solution.py:111
  241.2 2.9 collective-permute-start.27
  248.2 2.9 collective-permute-start.55
  251.3 2.9 collective-permute-start.59
  254.4 9.3 %collective-permute-done.31 = f32[1,128,128]{2,1,0:T(8,128)S(1)} collective-permute-done((f32[1,128,128]{2,1,0:T(8,128)S(1)}, f32[1,128,128]{2,1,0:T(8,128)S(1)}, u32[]{:S(2)}, u32[]{:S(2)}) %collective-permute-start.31) | collective-permute-done | bytes 65568 | tf_op jit(solution)/shard_map/ppermute | solution.py:111
  263.7 5.4 %collective-permute-done.23 = f32[1,128,128]{2,1,0:T(8,128)S(1)} collective-permute-done((f32[1,128,128]{2,1,0:T(8,128)S(1)}, f32[1,128,128]{2,1,0:T(8,128)S(1)}, u32[]{:S(2)}, u32[]{:S(2)}) %collective-permute-start.23) | collective-permute-done | bytes 65568 | tf_op jit(solution)/shard_map/ppermute | solution.py:111
  273.6 4.7 %collective-permute-done.28 = f32[2,128,128]{2,1,0:T(8,128)S(1)} collective-permute-done((f32[2,128,128]{2,1,0:T(8,128)S(1)}, f32[2,128,128]{2,1,0:T(8,128)S(1)}, u32[]{:S(2)}, u32[]{:S(2)}) %collective-permute-start.28) | collective-permute-done | bytes 131104 | tf_op jit(solution)/shard_map/ppermute | solution.py:111
  280.4 9.1 %collective-permute-done.32 = f32[2,128,128]{2,1,0:T(8,128)S(1)} collective-permute-done((f32[2,128,128]{2,1,0:T(8,128)S(1)}, f32[2,128,128]{2,1,0:T(8,128)S(1)}, u32[]{:S(2)}, u32[]{:S(2)}) %collective-permute-start.32) | collective-permute-done | bytes 131104 | tf_op jit(solution)/shard_map/ppermute | solution.py:111
  289.5 2.8 collective-permute-done.24
  298.3 8.9 %collective-permute-done.29 = f32[4,128,128]{2,1,0:T(8,128)S(1)} collective-permute-done((f32[4,128,128]{2,1,0:T(8,128)S(1)}, f32[4,128,128]{2,1,0:T(8,128)S(1)}, u32[]{:S(2)}, u32[]{:S(2)}) %collective-permute-start.29) | collective-permute-done | bytes 262176 | tf_op jit(solution)/shard_map/ppermute | solution.py:111
  314.1 4.2 %collective-permute-done.61 = f32[4,128,128]{2,1,0:T(8,128)S(1)} collective-permute-done((f32[4,128,128]{2,1,0:T(8,128)S(1)}, f32[4,128,128]{2,1,0:T(8,128)S(1)}, u32[]{:S(2)}, u32[]{:S(2)}) %collective-permute-start.61) | collective-permute-done | bytes 262176 | tf_op jit(solution)/shard_map/ppermute | solution.py:111
  322.3 7.3 %collective-permute-done.58 = f32[8,128,128]{2,1,0:T(8,128)S(1)} collective-permute-done((f32[8,128,128]{2,1,0:T(8,128)S(1)}, f32[8,128,128]{2,1,0:T(8,128)S(1)}, u32[]{:S(2)}, u32[]{:S(2)}) %collective-permute-start.58) | collective-permute-done | bytes 524320 | tf_op jit(solution)/shard_map/ppermute | solution.py:111
  331.0 9.9 %collective-permute-done.66 = f32[8,128,128]{2,1,0:T(8,128)S(1)} collective-permute-done((f32[8,128,128]{2,1,0:T(8,128)S(1)}, f32[8,128,128]{2,1,0:T(8,128)S(1)}, u32[]{:S(2)}, u32[]{:S(2)}) %collective-permute-start.66) | collective-permute-done | bytes 524320 | tf_op jit(solution)/shard_map/ppermute | solution.py:111
  344.4 7.7 %collective-permute-done.26 = f32[8,128,128]{2,1,0:T(8,128)S(1)} collective-permute-done((f32[8,128,128]{2,1,0:T(8,128)S(1)}, f32[8,128,128]{2,1,0:T(8,128)S(1)}, u32[]{:S(2)}, u32[]{:S(2)}) %collective-permute-start.26) | collective-permute-done | bytes 524320 | tf_op jit(solution)/shard_map/ppermute | solution.py:111
  352.1 7.4 %collective-permute-done.34 = f32[8,128,128]{2,1,0:T(8,128)S(1)} collective-permute-done((f32[8,128,128]{2,1,0:T(8,128)S(1)}, f32[8,128,128]{2,1,0:T(8,128)S(1)}, u32[]{:S(2)}, u32[]{:S(2)}) %collective-permute-start.34) | collective-permute-done | bytes 524320 | tf_op jit(solution)/shard_map/ppermute | solution.py:111
  359.7 3.1 collective-permute-done.30
  362.8 14.4 %update_panels0.1.slab_ref = f32[1024,2048]{1,0:T(8,128)} custom-call(s32[9]{0:T(128)S(1)} %stack.39.table, f32[4,1024,128]{2,1,0:T(8,128)} %blocks0.3, f32[4,1024,128]{2,1,0:T(8,128)} %collective-permute-done.blocks_ref.blocks1, f32[1024,2048]{1,0:T(8,128)} %slab_ref.9, f32[2,8,128,128]{3,2,1,0:T(8,128)S(1)} %bitcast.86, ...), custom_call_target="tpu_custom_call" | custom-call | flops 6442450944 | bytes 16777216 | tf_op jit(solution)/shard_map/update_panels0/pallas_call | solution.py:200
  377.2 14.1 %update_panels2.1 = f32[1024,2048]{1,0:T(8,128)} custom-call(s32[9]{0:T(128)S(1)} %stack.39.table, f32[4,1024,128]{2,1,0:T(8,128)} %blocks0.3, f32[4,1024,128]{2,1,0:T(8,128)} %collective-permute-done.blocks_ref.blocks1, f32[1024,2048]{1,0:T(8,128)} %update_panels0.1.slab_ref, f32[2,8,128,128]{3,2,1,0:T(8,128)S(1)} %bitcast.90, ...), custom_call_target="tpu_custom_call" | custom-call | flops 6442450944 | bytes 16777216 | tf_op jit(solution)/shard_map/update_panels2/pallas_call | solution.py:200
  (246 shorter events, 103.1 us)
Async XLA Ops:
  6.5 216.1 %all-reduce.2.cloned.1.call-start = ((), (), s32[]{:S(2)}) async-start(), calls=%async_computation | async-start | bytes 1572864 | tf_op jit(solution)/shard_map/psum | solution.py:233
  6.5 44.9 %collective-permute-start.9 = (f32[4,128,256]{2,1,0:T(8,128)}, f32[4,128,256]{2,1,0:T(8,128)}, u32[]{:S(2)}, u32[]{:S(2)}) collective-permute-start(f32[4,128,256]{2,1,0:T(8,128)} %param.5), channel_id=1, source_target_pairs={{1,0},{0,1},{3,2},{2,3},{5,4},{4,5},{7,6},{6,7},{9,8},{8,9},{11,10... | collective-permute-start | bytes 1572872 | tf_op jit(solution)/shard_map/ppermute | solution.py:220
  7.0 69.1 %collective-permute-start = (f32[4,1024,128]{2,1,0:T(8,128)}, f32[4,1024,128]{2,1,0:T(8,128)}, u32[]{:S(2)}, u32[]{:S(2)}) collective-permute-start(f32[4,1024,128]{2,1,0:T(8,128)} %blocks0.3), channel_id=1, source_target_pairs={{1,0},{0,1},{3,2},{2,3},{5,4},{4,5},{7,6},{6,7},{9,8},{8,9},{11,10... | collective-permute-start | bytes 6291464 | tf_op jit(solution)/shard_map/ppermute | solution.py:220
  21.6 16.0 %collective-permute-start.15 = (f32[8,128,128]{2,1,0:T(8,128)}, f32[8,128,128]{2,1,0:T(8,128)}, u32[]{:S(2)}, u32[]{:S(2)}) collective-permute-start(f32[8,128,128]{2,1,0:T(8,128)} %bitcast.26), channel_id=1, source_target_pairs={{0,4},{2,6},{4,0},{6,2},{8,12},{10,14},{12,8},{14,10},{16,20},{18,... | collective-permute-start | bytes 1572872 | tf_op jit(solution)/shard_map/ppermute | solution.py:111
  37.6 17.3 %collective-permute-start.2 = (f32[4,128,128]{2,1,0:T(8,128)S(1)}, f32[4,128,128]{2,1,0:T(8,128)S(1)}, u32[]{:S(2)}, u32[]{:S(2)}) collective-permute-start(f32[4,128,128]{2,1,0:T(8,128)S(1)} %get-tuple-element.74), channel_id=1, source_target_pairs={{0,4},{2,6},{4,0},{6,2},{8,12},{10,14},{12,8},{14,10},{16,20},{18,... | collective-permute-start | bytes 786440 | tf_op jit(solution)/shard_map/ppermute | solution.py:111
  90.3 21.0 %collective-permute-start.39 = (f32[8,128,128]{2,1,0:T(8,128)}, f32[8,128,128]{2,1,0:T(8,128)}, u32[]{:S(2)}, u32[]{:S(2)}) collective-permute-start(f32[8,128,128]{2,1,0:T(8,128)} %get-tuple-element.44), channel_id=1, source_target_pairs={{0,2},{2,0},{4,6},{6,4},{8,10},{10,8},{12,14},{14,12},{16,18},{18,... | collective-permute-start | bytes 1572872 | tf_op jit(solution)/shard_map/ppermute | solution.py:111
  91.9 22.2 %collective-permute-start.51 = (f32[8,128,128]{2,1,0:T(8,128)}, f32[8,128,128]{2,1,0:T(8,128)}, u32[]{:S(2)}, u32[]{:S(2)}) collective-permute-start(f32[8,128,128]{2,1,0:T(8,128)} %bitcast.39), channel_id=1, source_target_pairs={{0,4},{2,6},{4,0},{6,2},{8,12},{10,14},{12,8},{14,10},{16,20},{18,... | collective-permute-start | bytes 1572872 | tf_op jit(solution)/shard_map/ppermute | solution.py:111
  108.6 16.2 %collective-permute-start.5 = (f32[8,128,128]{2,1,0:T(8,128)}, f32[8,128,128]{2,1,0:T(8,128)}, u32[]{:S(2)}, u32[]{:S(2)}) collective-permute-start(f32[8,128,128]{2,1,0:T(8,128)} %get-tuple-element.32), channel_id=1, source_target_pairs={{0,2},{2,0},{4,6},{6,4},{8,10},{10,8},{12,14},{14,12},{16,18},{18,... | collective-permute-start | bytes 1572872 | tf_op jit(solution)/shard_map/ppermute | solution.py:111
  110.7 17.0 %collective-permute-start.19 = (f32[8,128,128]{2,1,0:T(8,128)S(1)}, f32[8,128,128]{2,1,0:T(8,128)S(1)}, u32[]{:S(2)}, u32[]{:S(2)}) collective-permute-start(f32[8,128,128]{2,1,0:T(8,128)S(1)} %bitcast.93), channel_id=1, source_target_pairs={{0,4},{2,6},{4,0},{6,2},{8,12},{10,14},{12,8},{14,10},{16,20},{18,... | collective-permute-start | bytes 1572872 | tf_op jit(solution)/shard_map/ppermute | solution.py:111
  112.5 19.9 %collective-permute-start.40 = (f32[4,128,128]{2,1,0:T(8,128)S(1)}, f32[4,128,128]{2,1,0:T(8,128)S(1)}, u32[]{:S(2)}, u32[]{:S(2)}) collective-permute-start(f32[4,128,128]{2,1,0:T(8,128)S(1)} %get-tuple-element.64), channel_id=1, source_target_pairs={{0,4},{2,6},{4,0},{6,2},{8,12},{10,14},{12,8},{14,10},{16,20},{18,... | collective-permute-start | bytes 786440 | tf_op jit(solution)/shard_map/ppermute | solution.py:111
  115.2 17.3 %collective-permute-start.52 = (f32[4,128,128]{2,1,0:T(8,128)S(1)}, f32[4,128,128]{2,1,0:T(8,128)S(1)}, u32[]{:S(2)}, u32[]{:S(2)}) collective-permute-start(f32[4,128,128]{2,1,0:T(8,128)S(1)} %get-tuple-element.60), channel_id=1, source_target_pairs={{0,2},{2,0},{4,6},{6,4},{8,10},{10,8},{12,14},{14,12},{16,18},{18,... | collective-permute-start | bytes 786440 | tf_op jit(solution)/shard_map/ppermute | solution.py:111
  132.4 90.2 %collective-permute-start.41 = (f32[2,128,128]{2,1,0:T(8,128)S(1)}, f32[2,128,128]{2,1,0:T(8,128)S(1)}, u32[]{:S(2)}, u32[]{:S(2)}) collective-permute-start(f32[2,128,128]{2,1,0:T(8,128)S(1)} %get-tuple-element.82), channel_id=1, source_target_pairs={{0,8},{2,10},{4,12},{6,14},{8,0},{10,2},{12,4},{14,6},{16,24},{18,... | collective-permute-start | bytes 393224 | tf_op jit(solution)/shard_map/ppermute | solution.py:111
  132.6 91.5 %collective-permute-start.53 = (f32[2,128,128]{2,1,0:T(8,128)S(1)}, f32[2,128,128]{2,1,0:T(8,128)S(1)}, u32[]{:S(2)}, u32[]{:S(2)}) collective-permute-start(f32[2,128,128]{2,1,0:T(8,128)S(1)} %get-tuple-element.78), channel_id=1, source_target_pairs={{0,8},{2,10},{4,12},{6,14},{8,0},{10,2},{12,4},{14,6},{16,24},{18,... | collective-permute-start | bytes 393224 | tf_op jit(solution)/shard_map/ppermute | solution.py:111
  135.9 89.9 %collective-permute-start.7 = (f32[2,128,128]{2,1,0:T(8,128)}, f32[2,128,128]{2,1,0:T(8,128)S(1)}, u32[]{:S(2)}, u32[]{:S(2)}) collective-permute-start(f32[2,128,128]{2,1,0:T(8,128)} %get-tuple-element.90), channel_id=1, source_target_pairs={{0,8},{2,10},{4,12},{6,14},{8,0},{10,2},{12,4},{14,6},{16,24},{18,... | collective-permute-start | bytes 393224 | tf_op jit(solution)/shard_map/ppermute | solution.py:111
  135.9 91.3 %collective-permute-start.21 = (f32[2,128,128]{2,1,0:T(8,128)S(1)}, f32[2,128,128]{2,1,0:T(8,128)S(1)}, u32[]{:S(2)}, u32[]{:S(2)}) collective-permute-start(f32[2,128,128]{2,1,0:T(8,128)S(1)} %get-tuple-element.86), channel_id=1, source_target_pairs={{0,8},{2,10},{4,12},{6,14},{8,0},{10,2},{12,4},{14,6},{16,24},{18,... | collective-permute-start | bytes 393224 | tf_op jit(solution)/shard_map/ppermute | solution.py:111
  246.5 24.8 %collective-permute-start.43 = (f32[1,128,128]{2,1,0:T(8,128)S(1)}, f32[1,128,128]{2,1,0:T(8,128)S(1)}, u32[]{:S(2)}, u32[]{:S(2)}) collective-permute-start(f32[1,128,128]{2,1,0:T(8,128)S(1)} %get-tuple-element.45.refs_8_), channel_id=1, source_target_pairs={{0,16},{2,18},{4,20},{6,22},{8,24},{10,26},{12,28},{14,30},{16,0},... | collective-permute-start | bytes 196616 | tf_op jit(solution)/shard_map/ppermute | solution.py:111
  248.2 20.9 %collective-permute-start.55 = (f32[1,128,128]{2,1,0:T(8,128)S(1)}, f32[1,128,128]{2,1,0:T(8,128)S(1)}, u32[]{:S(2)}, u32[]{:S(2)}) collective-permute-start(f32[1,128,128]{2,1,0:T(8,128)S(1)} %get-tuple-element.51), channel_id=1, source_target_pairs={{0,16},{2,18},{4,20},{6,22},{8,24},{10,26},{12,28},{14,30},{16,0},... | collective-permute-start | bytes 196616 | tf_op jit(solution)/shard_map/ppermute | solution.py:111
  251.1 20.1 %collective-permute-start.63 = (f32[1,128,128]{2,1,0:T(8,128)S(1)}, f32[1,128,128]{2,1,0:T(8,128)S(1)}, u32[]{:S(2)}, u32[]{:S(2)}) collective-permute-start(f32[1,128,128]{2,1,0:T(8,128)S(1)} %get-tuple-element.52), channel_id=1, source_target_pairs={{0,16},{2,18},{4,20},{6,22},{8,24},{10,26},{12,28},{14,30},{16,0},... | collective-permute-start | bytes 196616 | tf_op jit(solution)/shard_map/ppermute | solution.py:111
  251.3 22.1 %collective-permute-start.59 = (f32[1,128,128]{2,1,0:T(8,128)S(1)}, f32[1,128,128]{2,1,0:T(8,128)S(1)}, u32[]{:S(2)}, u32[]{:S(2)}) collective-permute-start(f32[1,128,128]{2,1,0:T(8,128)S(1)} %get-tuple-element.50.refs_9_), channel_id=1, source_target_pairs={{0,16},{2,18},{4,20},{6,22},{8,24},{10,26},{12,28},{14,30},{16,0},... | collective-permute-start | bytes 196616 | tf_op jit(solution)/shard_map/ppermute | solution.py:111
  271.2 22.5 %collective-permute-start.56 = (f32[2,128,128]{2,1,0:T(8,128)S(1)}, f32[2,128,128]{2,1,0:T(8,128)S(1)}, u32[]{:S(2)}, u32[]{:S(2)}) collective-permute-start(f32[2,128,128]{2,1,0:T(8,128)S(1)} %pad_maximum_fusion.32), channel_id=1, source_target_pairs={{0,8},{2,10},{4,12},{6,14},{8,0},{10,2},{12,4},{14,6},{16,24},{18,... | collective-permute-start | bytes 393224 | tf_op jit(solution)/shard_map/ppermute | solution.py:111
  271.3 23.2 %collective-permute-start.64 = (f32[2,128,128]{2,1,0:T(8,128)S(1)}, f32[2,128,128]{2,1,0:T(8,128)S(1)}, u32[]{:S(2)}, u32[]{:S(2)}) collective-permute-start(f32[2,128,128]{2,1,0:T(8,128)S(1)} %pad_maximum_fusion.34), channel_id=1, source_target_pairs={{0,8},{2,10},{4,12},{6,14},{8,0},{10,2},{12,4},{14,6},{16,24},{18,... | collective-permute-start | bytes 393224 | tf_op jit(solution)/shard_map/ppermute | solution.py:111
  273.4 22.8 %collective-permute-start.44 = (f32[2,128,128]{2,1,0:T(8,128)S(1)}, f32[2,128,128]{2,1,0:T(8,128)S(1)}, u32[]{:S(2)}, u32[]{:S(2)}) collective-permute-start(f32[2,128,128]{2,1,0:T(8,128)S(1)} %pad_maximum_fusion.31), channel_id=1, source_target_pairs={{0,8},{2,10},{4,12},{6,14},{8,0},{10,2},{12,4},{14,6},{16,24},{18,... | collective-permute-start | bytes 393224 | tf_op jit(solution)/shard_map/ppermute | solution.py:111
  292.3 16.2 %collective-permute-start.13 = (f32[4,128,128]{2,1,0:T(8,128)S(1)}, f32[4,128,128]{2,1,0:T(8,128)S(1)}, u32[]{:S(2)}, u32[]{:S(2)}) collective-permute-start(f32[4,128,128]{2,1,0:T(8,128)S(1)} %pad_maximum_fusion.19), channel_id=1, source_target_pairs={{0,4},{2,6},{4,0},{6,2},{8,12},{10,14},{12,8},{14,10},{16,20},{18,... | collective-permute-start | bytes 786440 | tf_op jit(solution)/shard_map/ppermute | solution.py:111
  296.7 16.1 %collective-permute-start.45 = (f32[4,128,128]{2,1,0:T(8,128)S(1)}, f32[4,128,128]{2,1,0:T(8,128)S(1)}, u32[]{:S(2)}, u32[]{:S(2)}) collective-permute-start(f32[4,128,128]{2,1,0:T(8,128)S(1)} %pad_maximum_fusion.23), channel_id=1, source_target_pairs={{0,4},{2,6},{4,0},{6,2},{8,12},{10,14},{12,8},{14,10},{16,20},{18,... | collective-permute-start | bytes 786440 | tf_op jit(solution)/shard_map/ppermute | solution.py:111
  310.8 18.8 %collective-permute-start.58 = (f32[8,128,128]{2,1,0:T(8,128)S(1)}, f32[8,128,128]{2,1,0:T(8,128)S(1)}, u32[]{:S(2)}, u32[]{:S(2)}) collective-permute-start(f32[8,128,128]{2,1,0:T(8,128)S(1)} %pad_maximum_fusion.15), channel_id=1, source_target_pairs={{0,4},{2,6},{4,0},{6,2},{8,12},{10,14},{12,8},{14,10},{16,20},{18,... | collective-permute-start | bytes 1572872 | tf_op jit(solution)/shard_map/ppermute | solution.py:111
  312.8 28.1 %collective-permute-start.66 = (f32[8,128,128]{2,1,0:T(8,128)S(1)}, f32[8,128,128]{2,1,0:T(8,128)S(1)}, u32[]{:S(2)}, u32[]{:S(2)}) collective-permute-start(f32[8,128,128]{2,1,0:T(8,128)S(1)} %pad_maximum_fusion.17), channel_id=1, source_target_pairs={{0,4},{2,6},{4,0},{6,2},{8,12},{10,14},{12,8},{14,10},{16,20},{18,... | collective-permute-start | bytes 1572872 | tf_op jit(solution)/shard_map/ppermute | solution.py:111
  318.4 24.2 %collective-permute-start.46 = (f32[8,128,128]{2,1,0:T(8,128)S(1)}, f32[8,128,128]{2,1,0:T(8,128)S(1)}, u32[]{:S(2)}, u32[]{:S(2)}) collective-permute-start(f32[8,128,128]{2,1,0:T(8,128)S(1)} %pad_maximum_fusion.14), channel_id=1, source_target_pairs={{0,2},{2,0},{4,6},{6,4},{8,10},{10,8},{12,14},{14,12},{16,18},{18,... | collective-permute-start | bytes 1572872 | tf_op jit(solution)/shard_map/ppermute | solution.py:111
  320.1 24.2 %collective-permute-start.62 = (f32[8,128,128]{2,1,0:T(8,128)S(1)}, f32[8,128,128]{2,1,0:T(8,128)S(1)}, u32[]{:S(2)}, u32[]{:S(2)}) collective-permute-start(f32[8,128,128]{2,1,0:T(8,128)S(1)} %pad_maximum_fusion.16), channel_id=1, source_target_pairs={{0,2},{2,0},{4,6},{6,4},{8,10},{10,8},{12,14},{14,12},{16,18},{18,... | collective-permute-start | bytes 1572872 | tf_op jit(solution)/shard_map/ppermute | solution.py:111
  321.8 30.2 %collective-permute-start.26 = (f32[8,128,128]{2,1,0:T(8,128)S(1)}, f32[8,128,128]{2,1,0:T(8,128)S(1)}, u32[]{:S(2)}, u32[]{:S(2)}) collective-permute-start(f32[8,128,128]{2,1,0:T(8,128)S(1)} %pad_maximum_fusion.11), channel_id=1, source_target_pairs={{0,4},{2,6},{4,0},{6,2},{8,12},{10,14},{12,8},{14,10},{16,20},{18,... | collective-permute-start | bytes 1572872 | tf_op jit(solution)/shard_map/ppermute | solution.py:111
  329.6 30.0 %collective-permute-start.34 = (f32[8,128,128]{2,1,0:T(8,128)S(1)}, f32[8,128,128]{2,1,0:T(8,128)S(1)}, u32[]{:S(2)}, u32[]{:S(2)}) collective-permute-start(f32[8,128,128]{2,1,0:T(8,128)S(1)} %pad_maximum_fusion.13), channel_id=1, source_target_pairs={{0,4},{2,6},{4,0},{6,2},{8,12},{10,14},{12,8},{14,10},{16,20},{18,... | collective-permute-start | bytes 1572872 | tf_op jit(solution)/shard_map/ppermute | solution.py:111
  340.9 18.8 %collective-permute-start.14 = (f32[8,128,128]{2,1,0:T(8,128)S(1)}, f32[8,128,128]{2,1,0:T(8,128)S(1)}, u32[]{:S(2)}, u32[]{:S(2)}) collective-permute-start(f32[8,128,128]{2,1,0:T(8,128)S(1)} %pad_maximum_fusion.10), channel_id=1, source_target_pairs={{0,2},{2,0},{4,6},{6,4},{8,10},{10,8},{12,14},{14,12},{16,18},{18,... | collective-permute-start | bytes 1572872 | tf_op jit(solution)/shard_map/ppermute | solution.py:111
  342.5 20.2 %collective-permute-start.30 = (f32[8,128,128]{2,1,0:T(8,128)S(1)}, f32[8,128,128]{2,1,0:T(8,128)S(1)}, u32[]{:S(2)}, u32[]{:S(2)}) collective-permute-start(f32[8,128,128]{2,1,0:T(8,128)S(1)} %pad_maximum_fusion.12), channel_id=1, source_target_pairs={{0,2},{2,0},{4,6},{6,4},{8,10},{10,8},{12,14},{14,12},{16,18},{18,... | collective-permute-start | bytes 1572872 | tf_op jit(solution)/shard_map/ppermute | solution.py:111
  (47 other events, 463.5 us)
Sparse Core Ops, SparseCore 0:
  110.8 111.7 all-reduce.1

commit v2 on v1

v2 whole, which is shorter than its diff:
```python
import functools

import jax
import jax.numpy as jnp
from jax import lax
from jax.experimental import pallas as pl
from jax.experimental.pallas import tpu as pltpu
from jax.sharding import PartitionSpec as P

LANES = 128
VMEM_LIMIT = 48 * 1024 * 1024


def halves(value):
    high = value.astype(jnp.bfloat16)
    low = (value - high.astype(jnp.float32)).astype(jnp.bfloat16)
    return high, low


def left_depth(value):
    high, low = halves(value)
    return jnp.concatenate([high, low, high], axis=1)


def right_depth(value):
    high, low = halves(value)
    return jnp.concatenate([high, high, low], axis=0)


def dot(left, right):
    return jnp.dot(left, right, preferred_element_type=jnp.float32)


def exact(left, right):
    return jnp.dot(left, right, precision=lax.Precision.HIGHEST, preferred_element_type=jnp.float32)


def params():
    return pltpu.CompilerParams(vmem_limit_bytes=VMEM_LIMIT)


def order_of(kind, slots):
    order = list(range(slots.bit_length() - 1))
    if kind:
        order[0], order[1] = order[1], order[0]
    return order


def block_of(slot, kind, slots):
    order = order_of(kind, slots)
    return sum(((slot >> (len(order) - 1 - place)) & 1) << bit for place, bit in enumerate(order))


def tables(slots):
    me = lax.axis_index("row") % slots
    half = slots // 2
    pairs = [(me ^ block_of(step, 0, slots)) >> 1 for step in range(half)]
    pieces = [me ^ block_of(slot, 1, slots) for slot in range(slots)]
    return jnp.stack(pairs + [me & 1]).astype(jnp.int32), jnp.stack(pieces).astype(jnp.int32)


def project_kernel(half, side, table, blocks_ref, slab_ref, keep0, send0, keep1, send1, left_ref):
    step = pl.program_id(0)

    @pl.when(step == 0)
    def _():
        for place in range(2):
            left_ref[pl.ds(place * LANES, LANES)] = left_depth(blocks_ref[place ^ side].T)

    proj = dot(left_ref[...], right_depth(slab_ref[...]))
    odd = table[half] == 1
    left, right = proj[:, :LANES], proj[:, LANES:]
    near = jnp.where(odd, right, left)
    far = jnp.where(odd, left, right)
    keep0[0] = near[:LANES]
    send0[0] = far[:LANES]

    @pl.when(step < half // 2)
    def _():
        keep1[0, 0] = near[LANES:]
        keep1[1, 0] = far[LANES:]

    @pl.when(step >= half // 2)
    def _():
        send1[0, 0] = near[LANES:]
        send1[1, 0] = far[LANES:]


def project(table, blocks, side, first, slab, slots):
    rows, columns = slab.shape
    half, quarter = slots // 2, slots // 4
    kind0 = jax.ShapeDtypeStruct((half, LANES, LANES), jnp.float32)
    kind1 = jax.ShapeDtypeStruct((2, quarter, LANES, LANES), jnp.float32)
    spec0 = pl.BlockSpec((1, LANES, LANES), lambda j, t: (j, 0, 0))
    keep1 = pl.BlockSpec((2, 1, LANES, LANES), lambda j, t: (0, jnp.minimum(j, quarter - 1), 0, 0))
    send1 = pl.BlockSpec((2, 1, LANES, LANES), lambda j, t: (0, jnp.maximum(j - quarter, 0), 0, 0))
    out = pl.pallas_call(
        functools.partial(project_kernel, half, side),
        grid_spec=pltpu.PrefetchScalarGridSpec(
            num_scalar_prefetch=1,
            grid=(half,),
            in_specs=[
                pl.BlockSpec((2, rows, LANES), lambda j, t: (first // 2, 0, 0)),
                pl.BlockSpec((rows, 2 * LANES), lambda j, t: (0, t[j])),
            ],
            out_specs=[spec0, spec0, keep1, send1],
            scratch_shapes=[pltpu.VMEM((2 * LANES, 3 * rows), jnp.bfloat16)],
        ),
        out_shape=[kind0, kind0, kind1, kind1],
        compiler_params=params(),
        cost_estimate=pl.CostEstimate(
            flops=3 * 2 * 2 * LANES * rows * columns, bytes_accessed=4 * rows * columns, transcendentals=0
        ),
        name=f"project_side{side}_panels{first}",
    )(table, blocks, slab)
    flat = lambda x: x.reshape(half, LANES, LANES)
    return (out[0], out[1]), (flat(out[2]), flat(out[3]))


def gram_kernel(slots, table, own_ref, side0_ref, side1_ref, keep_ref, send_ref, rows_ref):
    panels, _, width = own_ref.shape
    size = 2 * LANES
    for other in range(panels - 1):
        left = jnp.concatenate([own_ref[panel].T for panel in range(other + 1, panels)])
        right = jnp.concatenate([side0_ref[other], side1_ref[other]], axis=1)
        made = dot(left_depth(left), right_depth(right))
        for place, panel in enumerate(range(other + 1, panels)):
            at = (panel * (panel - 1) // 2 + other) * size
            rows_ref[:, pl.ds(at, size)] = made[place * width : (place + 1) * width]
    tall = width // slots
    for slot in range(slots):
        piece = rows_ref[pl.ds(pl.multiple_of(table[slot] * tall, tall), tall), :]
        out = keep_ref if slot < slots // 2 else send_ref
        for block in range(piece.shape[1] // LANES):
            out[slot % (slots // 2), pl.ds(block * tall, tall)] = piece[:, block * LANES : (block + 1) * LANES]


def gram(pieces, reflectors, sides, slots):
    panels, rows, width = reflectors.shape
    columns = panels * (panels - 1) // 2 * 2 * LANES
    shape = jax.ShapeDtypeStruct((slots // 2, width // slots * (columns // LANES), LANES), jnp.float32)
    return pl.pallas_call(
        functools.partial(gram_kernel, slots),
        grid_spec=pltpu.PrefetchScalarGridSpec(
            num_scalar_prefetch=1,
            grid=(1,),
            in_specs=[pl.BlockSpec(x.shape, lambda j, t: (0, 0, 0)) for x in (reflectors, *sides)],
            out_specs=[pl.BlockSpec(shape.shape, lambda j, t: (0, 0, 0))] * 2,
            scratch_shapes=[pltpu.VMEM((width, columns), jnp.float32)],
        ),
        out_shape=[shape, shape],
        compiler_params=params(),
        cost_estimate=pl.CostEstimate(
            flops=3 * 2 * width * rows * columns, bytes_accessed=12 * rows * panels * LANES, transcendentals=0
        ),
        name="gram_rows",
    )(pieces, reflectors, *sides)


def assemble_kernel(slots, width, table, *refs):
    parts, out = refs[:-1], refs[-1]
    size = 2 * LANES
    tall = width // slots
    for step, part in enumerate(parts):
        for slot in range(slots):
            start = step * width + pl.multiple_of(table[slot] * tall, tall)
            for block in range(out.shape[1] // LANES):
                out[pl.ds(start, tall), pl.ds(block * LANES, LANES)] = part[slot, pl.ds(block * tall, tall)]
        if step:
            for group in range(out.shape[1] // size):
                at = (pl.ds(step * width, width), pl.ds(group * size, size))
                out[at] = pltpu.roll(out[at], step * width, 1)


def assemble(pieces, parts, width, slots):
    tall = width // slots
    columns = parts[0].shape[1] // tall * LANES
    return pl.pallas_call(
        functools.partial(assemble_kernel, slots, width),
        grid_spec=pltpu.PrefetchScalarGridSpec(
            num_scalar_prefetch=1,
            grid=(1,),
            in_specs=[pl.BlockSpec(x.shape, lambda j, t: (0, 0, 0)) for x in parts],
            out_specs=pl.BlockSpec((width * len(parts), columns), lambda j, t: (0, 0)),
        ),
        out_shape=jax.ShapeDtypeStruct((width * len(parts), columns), jnp.float32),
        compiler_params=params(),
        name="assemble_gram",
    )(pieces, *parts)


def swap(value, bit):
    count = lax.axis_size("row")
    return lax.ppermute(value, "row", [(source, source ^ (1 << bit)) for source in range(count)])


def split_sum(keep, got):
    half = keep.shape[0] // 2
    return keep[:half] + got[:half], keep[half:] + got[half:]


def reduce_scatter(pair0, pair1, slots):
    pairs = [pair0, pair1]
    for place in range(2):
        got = [swap(pairs[kind][1], order_of(kind, slots)[place]) for kind in range(2)]
        pairs = [split_sum(pairs[kind][0], got[kind]) if place == 0 else pairs[kind][0] + got[kind] for kind in range(2)]
    total = jnp.concatenate(pairs, axis=1)
    count = slots.bit_length() - 1
    for bit in range(2, count):
        half = total.shape[0] // 2
        total = total[:half] + swap(total[half:], bit)
    for bit in range(count, lax.axis_size("row").bit_length() - 1):
        total = total + swap(total, bit)
    return total


def gather_high(block, slots):
    for bit in reversed(range(2, slots.bit_length() - 1)):
        block = jnp.concatenate([block, swap(block, bit)])
    return block


def gather_low(block, kind, slots):
    for bit in reversed(order_of(kind, slots)[:2]):
        block = jnp.concatenate([block, swap(block, bit)])
    return block


def solve_kernel(panel, *refs):
    proj_ref, factor = refs[:2]
    before, out = refs[3:-1], refs[-1]
    flip = lambda value, at: jnp.concatenate([value[LANES:], value[:LANES]]) if at % 2 else value
    size = 2 * LANES
    proj = flip(proj_ref[0, :size], panel)
    if panel:
        past = jnp.concatenate([flip(ref[0], at) for at, ref in enumerate(before)])
        proj = proj - exact(refs[2][...], past)
    out[0] = flip(exact(factor[0], proj), panel)


def solve(panel, proj, factors, gram_rows, before):
    size = factors.shape[-1]
    block = pl.BlockSpec((1, size, LANES), lambda j: (0, 0, 0))
    width = max(panel, 1) * size
    at = panel * (panel - 1) // 2 * size
    return pl.pallas_call(
        functools.partial(solve_kernel, panel),
        grid=(1,),
        in_specs=[
            pl.BlockSpec(proj.shape, lambda j: (0, 0, 0)),
            pl.BlockSpec((1, size, size), lambda j: (panel, 0, 0)),
            pl.BlockSpec((size, width), lambda j: (0, 0)),
        ]
        + [block] * len(before),
        out_specs=block,
        out_shape=jax.ShapeDtypeStruct((1, size, LANES), jnp.float32),
        compiler_params=params(),
        name=f"solve_panel{panel}",
    )(proj, factors, gram_rows[:, at : at + width], *before)


def update_kernel(half, count, table, *refs):
    blocks, slab_ref, weights = refs[: 2 * count], refs[2 * count], refs[2 * count + 1 : 4 * count + 1]
    out_ref, left_ref = refs[4 * count + 1 :]
    depth = 2 * count * LANES

    @pl.when(pl.program_id(0) == 0)
    def _():
        for place, ref in enumerate(blocks):
            high, low = halves(ref[0])
            for copy, value in enumerate([high, low, high]):
                left_ref[:, pl.ds(copy * depth + place * LANES, LANES)] = value

    odd = table[half] == 1
    near = jnp.concatenate([ref[0, 0, 0] if place % 2 else ref[0, 0] for place, ref in enumerate(weights)])
    far = jnp.concatenate([ref[0, 1, 0] if place % 2 else ref[1, 0] for place, ref in enumerate(weights)])
    both = jnp.concatenate([jnp.where(odd, far, near), jnp.where(odd, near, far)], axis=1)
    out_ref[...] = slab_ref[...] - dot(left_ref[...], right_depth(both))


def update(table, sides, panels, slab, weights, slots):
    rows, columns = slab.shape
    half, quarter = slots // 2, slots // 4
    column = pl.BlockSpec((rows, 2 * LANES), lambda j, t: (0, t[j]))
    block_specs, blocks, weight_specs, values = [], [], [], []
    for panel in panels:
        for kind in range(2):
            block_specs.append(pl.BlockSpec((1, rows, LANES), lambda j, t, panel=panel: (panel, 0, 0)))
            blocks.append(sides[panel % 2 ^ kind])
        weight_specs.append(pl.BlockSpec((2, 1, LANES, LANES), lambda j, t: (0, j, 0, 0)))
        values.append(weights[panel][0].reshape(2, half, LANES, LANES))
        weight_specs.append(pl.BlockSpec((1, 2, 1, LANES, LANES), lambda j, t: (j // quarter, 0, j % quarter, 0, 0)))
        values.append(weights[panel][1].reshape(2, 2, quarter, LANES, LANES))
    depth = 2 * len(panels) * LANES
    return pl.pallas_call(
        functools.partial(update_kernel, half, len(panels)),
        grid_spec=pltpu.PrefetchScalarGridSpec(
            num_scalar_prefetch=1,
            grid=(half,),
            in_specs=block_specs + [column] + weight_specs,
            out_specs=column,
            scratch_shapes=[pltpu.VMEM((rows, 3 * depth), jnp.bfloat16)],
        ),
        out_shape=jax.ShapeDtypeStruct((rows, columns), jnp.float32),
        compiler_params=params(),
        cost_estimate=pl.CostEstimate(
            flops=3 * 2 * depth * rows * columns, bytes_accessed=8 * rows * columns, transcendentals=0
        ),
        name="update_panels" + "".join(map(str, panels)),
    )(table, *blocks, slab, *values)


def shift(value, step):
    count = lax.axis_size("col")
    return lax.ppermute(value, "col", [((target + step) % count, target) for target in range(count)])


def body(eigvecs, reflectors, factors):
    panels, _, width = reflectors.shape
    size = factors.shape[-1]
    others = size // width
    slots = min(lax.axis_size("row"), eigvecs.shape[1] // LANES)
    table, pieces = tables(slots)

    parts = [reflectors] + [shift(reflectors, step) for step in range(1, others)]
    join = lambda some: some[0] if len(some) == 1 else jnp.concatenate(some, axis=2)
    sides = [join(parts[: others // 2]), join(parts[others // 2 :])]
    factor_rows = jnp.concatenate([factors] + [shift(factors, step) for step in range(1, others)], axis=1)
    start = lax.axis_index("col") * width
    factors = lax.dynamic_slice_in_dim(jnp.concatenate([factor_rows, factor_rows], axis=2), start, size, axis=2)

    chunks = {}
    for first in range(0, panels, 2):
        for side in range(2):
            kind0, kind1 = project(table, sides[side], side, first, eigvecs, slots)
            chunks[first + side, 0] = kind0
            chunks[first + 1 - side, 1] = kind1
    gram_pair = gram(pieces, reflectors, sides, slots)
    chunks[0, 1] = tuple(jnp.concatenate([a, b], axis=1) for a, b in zip(chunks[0, 1], gram_pair))

    sums = [reduce_scatter(chunks[panel, 0], chunks[panel, 1], slots) for panel in range(panels)]
    own = gather_low(gather_high(sums[0][:, size:], slots), 1, slots)
    gram_rows = assemble(pieces, [own] + [shift(own, step) for step in range(1, others)], width, slots)

    before, weights = [], []
    for panel in range(panels):
        before.append(solve(panel, sums[panel], factors, gram_rows if panel else factors[0], before))
        high = gather_high(before[panel], slots)
        weights.append([gather_low(high[:, kind * LANES : (kind + 1) * LANES], kind, slots) for kind in range(2)])
    slab = eigvecs
    for some in [list(range(0, panels - 2))] + [[panel] for panel in range(panels - 2, panels)]:
        slab = update(table, sides, some, slab, weights, slots)
    return slab


def solution(mesh):
    in_specs = (P("row", "col"), P(None, "row", "col"), P(None, "col", None))
    out_specs = P("row", "col")
    return jax.shard_map(body, mesh=mesh, in_specs=in_specs, out_specs=out_specs, check_vma=False)
```

time: 400 us -> 304 us (0.76)
  waiting for transfers between devices: 207 us -> 152 us
  starting transfers between devices: 77.8 us -> 51.2 us
  Pallas kernels: 72.3 us -> 86.2 us
  between operations: 14.2 us -> 0.67 us
  matrix products: 7.54 us -> 0 us
  local copies, waits for them, and re-layouts: 8.33 us -> 2.97 us
    psum x1 -> x0, waiting for transfers between devices: 84.7 us -> none  [rotated_gram(): return lax.psum(jnp.concatenate(parts, axis=1), 'row')]
    ppermute x64 -> x52, waiting for transfers between devices: 122 us -> 152 us  [swap(): lax.ppermute(value, 'row', [(source, source ^ 1 << bit) for source in ran...]
    ppermute x64 -> x52, starting transfers between devices: 77.3 us -> 50.6 us  [swap(): lax.ppermute(value, 'row', [(source, source ^ 1 << bit) for source in ran...]
    pallas_call x6 -> x9, Pallas kernels: 68 us -> 81.9 us  [the longest x4 39.1 us: project(): pl.pallas_call(functools.partial(project_kernel, half, side), grid_spec=p...]
    dot_general x6 -> x0, matrix products: 7.54 us -> none  [rotated_gram(): lax.dot_general(own_blocks[panel], blocks[other], (((0,), (0,)), ((), ())...]
    add x32 -> x24, other arithmetic: 8.18 us -> 6.84 us  [the longest x8 3.33 us: reduce_scatter(): pairs[kind][0] + got[kind]]
  transfers between devices with their start and end apart: 68 -> 55, of which waited for: 33 -> 28; matrix products, arithmetic and copies ran while one was open for 4% -> 3% of each run, Pallas kernels for 8% -> 10%
where the time goes in v2:
time: 304 us; the launch traced here: 302 us
  waiting for transfers between devices  152 us (50%)
  Pallas kernels  86.2 us (28%)
  starting transfers between devices  51.2 us (17%)
  other arithmetic  9.54 us (3%)
    ppermute x52, waiting for transfers between devices, swap(): lax.ppermute(value, 'row', [(source, source ^ 1 << bit) for source in ran...  152 us
    ppermute x52, starting transfers between devices, swap(): lax.ppermute(value, 'row', [(source, source ^ 1 << bit) for source in ran...  50.6 us
    pallas_call x4, Pallas kernels, project(): pl.pallas_call(functools.partial(project_kernel, half, side), grid_spec=p...  39.1 us
    pallas_call x3, Pallas kernels, update(): pl.pallas_call(functools.partial(update_kernel, half, len(panels)), grid_...  37.4 us
  transfers between devices with their start and end apart: 55, of which 28 were waited for; matrix products, arithmetic and copies ran while one was open for 3% of the time, Pallas kernels for 10%

profile of v2, /device:TPU:0, one launch (start us, length us, event | category | flops | bytes accessed | tf_op | source)
XLA Modules:
  0.0 302.2 jit_solution(303573675775277072)
XLA Ops:
  0.1 10.3 %project_side0_panels0.1 = (f32[8,128,128]{2,1,0:T(8,128)S(1)}, f32[8,128,128]{2,1,0:T(8,128)}, f32[2,4,128,128]{3,2,1,0:T(8,128)S(1)}, f32[2,4,128,128]{3,2,1,0:T(8,128)}) custom-call(s32[9]{0:T(128)S(1)} %stack.90.table, f32[4,1024,128]{2,1,0:T(8,128)} %refs_1_.1, f32[1024,2048]{1,0:T(8,128)} %slab_ref.7), custom_call_target="tpu_custom_call" | custom-call | flops 3221225472 | bytes 8388608 | tf_op jit(solution)/shard_map/project_side0_panels0/pallas_call | solution.py:97
  11.1 3.0 collective-permute-start.16
  16.1 10.2 %project_side0_panels2.1 = (f32[8,128,128]{2,1,0:T(8,128)S(1)}, f32[8,128,128]{2,1,0:T(8,128)S(1)}, f32[2,4,128,128]{3,2,1,0:T(8,128)S(1)}, f32[2,4,128,128]{3,2,1,0:T(8,128)}) custom-call(s32[9]{0:T(128)S(1)} %stack.90.table, f32[4,1024,128]{2,1,0:T(8,128)} %refs_1_.1, f32[1024,2048]{1,0:T(8,128)} %slab_ref.7), custom_call_target="tpu_custom_call" | custom-call | flops 3221225472 | bytes 8388608 | tf_op jit(solution)/shard_map/project_side0_panels2/pallas_call | solution.py:97
  35.8 7.2 %collective-permute-done.45 = f32[8,128,128]{2,1,0:T(8,128)} collective-permute-done((f32[8,128,128]{2,1,0:T(8,128)}, f32[8,128,128]{2,1,0:T(8,128)}, u32[]{:S(2)}, u32[]{:S(2)}) %collective-permute-start.45) | collective-permute-done | bytes 524320 | tf_op jit(solution)/shard_map/ppermute | solution.py:194
  45.3 4.0 %collective-permute-done.17 = f32[4,128,128]{2,1,0:T(8,128)S(1)} collective-permute-done((f32[4,128,128]{2,1,0:T(8,128)S(1)}, f32[4,128,128]{2,1,0:T(8,128)S(1)}, u32[]{:S(2)}, u32[]{:S(2)}) %collective-permute-start.17) | collective-permute-done | bytes 262176 | tf_op jit(solution)/shard_map/ppermute | solution.py:194
  54.4 9.3 %project_side1_panels2.1 = (f32[8,128,128]{2,1,0:T(8,128)S(1)}, f32[8,128,128]{2,1,0:T(8,128)S(1)}, f32[2,4,128,128]{3,2,1,0:T(8,128)S(1)}, f32[2,4,128,128]{3,2,1,0:T(8,128)S(1)}) custom-call(s32[9]{0:T(128)S(1)} %stack.90.table, f32[4,1024,128]{2,1,0:T(8,128)S(1)} %collective-permute-done.blocks_ref.side1_ref.refs_1_.refs_2_.refs_0_, f32[1024,2048]{1,0:T(8,128)} %slab_ref.7), custom_call_target="tpu_custom_call" | custom-call | flops 3221225472 | bytes 8388608 | tf_op jit(solution)/shard_map/project_side1_panels2/pallas_call | solution.py:97
  65.8 9.3 %project_side1_panels0.1 = (f32[8,128,128]{2,1,0:T(8,128)S(1)}, f32[8,128,128]{2,1,0:T(8,128)S(1)}, f32[2,4,128,128]{3,2,1,0:T(8,128)S(1)}, f32[2,4,128,128]{3,2,1,0:T(8,128)S(1)}) custom-call(s32[9]{0:T(128)S(1)} %stack.90.table, f32[4,1024,128]{2,1,0:T(8,128)S(1)} %collective-permute-done.blocks_ref.side1_ref.refs_1_.refs_2_.refs_0_, f32[1024,2048]{1,0:T(8,128)} %slab_ref.7), custom_call_target="tpu_custom_call" | custom-call | flops 3221225472 | bytes 8388608 | tf_op jit(solution)/shard_map/project_side1_panels0/pallas_call | solution.py:97
  76.8 4.8 %gram_rows.1 = (f32[8,96,128]{2,1,0:T(8,128)S(1)}, f32[8,96,128]{2,1,0:T(8,128)S(1)}) custom-call(s32[16]{0:T(128)S(1)} %stack.107.table, f32[4,1024,128]{2,1,0:T(8,128)} %refs_1_.1, f32[4,1024,128]{2,1,0:T(8,128)} %refs_1_.1, f32[4,1024,128]{2,1,0:T(8,128)S(1)} %collective-permute-done.blocks_ref.side1_ref.refs_1_.refs_2_.refs_0_), custom_call_target="tpu_custom_call" | custom-call | flops 1207959552 | bytes 6291456 | tf_op jit(solution)/shard_map/gram_rows/pallas_call | solution.py:142
  84.4 5.7 %collective-permute-done.14 = f32[8,128,128]{2,1,0:T(8,128)S(1)} collective-permute-done((f32[8,128,128]{2,1,0:T(8,128)S(1)}, f32[8,128,128]{2,1,0:T(8,128)S(1)}, u32[]{:S(2)}, u32[]{:S(2)}) %collective-permute-start.14) | collective-permute-done | bytes 524320 | tf_op jit(solution)/shard_map/ppermute | solution.py:194
  90.6 3.6 %collective-permute-done.34 = f32[4,128,128]{2,1,0:T(8,128)S(1)} collective-permute-done((f32[4,128,128]{2,1,0:T(8,128)S(1)}, f32[4,128,128]{2,1,0:T(8,128)S(1)}, u32[]{:S(2)}, u32[]{:S(2)}) %collective-permute-start.34) | collective-permute-done | bytes 262176 | tf_op jit(solution)/shard_map/ppermute | solution.py:194
  94.3 10.7 %collective-permute-done.3 = f32[8,224,128]{2,1,0:T(8,128)S(1)} collective-permute-done((f32[8,224,128]{2,1,0:T(8,128)S(1)}, f32[8,224,128]{2,1,0:T(8,128)S(1)}, u32[]{:S(2)}, u32[]{:S(2)}) %collective-permute-start.3) | collective-permute-done | bytes 917536 | tf_op jit(solution)/shard_map/ppermute | solution.py:194
  107.3 2.8 collective-permute-done.44
  118.6 13.2 %collective-permute-done.5 = f32[2,352,128]{2,1,0:T(8,128)S(1)} collective-permute-done((f32[2,352,128]{2,1,0:T(8,128)S(1)}, f32[2,352,128]{2,1,0:T(8,128)S(1)}, u32[]{:S(2)}, u32[]{:S(2)}) %collective-permute-start.5) | collective-permute-done | bytes 360480 | tf_op jit(solution)/shard_map/ppermute | solution.py:194
  135.0 12.3 %collective-permute-done.6 = f32[1,352,128]{2,1,0:T(8,128)S(1)} collective-permute-done((f32[1,352,128]{2,1,0:T(8,128)S(1)}, f32[1,352,128]{2,1,0:T(8,128)S(1)}, u32[]{:S(2)}, u32[]{:S(2)}) %collective-permute-start.6) | collective-permute-done | bytes 180256 | tf_op jit(solution)/shard_map/ppermute | solution.py:194
  147.5 3.0 collective-permute-start.19
  152.9 6.0 %collective-permute-done.21 = f32[2,96,128]{2,1,0:T(8,128)S(1)} collective-permute-done((f32[2,96,128]{2,1,0:T(8,128)S(1)}, f32[2,96,128]{2,1,0:T(8,128)S(1)}, u32[]{:S(2)}, u32[]{:S(2)}) %collective-permute-start.21) | collective-permute-done | bytes 98336 | tf_op jit(solution)/shard_map/ppermute | solution.py:194
  159.3 5.4 %collective-permute-done.22 = f32[4,96,128]{2,1,0:T(8,128)S(1)} collective-permute-done((f32[4,96,128]{2,1,0:T(8,128)S(1)}, f32[4,96,128]{2,1,0:T(8,128)S(1)}, u32[]{:S(2)}, u32[]{:S(2)}) %collective-permute-start.22) | collective-permute-done | bytes 196640 | tf_op jit(solution)/shard_map/ppermute | solution.py:194
  167.6 4.9 %collective-permute-done.23 = f32[8,96,128]{2,1,0:T(8,128)S(1)} collective-permute-done((f32[8,96,128]{2,1,0:T(8,128)S(1)}, f32[8,96,128]{2,1,0:T(8,128)S(1)}, u32[]{:S(2)}, u32[]{:S(2)}) %collective-permute-start.23) | collective-permute-done | bytes 393248 | tf_op jit(solution)/shard_map/ppermute | solution.py:194
  174.8 6.6 %collective-permute-done.10 = f32[4,128,128]{2,1,0:T(8,128)S(1)} collective-permute-done((f32[4,128,128]{2,1,0:T(8,128)S(1)}, f32[4,128,128]{2,1,0:T(8,128)S(1)}, u32[]{:S(2)}, u32[]{:S(2)}) %collective-permute-start.10) | collective-permute-done | bytes 262176 | tf_op jit(solution)/shard_map/ppermute | solution.py:194
  186.6 3.5 %collective-permute-done.13 = f32[8,128,128]{2,1,0:T(8,128)S(1)} collective-permute-done((f32[8,128,128]{2,1,0:T(8,128)S(1)}, f32[8,128,128]{2,1,0:T(8,128)S(1)}, u32[]{:S(2)}, u32[]{:S(2)}) %collective-permute-start.13) | collective-permute-done | bytes 524320 | tf_op jit(solution)/shard_map/ppermute | solution.py:194
  190.3 2.9 collective-permute-start.37
  193.2 6.7 %collective-permute-done.49 = f32[1,256,128]{2,1,0:T(8,128)S(1)} collective-permute-done((f32[1,256,128]{2,1,0:T(8,128)S(1)}, f32[1,256,128]{2,1,0:T(8,128)S(1)}, u32[]{:S(2)}, u32[]{:S(2)}) %collective-permute-start.49) | collective-permute-done | bytes 131104 | tf_op jit(solution)/shard_map/ppermute | solution.py:194
  204.9 4.9 %collective-permute-done.50 = f32[2,256,128]{2,1,0:T(8,128)S(1)} collective-permute-done((f32[2,256,128]{2,1,0:T(8,128)S(1)}, f32[2,256,128]{2,1,0:T(8,128)S(1)}, u32[]{:S(2)}, u32[]{:S(2)}) %collective-permute-start.50) | collective-permute-done | bytes 262176 | tf_op jit(solution)/shard_map/ppermute | solution.py:194
  211.5 6.7 %collective-permute-done.38 = f32[2,256,128]{2,1,0:T(8,128)S(1)} collective-permute-done((f32[2,256,128]{2,1,0:T(8,128)S(1)}, f32[2,256,128]{2,1,0:T(8,128)S(1)}, u32[]{:S(2)}, u32[]{:S(2)}) %collective-permute-start.38) | collective-permute-done | bytes 262176 | tf_op jit(solution)/shard_map/ppermute | solution.py:194
  222.7 4.8 %collective-permute-done.41 = f32[4,128,128]{2,1,0:T(8,128)S(1)} collective-permute-done((f32[4,128,128]{2,1,0:T(8,128)S(1)}, f32[4,128,128]{2,1,0:T(8,128)S(1)}, u32[]{:S(2)}, u32[]{:S(2)}) %collective-permute-start.41) | collective-permute-done | bytes 262176 | tf_op jit(solution)/shard_map/ppermute | solution.py:194
  228.3 7.1 %collective-permute-done.39 = f32[4,128,128]{2,1,0:T(8,128)S(1)} collective-permute-done((f32[4,128,128]{2,1,0:T(8,128)S(1)}, f32[4,128,128]{2,1,0:T(8,128)S(1)}, u32[]{:S(2)}, u32[]{:S(2)}) %collective-permute-start.39) | collective-permute-done | bytes 262176 | tf_op jit(solution)/shard_map/ppermute | solution.py:194
  238.3 8.3 %collective-permute-done.54 = f32[8,128,128]{2,1,0:T(8,128)S(1)} collective-permute-done((f32[8,128,128]{2,1,0:T(8,128)S(1)}, f32[8,128,128]{2,1,0:T(8,128)S(1)}, u32[]{:S(2)}, u32[]{:S(2)}) %collective-permute-start.54) | collective-permute-done | bytes 524320 | tf_op jit(solution)/shard_map/ppermute | solution.py:194
  247.4 10.4 %collective-permute-done.42 = f32[8,128,128]{2,1,0:T(8,128)S(1)} collective-permute-done((f32[8,128,128]{2,1,0:T(8,128)S(1)}, f32[8,128,128]{2,1,0:T(8,128)S(1)}, u32[]{:S(2)}, u32[]{:S(2)}) %collective-permute-start.42) | collective-permute-done | bytes 524320 | tf_op jit(solution)/shard_map/ppermute | solution.py:194
  258.0 6.7 %collective-permute-done.30 = f32[8,128,128]{2,1,0:T(8,128)S(1)} collective-permute-done((f32[8,128,128]{2,1,0:T(8,128)S(1)}, f32[8,128,128]{2,1,0:T(8,128)S(1)}, u32[]{:S(2)}, u32[]{:S(2)}) %collective-permute-start.30) | collective-permute-done | bytes 524320 | tf_op jit(solution)/shard_map/ppermute | solution.py:194
  264.9 14.4 %update_panels01.1.refs_2_ = f32[1024,2048]{1,0:T(8,128)} custom-call(s32[9]{0:T(128)S(1)} %stack.90.table, f32[4,1024,128]{2,1,0:T(8,128)} %refs_1_.1, f32[4,1024,128]{2,1,0:T(8,128)} %copy-done, f32[4,1024,128]{2,1,0:T(8,128)} %copy-done, f32[4,1024,128]{2,1,0:T(8,128)} %refs_1_.1, f32[1024,2048]{1,0:T(8,128)} %slab_ref.7, ...), custom_call_target="tpu_custom_call" | custom-call | flops 6442450944 | bytes 16777216 | tf_op jit(solution)/shard_map/update_panels01/pallas_call | solution.py:295
  279.3 11.6 %update_panels2.1.refs_2_ = f32[1024,2048]{1,0:T(8,128)} custom-call(s32[9]{0:T(128)S(1)} %stack.90.table, f32[4,1024,128]{2,1,0:T(8,128)} %refs_1_.1, f32[4,1024,128]{2,1,0:T(8,128)} %copy-done, f32[1024,2048]{1,0:T(8,128)} %update_panels01.1.refs_2_, f32[2,8,128,128]{3,2,1,0:T(8,128)S(1)} %bitcast.57, f32[2,2,4,128,128]{4,3,2,1,0:T(8,128)S(1)} %bitcast.56), custom_call_target="tpu_custom_call" | custom-call | flops 3221225472 | bytes 16777216 | tf_op jit(solution)/shard_map/update_panels2/pallas_call | solution.py:295
  290.9 11.3 %update_panels3.1 = f32[1024,2048]{1,0:T(8,128)} custom-call(s32[9]{0:T(128)S(1)} %stack.90.table, f32[4,1024,128]{2,1,0:T(8,128)S(1)} %copy-done.1, f32[4,1024,128]{2,1,0:T(8,128)} %refs_1_.1, f32[1024,2048]{1,0:T(8,128)} %update_panels2.1.refs_2_, f32[2,8,128,128]{3,2,1,0:T(8,128)S(1)} %bitcast.55, f32[2,2,4,128,128]{4,3,2,1,0:T(8,128)S(1)} %bitcast.54), custom_call_target="tpu_custom_call" | custom-call | flops 3221225472 | bytes 16777216 | tf_op jit(solution)/shard_map/update_panels3/pallas_call | solution.py:295
  (181 shorter events, 70.1 us)
Async XLA Ops:
  11.1 17.4 %collective-permute-start.16 = (f32[8,128,128]{2,1,0:T(8,128)}, f32[8,128,128]{2,1,0:T(8,128)}, u32[]{:S(2)}, u32[]{:S(2)}) collective-permute-start(f32[8,128,128]{2,1,0:T(8,128)} %bitcast.31), channel_id=1, source_target_pairs={{0,4},{2,6},{4,0},{6,2},{8,12},{10,14},{12,8},{14,10},{16,20},{18,... | collective-permute-start | bytes 1572872 | tf_op jit(solution)/shard_map/ppermute | solution.py:194
  14.1 40.3 %collective-permute-start = (f32[4,1024,128]{2,1,0:T(8,128)}, f32[4,1024,128]{2,1,0:T(8,128)S(1)}, u32[]{:S(2)}, u32[]{:S(2)}) collective-permute-start(f32[4,1024,128]{2,1,0:T(8,128)} %refs_1_.1), channel_id=1, source_target_pairs={{1,0},{0,1},{3,2},{2,3},{5,4},{4,5},{7,6},{6,7},{9,8},{8,9},{11,10... | collective-permute-start | bytes 6291464 | tf_op jit(solution)/shard_map/ppermute | solution.py:315
  14.1 18.7 %collective-permute-start.7 = (f32[4,128,256]{2,1,0:T(8,128)}, f32[4,128,256]{2,1,0:T(8,128)}, u32[]{:S(2)}, u32[]{:S(2)}) collective-permute-start(f32[4,128,256]{2,1,0:T(8,128)} %param.5), channel_id=1, source_target_pairs={{1,0},{0,1},{3,2},{2,3},{5,4},{4,5},{7,6},{6,7},{9,8},{8,9},{11,10... | collective-permute-start | bytes 1572872 | tf_op jit(solution)/shard_map/ppermute | solution.py:315
  14.6 15.1 %collective-permute-start.1 = (f32[8,128,128]{2,1,0:T(8,128)}, f32[8,128,128]{2,1,0:T(8,128)}, u32[]{:S(2)}, u32[]{:S(2)}) collective-permute-start(f32[8,128,128]{2,1,0:T(8,128)} %get-tuple-element.24), channel_id=1, source_target_pairs={{0,2},{2,0},{4,6},{6,4},{8,10},{10,8},{12,14},{14,12},{16,18},{18,... | collective-permute-start | bytes 1572872 | tf_op jit(solution)/shard_map/ppermute | solution.py:194
  27.9 15.1 %collective-permute-start.45 = (f32[8,128,128]{2,1,0:T(8,128)}, f32[8,128,128]{2,1,0:T(8,128)}, u32[]{:S(2)}, u32[]{:S(2)}) collective-permute-start(f32[8,128,128]{2,1,0:T(8,128)} %bitcast.41), channel_id=1, source_target_pairs={{0,4},{2,6},{4,0},{6,2},{8,12},{10,14},{12,8},{14,10},{16,20},{18,... | collective-permute-start | bytes 1572872 | tf_op jit(solution)/shard_map/ppermute | solution.py:194
  28.5 16.1 %collective-permute-start.31 = (f32[8,128,128]{2,1,0:T(8,128)}, f32[8,128,128]{2,1,0:T(8,128)S(1)}, u32[]{:S(2)}, u32[]{:S(2)}) collective-permute-start(f32[8,128,128]{2,1,0:T(8,128)} %copy-done.6), channel_id=1, source_target_pairs={{0,2},{2,0},{4,6},{6,4},{8,10},{10,8},{12,14},{14,12},{16,18},{18,... | collective-permute-start | bytes 1572872 | tf_op jit(solution)/shard_map/ppermute | solution.py:194
  29.7 19.5 %collective-permute-start.17 = (f32[4,128,128]{2,1,0:T(8,128)S(1)}, f32[4,128,128]{2,1,0:T(8,128)S(1)}, u32[]{:S(2)}, u32[]{:S(2)}) collective-permute-start(f32[4,128,128]{2,1,0:T(8,128)S(1)} %slice_add_fusion.9), channel_id=1, source_target_pairs={{0,2},{2,0},{4,6},{6,4},{8,10},{10,8},{12,14},{14,12},{16,18},{18,... | collective-permute-start | bytes 786440 | tf_op jit(solution)/shard_map/ppermute | solution.py:194
  32.8 17.5 %collective-permute-start.2 = (f32[4,128,128]{2,1,0:T(8,128)S(1)}, f32[4,128,128]{2,1,0:T(8,128)S(1)}, u32[]{:S(2)}, u32[]{:S(2)}) collective-permute-start(f32[4,128,128]{2,1,0:T(8,128)S(1)} %slice_add_fusion.13), channel_id=1, source_target_pairs={{0,4},{2,6},{4,0},{6,2},{8,12},{10,14},{12,8},{14,10},{16,20},{18,... | collective-permute-start | bytes 786440 | tf_op jit(solution)/shard_map/ppermute | solution.py:194
  63.7 18.5 %collective-permute-start.33 = (f32[8,128,128]{2,1,0:T(8,128)S(1)}, f32[8,128,128]{2,1,0:T(8,128)S(1)}, u32[]{:S(2)}, u32[]{:S(2)}) collective-permute-start(f32[8,128,128]{2,1,0:T(8,128)S(1)} %bitcast.63), channel_id=1, source_target_pairs={{0,4},{2,6},{4,0},{6,2},{8,12},{10,14},{12,8},{14,10},{16,20},{18,... | collective-permute-start | bytes 1572872 | tf_op jit(solution)/shard_map/ppermute | solution.py:194
  65.3 17.3 %collective-permute-start.43 = (f32[8,128,128]{2,1,0:T(8,128)S(1)}, f32[8,128,128]{2,1,0:T(8,128)S(1)}, u32[]{:S(2)}, u32[]{:S(2)}) collective-permute-start(f32[8,128,128]{2,1,0:T(8,128)S(1)} %get-tuple-element.38), channel_id=1, source_target_pairs={{0,2},{2,0},{4,6},{6,4},{8,10},{10,8},{12,14},{14,12},{16,18},{18,... | collective-permute-start | bytes 1572872 | tf_op jit(solution)/shard_map/ppermute | solution.py:194
  75.2 14.9 %collective-permute-start.14 = (f32[8,128,128]{2,1,0:T(8,128)S(1)}, f32[8,128,128]{2,1,0:T(8,128)S(1)}, u32[]{:S(2)}, u32[]{:S(2)}) collective-permute-start(f32[8,128,128]{2,1,0:T(8,128)S(1)} %get-tuple-element.30), channel_id=1, source_target_pairs={{0,2},{2,0},{4,6},{6,4},{8,10},{10,8},{12,14},{14,12},{16,18},{18,... | collective-permute-start | bytes 1572872 | tf_op jit(solution)/shard_map/ppermute | solution.py:194
  81.6 23.4 %collective-permute-start.3 = (f32[8,224,128]{2,1,0:T(8,128)S(1)}, f32[8,224,128]{2,1,0:T(8,128)S(1)}, u32[]{:S(2)}, u32[]{:S(2)}) collective-permute-start(f32[8,224,128]{2,1,0:T(8,128)S(1)} %pad_maximum_fusion.8), channel_id=1, source_target_pairs={{0,4},{2,6},{4,0},{6,2},{8,12},{10,14},{12,8},{14,10},{16,20},{18,... | collective-permute-start | bytes 2752520 | tf_op jit(solution)/shard_map/ppermute | solution.py:194
  82.6 27.4 %collective-permute-start.44 = (f32[4,128,128]{2,1,0:T(8,128)S(1)}, f32[4,128,128]{2,1,0:T(8,128)S(1)}, u32[]{:S(2)}, u32[]{:S(2)}) collective-permute-start(f32[4,128,128]{2,1,0:T(8,128)S(1)} %slice_add_fusion.3), channel_id=1, source_target_pairs={{0,4},{2,6},{4,0},{6,2},{8,12},{10,14},{12,8},{14,10},{16,20},{18,... | collective-permute-start | bytes 786440 | tf_op jit(solution)/shard_map/ppermute | solution.py:194
  90.1 25.2 %collective-permute-start.15 = (f32[4,128,128]{2,1,0:T(8,128)S(1)}, f32[4,128,128]{2,1,0:T(8,128)S(1)}, u32[]{:S(2)}, u32[]{:S(2)}) collective-permute-start(f32[4,128,128]{2,1,0:T(8,128)S(1)} %slice_add_fusion.11), channel_id=1, source_target_pairs={{0,4},{2,6},{4,0},{6,2},{8,12},{10,14},{12,8},{14,10},{16,20},{18,... | collective-permute-start | bytes 786440 | tf_op jit(solution)/shard_map/ppermute | solution.py:194
  110.1 23.5 %collective-permute-start.47 = (f32[2,256,128]{2,1,0:T(8,128)S(1)}, f32[2,256,128]{2,1,0:T(8,128)S(1)}, u32[]{:S(2)}, u32[]{:S(2)}) collective-permute-start(f32[2,256,128]{2,1,0:T(8,128)S(1)} %pad_maximum_fusion.24), channel_id=1, source_target_pairs={{0,8},{2,10},{4,12},{6,14},{8,0},{10,2},{12,4},{14,6},{16,24},{18,... | collective-permute-start | bytes 786440 | tf_op jit(solution)/shard_map/ppermute | solution.py:194
  113.7 18.2 %collective-permute-start.5 = (f32[2,352,128]{2,1,0:T(8,128)S(1)}, f32[2,352,128]{2,1,0:T(8,128)S(1)}, u32[]{:S(2)}, u32[]{:S(2)}) collective-permute-start(f32[2,352,128]{2,1,0:T(8,128)S(1)} %pad_maximum_fusion.23), channel_id=1, source_target_pairs={{0,8},{2,10},{4,12},{6,14},{8,0},{10,2},{12,4},{14,6},{16,24},{18,... | collective-permute-start | bytes 1081352 | tf_op jit(solution)/shard_map/ppermute | solution.py:194
  115.4 32.0 %collective-permute-start.18 = (f32[2,256,128]{2,1,0:T(8,128)S(1)}, f32[2,256,128]{2,1,0:T(8,128)S(1)}, u32[]{:S(2)}, u32[]{:S(2)}) collective-permute-start(f32[2,256,128]{2,1,0:T(8,128)S(1)} %pad_maximum_fusion.26), channel_id=1, source_target_pairs={{0,8},{2,10},{4,12},{6,14},{8,0},{10,2},{12,4},{14,6},{16,24},{18,... | collective-permute-start | bytes 786440 | tf_op jit(solution)/shard_map/ppermute | solution.py:194
  116.4 56.6 %collective-permute-start.36 = (f32[1,256,128]{2,1,0:T(8,128)S(1)}, f32[1,256,128]{2,1,0:T(8,128)S(1)}, u32[]{:S(2)}, u32[]{:S(2)}) collective-permute-start(f32[1,256,128]{2,1,0:T(8,128)S(1)} %slice.300), channel_id=1, source_target_pairs={{0,16},{2,18},{4,20},{6,22},{8,24},{10,26},{12,28},{14,30},{16,0},... | collective-permute-start | bytes 393224 | tf_op jit(solution)/shard_map/ppermute | solution.py:194
  131.9 15.4 %collective-permute-start.6 = (f32[1,352,128]{2,1,0:T(8,128)S(1)}, f32[1,352,128]{2,1,0:T(8,128)S(1)}, u32[]{:S(2)}, u32[]{:S(2)}) collective-permute-start(f32[1,352,128]{2,1,0:T(8,128)S(1)} %slice.277), channel_id=1, source_target_pairs={{0,16},{2,18},{4,20},{6,22},{8,24},{10,26},{12,28},{14,30},{16,0},... | collective-permute-start | bytes 540680 | tf_op jit(solution)/shard_map/ppermute | solution.py:194
  133.7 48.0 %collective-permute-start.48 = (f32[1,256,128]{2,1,0:T(8,128)S(1)}, f32[1,256,128]{2,1,0:T(8,128)S(1)}, u32[]{:S(2)}, u32[]{:S(2)}) collective-permute-start(f32[1,256,128]{2,1,0:T(8,128)S(1)} %slice.311), channel_id=1, source_target_pairs={{0,16},{2,18},{4,20},{6,22},{8,24},{10,26},{12,28},{14,30},{16,0},... | collective-permute-start | bytes 393224 | tf_op jit(solution)/shard_map/ppermute | solution.py:194
  147.5 34.3 %collective-permute-start.19 = (f32[1,256,128]{2,1,0:T(8,128)S(1)}, f32[1,256,128]{2,1,0:T(8,128)S(1)}, u32[]{:S(2)}, u32[]{:S(2)}) collective-permute-start(f32[1,256,128]{2,1,0:T(8,128)S(1)} %slice.288), channel_id=1, source_target_pairs={{0,16},{2,18},{4,20},{6,22},{8,24},{10,26},{12,28},{14,30},{16,0},... | collective-permute-start | bytes 393224 | tf_op jit(solution)/shard_map/ppermute | solution.py:194
  173.2 16.9 %collective-permute-start.13 = (f32[8,128,128]{2,1,0:T(8,128)S(1)}, f32[8,128,128]{2,1,0:T(8,128)S(1)}, u32[]{:S(2)}, u32[]{:S(2)}) collective-permute-start(f32[8,128,128]{2,1,0:T(8,128)S(1)} %pad_maximum_fusion.11), channel_id=1, source_target_pairs={{0,4},{2,6},{4,0},{6,2},{8,12},{10,14},{12,8},{14,10},{16,20},{18,... | collective-permute-start | bytes 1572872 | tf_op jit(solution)/shard_map/ppermute | solution.py:194
  181.4 18.5 %collective-permute-start.11 = (f32[8,128,128]{2,1,0:T(8,128)S(1)}, f32[8,128,128]{2,1,0:T(8,128)S(1)}, u32[]{:S(2)}, u32[]{:S(2)}) collective-permute-start(f32[8,128,128]{2,1,0:T(8,128)S(1)} %pad_maximum_fusion.10), channel_id=1, source_target_pairs={{0,2},{2,0},{4,6},{6,4},{8,10},{10,8},{12,14},{14,12},{16,18},{18,... | collective-permute-start | bytes 1572872 | tf_op jit(solution)/shard_map/ppermute | solution.py:194
  202.7 16.3 %collective-permute-start.26 = (f32[2,256,128]{2,1,0:T(8,128)S(1)}, f32[2,256,128]{2,1,0:T(8,128)S(1)}, u32[]{:S(2)}, u32[]{:S(2)}) collective-permute-start(f32[2,256,128]{2,1,0:T(8,128)S(1)} %pad_maximum_fusion.28), channel_id=1, source_target_pairs={{0,8},{2,10},{4,12},{6,14},{8,0},{10,2},{12,4},{14,6},{16,24},{18,... | collective-permute-start | bytes 786440 | tf_op jit(solution)/shard_map/ppermute | solution.py:194
  219.1 16.3 %collective-permute-start.29 = (f32[4,128,128]{2,1,0:T(8,128)S(1)}, f32[4,128,128]{2,1,0:T(8,128)S(1)}, u32[]{:S(2)}, u32[]{:S(2)}) collective-permute-start(f32[4,128,128]{2,1,0:T(8,128)S(1)} %get-tuple-element.45), channel_id=1, source_target_pairs={{0,2},{2,0},{4,6},{6,4},{8,10},{10,8},{12,14},{14,12},{16,18},{18,... | collective-permute-start | bytes 786440 | tf_op jit(solution)/shard_map/ppermute | solution.py:194
  220.5 16.6 %collective-permute-start.27 = (f32[4,128,128]{2,1,0:T(8,128)S(1)}, f32[4,128,128]{2,1,0:T(8,128)S(1)}, u32[]{:S(2)}, u32[]{:S(2)}) collective-permute-start(f32[4,128,128]{2,1,0:T(8,128)S(1)} %get-tuple-element.46), channel_id=1, source_target_pairs={{0,4},{2,6},{4,0},{6,2},{8,12},{10,14},{12,8},{14,10},{16,20},{18,... | collective-permute-start | bytes 786440 | tf_op jit(solution)/shard_map/ppermute | solution.py:194
  222.6 24.0 %collective-permute-start.54 = (f32[8,128,128]{2,1,0:T(8,128)S(1)}, f32[8,128,128]{2,1,0:T(8,128)S(1)}, u32[]{:S(2)}, u32[]{:S(2)}) collective-permute-start(f32[8,128,128]{2,1,0:T(8,128)S(1)} %pad_maximum_fusion.20), channel_id=1, source_target_pairs={{0,4},{2,6},{4,0},{6,2},{8,12},{10,14},{12,8},{14,10},{16,20},{18,... | collective-permute-start | bytes 1572872 | tf_op jit(solution)/shard_map/ppermute | solution.py:194
  227.6 19.8 %collective-permute-start.52 = (f32[8,128,128]{2,1,0:T(8,128)S(1)}, f32[8,128,128]{2,1,0:T(8,128)S(1)}, u32[]{:S(2)}, u32[]{:S(2)}) collective-permute-start(f32[8,128,128]{2,1,0:T(8,128)S(1)} %pad_maximum_fusion.19), channel_id=1, source_target_pairs={{0,2},{2,0},{4,6},{6,4},{8,10},{10,8},{12,14},{14,12},{16,18},{18,... | collective-permute-start | bytes 1572872 | tf_op jit(solution)/shard_map/ppermute | solution.py:194
  235.4 22.5 %collective-permute-start.42 = (f32[8,128,128]{2,1,0:T(8,128)S(1)}, f32[8,128,128]{2,1,0:T(8,128)S(1)}, u32[]{:S(2)}, u32[]{:S(2)}) collective-permute-start(f32[8,128,128]{2,1,0:T(8,128)S(1)} %pad_maximum_fusion.17), channel_id=1, source_target_pairs={{0,4},{2,6},{4,0},{6,2},{8,12},{10,14},{12,8},{14,10},{16,20},{18,... | collective-permute-start | bytes 1572872 | tf_op jit(solution)/shard_map/ppermute | solution.py:194
  235.4 22.5 %collective-permute-start.40 = (f32[8,128,128]{2,1,0:T(8,128)S(1)}, f32[8,128,128]{2,1,0:T(8,128)S(1)}, u32[]{:S(2)}, u32[]{:S(2)}) collective-permute-start(f32[8,128,128]{2,1,0:T(8,128)S(1)} %pad_maximum_fusion.16), channel_id=1, source_target_pairs={{0,2},{2,0},{4,6},{6,4},{8,10},{10,8},{12,14},{14,12},{16,18},{18,... | collective-permute-start | bytes 1572872 | tf_op jit(solution)/shard_map/ppermute | solution.py:194
  237.1 27.6 %collective-permute-start.30 = (f32[8,128,128]{2,1,0:T(8,128)S(1)}, f32[8,128,128]{2,1,0:T(8,128)S(1)}, u32[]{:S(2)}, u32[]{:S(2)}) collective-permute-start(f32[8,128,128]{2,1,0:T(8,128)S(1)} %pad_maximum_fusion.14), channel_id=1, source_target_pairs={{0,4},{2,6},{4,0},{6,2},{8,12},{10,14},{12,8},{14,10},{16,20},{18,... | collective-permute-start | bytes 1572872 | tf_op jit(solution)/shard_map/ppermute | solution.py:194
  246.6 18.2 %collective-permute-start.28 = (f32[8,128,128]{2,1,0:T(8,128)S(1)}, f32[8,128,128]{2,1,0:T(8,128)S(1)}, u32[]{:S(2)}, u32[]{:S(2)}) collective-permute-start(f32[8,128,128]{2,1,0:T(8,128)S(1)} %pad_maximum_fusion.13), channel_id=1, source_target_pairs={{0,2},{2,0},{4,6},{6,4},{8,10},{10,8},{12,14},{14,12},{16,18},{18,... | collective-permute-start | bytes 1572872 | tf_op jit(solution)/shard_map/ppermute | solution.py:194
  (30 other events, 292.8 us)

commit v3 on v0

v3 whole, which is shorter than its diff:
```python
import functools

import jax
import jax.numpy as jnp
from jax import lax
from jax.experimental import pallas as pl
from jax.experimental.pallas import tpu as pltpu
from jax.sharding import PartitionSpec as P

LANES = 128
SIZE = 2 * LANES
QUARTERS = 4
VMEM_LIMIT = 40 * 1024 * 1024
F32 = jnp.float32

GROUPS = (
    (((0, 0, 0, 128), (2, 0, 0, 64)), ((1, 0, 0, 128), (2, 0, 64, 128))),
    (((0, 1, 0, 128), (2, 1, 0, 64)), ((1, 1, 0, 128), (2, 1, 64, 128))),
    (((3, 0, 0, 128),), ((3, 1, 0, 128),)),
)
GRAM_GROUP = 1


def rows_of(chunk):
    return sum(last - first for _, _, first, last in chunk)


def pieces_of(panel, side):
    found = []
    for group, chunks in enumerate(GROUPS):
        for kind, chunk in enumerate(chunks):
            row = 0
            for some, of, first, last in chunk:
                if (some, of) == (panel, side):
                    found.append((first, group, kind, row, last - first))
                row += last - first
    return [piece[1:] for piece in sorted(found)]


def schedule(middle):
    if middle == 3:
        return (
            ["p0", "g", "p1", "k1.0", "k1.1", "k2.0", "p2", "k2.1", "k3.0", "k1.2", "k2.2", "k3.1", "k4.0", "k3.2"]
            + ["k5.0", "k4.1", "k4.2", "k6.0", "k5.1", "f.0", "k5.2", "k6.1", "k6.2", "f.1", "u0", "f.2", "u1"]
        )
    groups = range(len(GROUPS))
    steps = [f"k{step}.{group}" for step in range(1, middle + 4) for group in groups]
    return ["p0", "g"] + [f"p{group}" for group in groups[1:]] + steps + ["u0", "u1"]


def halves(value):
    high = value.astype(jnp.bfloat16)
    low = (value - high.astype(F32)).astype(jnp.bfloat16)
    return high, low


def left_depth(value):
    high, low = halves(value)
    return jnp.concatenate([high, low, high], axis=1)


def right_depth(value):
    high, low = halves(value)
    return jnp.concatenate([high, high, low], axis=0)


def dot(left, right):
    return jnp.dot(left, right, preferred_element_type=F32)


def block_of(slot, kind):
    return (slot >> 1) | ((slot & 1) << 1) if kind == 0 else slot


def slot_of(block, kind):
    return block_of(block, kind)


def shape(*dims):
    return jax.ShapeDtypeStruct(dims, F32)


TOKEN = shape(8, LANES)
ANY = pl.BlockSpec(memory_space=pl.ANY)
SMEM = pl.BlockSpec(memory_space=pltpu.SMEM)

COST = pl.CostEstimate(flops=1, bytes_accessed=1, transcendentals=0)


def params():
    return pltpu.CompilerParams(vmem_limit_bytes=VMEM_LIMIT)


def whole(array):
    rank = len(array.shape)
    return pl.BlockSpec(array.shape, lambda *at: (0,) * rank, pipeline_mode=pl.Buffered(1))


def small_call(kernel, name, after, place, ins, outs):
    def run(place_ref, *refs):
        refs = refs[len(after) :]
        kernel(place_ref, refs[: len(ins)], refs[len(ins) : -1])
        refs[-1][...] = jnp.zeros(TOKEN.shape, F32)

    return pl.pallas_call(
        run,
        in_specs=[SMEM] + [ANY] * len(after) + [pl.BlockSpec(memory_space=pltpu.VMEM)] * len(ins),
        out_shape=list(outs) + [TOKEN],
        compiler_params=params(),
        cost_estimate=COST,
        name=name,
    )(place, *after, *ins)


def project_kernel(steps, group, blocks, skip, grams, place, *refs):
    block_refs, slab_ref, refs = refs[skip : skip + len(blocks)], refs[skip + len(blocks)], refs[skip + len(blocks) + 1 :]
    gram_refs, (keep0, send0, keep1, send1, token_out, total) = refs[:grams], refs[grams:]
    step = pl.program_id(0)
    turned = {block: ref[0].T for block, ref in zip(blocks, block_refs)}
    left = left_depth(
        jnp.concatenate([turned[panel, side][first:last] for chunk in group for panel, side, first, last in chunk])
    )
    tall = rows_of(group[0])
    columns = slab_ref.shape[1] // QUARTERS
    for quarter in range(QUARTERS):
        at = pl.ds(quarter * columns, columns)
        made = dot(left, right_depth(slab_ref[:, at]))

        @pl.when(step == 0)
        def _():
            total[:, at] = made

        @pl.when(step > 0)
        def _():
            total[:, at] += made

    @pl.when(step == steps - 1)
    def _():
        token_out[...] = jnp.zeros(TOKEN.shape, F32)
        for kind, outs in enumerate([(keep0, send0), (keep1, send1)]):
            for slot in range(QUARTERS):
                quarter = place[0] ^ block_of(slot, kind)
                part = total[pl.ds(kind * tall, tall), pl.ds(pl.multiple_of(quarter * columns, LANES), columns)]
                out = outs[slot // 2]
                out[slot % 2, :tall] = part
                if grams:
                    out[slot % 2, tall:] = gram_refs[kind][slot]


def project(place, after, sides, group, slab, grams):
    rows, columns = slab.shape
    steps = 4
    deep = rows // steps
    tall = rows_of(group[0]) + (grams[0].shape[1] if grams else 0)
    half = shape(2, tall, columns // QUARTERS)
    spec = pl.BlockSpec(half.shape, lambda j: (0, 0, 0))
    blocks = sorted({(panel, side) for chunk in group for panel, side, _, _ in chunk})
    specs = [pl.BlockSpec((1, deep, LANES), lambda j, panel=panel: (panel, j, 0)) for panel, _ in blocks]
    strip = pl.BlockSpec((deep, columns), lambda j: (j, 0))
    out = pl.pallas_call(
        functools.partial(project_kernel, steps, group, blocks, len(after), len(grams)),
        grid=(steps,),
        in_specs=[SMEM] + [ANY] * len(after) + specs + [strip] + [whole(x) for x in grams],
        out_specs=[spec] * 4 + [pl.BlockSpec(TOKEN.shape, lambda j: (0, 0))],
        scratch_shapes=[pltpu.VMEM((2 * rows_of(group[0]), columns), F32)],
        out_shape=[half] * 4 + [TOKEN],
        compiler_params=params(),
        cost_estimate=COST,
        name="project_" + "_".join(f"{panel}{side}" for panel, side in blocks),
    )(place, *after, *[sides[side] for _, side in blocks], slab, *grams)
    return [(out[0], out[1]), (out[2], out[3])], out[4]


def gram_tiles(rows_shape, piece_shape, quarter, kind):
    (width, wide), (high, columns) = rows_shape, piece_shape
    across, lanes = columns // LANES, wide // LANES
    for tile in range(high // 8 * across):
        row, lane = divmod(kind * (high // 8 * across) + tile, lanes)
        start = pl.multiple_of(quarter * (width // QUARTERS) + 8 * row, 8)
        inside = (pl.ds(tile // across * 8, 8), pl.ds(tile % across * LANES, LANES))
        yield inside, (pl.ds(start, 8), pl.ds(lane * LANES, LANES))


def gram_kernel(place, *refs):
    own_ref, side0_ref, side1_ref, out0, out1, token_out, rows_ref = refs[-7:]
    panels, _, width = own_ref.shape
    for other in range(panels - 1):
        left = jnp.concatenate([own_ref[panel].T for panel in range(other + 1, panels)])
        right = jnp.concatenate([side0_ref[other], side1_ref[other]], axis=1)
        made = dot(left_depth(left), right_depth(right))
        for row, panel in enumerate(range(other + 1, panels)):
            at = (panel * (panel - 1) // 2 + other) * SIZE
            rows_ref[:, pl.ds(at, SIZE)] = made[row * width : (row + 1) * width]
    for kind, out in enumerate([out0, out1]):
        for slot in range(QUARTERS):
            quarter = place[0] ^ block_of(slot, kind)
            for inside, outside in gram_tiles(rows_ref.shape, out.shape[1:], quarter, kind):
                out[(slot, *inside)] = rows_ref[outside]
    token_out[...] = jnp.zeros(TOKEN.shape, F32)


def gram(place, after, reflectors, sides, columns):
    panels, rows, width = reflectors.shape
    wide = panels * (panels - 1) // 2 * SIZE
    out = shape(QUARTERS, width // QUARTERS * (wide // columns) // 2, columns)
    ins = [reflectors, *sides]
    return pl.pallas_call(
        gram_kernel,
        in_specs=[SMEM] + [ANY] * len(after) + [pl.BlockSpec(memory_space=pltpu.VMEM)] * 3,
        scratch_shapes=[pltpu.VMEM((width, wide), F32)],
        out_shape=[out, out, TOKEN],
        compiler_params=params(),
        cost_estimate=COST,
        name="gram_rows",
    )(place, *after, *ins)


def gram_rows_kernel(place, ins, outs):
    (out,) = outs
    above = rows_of(GROUPS[GRAM_GROUP][0])
    _, tall, columns = ins[0].shape
    for kind in range(2):
        for slot in range(QUARTERS):
            ref = ins[2 * kind + slot // 2]
            quarter = place[0] ^ block_of(slot, kind)
            for (rows, lanes), outside in gram_tiles(out.shape, (tall - above, columns), quarter, kind):
                out[outside] = ref[slot % 2, pl.ds(above + rows.start, 8), lanes]


def first_kernel(place, ins, outs):
    for kind in range(2):
        keep, got = ins[2 * kind : 2 * kind + 2]
        for half in range(2):
            outs[2 * kind + half][...] = keep[half] + got[half]


def second_kernel(place, ins, outs):
    for kind in range(2):
        outs[0][kind] = ins[2 * kind][...] + ins[2 * kind + 1][...]


def add_kernel(place, ins, outs):
    outs[0][...] = ins[0][...] + ins[1][...]


def add_split_kernel(place, ins, outs):
    for kind in range(2):
        outs[kind][...] = ins[0][kind] + ins[1][kind]


def take_split_kernel(place, ins, outs):
    outer = place[1] == 1
    for kind in range(2):
        outs[kind][...] = jnp.where(outer, ins[1][kind], ins[0][kind])


def join_kernel(place, ins, outs):
    for kind in range(2):
        for half in range(2):
            outs[kind][half] = ins[2 * kind + half][...]


def update_kernel(panels, last, skip, groups, place, *refs):
    count = len(panels)
    factor_ref, refs = refs[skip], refs[skip + 1 :]
    summed = {group: refs[4 * at : 4 * at + 4] for at, group in enumerate(groups)}
    refs = refs[4 * len(groups) :]
    blocks, slab_ref, extra_ref, out_ref = refs[: 2 * count], *refs[2 * count : 2 * count + 3]
    depth_ref = refs[-1]
    depth = count * SIZE

    def gram_times(panel, past):
        total = None
        for other, weights in enumerate(past):
            start = (panel * (panel - 1) // 2 + other) * SIZE
            term = dot(left_depth(extra_ref[:, pl.ds(start, SIZE)]), weights)
            total = term if total is None else total + term
        return total

    @pl.when(pl.program_id(0) == 0)
    def _():
        columns = summed[groups[0]][0].shape[2]
        for block in range(QUARTERS):
            quarter = place[0] ^ block
            at = pl.ds(pl.multiple_of(quarter * columns, LANES), columns)
            past = []
            for row, panel in enumerate(panels):
                proj = []
                for side in range(2):
                    for group, kind, first, tall in pieces_of(panel, side):
                        slot = slot_of(block, kind)
                        proj.append(summed[group][2 * kind + slot // 2][slot % 2, pl.ds(first, tall)])
                proj = jnp.concatenate(proj)
                if last:
                    proj = proj - extra_ref[:, at]
                elif past:
                    proj = proj - gram_times(panel, past)
                high, low = halves(dot(left_depth(factor_ref[row]), right_depth(proj)))
                past.append(jnp.concatenate([high, high, low]))
                for copy, value in enumerate([high, high, low]):
                    depth_ref[pl.ds(copy * depth + row * SIZE, SIZE), at] = value
            if not last:
                refs[2 * count + 3][:, at] = gram_times(count, past)

    left = left_depth(jnp.concatenate([ref[0] for ref in blocks], axis=1))
    wide = slab_ref.shape[1] // QUARTERS
    for quarter in range(QUARTERS):
        at = pl.ds(quarter * wide, wide)
        out_ref[:, at] = slab_ref[:, at] - dot(left, depth_ref[:, at])


def update(place, after, panels, sides, factors, slab, state, extra, last):
    rows, columns = slab.shape
    steps = 4
    deep = rows // steps
    first, count = panels[0], len(panels)
    size = factors.shape[-1]
    groups = sorted({piece[0] for panel in panels for side in range(2) for piece in pieces_of(panel, side)})
    strip = pl.BlockSpec((deep, columns), lambda j: (j, 0))
    specs, blocks = [], []
    for panel in panels:
        for side in range(2):
            specs.append(pl.BlockSpec((1, deep, LANES), lambda j, panel=panel: (panel, j, 0)))
            blocks.append(sides[side])
    factor = pl.BlockSpec((count, size, size), lambda j: (first // count, 0, 0), pipeline_mode=pl.Buffered(1))
    pieces = [x for group in groups for x in state[group]]
    carry = shape(size, columns)
    outs, out_specs = [shape(rows, columns)], [strip]
    if not last:
        outs, out_specs = outs + [carry], out_specs + [pl.BlockSpec(carry.shape, lambda j: (0, 0))]
    return pl.pallas_call(
        functools.partial(update_kernel, panels, last, len(after), groups),
        grid=(steps,),
        in_specs=[SMEM] + [ANY] * len(after) + [factor] + [whole(x) for x in pieces] + specs + [strip, whole(extra)],
        out_specs=out_specs,
        scratch_shapes=[pltpu.VMEM((3 * count * size, columns), jnp.bfloat16)],
        out_shape=outs,
        compiler_params=params(),
        cost_estimate=COST,
        name="update_panels" + "".join(map(str, panels)),
    )(place, *after, factors, *pieces, *blocks, slab, extra)


def send(value, pairs):
    return lax.ppermute(value, "row", pairs)


def swap(value, bit):
    return send(value, [(source, source ^ (1 << bit)) for source in range(lax.axis_size("row"))])


def shift(value, step):
    count = lax.axis_size("col")
    return lax.ppermute(value, "col", [((target + step) % count, target) for target in range(count)])


def line(value, step):
    moves = [((0, 1), (3, 2)), ((1, 2), (2, 1)), ((1, 0), (2, 3))][step]
    return send(value, [(QUARTERS * a + low, QUARTERS * b + low) for a, b in moves for low in range(QUARTERS)])


def body(eigvecs, reflectors, factors):
    panels, _, width = reflectors.shape
    size = factors.shape[-1]
    others = size // width
    columns = eigvecs.shape[1] // QUARTERS
    count = lax.axis_size("row")
    bits = count.bit_length() - 1
    in_line = bits == 4
    middle = 3 if in_line else bits - 2
    me = lax.axis_index("row")
    level = me // QUARTERS
    outer = ((level == 0) | (level == 3)).astype(jnp.int32)
    place = jnp.stack([me % QUARTERS, outer]).astype(jnp.int32)

    parts = [reflectors] + [shift(reflectors, step) for step in range(1, others)]
    join = lambda some: some[0] if len(some) == 1 else jnp.concatenate(some, axis=2)
    sides = [join(parts[: others // 2]), join(parts[others // 2 :])]
    factor_rows = jnp.concatenate([factors] + [shift(factors, step) for step in range(1, others)], axis=1)
    start = lax.axis_index("col") * width
    factors = lax.dynamic_slice_in_dim(jnp.concatenate([factor_rows, factor_rows], axis=2), start, size, axis=2)

    after = [jnp.zeros(TOKEN.shape, F32)]
    state, grams, slab = {}, [], eigvecs

    def kernel(function, name, ins, outs):
        nonlocal after
        *made, token = small_call(function, name, after, place, ins, outs)
        after = [token]
        return made

    for event in schedule(middle):
        if event[0] == "p":
            group = int(event[1:])
            extra = grams if group == GRAM_GROUP else []
            after = after + ([factors] if group == 1 else [])
            pairs, token = project(place, after, sides, GROUPS[group], eigvecs, extra)
            after = [token]
            state[group] = [pairs[0][0], swap(pairs[0][1], 0), pairs[1][0], swap(pairs[1][1], 1)]
        elif event == "g":
            *grams, token = gram(place, after, reflectors, sides, columns)
            after = [token]
        elif event[0] == "k":
            step, group = map(int, event[1:].split("."))
            held = state[group]
            tall = held[0].shape[-2]
            flat, pair = shape(tall, columns), shape(2, tall, columns)
            if step == 1:
                keep0, send0, keep1, send1 = kernel(first_kernel, f"halve_{group}", held, [flat] * 4)
                state[group] = [keep0, swap(send0, 1), keep1, swap(send1, 0)]
            elif step <= middle + 1:
                function = second_kernel if step == 2 else add_kernel
                (total,) = kernel(function, f"sum{step}_{group}", held, [pair])
                state[group] = [total, line(total, step - 2) if in_line else swap(total, step)]
            elif step == middle + 2:
                function = take_split_kernel if in_line else add_split_kernel
                one, two = kernel(function, f"sum{step}_{group}", held, [flat] * 2)
                state[group] = [one, swap(one, 1), two, swap(two, 0)]
            else:
                one, two = kernel(join_kernel, f"join_{group}", held, [pair] * 2)
                state[group] = [one, swap(one, 0), two, swap(two, 1)]
        elif event[0] == "f":
            after = after + state[int(event[2:])]
        elif event == "u0":
            wide = panels * (panels - 1) // 2 * size
            (own,) = kernel(gram_rows_kernel, "gram_own", state[GRAM_GROUP], [shape(width, wide)])
            rows = [own]
            for step in range(1, others):
                part = shift(own, step).reshape(width, wide // size, size)
                rows.append(jnp.roll(part, step * width, axis=2).reshape(width, wide))
            slab, carry = update(
                place, after, tuple(range(panels - 1)), sides, factors, slab, state, jnp.concatenate(rows), False
            )
        else:
            (slab,) = update(place, after, (panels - 1,), sides, factors, slab, state, carry, True)
    return slab


def solution(mesh):
    in_specs = (P("row", "col"), P(None, "row", "col"), P(None, "col", None))
    out_specs = P("row", "col")
    return jax.shard_map(body, mesh=mesh, in_specs=in_specs, out_specs=out_specs, check_vma=False)
```

time: 675 us -> 258 us (0.38)
  waiting for transfers between devices: 519 us -> 101 us
  matrix products: 105 us -> 0 us
  Pallas kernels: 0 us -> 83.8 us
  starting transfers between devices: 0.2 us -> 44.8 us
  between operations: 14 us -> 0.43 us
  local copies, waits for them, and re-layouts: 28.6 us -> 21 us
    psum x4 -> x0, waiting for transfers between devices: 501 us -> none  [body(): totals = lax.psum(partial_proj, 'row')]
    dot_general x12 -> x0, matrix products: 105 us -> none  [the longest x8 69.1 us: matmul(): jnp.dot(left, right, precision=lax.Precision.HIGHEST, preferred_element_t...]
    ppermute x0 -> x36, waiting for transfers between devices: none -> 101 us  [the longest x33 101 us: send(): return lax.ppermute(value, 'row', pairs)]
    pallas_call x0 -> x25, Pallas kernels: none -> 83.8 us  [the longest x2 35.2 us: update(): pl.pallas_call(functools.partial(update_kernel, panels, last, len(after),...]
    ppermute x0 -> x36, starting transfers between devices: none -> 44.8 us  [the longest x33 44.3 us: send(): return lax.ppermute(value, 'row', pairs)]
    all_gather x2 -> x0, waiting for transfers between devices: 16.6 us -> none  [the longest x1 16.6 us: body(): lax.all_gather(reflectors, 'col', axis=2, tiled=True)]
    sub x1 -> x0, local copies, waits for them, and re-layouts: 9.12 us -> none  [body(): slab = slab - matmul(reflect_block, weights)]
    unnamed x15 -> x48, local copies, waits for them, and re-layouts: 19.4 us -> 15.2 us
  transfers between devices with their start and end apart: 6 -> 36, of which waited for: 5 -> 22; matrix products, arithmetic and copies ran while one was open for 3% -> 4% of each run, Pallas kernels for 0% -> 28%
where the time goes in v3:
time: 258 us; the launch traced here: 255 us
  waiting for transfers between devices  101 us (39%)
  Pallas kernels  83.8 us (32%)
  starting transfers between devices  44.8 us (17%)
  local copies, waits for them, and re-layouts  21 us (8%)
  other arithmetic  4.06 us (2%)
    ppermute x33, waiting for transfers between devices, send(): return lax.ppermute(value, 'row', pairs)  101 us
    ppermute x33, starting transfers between devices, send(): return lax.ppermute(value, 'row', pairs)  44.3 us
    pallas_call x2, Pallas kernels, update(): pl.pallas_call(functools.partial(update_kernel, panels, last, len(after),...  35.2 us
    pallas_call x3, Pallas kernels, project(): pl.pallas_call(functools.partial(project_kernel, steps, group, blocks, le...  31 us
    unnamed x48, local copies, waits for them, and re-layouts  15.2 us
    pallas_call x19, Pallas kernels, small_call(): pl.pallas_call(run, in_specs=[SMEM] + [ANY] * len(after) + [pl.BlockSpec(...  14 us
  transfers between devices with their start and end apart: 36, of which 22 were waited for; matrix products, arithmetic and copies ran while one was open for 4% of the time, Pallas kernels for 28%

profile of v3, /device:TPU:0, one launch (start us, length us, event | category | flops | bytes accessed | tf_op | source)
XLA Modules:
  0.0 255.4 jit_solution(5084381776478449473)
XLA Ops:
  2.2 3.4 %copy-done.2 = f32[1024,2048]{1,0:T(8,128)S(1)} copy-done((f32[1024,2048]{1,0:T(8,128)S(1)}, f32[1024,2048]{1,0:T(8,128)}, u32[]{:S(2)}) %copy-start.2) | copy-done | bytes 8388632
  5.6 11.0 %project_00_10_20.1 = (f32[2,192,512]{2,1,0:T(8,128)S(1)}, f32[2,192,512]{2,1,0:T(8,128)}, f32[2,192,512]{2,1,0:T(8,128)S(1)}, f32[2,192,512]{2,1,0:T(8,128)}, f32[8,128]{1,0:T(8,128)S(1)}) custom-call(s32[2]{0:T(128)S(1)} %pad_add_fusion.place.place_ref, f32[8,128]{1,0:T(8,128)S(1)} %broadcast_in_dim.3.refs_0_, f32[4,1024,128]{2,1,0:T(8,128)S(1)} %copy-done, ...), custom_call_target="tpu_custom_call" | custom-call | flops 1 | bytes 1 | tf_op jit(solution)/shard_map/project_00_10_20/pallas_call | solution.py:160
  18.3 2.9 %collective-permute-start.2 = (f32[2,192,512]{2,1,0:T(8,128)}, f32[2,192,512]{2,1,0:T(8,128)}, u32[]{:S(2)}, u32[]{:S(2)}) collective-permute-start(f32[2,192,512]{2,1,0:T(8,128)} %get-tuple-element.84), channel_id=1, source_target_pairs={{0,2},{2,0},{4,6},{6,4},{8,10},{10,8},{12,14},{14,12},{16,18},{18,... | collective-permute-start | bytes 2359304 | tf_op jit(solution)/shard_map/ppermute | solution.py:345
  24.2 3.6 %gram_rows.1 = (f32[4,48,512]{2,1,0:T(8,128)S(1)}, f32[4,48,512]{2,1,0:T(8,128)S(1)}, f32[8,128]{1,0:T(8,128)S(1)}) custom-call(s32[2]{0:T(128)S(1)} %pad_add_fusion.place.place_ref, f32[8,128]{1,0:T(8,128)S(1)} %get-tuple-element.78.refs_0_, f32[4,1024,128]{2,1,0:T(8,128)S(1)} %copy-done.1, f32[4,1024,128]{2,1,0:T(8,128)S(1)} %copy-done.1, ...), custom_call_target="tpu_custom_call" | custom-call | flops 1 | bytes 1 | tf_op jit(solution)/shard_map/gram_rows/pallas_call | solution.py:207
  27.9 11.2 %project_01_11_21.1 = (f32[2,240,512]{2,1,0:T(8,128)S(1)}, f32[2,240,512]{2,1,0:T(8,128)S(1)}, f32[2,240,512]{2,1,0:T(8,128)S(1)}, f32[2,240,512]{2,1,0:T(8,128)S(1)}, f32[8,128]{1,0:T(8,128)S(1)}) custom-call(s32[2]{0:T(128)S(1)} %pad_add_fusion.place.place_ref, f32[8,128]{1,0:T(8,128)S(1)} %get-tuple-element.79.refs_0_, ...), custom_call_target="tpu_custom_call" | custom-call | flops 1 | bytes 1 | tf_op jit(solution)/shard_map/project_01_11_21/pallas_call | solution.py:160
  42.4 1.7 collective-permute-start.6
  44.9 19.0 %collective-permute-done.4.refs_2_ = f32[2,240,512]{2,1,0:T(8,128)S(1)} collective-permute-done((f32[2,240,512]{2,1,0:T(8,128)S(1)}, f32[2,240,512]{2,1,0:T(8,128)S(1)}, u32[]{:S(2)}, u32[]{:S(2)}) %collective-permute-start.4) | collective-permute-done | bytes 983072 | tf_op jit(solution)/shard_map/ppermute | solution.py:345
  65.3 1.9 collective-permute-start.9
  67.2 5.6 %collective-permute-done.6.refs_2_ = f32[192,512]{1,0:T(8,128)S(1)} collective-permute-done((f32[192,512]{1,0:T(8,128)S(1)}, f32[192,512]{1,0:T(8,128)S(1)}, u32[]{:S(2)}, u32[]{:S(2)}) %collective-permute-start.6) | collective-permute-done | bytes 393248 | tf_op jit(solution)/shard_map/ppermute | solution.py:345
  73.5 3.5 %collective-permute-start.10 = (f32[2,192,512]{2,1,0:T(8,128)S(1)}, f32[2,192,512]{2,1,0:T(8,128)S(1)}, u32[]{:S(2)}, u32[]{:S(2)}) collective-permute-start(f32[2,192,512]{2,1,0:T(8,128)S(1)} %get-tuple-element.104.refs_1_), channel_id=1, source_target_pairs={{0,8},{2,10},{4,12},{6,14},{24,16},{26,18},{28,20},{30,22},{1,9},{... | collective-permute-start | bytes 2359304 | tf_op jit(solution)/shard_map/ppermute | solution.py:345
  77.0 8.9 %project_30_31.1 = (f32[2,128,512]{2,1,0:T(8,128)S(1)}, f32[2,128,512]{2,1,0:T(8,128)S(1)}, f32[2,128,512]{2,1,0:T(8,128)S(1)}, f32[2,128,512]{2,1,0:T(8,128)S(1)}, f32[8,128]{1,0:T(8,128)S(1)}) custom-call(s32[2]{0:T(128)S(1)} %pad_add_fusion.place.place_ref, f32[8,128]{1,0:T(8,128)S(1)} %get-tuple-element.97.refs_0_, f32[4,1024,128]{2,1,0:T(8,128)S(1)} %copy-done.1, ...), custom_call_target="tpu_custom_call" | custom-call | flops 1 | bytes 1 | tf_op jit(solution)/shard_map/project_30_31/pallas_call | solution.py:160
  90.0 5.0 %collective-permute-done.10.refs_2_ = f32[2,192,512]{2,1,0:T(8,128)S(1)} collective-permute-done((f32[2,192,512]{2,1,0:T(8,128)S(1)}, f32[2,192,512]{2,1,0:T(8,128)S(1)}, u32[]{:S(2)}, u32[]{:S(2)}) %collective-permute-start.10) | collective-permute-done | bytes 786464 | tf_op jit(solution)/shard_map/ppermute | solution.py:345
  96.3 1.9 collective-permute-done.11.refs_2_
  98.2 2.6 %collective-permute-done.12.refs_4_ = f32[2,128,512]{2,1,0:T(8,128)S(1)} collective-permute-done((f32[2,128,512]{2,1,0:T(8,128)S(1)}, f32[2,128,512]{2,1,0:T(8,128)S(1)}, u32[]{:S(2)}, u32[]{:S(2)}) %collective-permute-start.12) | collective-permute-done | bytes 524320 | tf_op jit(solution)/shard_map/ppermute | solution.py:345
  102.6 5.3 %collective-permute-done.13.refs_2_ = f32[128,512]{1,0:T(8,128)S(1)} collective-permute-done((f32[128,512]{1,0:T(8,128)S(1)}, f32[128,512]{1,0:T(8,128)S(1)}, u32[]{:S(2)}, u32[]{:S(2)}) %collective-permute-start.13) | collective-permute-done | bytes 262176 | tf_op jit(solution)/shard_map/ppermute | solution.py:345
  109.0 2.3 collective-permute-done.15.refs_2_
  114.7 7.2 %collective-permute-start.17 = (f32[2,128,512]{2,1,0:T(8,128)S(1)}, f32[2,128,512]{2,1,0:T(8,128)S(1)}, u32[]{:S(2)}, u32[]{:S(2)}) collective-permute-start(f32[2,128,512]{2,1,0:T(8,128)S(1)} %get-tuple-element.120.refs_1_), channel_id=1, source_target_pairs={{0,8},{2,10},{4,12},{6,14},{24,16},{26,18},{28,20},{30,22},{1,9},{... | collective-permute-start | bytes 1572872 | tf_op jit(solution)/shard_map/ppermute | solution.py:345
  121.9 6.6 %collective-permute-done.17.refs_2_ = f32[2,128,512]{2,1,0:T(8,128)S(1)} collective-permute-done((f32[2,128,512]{2,1,0:T(8,128)S(1)}, f32[2,128,512]{2,1,0:T(8,128)S(1)}, u32[]{:S(2)}, u32[]{:S(2)}) %collective-permute-start.17) | collective-permute-done | bytes 524320 | tf_op jit(solution)/shard_map/ppermute | solution.py:345
  129.2 3.6 %collective-permute-done.18.refs_2_ = f32[2,192,512]{2,1,0:T(8,128)S(1)} collective-permute-done((f32[2,192,512]{2,1,0:T(8,128)S(1)}, f32[2,192,512]{2,1,0:T(8,128)S(1)}, u32[]{:S(2)}, u32[]{:S(2)}) %collective-permute-start.18) | collective-permute-done | bytes 786464 | tf_op jit(solution)/shard_map/ppermute | solution.py:345
  138.7 7.0 %collective-permute-done.21.refs_2_ = f32[192,512]{1,0:T(8,128)S(1)} collective-permute-done((f32[192,512]{1,0:T(8,128)S(1)}, f32[192,512]{1,0:T(8,128)S(1)}, u32[]{:S(2)}, u32[]{:S(2)}) %collective-permute-start.21) | collective-permute-done | bytes 393248 | tf_op jit(solution)/shard_map/ppermute | solution.py:345
  145.7 2.6 %collective-permute-done.22.refs_4_ = f32[192,512]{1,0:T(8,128)S(1)} collective-permute-done((f32[192,512]{1,0:T(8,128)S(1)}, f32[192,512]{1,0:T(8,128)S(1)}, u32[]{:S(2)}, u32[]{:S(2)}) %collective-permute-start.22) | collective-permute-done | bytes 393248 | tf_op jit(solution)/shard_map/ppermute | solution.py:345
  153.2 6.6 %collective-permute-done.23.refs_2_ = f32[2,240,512]{2,1,0:T(8,128)S(1)} collective-permute-done((f32[2,240,512]{2,1,0:T(8,128)S(1)}, f32[2,240,512]{2,1,0:T(8,128)S(1)}, u32[]{:S(2)}, u32[]{:S(2)}) %collective-permute-start.23) | collective-permute-done | bytes 983072 | tf_op jit(solution)/shard_map/ppermute | solution.py:345
  160.5 1.7 collective-permute-start.27
  162.5 3.0 %collective-permute-done.26.refs_6_ = f32[2,128,512]{2,1,0:T(8,128)S(1)} collective-permute-done((f32[2,128,512]{2,1,0:T(8,128)S(1)}, f32[2,128,512]{2,1,0:T(8,128)S(1)}, u32[]{:S(2)}, u32[]{:S(2)}) %collective-permute-start.26) | collective-permute-done | bytes 524320 | tf_op jit(solution)/shard_map/ppermute | solution.py:345
  165.4 1.8 collective-permute-done.24.refs_2_.refs_3_
  168.5 5.6 %collective-permute-done.27.refs_2_ = f32[240,512]{1,0:T(8,128)S(1)} collective-permute-done((f32[240,512]{1,0:T(8,128)S(1)}, f32[240,512]{1,0:T(8,128)S(1)}, u32[]{:S(2)}, u32[]{:S(2)}) %collective-permute-start.27) | collective-permute-done | bytes 491552 | tf_op jit(solution)/shard_map/ppermute | solution.py:345
  174.0 2.5 collective-permute-done.28.refs_4_
  181.4 16.6 %collective-permute-done.29.refs_2_ = f32[128,512]{1,0:T(8,128)S(1)} collective-permute-done((f32[128,512]{1,0:T(8,128)S(1)}, f32[128,512]{1,0:T(8,128)S(1)}, u32[]{:S(2)}, u32[]{:S(2)}) %collective-permute-start.29) | collective-permute-done | bytes 262176 | tf_op jit(solution)/shard_map/ppermute | solution.py:345
  205.5 2.3 copy.4
  209.9 2.3 copy.5
  220.2 24.1 %update_panels012.1 = (f32[1024,2048]{1,0:T(8,128)}, f32[256,2048]{1,0:T(8,128)S(1)}) custom-call(s32[2]{0:T(128)S(1)} %pad_add_fusion.place.place_ref, f32[8,128]{1,0:T(8,128)S(1)} %get-tuple-element.145.refs_0_, f32[4,256,256]{2,1,0:T(8,128)S(1)} %fusion.1.refs_1_.refs_5_, f32[2,192,512]{2,1,0:T(8,128)S(1)} %copy-done.12, f32[2,192,512]{2,1,0:T(8,128)S(1)} %copy-done.16, ...), custom_call_target="tpu_custom_call" | custom-call | flops 1 | bytes 1 | tf_op jit(solution)/shard_map/update_panels012/pallas_call | solution.py:331
  244.3 11.1 %update_panels3.1 = f32[1024,2048]{1,0:T(8,128)} custom-call(s32[2]{0:T(128)S(1)} %pad_add_fusion.place.place_ref, f32[8,128]{1,0:T(8,128)S(1)} %get-tuple-element.145.refs_0_, f32[2,128,512]{2,1,0:T(8,128)} %get-tuple-element.146.refs_1_.refs_6_, f32[2,128,512]{2,1,0:T(8,128)} %collective-permute-done.33.refs_2_.refs_7_, ...), custom_call_target="tpu_custom_call" | custom-call | flops 1 | bytes 1 | tf_op jit(solution)/shard_map/update_panels3/pallas_call | solution.py:331
  (121 shorter events, 60.2 us)
Async XLA Ops:
  0.0 24.2 %collective-permute-start = (f32[4,1024,128]{2,1,0:T(8,128)}, f32[4,1024,128]{2,1,0:T(8,128)}, u32[]{:S(2)}, u32[]{:S(2)}) collective-permute-start(f32[4,1024,128]{2,1,0:T(8,128)} %refs_10_.3), channel_id=1, source_target_pairs={{1,0},{0,1},{3,2},{2,3},{5,4},{4,5},{7,6},{6,7},{9,8},{8,9},{11,10... | collective-permute-start | bytes 6291464 | tf_op jit(solution)/shard_map/ppermute | solution.py:354
  0.5 22.3 %collective-permute-start.1 = (f32[4,128,256]{2,1,0:T(8,128)}, f32[4,128,256]{2,1,0:T(8,128)}, u32[]{:S(2)}, u32[]{:S(2)}) collective-permute-start(f32[4,128,256]{2,1,0:T(8,128)} %param.5), channel_id=1, source_target_pairs={{1,0},{0,1},{3,2},{2,3},{5,4},{4,5},{7,6},{6,7},{9,8},{8,9},{11,10... | collective-permute-start | bytes 1572872 | tf_op jit(solution)/shard_map/ppermute | solution.py:354
  18.3 21.5 %collective-permute-start.2 = (f32[2,192,512]{2,1,0:T(8,128)}, f32[2,192,512]{2,1,0:T(8,128)}, u32[]{:S(2)}, u32[]{:S(2)}) collective-permute-start(f32[2,192,512]{2,1,0:T(8,128)} %get-tuple-element.84), channel_id=1, source_target_pairs={{0,2},{2,0},{4,6},{6,4},{8,10},{10,8},{12,14},{14,12},{16,18},{18,... | collective-permute-start | bytes 2359304 | tf_op jit(solution)/shard_map/ppermute | solution.py:345
  21.3 19.5 %collective-permute-start.3 = (f32[2,192,512]{2,1,0:T(8,128)}, f32[2,192,512]{2,1,0:T(8,128)}, u32[]{:S(2)}, u32[]{:S(2)}) collective-permute-start(f32[2,192,512]{2,1,0:T(8,128)} %get-tuple-element.86), channel_id=1, source_target_pairs={{0,4},{2,6},{4,0},{6,2},{8,12},{10,14},{12,8},{14,10},{16,20},{18,... | collective-permute-start | bytes 2359304 | tf_op jit(solution)/shard_map/ppermute | solution.py:345
  39.1 24.8 %collective-permute-start.4 = (f32[2,240,512]{2,1,0:T(8,128)S(1)}, f32[2,240,512]{2,1,0:T(8,128)S(1)}, u32[]{:S(2)}, u32[]{:S(2)}) collective-permute-start(f32[2,240,512]{2,1,0:T(8,128)S(1)} %get-tuple-element.89), channel_id=1, source_target_pairs={{0,2},{2,0},{4,6},{6,4},{8,10},{10,8},{12,14},{14,12},{16,18},{18,... | collective-permute-start | bytes 2949128 | tf_op jit(solution)/shard_map/ppermute | solution.py:345
  39.7 24.7 %collective-permute-start.5 = (f32[2,240,512]{2,1,0:T(8,128)S(1)}, f32[2,240,512]{2,1,0:T(8,128)S(1)}, u32[]{:S(2)}, u32[]{:S(2)}) collective-permute-start(f32[2,240,512]{2,1,0:T(8,128)S(1)} %get-tuple-element.91), channel_id=1, source_target_pairs={{0,4},{2,6},{4,0},{6,2},{8,12},{10,14},{12,8},{14,10},{16,20},{18,... | collective-permute-start | bytes 2949128 | tf_op jit(solution)/shard_map/ppermute | solution.py:345
  42.4 30.5 %collective-permute-start.6 = (f32[192,512]{1,0:T(8,128)S(1)}, f32[192,512]{1,0:T(8,128)S(1)}, u32[]{:S(2)}, u32[]{:S(2)}) collective-permute-start(f32[192,512]{1,0:T(8,128)S(1)} %get-tuple-element.94), channel_id=1, source_target_pairs={{0,4},{2,6},{4,0},{6,2},{8,12},{10,14},{12,8},{14,10},{16,20},{18,... | collective-permute-start | bytes 1179656 | tf_op jit(solution)/shard_map/ppermute | solution.py:345
  44.1 28.8 %collective-permute-start.7 = (f32[192,512]{1,0:T(8,128)S(1)}, f32[192,512]{1,0:T(8,128)S(1)}, u32[]{:S(2)}, u32[]{:S(2)}) collective-permute-start(f32[192,512]{1,0:T(8,128)S(1)} %get-tuple-element.96), channel_id=1, source_target_pairs={{0,2},{2,0},{4,6},{6,4},{8,10},{10,8},{12,14},{14,12},{16,18},{18,... | collective-permute-start | bytes 1179656 | tf_op jit(solution)/shard_map/ppermute | solution.py:345
  65.2 20.7 %collective-permute-start.8 = (f32[240,512]{1,0:T(8,128)S(1)}, f32[240,512]{1,0:T(8,128)S(1)}, u32[]{:S(2)}, u32[]{:S(2)}) collective-permute-start(f32[240,512]{1,0:T(8,128)S(1)} %get-tuple-element.100), channel_id=1, source_target_pairs={{0,4},{2,6},{4,0},{6,2},{8,12},{10,14},{12,8},{14,10},{16,20},{18,... | collective-permute-start | bytes 1474568 | tf_op jit(solution)/shard_map/ppermute | solution.py:345
  65.3 20.6 %collective-permute-start.9 = (f32[240,512]{1,0:T(8,128)S(1)}, f32[240,512]{1,0:T(8,128)S(1)}, u32[]{:S(2)}, u32[]{:S(2)}) collective-permute-start(f32[240,512]{1,0:T(8,128)S(1)} %get-tuple-element.102), channel_id=1, source_target_pairs={{0,2},{2,0},{4,6},{6,4},{8,10},{10,8},{12,14},{14,12},{16,18},{18,... | collective-permute-start | bytes 1474568 | tf_op jit(solution)/shard_map/ppermute | solution.py:345
  73.5 21.5 %collective-permute-start.10 = (f32[2,192,512]{2,1,0:T(8,128)S(1)}, f32[2,192,512]{2,1,0:T(8,128)S(1)}, u32[]{:S(2)}, u32[]{:S(2)}) collective-permute-start(f32[2,192,512]{2,1,0:T(8,128)S(1)} %get-tuple-element.104.refs_1_), channel_id=1, source_target_pairs={{0,8},{2,10},{4,12},{6,14},{24,16},{26,18},{28,20},{30,22},{1,9},{... | collective-permute-start | bytes 2359304 | tf_op jit(solution)/shard_map/ppermute | solution.py:345
  86.5 24.8 %collective-permute-start.15 = (f32[2,240,512]{2,1,0:T(8,128)S(1)}, f32[2,240,512]{2,1,0:T(8,128)S(1)}, u32[]{:S(2)}, u32[]{:S(2)}) collective-permute-start(f32[2,240,512]{2,1,0:T(8,128)S(1)} %get-tuple-element.116.refs_1_), channel_id=1, source_target_pairs={{0,8},{2,10},{4,12},{6,14},{24,16},{26,18},{28,20},{30,22},{1,9},{... | collective-permute-start | bytes 2949128 | tf_op jit(solution)/shard_map/ppermute | solution.py:345
  87.9 10.3 %collective-permute-start.11 = (f32[2,128,512]{2,1,0:T(8,128)S(1)}, f32[2,128,512]{2,1,0:T(8,128)S(1)}, u32[]{:S(2)}, u32[]{:S(2)}) collective-permute-start(f32[2,128,512]{2,1,0:T(8,128)S(1)} %get-tuple-element.107), channel_id=1, source_target_pairs={{0,2},{2,0},{4,6},{6,4},{8,10},{10,8},{12,14},{14,12},{16,18},{18,... | collective-permute-start | bytes 1572872 | tf_op jit(solution)/shard_map/ppermute | solution.py:345
  89.5 11.4 %collective-permute-start.12 = (f32[2,128,512]{2,1,0:T(8,128)S(1)}, f32[2,128,512]{2,1,0:T(8,128)S(1)}, u32[]{:S(2)}, u32[]{:S(2)}) collective-permute-start(f32[2,128,512]{2,1,0:T(8,128)S(1)} %get-tuple-element.109), channel_id=1, source_target_pairs={{0,4},{2,6},{4,0},{6,2},{8,12},{10,14},{12,8},{14,10},{16,20},{18,... | collective-permute-start | bytes 1572872 | tf_op jit(solution)/shard_map/ppermute | solution.py:345
  95.6 17.2 %collective-permute-start.16 = (f32[2,192,512]{2,1,0:T(8,128)S(1)}, f32[2,192,512]{2,1,0:T(8,128)S(1)}, u32[]{:S(2)}, u32[]{:S(2)}) collective-permute-start(f32[2,192,512]{2,1,0:T(8,128)S(1)} %get-tuple-element.118.refs_1_), channel_id=1, source_target_pairs={{8,16},{10,18},{12,20},{14,22},{16,8},{18,10},{20,12},{22,14},{9,1... | collective-permute-start | bytes 2359304 | tf_op jit(solution)/shard_map/ppermute | solution.py:345
  112.0 21.4 %collective-permute-start.19 = (f32[2,240,512]{2,1,0:T(8,128)S(1)}, f32[2,240,512]{2,1,0:T(8,128)S(1)}, u32[]{:S(2)}, u32[]{:S(2)}) collective-permute-start(f32[2,240,512]{2,1,0:T(8,128)S(1)} %get-tuple-element.124.refs_1_), channel_id=1, source_target_pairs={{8,16},{10,18},{12,20},{14,22},{16,8},{18,10},{20,12},{22,14},{9,1... | collective-permute-start | bytes 2949128 | tf_op jit(solution)/shard_map/ppermute | solution.py:345
  113.4 19.4 %collective-permute-start.18 = (f32[2,192,512]{2,1,0:T(8,128)S(1)}, f32[2,192,512]{2,1,0:T(8,128)S(1)}, u32[]{:S(2)}, u32[]{:S(2)}) collective-permute-start(f32[2,192,512]{2,1,0:T(8,128)S(1)} %get-tuple-element.122.refs_1_), channel_id=1, source_target_pairs={{8,0},{10,2},{12,4},{14,6},{16,24},{18,26},{20,28},{22,30},{9,1},{... | collective-permute-start | bytes 2359304 | tf_op jit(solution)/shard_map/ppermute | solution.py:345
  114.7 13.9 %collective-permute-start.17 = (f32[2,128,512]{2,1,0:T(8,128)S(1)}, f32[2,128,512]{2,1,0:T(8,128)S(1)}, u32[]{:S(2)}, u32[]{:S(2)}) collective-permute-start(f32[2,128,512]{2,1,0:T(8,128)S(1)} %get-tuple-element.120.refs_1_), channel_id=1, source_target_pairs={{0,8},{2,10},{4,12},{6,14},{24,16},{26,18},{28,20},{30,22},{1,9},{... | collective-permute-start | bytes 1572872 | tf_op jit(solution)/shard_map/ppermute | solution.py:345
  134.1 25.7 %collective-permute-start.23 = (f32[2,240,512]{2,1,0:T(8,128)S(1)}, f32[2,240,512]{2,1,0:T(8,128)S(1)}, u32[]{:S(2)}, u32[]{:S(2)}) collective-permute-start(f32[2,240,512]{2,1,0:T(8,128)S(1)} %get-tuple-element.131.refs_1_), channel_id=1, source_target_pairs={{8,0},{10,2},{12,4},{14,6},{16,24},{18,26},{20,28},{22,30},{9,1},{... | collective-permute-start | bytes 2949128 | tf_op jit(solution)/shard_map/ppermute | solution.py:345
  136.1 9.6 %collective-permute-start.21 = (f32[192,512]{1,0:T(8,128)S(1)}, f32[192,512]{1,0:T(8,128)S(1)}, u32[]{:S(2)}, u32[]{:S(2)}) collective-permute-start(f32[192,512]{1,0:T(8,128)S(1)} %get-tuple-element.128.refs_1_), channel_id=1, source_target_pairs={{0,4},{2,6},{4,0},{6,2},{8,12},{10,14},{12,8},{14,10},{16,20},{18,... | collective-permute-start | bytes 1179656 | tf_op jit(solution)/shard_map/ppermute | solution.py:345
  137.4 11.0 %collective-permute-start.22 = (f32[192,512]{1,0:T(8,128)S(1)}, f32[192,512]{1,0:T(8,128)S(1)}, u32[]{:S(2)}, u32[]{:S(2)}) collective-permute-start(f32[192,512]{1,0:T(8,128)S(1)} %get-tuple-element.129.refs_3_), channel_id=1, source_target_pairs={{0,2},{2,0},{4,6},{6,4},{8,10},{10,8},{12,14},{14,12},{16,18},{18,... | collective-permute-start | bytes 1179656 | tf_op jit(solution)/shard_map/ppermute | solution.py:345
  149.0 18.3 %collective-permute-start.24 = (f32[2,192,512]{2,1,0:T(8,128)S(1)}, f32[2,192,512]{2,1,0:T(8,128)S(1)}, u32[]{:S(2)}, u32[]{:S(2)}) collective-permute-start(f32[2,192,512]{2,1,0:T(8,128)S(1)} %get-tuple-element.133.refs_1_.refs_2_), channel_id=1, source_target_pairs={{0,2},{2,0},{4,6},{6,4},{8,10},{10,8},{12,14},{14,12},{16,18},{18,... | collective-permute-start | bytes 2359304 | tf_op jit(solution)/shard_map/ppermute | solution.py:345
  150.2 17.1 %collective-permute-start.25 = (f32[2,192,512]{2,1,0:T(8,128)S(1)}, f32[2,192,512]{2,1,0:T(8,128)S(1)}, u32[]{:S(2)}, u32[]{:S(2)}) collective-permute-start(f32[2,192,512]{2,1,0:T(8,128)S(1)} %get-tuple-element.134.refs_3_.refs_4_), channel_id=1, source_target_pairs={{0,4},{2,6},{4,0},{6,2},{8,12},{10,14},{12,8},{14,10},{16,20},{18,... | collective-permute-start | bytes 2359304 | tf_op jit(solution)/shard_map/ppermute | solution.py:345
  151.8 13.7 %collective-permute-start.26 = (f32[2,128,512]{2,1,0:T(8,128)S(1)}, f32[2,128,512]{2,1,0:T(8,128)S(1)}, u32[]{:S(2)}, u32[]{:S(2)}) collective-permute-start(f32[2,128,512]{2,1,0:T(8,128)S(1)} %get-tuple-element.135.refs_5_), channel_id=1, source_target_pairs={{8,0},{10,2},{12,4},{14,6},{16,24},{18,26},{20,28},{22,30},{9,1},{... | collective-permute-start | bytes 1572872 | tf_op jit(solution)/shard_map/ppermute | solution.py:345
  160.5 13.5 %collective-permute-start.27 = (f32[240,512]{1,0:T(8,128)S(1)}, f32[240,512]{1,0:T(8,128)S(1)}, u32[]{:S(2)}, u32[]{:S(2)}) collective-permute-start(f32[240,512]{1,0:T(8,128)S(1)} %get-tuple-element.137.refs_1_), channel_id=1, source_target_pairs={{0,4},{2,6},{4,0},{6,2},{8,12},{10,14},{12,8},{14,10},{16,20},{18,... | collective-permute-start | bytes 1474568 | tf_op jit(solution)/shard_map/ppermute | solution.py:345
  162.1 14.4 %collective-permute-start.28 = (f32[240,512]{1,0:T(8,128)S(1)}, f32[240,512]{1,0:T(8,128)S(1)}, u32[]{:S(2)}, u32[]{:S(2)}) collective-permute-start(f32[240,512]{1,0:T(8,128)S(1)} %get-tuple-element.138.refs_3_), channel_id=1, source_target_pairs={{0,2},{2,0},{4,6},{6,4},{8,10},{10,8},{12,14},{14,12},{16,18},{18,... | collective-permute-start | bytes 1474568 | tf_op jit(solution)/shard_map/ppermute | solution.py:345
  177.3 23.6 %collective-permute-start.31 = (f32[2,240,512]{2,1,0:T(8,128)S(1)}, f32[2,240,512]{2,1,0:T(8,128)S(1)}, u32[]{:S(2)}, u32[]{:S(2)}) collective-permute-start(f32[2,240,512]{2,1,0:T(8,128)S(1)} %get-tuple-element.143.refs_1_.refs_5_.refs_6_), channel_id=1, source_target_pairs={{0,2},{2,0},{4,6},{6,4},{8,10},{10,8},{12,14},{14,12},{16,18},{18,... | collective-permute-start | bytes 2949128 | tf_op jit(solution)/shard_map/ppermute | solution.py:345
  178.5 22.4 %collective-permute-start.32 = (f32[2,240,512]{2,1,0:T(8,128)S(1)}, f32[2,240,512]{2,1,0:T(8,128)S(1)}, u32[]{:S(2)}, u32[]{:S(2)}) collective-permute-start(f32[2,240,512]{2,1,0:T(8,128)S(1)} %get-tuple-element.144.refs_3_.refs_7_.refs_8_), channel_id=1, source_target_pairs={{0,4},{2,6},{4,0},{6,2},{8,12},{10,14},{12,8},{14,10},{16,20},{18,... | collective-permute-start | bytes 2949128 | tf_op jit(solution)/shard_map/ppermute | solution.py:345
  180.0 18.0 %collective-permute-start.29 = (f32[128,512]{1,0:T(8,128)S(1)}, f32[128,512]{1,0:T(8,128)S(1)}, u32[]{:S(2)}, u32[]{:S(2)}) collective-permute-start(f32[128,512]{1,0:T(8,128)S(1)} %get-tuple-element.140.refs_1_), channel_id=1, source_target_pairs={{0,4},{2,6},{4,0},{6,2},{8,12},{10,14},{12,8},{14,10},{16,20},{18,... | collective-permute-start | bytes 786440 | tf_op jit(solution)/shard_map/ppermute | solution.py:345
  180.5 18.8 %collective-permute-start.30 = (f32[128,512]{1,0:T(8,128)S(1)}, f32[128,512]{1,0:T(8,128)S(1)}, u32[]{:S(2)}, u32[]{:S(2)}) collective-permute-start(f32[128,512]{1,0:T(8,128)S(1)} %get-tuple-element.141.refs_3_), channel_id=1, source_target_pairs={{0,2},{2,0},{4,6},{6,4},{8,10},{10,8},{12,14},{14,12},{16,18},{18,... | collective-permute-start | bytes 786440 | tf_op jit(solution)/shard_map/ppermute | solution.py:345
  203.0 41.3 %collective-permute-start.33 = (f32[2,128,512]{2,1,0:T(8,128)}, f32[2,128,512]{2,1,0:T(8,128)}, u32[]{:S(2)}, u32[]{:S(2)}) collective-permute-start(f32[2,128,512]{2,1,0:T(8,128)} %get-tuple-element.146.refs_1_.refs_6_), channel_id=1, source_target_pairs={{0,2},{2,0},{4,6},{6,4},{8,10},{10,8},{12,14},{14,12},{16,18},{18,... | collective-permute-start | bytes 1572872 | tf_op jit(solution)/shard_map/ppermute | solution.py:345
  203.7 40.6 %collective-permute-start.34 = (f32[2,128,512]{2,1,0:T(8,128)}, f32[2,128,512]{2,1,0:T(8,128)}, u32[]{:S(2)}, u32[]{:S(2)}) collective-permute-start(f32[2,128,512]{2,1,0:T(8,128)} %get-tuple-element.147.refs_3_.refs_8_), channel_id=1, source_target_pairs={{0,4},{2,6},{4,0},{6,2},{8,12},{10,14},{12,8},{14,10},{16,20},{18,... | collective-permute-start | bytes 1572872 | tf_op jit(solution)/shard_map/ppermute | solution.py:345
  (28 other events, 159.5 us)

commit v4 on v0

v4 whole, which is shorter than its diff:
```python
import functools

import jax
import jax.numpy as jnp
from jax import lax
from jax.experimental import pallas as pl
from jax.experimental.pallas import tpu as pltpu
from jax.sharding import PartitionSpec as P

LANES = 128
SIZE = 2 * LANES
VMEM_LIMIT = 40 * 1024 * 1024
F32 = jnp.float32

GROUPS = (
    ((0, 0, 0, 128), (1, 0, 0, 64)),
    ((0, 1, 0, 128), (1, 1, 0, 64)),
    ((1, 0, 64, 128), (1, 1, 64, 128), (2, 0, 0, 128)),
    ((2, 1, 0, 128), (3, 0, 0, 128)),
    ((3, 1, 0, 128),),
)
GRAM_GROUP = 1
CALLS = ((0,), (1,), (2,), (3, 4))
UPDATES = ((0, 1), (2,), (3,))
ORDER = (
    ["p0", "g", "p1", "k1.0", "p2", "k2.0", "p3", "k1.1", "k1.2", "k2.1", "k1.3", "k1.4", "k3.0", "k2.2", "k3.1"]
    + ["k3.2", "k2.3", "k2.4", "k4.0", "k3.3", "k4.1", "k3.4", "k4.2", "k5.0", "k4.3", "k6.0", "k5.1", "k4.4"]
    + ["k6.1", "k5.2", "k7.0", "k5.3", "k5.4", "k6.2", "f.0", "k7.1", "k6.3", "k6.4", "k7.2", "f.1", "x", "k7.3"]
    + ["k7.4", "f.2", "u0", "f.3", "u1", "f.4", "u2"]
)


def schedule(steps):
    if steps == 7:
        return ORDER
    groups = range(len(GROUPS))
    order = ["p0", "g"] + [f"p{call}" for call in range(1, len(CALLS))]
    order += [f"k{step}.{group}" for step in range(1, steps + 1) for group in groups]
    return order + ["x"] + [f"u{update}" for update in range(len(UPDATES))]


def rows_of(chunk):
    return sum(last - first for _, _, first, last in chunk)


def pieces_of(panel):
    found = []
    for group, chunk in enumerate(GROUPS):
        row = 0
        for some, side, first, last in chunk:
            if some == panel:
                found.append((side * LANES + first, group, row, last - first))
            row += last - first
    return sorted(found)


def halves(value):
    high = value.astype(jnp.bfloat16)
    low = (value - high.astype(F32)).astype(jnp.bfloat16)
    return high, low


def left_depth(value):
    high, low = halves(value)
    return jnp.concatenate([high, low, high], axis=1)


def right_depth(value):
    high, low = halves(value)
    return jnp.concatenate([high, high, low], axis=0)


def dot(left, right):
    return jnp.dot(left, right, preferred_element_type=F32)


def shape(*dims):
    return jax.ShapeDtypeStruct(dims, F32)


TOKEN = shape(8, LANES)
ANY = pl.BlockSpec(memory_space=pl.ANY)
SMEM = pl.BlockSpec(memory_space=pltpu.SMEM)

COST = pl.CostEstimate(flops=1, bytes_accessed=1, transcendentals=0)


def params():
    return pltpu.CompilerParams(vmem_limit_bytes=VMEM_LIMIT)


def whole(array):
    rank = len(array.shape)
    return pl.BlockSpec(array.shape, lambda *at: (0,) * rank, pipeline_mode=pl.Buffered(1))


def small_call(kernel, name, after, place, ins, outs):
    def run(place_ref, *refs):
        refs = refs[len(after) :]
        kernel(place_ref, refs[: len(ins)], refs[len(ins) : -1])
        refs[-1][...] = jnp.zeros(TOKEN.shape, F32)

    return pl.pallas_call(
        run,
        in_specs=[SMEM] + [ANY] * len(after) + [pl.BlockSpec(memory_space=pltpu.VMEM)] * len(ins),
        out_shape=list(outs) + [TOKEN],
        compiler_params=params(),
        cost_estimate=COST,
        name=name,
    )(place, *after, *ins)


def project_kernel(steps, call, blocks, skip, grams, place, *refs):
    block_refs, slab_ref, refs = refs[skip : skip + len(blocks)], refs[skip + len(blocks)], refs[skip + len(blocks) + 1 :]
    gram_refs, outs, token_out, total = refs[:grams], refs[grams:-2], refs[-2], refs[-1]
    step = pl.program_id(0)
    turned = {block: ref[0].T for block, ref in zip(blocks, block_refs)}
    left = left_depth(
        jnp.concatenate([turned[panel, side][first:last] for group in call for panel, side, first, last in GROUPS[group]])
    )
    wide = slab_ref.shape[1] // 4
    for quarter in range(4):
        at = pl.ds(quarter * wide, wide)
        made = dot(left, right_depth(slab_ref[:, at]))

        @pl.when(step == 0)
        def _():
            total[:, at] = made

        @pl.when(step > 0)
        def _():
            total[:, at] += made

    @pl.when(step == steps - 1)
    def _():
        token_out[...] = jnp.zeros(TOKEN.shape, F32)
        half = outs[0].shape[0]
        above = 0
        for at, group in enumerate(call):
            tall = rows_of(GROUPS[group])
            for slot in range(2 * half):
                out = outs[2 * at + slot // half]
                lanes = pl.ds(pl.multiple_of((place[0] ^ slot) * LANES, LANES), LANES)
                out[slot % half, :tall] = total[pl.ds(above, tall), lanes]
                if gram_refs:
                    out[slot % half, tall:] = gram_refs[0][slot]
            above += tall


def project(place, after, sides, call, slab, grams, slots):
    rows, columns = slab.shape
    steps = 2
    deep = rows // steps
    above = sum(rows_of(GROUPS[group]) for group in call)
    halves_of = []
    for group in call:
        tall = rows_of(GROUPS[group]) + sum(x.shape[1] for x in grams)
        halves_of += [shape(slots // 2, tall, LANES)] * 2
    blocks = sorted({(panel, side) for group in call for panel, side, _, _ in GROUPS[group]})
    specs = [pl.BlockSpec((1, deep, LANES), lambda j, panel=panel: (panel, j, 0)) for panel, _ in blocks]
    strip = pl.BlockSpec((deep, columns), lambda j: (j, 0))
    out = pl.pallas_call(
        functools.partial(project_kernel, steps, call, blocks, len(after), len(grams)),
        grid=(steps,),
        in_specs=[SMEM] + [ANY] * len(after) + specs + [strip] + [whole(x) for x in grams],
        out_specs=[pl.BlockSpec(x.shape, lambda j: (0, 0, 0)) for x in halves_of]
        + [pl.BlockSpec(TOKEN.shape, lambda j: (0, 0))],
        scratch_shapes=[pltpu.VMEM((above, columns), F32)],
        out_shape=halves_of + [TOKEN],
        compiler_params=params(),
        cost_estimate=COST,
        name="project_" + "".join(map(str, call)),
    )(place, *after, *[sides[side] for _, side in blocks], slab, *grams)
    return [(out[2 * at], out[2 * at + 1]) for at in range(len(call))], out[-1]


def gram_kernel(place, *refs):
    own_ref, side0_ref, side1_ref, out, token_out, rows_ref = refs[-6:]
    panels, _, width = own_ref.shape
    for other in range(panels - 1):
        left = jnp.concatenate([own_ref[panel].T for panel in range(other + 1, panels)])
        right = jnp.concatenate([side0_ref[other], side1_ref[other]], axis=1)
        made = dot(left_depth(left), right_depth(right))
        for row, panel in enumerate(range(other + 1, panels)):
            at = (panel * (panel - 1) // 2 + other) * SIZE
            rows_ref[:, pl.ds(at, SIZE)] = made[row * width : (row + 1) * width]
    slots = out.shape[0]
    tall = width // slots
    for slot in range(slots):
        rows = pl.ds(pl.multiple_of((place[0] ^ slot) * tall, tall), tall)
        for block in range(rows_ref.shape[1] // LANES):
            out[slot, pl.ds(block * tall, tall)] = rows_ref[rows, pl.ds(block * LANES, LANES)]
    token_out[...] = jnp.zeros(TOKEN.shape, F32)


def gram(place, after, reflectors, sides, slots):
    panels, _, width = reflectors.shape
    wide = panels * (panels - 1) // 2 * SIZE
    ins = [reflectors, *sides]
    return pl.pallas_call(
        gram_kernel,
        in_specs=[SMEM] + [ANY] * len(after) + [pl.BlockSpec(memory_space=pltpu.VMEM)] * 3,
        scratch_shapes=[pltpu.VMEM((width, wide), F32)],
        out_shape=[shape(slots, width // slots * (wide // LANES), LANES), TOKEN],
        compiler_params=params(),
        cost_estimate=COST,
        name="gram_rows",
    )(place, *after, *ins)


def gram_rows_kernel(place, ins, outs):
    (out,) = outs
    above = rows_of(GROUPS[GRAM_GROUP])
    half = ins[0].shape[0]
    tall = out.shape[0] // (2 * half)
    for slot in range(2 * half):
        rows = pl.ds(pl.multiple_of((place[0] ^ slot) * tall, tall), tall)
        for block in range(out.shape[1] // LANES):
            out[rows, pl.ds(block * LANES, LANES)] = ins[slot // half][slot % half, pl.ds(above + block * tall, tall)]


def halve_kernel(place, ins, outs):
    keep, got = ins
    half = outs[0].shape[0]
    outs[0][...] = keep[:half] + got[:half]
    outs[1][...] = keep[half:] + got[half:]


def add_kernel(place, ins, outs):
    outs[0][...] = ins[0][...] + ins[1][...]


def join_kernel(place, ins, outs):
    half = ins[0].shape[0]
    outs[0][:half] = ins[0][...]
    outs[0][half:] = ins[1][...]


def update_kernel(panels, parts, carried, left_over, skip, groups, place, *refs):
    count = len(panels)
    factor_ref, refs = refs[skip], refs[skip + 1 :]
    summed = {group: refs[2 * at : 2 * at + 2] for at, group in enumerate(groups)}
    refs = refs[2 * len(groups) :]
    gram_refs, refs = refs[:parts], refs[parts:]
    carry_ref, refs = (refs[0], refs[1:]) if carried else (None, refs)
    blocks, slab_ref, out_ref = refs[: 2 * count], refs[2 * count], refs[2 * count + 1]
    depth_ref, proj_ref = refs[-2:]
    depth = count * SIZE
    columns = slab_ref.shape[1]
    wide = columns // 4

    def gram_block(panel, other):
        at = pl.ds((panel * (panel - 1) // 2 + other) * SIZE, SIZE)
        width = gram_refs[0].shape[0]
        rows = [ref[:, at] for ref in gram_refs]
        return jnp.concatenate([pltpu.roll(part, step * width, 1) if step else part for step, part in enumerate(rows)])

    @pl.when(pl.program_id(0) == 0)
    def _():
        for row, panel in enumerate(panels):
            for at, group, first, tall in pieces_of(panel):
                half = summed[group][0].shape[0]
                for slot in range(2 * half):
                    lanes = pl.ds(pl.multiple_of((place[0] ^ slot) * LANES, LANES), LANES)
                    proj_ref[pl.ds(row * SIZE + at, tall), lanes] = summed[group][slot // half][
                        slot % half, pl.ds(first, tall)
                    ]
        factor = [left_depth(factor_ref[row]) for row in range(count)]
        later = [panels[-1] + 1 + more for more in range(left_over)]
        grams = {
            (panel, row): left_depth(gram_block(panel, panels[row]))
            for panel in list(panels) + later
            for row in range(count)
            if panels[row] < panel
        }
        for quarter in range(4):
            at = pl.ds(quarter * wide, wide)
            past = []

            def less(value, panel, sign):
                for row, weights in enumerate(past):
                    value = value + sign * dot(grams[panel, row], weights)
                return value

            for row in range(count):
                proj = proj_ref[pl.ds(row * SIZE, SIZE), at]
                if carried:
                    proj = proj - carry_ref[pl.ds(row * SIZE, SIZE), at]
                proj = less(proj, panels[row], -1.0)
                high, low = halves(dot(factor[row], right_depth(proj)))
                past.append(jnp.concatenate([high, high, low]))
                for copy, value in enumerate([high, high, low]):
                    depth_ref[pl.ds(copy * depth + row * SIZE, SIZE), at] = value
            for more, panel in enumerate(later):
                value = carry_ref[pl.ds((count + more) * SIZE, SIZE), at] if carried else jnp.zeros((SIZE, wide), F32)
                refs[2 * count + 2][pl.ds(more * SIZE, SIZE), at] = less(value, panel, 1.0)

    left = left_depth(jnp.concatenate([ref[0] for ref in blocks], axis=1))
    for quarter in range(4):
        at = pl.ds(quarter * wide, wide)
        out_ref[:, at] = slab_ref[:, at] - dot(left, depth_ref[:, at])


def update(place, after, panels, left_over, sides, factors, slab, state, grams, carry):
    rows, columns = slab.shape
    steps = 4
    deep = rows // steps
    first, count = panels[0], len(panels)
    size = factors.shape[-1]
    groups = sorted({piece[1] for panel in panels for piece in pieces_of(panel)})
    strip = pl.BlockSpec((deep, columns), lambda j: (j, 0))
    specs, blocks = [], []
    for panel in panels:
        for side in range(2):
            specs.append(pl.BlockSpec((1, deep, LANES), lambda j, panel=panel: (panel, j, 0)))
            blocks.append(sides[side])
    factor = pl.BlockSpec((count, size, size), lambda j: (first // count, 0, 0), pipeline_mode=pl.Buffered(1))
    grams = grams if left_over or count > 1 else []
    carries = [] if carry is None else [carry]
    constant = [x for group in groups for x in state[group]] + list(grams) + carries
    outs, out_specs = [shape(rows, columns)], [strip]
    if left_over:
        outs.append(shape(left_over * size, columns))
        out_specs.append(pl.BlockSpec(outs[1].shape, lambda j: (0, 0)))
    made = pl.pallas_call(
        functools.partial(update_kernel, panels, len(grams), len(carries), left_over, len(after), groups),
        grid=(steps,),
        in_specs=[SMEM] + [ANY] * len(after) + [factor] + [whole(x) for x in constant] + specs + [strip],
        out_specs=out_specs,
        scratch_shapes=[pltpu.VMEM((3 * count * size, columns), jnp.bfloat16), pltpu.VMEM((count * size, columns), F32)],
        out_shape=outs,
        compiler_params=params(),
        cost_estimate=COST,
        name="update_panels" + "".join(map(str, panels)),
    )(place, *after, factors, *constant, *blocks, slab)
    return made[0], made[1] if left_over else None


def order_of(kind, bits):
    first, second = (0, 1) if kind == 0 else (1, 0)
    order = [first, 2, second] + list(range(3, bits)) if bits > 2 else [first, second]
    return order[:bits]


def swap(value, step):
    rows, cores = lax.axis_size("row"), lax.axis_size("col")
    bits = rows.bit_length() - 1
    pairs = [
        (row * cores + core, (row ^ (1 << order_of(core % 2, bits)[step])) * cores + core)
        for row in range(rows)
        for core in range(cores)
    ]
    return lax.ppermute(value, ("row", "col"), pairs)


def shift(value, step):
    count = lax.axis_size("col")
    return lax.ppermute(value, "col", [((target + step) % count, target) for target in range(count)])


def body(eigvecs, reflectors, factors):
    panels, _, width = reflectors.shape
    size = factors.shape[-1]
    others = size // width
    bits = lax.axis_size("row").bit_length() - 1
    slots = min(lax.axis_size("row"), eigvecs.shape[1] // LANES)
    cuts = slots.bit_length() - 1
    me, core = lax.axis_index("row"), lax.axis_index("col")
    own = [
        sum(((me >> bit) & 1) << (cuts - 1 - at) for at, bit in enumerate(order_of(kind, bits)[:cuts])) for kind in range(2)
    ]
    place = jnp.stack([jnp.where(core % 2 == 0, own[0], own[1])]).astype(jnp.int32)

    parts = [reflectors] + [shift(reflectors, step) for step in range(1, others)]
    join = lambda some: some[0] if len(some) == 1 else jnp.concatenate(some, axis=2)
    sides = [join(parts[: others // 2]), join(parts[others // 2 :])]
    factor_rows = jnp.concatenate([factors] + [shift(factors, step) for step in range(1, others)], axis=1)
    factors = lax.dynamic_slice_in_dim(jnp.concatenate([factor_rows, factor_rows], axis=2), core * width, size, axis=2)

    after = [jnp.zeros(TOKEN.shape, F32)]
    state, grams, slab, carry = {}, [], eigvecs, None

    def kernel(function, name, ins, outs):
        nonlocal after
        *made, token = small_call(function, name, after, place, ins, outs)
        after = [token]
        return made

    for event in schedule(bits + cuts - 1):
        if event[0] == "p":
            call = CALLS[int(event[1:])]
            after = after + ([factors] if event == "p1" else [])
            made, token = project(place, after, sides, call, eigvecs, grams if call == (GRAM_GROUP,) else [], slots)
            after = [token]
            for group, (keep, send) in zip(call, made):
                state[group] = [keep, swap(send, 0)]
        elif event == "g":
            rows, token = gram(place, after, reflectors, sides, slots)
            grams, after = [rows], [token]
        elif event[0] == "k":
            step, group = map(int, event[1:].split("."))
            held = state[group]
            wide, tall, _ = held[0].shape
            if step < cuts:
                keep, send = kernel(halve_kernel, f"halve{step}_{group}", held, [shape(wide // 2, tall, LANES)] * 2)
                state[group] = [keep, swap(send, step)]
            elif step <= bits:
                (total,) = kernel(add_kernel, f"sum{step}_{group}", held, [shape(*held[0].shape)])
                state[group] = [total, swap(total, step if step < bits else cuts - 1)]
            else:
                (block,) = kernel(join_kernel, f"join{step}_{group}", held, [shape(2 * wide, tall, LANES)])
                state[group] = [block, swap(block, cuts - 1 - (step - bits))]
        elif event[0] == "f":
            after = after + [state[int(event[2:])][1]]
        elif event == "x":
            wide = panels * (panels - 1) // 2 * size
            (rows,) = kernel(gram_rows_kernel, "gram_own", state[GRAM_GROUP], [shape(width, wide)])
            grams = [rows] + [shift(rows, step) for step in range(1, others)]
        else:
            some = UPDATES[int(event[1:])]
            slab, carry = update(
                place, after, some, panels - 1 - some[-1], sides, factors, slab, state, grams, carry
            )
            after = [slab]
    return slab


def solution(mesh):
    in_specs = (P("row", "col"), P(None, "row", "col"), P(None, "col", None))
    out_specs = P("row", "col")
    return jax.shard_map(body, mesh=mesh, in_specs=in_specs, out_specs=out_specs, check_vma=False)
```

time: 675 us -> 235 us (0.35); the launches traced: 666 us -> 235 us
  waiting for transfers between devices: 519 us -> 98.3 us
  matrix products: 105 us -> 0 us
  Pallas kernels: 0 us -> 79.4 us
  starting transfers between devices: 0.2 us -> 50.8 us
  local copies, waits for them, and re-layouts: 28.6 us -> 4.98 us
  between operations: 14 us -> 0.31 us
    psum x4 -> x0, waiting for transfers between devices: 501 us -> none  [body(): totals = lax.psum(partial_proj, 'row')]
    dot_general x12 -> x0, matrix products: 105 us -> none  [the longest x8 69.1 us: matmul(): jnp.dot(left, right, precision=lax.Precision.HIGHEST, preferred_element_t...]
    ppermute x0 -> x43, waiting for transfers between devices: none -> 98.3 us  [the longest x40 98.3 us: swap(): return lax.ppermute(value, ('row', 'col'), pairs)]
    pallas_call x0 -> x44, Pallas kernels: none -> 79.4 us  [the longest x3 43.3 us: update(): pl.pallas_call(functools.partial(update_kernel, panels, len(grams), len(c...]
    ppermute x0 -> x43, starting transfers between devices: none -> 50.8 us  [the longest x40 50.3 us: swap(): return lax.ppermute(value, ('row', 'col'), pairs)]
    all_gather x2 -> x0, waiting for transfers between devices: 16.6 us -> none  [the longest x1 16.6 us: body(): lax.all_gather(reflectors, 'col', axis=2, tiled=True)]
    unnamed x15 -> x8, local copies, waits for them, and re-layouts: 19.4 us -> 4.98 us
    sub x1 -> x0, local copies, waits for them, and re-layouts: 9.12 us -> none  [body(): slab = slab - matmul(reflect_block, weights)]
  transfers between devices with their start and end apart: 6 -> 43, of which waited for: 5 -> 24; matrix products, arithmetic and copies ran while one was open for 3% -> 1% of each run, Pallas kernels for 0% -> 29%
where the time goes in v4:
time: 235 us
  waiting for transfers between devices  98.3 us (42%)
  Pallas kernels  79.4 us (34%)
  starting transfers between devices  50.8 us (22%)
  local copies, waits for them, and re-layouts  4.98 us (2%)
    ppermute x40, waiting for transfers between devices, swap(): return lax.ppermute(value, ('row', 'col'), pairs)  98.3 us
    ppermute x40, starting transfers between devices, swap(): return lax.ppermute(value, ('row', 'col'), pairs)  50.3 us
    pallas_call x3, Pallas kernels, update(): pl.pallas_call(functools.partial(update_kernel, panels, len(grams), len(c...  43.3 us
    pallas_call x4, Pallas kernels, project(): pl.pallas_call(functools.partial(project_kernel, steps, call, blocks, len...  29.9 us
    unnamed x8, local copies, waits for them, and re-layouts  4.98 us
  transfers between devices with their start and end apart: 43, of which 24 were waited for; matrix products, arithmetic and copies ran while one was open for 1% of the time, Pallas kernels for 29%

profile of v4, /device:TPU:0, one launch (start us, length us, event | category | flops | bytes accessed | tf_op | source)
XLA Modules:
  0.0 235.0 jit_solution(16150033961426015112)
XLA Ops:
  2.1 3.4 %copy-done.2 = f32[1024,2048]{1,0:T(8,128)S(1)} copy-done((f32[1024,2048]{1,0:T(8,128)S(1)}, f32[1024,2048]{1,0:T(8,128)}, u32[]{:S(2)}) %copy-start.2) | copy-done | bytes 8388632
  5.5 5.5 %project_0.1 = (f32[8,192,128]{2,1,0:T(8,128)S(1)}, f32[8,192,128]{2,1,0:T(8,128)}, f32[8,128]{1,0:T(8,128)S(1)}) custom-call(s32[1]{0:T(128)} %bitcast.place.place_ref, f32[8,128]{1,0:T(8,128)S(1)} %broadcast_in_dim.3.refs_0_, f32[4,1024,128]{2,1,0:T(8,128)S(1)} %copy-done, f32[4,1024,128]{2,1,0:T(8,128)S(1)} %copy-done, f32[1024,2048]{1,0:T(8,128)S(1)} %copy-done.2), custom_call_target="tpu_custom_call" | custom-call | flops 1 | bytes 1 | tf_op jit(solution)/shard_map/project_0/pallas_call | solution.py:162
  11.0 3.0 %collective-permute-start.2 = (f32[8,192,128]{2,1,0:T(8,128)}, f32[8,192,128]{2,1,0:T(8,128)}, u32[]{:S(2)}, u32[]{:S(2)}) collective-permute-start(f32[8,192,128]{2,1,0:T(8,128)} %get-tuple-element.117), channel_id=1, source_target_pairs={{0,2},{1,5},{2,0},{3,7},{4,6},{5,1},{6,4},{7,3},{8,10},{9,13},{10,... | collective-permute-start | bytes 2359304 | tf_op jit(solution)/shard_map/ppermute | solution.py:353
  15.3 3.5 %gram_rows.1 = (f32[16,96,128]{2,1,0:T(8,128)S(1)}, f32[8,128]{1,0:T(8,128)S(1)}) custom-call(s32[1]{0:T(128)} %bitcast.place.place_ref, f32[8,128]{1,0:T(8,128)S(1)} %get-tuple-element.112.refs_0_, f32[4,1024,128]{2,1,0:T(8,128)S(1)} %copy-done.1, f32[4,1024,128]{2,1,0:T(8,128)S(1)} %copy-done.1, ...), custom_call_target="tpu_custom_call" | custom-call | flops 1 | bytes 1 | tf_op jit(solution)/shard_map/gram_rows/pallas_call | solution.py:200
  18.8 6.9 %project_1.1 = (f32[8,288,128]{2,1,0:T(8,128)S(1)}, f32[8,288,128]{2,1,0:T(8,128)S(1)}, f32[8,128]{1,0:T(8,128)S(1)}) custom-call(s32[1]{0:T(128)} %bitcast.place.place_ref, f32[8,128]{1,0:T(8,128)S(1)} %get-tuple-element.113.refs_0_, f32[4,256,256]{2,1,0:T(8,128)S(1)} %fusion.1.refs_1_.refs_2_, ...), custom_call_target="tpu_custom_call" | custom-call | flops 1 | bytes 1 | tf_op jit(solution)/shard_map/project_1/pallas_call | solution.py:162
  29.2 7.8 %project_2.1 = (f32[8,256,128]{2,1,0:T(8,128)S(1)}, f32[8,256,128]{2,1,0:T(8,128)S(1)}, f32[8,128]{1,0:T(8,128)S(1)}) custom-call(s32[1]{0:T(128)} %bitcast.place.place_ref, f32[8,128]{1,0:T(8,128)S(1)} %get-tuple-element.118.refs_0_, f32[4,1024,128]{2,1,0:T(8,128)S(1)} %copy-done.1, ...), custom_call_target="tpu_custom_call" | custom-call | flops 1 | bytes 1 | tf_op jit(solution)/shard_map/project_2/pallas_call | solution.py:162
  38.5 9.7 %project_34.1 = (f32[8,256,128]{2,1,0:T(8,128)S(1)}, f32[8,256,128]{2,1,0:T(8,128)S(1)}, f32[8,128,128]{2,1,0:T(8,128)S(1)}, f32[8,128,128]{2,1,0:T(8,128)S(1)}, f32[8,128]{1,0:T(8,128)S(1)}) custom-call(s32[1]{0:T(128)} %bitcast.place.place_ref, f32[8,128]{1,0:T(8,128)S(1)} %get-tuple-element.122.refs_0_, ...), custom_call_target="tpu_custom_call" | custom-call | flops 1 | bytes 1 | tf_op jit(solution)/shard_map/project_34/pallas_call | solution.py:162
  54.9 11.2 %collective-permute-done.6.refs_2_ = f32[4,288,128]{2,1,0:T(8,128)S(1)} collective-permute-done((f32[4,288,128]{2,1,0:T(8,128)S(1)}, f32[4,288,128]{2,1,0:T(8,128)S(1)}, u32[]{:S(2)}, u32[]{:S(2)}) %collective-permute-start.6) | collective-permute-done | bytes 589856 | tf_op jit(solution)/shard_map/ppermute | solution.py:353
  69.9 2.7 %collective-permute-done.8.refs_2_ = f32[8,128,128]{2,1,0:T(8,128)S(1)} collective-permute-done((f32[8,128,128]{2,1,0:T(8,128)S(1)}, f32[8,128,128]{2,1,0:T(8,128)S(1)}, u32[]{:S(2)}, u32[]{:S(2)}) %collective-permute-start.8) | collective-permute-done | bytes 524320 | tf_op jit(solution)/shard_map/ppermute | solution.py:353
  73.6 3.7 %collective-permute-done.10.refs_2_ = f32[4,256,128]{2,1,0:T(8,128)S(1)} collective-permute-done((f32[4,256,128]{2,1,0:T(8,128)S(1)}, f32[4,256,128]{2,1,0:T(8,128)S(1)}, u32[]{:S(2)}, u32[]{:S(2)}) %collective-permute-start.10) | collective-permute-done | bytes 524320 | tf_op jit(solution)/shard_map/ppermute | solution.py:353
  80.3 3.5 %collective-permute-done.12.refs_2_ = f32[2,256,128]{2,1,0:T(8,128)S(1)} collective-permute-done((f32[2,256,128]{2,1,0:T(8,128)S(1)}, f32[2,256,128]{2,1,0:T(8,128)S(1)}, u32[]{:S(2)}, u32[]{:S(2)}) %collective-permute-start.12) | collective-permute-done | bytes 262176 | tf_op jit(solution)/shard_map/ppermute | solution.py:353
  83.8 4.6 %collective-permute-done.13.refs_2_ = f32[4,256,128]{2,1,0:T(8,128)S(1)} collective-permute-done((f32[4,256,128]{2,1,0:T(8,128)S(1)}, f32[4,256,128]{2,1,0:T(8,128)S(1)}, u32[]{:S(2)}, u32[]{:S(2)}) %collective-permute-start.13) | collective-permute-done | bytes 524320 | tf_op jit(solution)/shard_map/ppermute | solution.py:353
  88.5 2.4 %collective-permute-start.16 = (f32[2,256,128]{2,1,0:T(8,128)S(1)}, f32[2,256,128]{2,1,0:T(8,128)S(1)}, u32[]{:S(2)}, u32[]{:S(2)}) collective-permute-start(f32[2,256,128]{2,1,0:T(8,128)S(1)} %get-tuple-element.161), channel_id=1, source_target_pairs={{0,4},{1,3},{2,6},{3,1},{4,0},{5,7},{6,2},{7,5},{8,12},{9,11},{10,... | collective-permute-start | bytes 786440 | tf_op jit(solution)/shard_map/ppermute | solution.py:353
  95.2 2.6 %collective-permute-start.19 = (f32[1,256,128]{2,1,0:T(8,128)S(1)}, f32[1,256,128]{2,1,0:T(8,128)S(1)}, u32[]{:S(2)}, u32[]{:S(2)}) collective-permute-start(f32[1,256,128]{2,1,0:T(8,128)S(1)} %get-tuple-element.170), channel_id=1, source_target_pairs={{0,16},{1,17},{2,18},{3,19},{4,20},{5,21},{6,22},{7,23},{8,24},{9,... | collective-permute-start | bytes 393224 | tf_op jit(solution)/shard_map/ppermute | solution.py:353
  97.8 5.7 %collective-permute-done.15.refs_2_ = f32[1,192,128]{2,1,0:T(8,128)S(1)} collective-permute-done((f32[1,192,128]{2,1,0:T(8,128)S(1)}, f32[1,192,128]{2,1,0:T(8,128)S(1)}, u32[]{:S(2)}, u32[]{:S(2)}) %collective-permute-start.15) | collective-permute-done | bytes 98336 | tf_op jit(solution)/shard_map/ppermute | solution.py:353
  103.7 3.0 %collective-permute-done.17.refs_2_ = f32[1,288,128]{2,1,0:T(8,128)S(1)} collective-permute-done((f32[1,288,128]{2,1,0:T(8,128)S(1)}, f32[1,288,128]{2,1,0:T(8,128)S(1)}, u32[]{:S(2)}, u32[]{:S(2)}) %collective-permute-start.17) | collective-permute-done | bytes 147488 | tf_op jit(solution)/shard_map/ppermute | solution.py:353
  106.8 2.8 %collective-permute-done.19.refs_2_ = f32[1,256,128]{2,1,0:T(8,128)S(1)} collective-permute-done((f32[1,256,128]{2,1,0:T(8,128)S(1)}, f32[1,256,128]{2,1,0:T(8,128)S(1)}, u32[]{:S(2)}, u32[]{:S(2)}) %collective-permute-start.19) | collective-permute-done | bytes 131104 | tf_op jit(solution)/shard_map/ppermute | solution.py:353
  111.3 2.9 %collective-permute-start.23 = (f32[1,288,128]{2,1,0:T(8,128)S(1)}, f32[1,288,128]{2,1,0:T(8,128)S(1)}, u32[]{:S(2)}, u32[]{:S(2)}) collective-permute-start(f32[1,288,128]{2,1,0:T(8,128)S(1)} %get-tuple-element.179.refs_1_), channel_id=1, source_target_pairs={{0,16},{1,17},{2,18},{3,19},{4,20},{5,21},{6,22},{7,23},{8,24},{9,... | collective-permute-start | bytes 442376 | tf_op jit(solution)/shard_map/ppermute | solution.py:353
  114.2 7.4 %collective-permute-done.21.refs_2_ = f32[1,256,128]{2,1,0:T(8,128)S(1)} collective-permute-done((f32[1,256,128]{2,1,0:T(8,128)S(1)}, f32[1,256,128]{2,1,0:T(8,128)S(1)}, u32[]{:S(2)}, u32[]{:S(2)}) %collective-permute-start.21) | collective-permute-done | bytes 131104 | tf_op jit(solution)/shard_map/ppermute | solution.py:353
  121.8 1.9 collective-permute-done.23.refs_2_
  125.2 2.2 collective-permute-start.24
  127.3 8.4 %collective-permute-done.24.refs_2_ = f32[1,128,128]{2,1,0:T(8,128)S(1)} collective-permute-done((f32[1,128,128]{2,1,0:T(8,128)S(1)}, f32[1,128,128]{2,1,0:T(8,128)S(1)}, u32[]{:S(2)}, u32[]{:S(2)}) %collective-permute-start.24) | collective-permute-done | bytes 65568 | tf_op jit(solution)/shard_map/ppermute | solution.py:353
  138.4 1.9 collective-permute-start.28
  141.3 10.6 %collective-permute-done.28.refs_2_ = f32[1,256,128]{2,1,0:T(8,128)S(1)} collective-permute-done((f32[1,256,128]{2,1,0:T(8,128)S(1)}, f32[1,256,128]{2,1,0:T(8,128)S(1)}, u32[]{:S(2)}, u32[]{:S(2)}) %collective-permute-start.28) | collective-permute-done | bytes 131104 | tf_op jit(solution)/shard_map/ppermute | solution.py:353
  152.7 2.1 collective-permute-done.32.refs_3_
  158.3 7.0 %collective-permute-done.33.refs_2_ = f32[2,256,128]{2,1,0:T(8,128)S(1)} collective-permute-done((f32[2,256,128]{2,1,0:T(8,128)S(1)}, f32[2,256,128]{2,1,0:T(8,128)S(1)}, u32[]{:S(2)}, u32[]{:S(2)}) %collective-permute-start.33) | collective-permute-done | bytes 262176 | tf_op jit(solution)/shard_map/ppermute | solution.py:353
  167.7 4.8 %collective-permute-done.34.refs_2_ = f32[2,128,128]{2,1,0:T(8,128)S(1)} collective-permute-done((f32[2,128,128]{2,1,0:T(8,128)S(1)}, f32[2,128,128]{2,1,0:T(8,128)S(1)}, u32[]{:S(2)}, u32[]{:S(2)}) %collective-permute-start.34) | collective-permute-done | bytes 131104 | tf_op jit(solution)/shard_map/ppermute | solution.py:353
  174.1 6.6 %collective-permute-done.37.refs_2_ = f32[4,256,128]{2,1,0:T(8,128)S(1)} collective-permute-done((f32[4,256,128]{2,1,0:T(8,128)S(1)}, f32[4,256,128]{2,1,0:T(8,128)S(1)}, u32[]{:S(2)}, u32[]{:S(2)}) %collective-permute-start.37) | collective-permute-done | bytes 524320 | tf_op jit(solution)/shard_map/ppermute | solution.py:353
  182.9 7.4 %collective-permute-done.38.refs_2_ = f32[4,128,128]{2,1,0:T(8,128)S(1)} collective-permute-done((f32[4,128,128]{2,1,0:T(8,128)S(1)}, f32[4,128,128]{2,1,0:T(8,128)S(1)}, u32[]{:S(2)}, u32[]{:S(2)}) %collective-permute-start.38) | collective-permute-done | bytes 262176 | tf_op jit(solution)/shard_map/ppermute | solution.py:353
  191.7 19.3 %update_panels01.1 = (f32[1024,2048]{1,0:T(8,128)}, f32[512,2048]{1,0:T(8,128)}) custom-call(s32[1]{0:T(128)} %bitcast.place.place_ref, f32[8,128]{1,0:T(8,128)S(1)} %get-tuple-element.210.refs_0_, f32[8,256,128]{2,1,0:T(8,128)S(1)} %collective-permute-done.39.refs_1_.refs_8_.refs_4_, f32[4,256,256]{2,1,0:T(8,128)S(1)} %fusion.1.refs_1_.refs_2_, ...), custom_call_target="tpu_custom_call" | custom-call | flops 1 | bytes 1 | tf_op jit(solution)/shard_map/update_panels01/pallas_call | solution.py:325
  211.0 13.5 %update_panels2.1 = (f32[1024,2048]{1,0:T(8,128)}, f32[256,2048]{1,0:T(8,128)S(1)}) custom-call(s32[1]{0:T(128)} %bitcast.place.place_ref, f32[1024,2048]{1,0:T(8,128)} %get-tuple-element.213.refs_0_.refs_12_, f32[8,256,128]{2,1,0:T(8,128)S(1)} %collective-permute-done.41.refs_1_.refs_6_.refs_4_, f32[4,256,256]{2,1,0:T(8,128)S(1)} %fusion.1.refs_1_.refs_2_, ...), custom_call_target="tpu_custom_call" | custom-call | flops 1 | bytes 1 | tf_op jit(solution)/shard_map/update_panels2/pallas_call | solution.py:325
  224.5 10.5 %update_panels3.1 = f32[1024,2048]{1,0:T(8,128)} custom-call(s32[1]{0:T(128)} %bitcast.place.place_ref, f32[1024,2048]{1,0:T(8,128)} %get-tuple-element.216.refs_0_.refs_10_, f32[8,128,128]{2,1,0:T(8,128)S(1)} %collective-permute-done.42.refs_1_.refs_6_, f32[4,256,256]{2,1,0:T(8,128)S(1)} %fusion.1.refs_1_.refs_2_, ...), custom_call_target="tpu_custom_call" | custom-call | flops 1 | bytes 1 | tf_op jit(solution)/shard_map/update_panels3/pallas_call | solution.py:325
  (108 shorter events, 46.4 us)
Async XLA Ops:
  0.0 15.3 %collective-permute-start = (f32[4,1024,128]{2,1,0:T(8,128)}, f32[4,1024,128]{2,1,0:T(8,128)}, u32[]{:S(2)}, u32[]{:S(2)}) collective-permute-start(f32[4,1024,128]{2,1,0:T(8,128)} %refs_8_.1), channel_id=1, source_target_pairs={{1,0},{0,1},{3,2},{2,3},{5,4},{4,5},{7,6},{6,7},{9,8},{8,9},{11,10... | collective-permute-start | bytes 6291464 | tf_op jit(solution)/shard_map/ppermute | solution.py:358
  0.5 13.5 %collective-permute-start.1 = (f32[4,128,256]{2,1,0:T(8,128)}, f32[4,128,256]{2,1,0:T(8,128)}, u32[]{:S(2)}, u32[]{:S(2)}) collective-permute-start(f32[4,128,256]{2,1,0:T(8,128)} %param.5), channel_id=1, source_target_pairs={{1,0},{0,1},{3,2},{2,3},{5,4},{4,5},{7,6},{6,7},{9,8},{8,9},{11,10... | collective-permute-start | bytes 1572872 | tf_op jit(solution)/shard_map/ppermute | solution.py:358
  11.0 15.1 %collective-permute-start.2 = (f32[8,192,128]{2,1,0:T(8,128)}, f32[8,192,128]{2,1,0:T(8,128)}, u32[]{:S(2)}, u32[]{:S(2)}) collective-permute-start(f32[8,192,128]{2,1,0:T(8,128)} %get-tuple-element.117), channel_id=1, source_target_pairs={{0,2},{1,5},{2,0},{3,7},{4,6},{5,1},{6,4},{7,3},{8,10},{9,13},{10,... | collective-permute-start | bytes 2359304 | tf_op jit(solution)/shard_map/ppermute | solution.py:353
  25.6 23.9 %collective-permute-start.4 = (f32[8,288,128]{2,1,0:T(8,128)S(1)}, f32[8,288,128]{2,1,0:T(8,128)S(1)}, u32[]{:S(2)}, u32[]{:S(2)}) collective-permute-start(f32[8,288,128]{2,1,0:T(8,128)S(1)} %get-tuple-element.125), channel_id=1, source_target_pairs={{0,2},{1,5},{2,0},{3,7},{4,6},{5,1},{6,4},{7,3},{8,10},{9,13},{10,... | collective-permute-start | bytes 3538952 | tf_op jit(solution)/shard_map/ppermute | solution.py:353
  36.9 16.2 %collective-permute-start.5 = (f32[8,256,128]{2,1,0:T(8,128)S(1)}, f32[8,256,128]{2,1,0:T(8,128)S(1)}, u32[]{:S(2)}, u32[]{:S(2)}) collective-permute-start(f32[8,256,128]{2,1,0:T(8,128)S(1)} %get-tuple-element.128), channel_id=1, source_target_pairs={{0,2},{1,5},{2,0},{3,7},{4,6},{5,1},{6,4},{7,3},{8,10},{9,13},{10,... | collective-permute-start | bytes 3145736 | tf_op jit(solution)/shard_map/ppermute | solution.py:353
  48.2 17.9 %collective-permute-start.7 = (f32[8,256,128]{2,1,0:T(8,128)S(1)}, f32[8,256,128]{2,1,0:T(8,128)S(1)}, u32[]{:S(2)}, u32[]{:S(2)}) collective-permute-start(f32[8,256,128]{2,1,0:T(8,128)S(1)} %get-tuple-element.134), channel_id=1, source_target_pairs={{0,2},{1,5},{2,0},{3,7},{4,6},{5,1},{6,4},{7,3},{8,10},{9,13},{10,... | collective-permute-start | bytes 3145736 | tf_op jit(solution)/shard_map/ppermute | solution.py:353
  49.7 16.3 %collective-permute-start.6 = (f32[4,288,128]{2,1,0:T(8,128)S(1)}, f32[4,288,128]{2,1,0:T(8,128)S(1)}, u32[]{:S(2)}, u32[]{:S(2)}) collective-permute-start(f32[4,288,128]{2,1,0:T(8,128)S(1)} %get-tuple-element.131), channel_id=1, source_target_pairs={{0,8},{1,9},{2,10},{3,11},{4,12},{5,13},{6,14},{7,15},{8,0},{9,1},... | collective-permute-start | bytes 1769480 | tf_op jit(solution)/shard_map/ppermute | solution.py:353
  51.3 21.2 %collective-permute-start.8 = (f32[8,128,128]{2,1,0:T(8,128)S(1)}, f32[8,128,128]{2,1,0:T(8,128)S(1)}, u32[]{:S(2)}, u32[]{:S(2)}) collective-permute-start(f32[8,128,128]{2,1,0:T(8,128)S(1)} %get-tuple-element.137), channel_id=1, source_target_pairs={{0,2},{1,5},{2,0},{3,7},{4,6},{5,1},{6,4},{7,3},{8,10},{9,13},{10,... | collective-permute-start | bytes 1572872 | tf_op jit(solution)/shard_map/ppermute | solution.py:353
  53.2 24.0 %collective-permute-start.10 = (f32[4,256,128]{2,1,0:T(8,128)S(1)}, f32[4,256,128]{2,1,0:T(8,128)S(1)}, u32[]{:S(2)}, u32[]{:S(2)}) collective-permute-start(f32[4,256,128]{2,1,0:T(8,128)S(1)} %get-tuple-element.143), channel_id=1, source_target_pairs={{0,8},{1,9},{2,10},{3,11},{4,12},{5,13},{6,14},{7,15},{8,0},{9,1},... | collective-permute-start | bytes 1572872 | tf_op jit(solution)/shard_map/ppermute | solution.py:353
  66.2 22.2 %collective-permute-start.13 = (f32[4,256,128]{2,1,0:T(8,128)S(1)}, f32[4,256,128]{2,1,0:T(8,128)S(1)}, u32[]{:S(2)}, u32[]{:S(2)}) collective-permute-start(f32[4,256,128]{2,1,0:T(8,128)S(1)} %get-tuple-element.152), channel_id=1, source_target_pairs={{0,8},{1,9},{2,10},{3,11},{4,12},{5,13},{6,14},{7,15},{8,0},{9,1},... | collective-permute-start | bytes 1572872 | tf_op jit(solution)/shard_map/ppermute | solution.py:353
  78.7 15.1 %collective-permute-start.14 = (f32[4,128,128]{2,1,0:T(8,128)S(1)}, f32[4,128,128]{2,1,0:T(8,128)S(1)}, u32[]{:S(2)}, u32[]{:S(2)}) collective-permute-start(f32[4,128,128]{2,1,0:T(8,128)S(1)} %get-tuple-element.155), channel_id=1, source_target_pairs={{0,8},{1,9},{2,10},{3,11},{4,12},{5,13},{6,14},{7,15},{8,0},{9,1},... | collective-permute-start | bytes 786440 | tf_op jit(solution)/shard_map/ppermute | solution.py:353
  88.5 15.2 %collective-permute-start.16 = (f32[2,256,128]{2,1,0:T(8,128)S(1)}, f32[2,256,128]{2,1,0:T(8,128)S(1)}, u32[]{:S(2)}, u32[]{:S(2)}) collective-permute-start(f32[2,256,128]{2,1,0:T(8,128)S(1)} %get-tuple-element.161), channel_id=1, source_target_pairs={{0,4},{1,3},{2,6},{3,1},{4,0},{5,7},{6,2},{7,5},{8,12},{9,11},{10,... | collective-permute-start | bytes 786440 | tf_op jit(solution)/shard_map/ppermute | solution.py:353
  90.8 12.7 %collective-permute-start.15 = (f32[1,192,128]{2,1,0:T(8,128)S(1)}, f32[1,192,128]{2,1,0:T(8,128)S(1)}, u32[]{:S(2)}, u32[]{:S(2)}) collective-permute-start(f32[1,192,128]{2,1,0:T(8,128)S(1)} %get-tuple-element.158), channel_id=1, source_target_pairs={{0,16},{1,17},{2,18},{3,19},{4,20},{5,21},{6,22},{7,23},{8,24},{9,... | collective-permute-start | bytes 294920 | tf_op jit(solution)/shard_map/ppermute | solution.py:353
  92.5 14.2 %collective-permute-start.17 = (f32[1,288,128]{2,1,0:T(8,128)S(1)}, f32[1,288,128]{2,1,0:T(8,128)S(1)}, u32[]{:S(2)}, u32[]{:S(2)}) collective-permute-start(f32[1,288,128]{2,1,0:T(8,128)S(1)} %get-tuple-element.164), channel_id=1, source_target_pairs={{0,16},{1,17},{2,18},{3,19},{4,20},{5,21},{6,22},{7,23},{8,24},{9,... | collective-permute-start | bytes 442376 | tf_op jit(solution)/shard_map/ppermute | solution.py:353
  93.8 12.9 %collective-permute-start.18 = (f32[2,128,128]{2,1,0:T(8,128)S(1)}, f32[2,128,128]{2,1,0:T(8,128)S(1)}, u32[]{:S(2)}, u32[]{:S(2)}) collective-permute-start(f32[2,128,128]{2,1,0:T(8,128)S(1)} %get-tuple-element.167), channel_id=1, source_target_pairs={{0,4},{1,3},{2,6},{3,1},{4,0},{5,7},{6,2},{7,5},{8,12},{9,11},{10,... | collective-permute-start | bytes 393224 | tf_op jit(solution)/shard_map/ppermute | solution.py:353
  95.2 14.3 %collective-permute-start.19 = (f32[1,256,128]{2,1,0:T(8,128)S(1)}, f32[1,256,128]{2,1,0:T(8,128)S(1)}, u32[]{:S(2)}, u32[]{:S(2)}) collective-permute-start(f32[1,256,128]{2,1,0:T(8,128)S(1)} %get-tuple-element.170), channel_id=1, source_target_pairs={{0,16},{1,17},{2,18},{3,19},{4,20},{5,21},{6,22},{7,23},{8,24},{9,... | collective-permute-start | bytes 393224 | tf_op jit(solution)/shard_map/ppermute | solution.py:353
  110.6 11.1 %collective-permute-start.22 = (f32[2,192,128]{2,1,0:T(8,128)S(1)}, f32[2,192,128]{2,1,0:T(8,128)S(1)}, u32[]{:S(2)}, u32[]{:S(2)}) collective-permute-start(f32[2,192,128]{2,1,0:T(8,128)S(1)} %get-tuple-element.177.refs_1_), channel_id=1, source_target_pairs={{0,4},{1,3},{2,6},{3,1},{4,0},{5,7},{6,2},{7,5},{8,12},{9,11},{10,... | collective-permute-start | bytes 589832 | tf_op jit(solution)/shard_map/ppermute | solution.py:353
  111.3 12.4 %collective-permute-start.23 = (f32[1,288,128]{2,1,0:T(8,128)S(1)}, f32[1,288,128]{2,1,0:T(8,128)S(1)}, u32[]{:S(2)}, u32[]{:S(2)}) collective-permute-start(f32[1,288,128]{2,1,0:T(8,128)S(1)} %get-tuple-element.179.refs_1_), channel_id=1, source_target_pairs={{0,16},{1,17},{2,18},{3,19},{4,20},{5,21},{6,22},{7,23},{8,24},{9,... | collective-permute-start | bytes 442376 | tf_op jit(solution)/shard_map/ppermute | solution.py:353
  121.7 14.5 %collective-permute-start.27 = (f32[4,192,128]{2,1,0:T(8,128)S(1)}, f32[4,192,128]{2,1,0:T(8,128)S(1)}, u32[]{:S(2)}, u32[]{:S(2)}) collective-permute-start(f32[4,192,128]{2,1,0:T(8,128)S(1)} %get-tuple-element.188.refs_1_), channel_id=1, source_target_pairs={{0,8},{1,9},{2,10},{3,11},{4,12},{5,13},{6,14},{7,15},{8,0},{9,1},... | collective-permute-start | bytes 1179656 | tf_op jit(solution)/shard_map/ppermute | solution.py:353
  123.7 12.0 %collective-permute-start.25 = (f32[2,288,128]{2,1,0:T(8,128)S(1)}, f32[2,288,128]{2,1,0:T(8,128)S(1)}, u32[]{:S(2)}, u32[]{:S(2)}) collective-permute-start(f32[2,288,128]{2,1,0:T(8,128)S(1)} %get-tuple-element.184.refs_1_), channel_id=1, source_target_pairs={{0,4},{1,3},{2,6},{3,1},{4,0},{5,7},{6,2},{7,5},{8,12},{9,11},{10,... | collective-permute-start | bytes 884744 | tf_op jit(solution)/shard_map/ppermute | solution.py:353
  124.4 11.4 %collective-permute-start.26 = (f32[1,256,128]{2,1,0:T(8,128)S(1)}, f32[1,256,128]{2,1,0:T(8,128)S(1)}, u32[]{:S(2)}, u32[]{:S(2)}) collective-permute-start(f32[1,256,128]{2,1,0:T(8,128)S(1)} %get-tuple-element.186.refs_1_), channel_id=1, source_target_pairs={{0,16},{1,17},{2,18},{3,19},{4,20},{5,21},{6,22},{7,23},{8,24},{9,... | collective-permute-start | bytes 393224 | tf_op jit(solution)/shard_map/ppermute | solution.py:353
  136.3 18.5 %collective-permute-start.31 = (f32[8,192,128]{2,1,0:T(8,128)S(1)}, f32[8,192,128]{2,1,0:T(8,128)S(1)}, u32[]{:S(2)}, u32[]{:S(2)}) collective-permute-start(f32[8,192,128]{2,1,0:T(8,128)S(1)} %get-tuple-element.196.refs_3_), channel_id=1, source_target_pairs={{0,2},{1,5},{2,0},{3,7},{4,6},{5,1},{6,4},{7,3},{8,10},{9,13},{10,... | collective-permute-start | bytes 2359304 | tf_op jit(solution)/shard_map/ppermute | solution.py:353
  138.0 16.8 %collective-permute-start.32 = (f32[4,288,128]{2,1,0:T(8,128)S(1)}, f32[4,288,128]{2,1,0:T(8,128)S(1)}, u32[]{:S(2)}, u32[]{:S(2)}) collective-permute-start(f32[4,288,128]{2,1,0:T(8,128)S(1)} %get-tuple-element.197.refs_2_), channel_id=1, source_target_pairs={{0,8},{1,9},{2,10},{3,11},{4,12},{5,13},{6,14},{7,15},{8,0},{9,1},... | collective-permute-start | bytes 1769480 | tf_op jit(solution)/shard_map/ppermute | solution.py:353
  138.0 14.6 %collective-permute-start.30 = (f32[2,256,128]{2,1,0:T(8,128)S(1)}, f32[2,256,128]{2,1,0:T(8,128)S(1)}, u32[]{:S(2)}, u32[]{:S(2)}) collective-permute-start(f32[2,256,128]{2,1,0:T(8,128)S(1)} %get-tuple-element.194.refs_1_), channel_id=1, source_target_pairs={{0,4},{1,3},{2,6},{3,1},{4,0},{5,7},{6,2},{7,5},{8,12},{9,11},{10,... | collective-permute-start | bytes 786440 | tf_op jit(solution)/shard_map/ppermute | solution.py:353
  138.4 13.5 %collective-permute-start.28 = (f32[1,256,128]{2,1,0:T(8,128)S(1)}, f32[1,256,128]{2,1,0:T(8,128)S(1)}, u32[]{:S(2)}, u32[]{:S(2)}) collective-permute-start(f32[1,256,128]{2,1,0:T(8,128)S(1)} %get-tuple-element.190.refs_1_), channel_id=1, source_target_pairs={{0,16},{1,17},{2,18},{3,19},{4,20},{5,21},{6,22},{7,23},{8,24},{9,... | collective-permute-start | bytes 393224 | tf_op jit(solution)/shard_map/ppermute | solution.py:353
  140.3 12.3 %collective-permute-start.29 = (f32[1,128,128]{2,1,0:T(8,128)S(1)}, f32[1,128,128]{2,1,0:T(8,128)S(1)}, u32[]{:S(2)}, u32[]{:S(2)}) collective-permute-start(f32[1,128,128]{2,1,0:T(8,128)S(1)} %get-tuple-element.192.refs_1_), channel_id=1, source_target_pairs={{0,16},{1,17},{2,18},{3,19},{4,20},{5,21},{6,22},{7,23},{8,24},{9,... | collective-permute-start | bytes 196616 | tf_op jit(solution)/shard_map/ppermute | solution.py:353
  154.9 19.1 %collective-permute-start.36 = (f32[8,288,128]{2,1,0:T(8,128)S(1)}, f32[8,288,128]{2,1,0:T(8,128)S(1)}, u32[]{:S(2)}, u32[]{:S(2)}) collective-permute-start(f32[8,288,128]{2,1,0:T(8,128)S(1)} %get-tuple-element.205.refs_2_.refs_5_), channel_id=1, source_target_pairs={{0,2},{1,5},{2,0},{3,7},{4,6},{5,1},{6,4},{7,3},{8,10},{9,13},{10,... | collective-permute-start | bytes 3538952 | tf_op jit(solution)/shard_map/ppermute | solution.py:353
  157.8 14.9 %collective-permute-start.35 = (f32[4,256,128]{2,1,0:T(8,128)S(1)}, f32[4,256,128]{2,1,0:T(8,128)S(1)}, u32[]{:S(2)}, u32[]{:S(2)}) collective-permute-start(f32[4,256,128]{2,1,0:T(8,128)S(1)} %get-tuple-element.203.refs_1_), channel_id=1, source_target_pairs={{0,8},{1,9},{2,10},{3,11},{4,12},{5,13},{6,14},{7,15},{8,0},{9,1},... | collective-permute-start | bytes 1572872 | tf_op jit(solution)/shard_map/ppermute | solution.py:353
  165.4 15.3 %collective-permute-start.37 = (f32[4,256,128]{2,1,0:T(8,128)S(1)}, f32[4,256,128]{2,1,0:T(8,128)S(1)}, u32[]{:S(2)}, u32[]{:S(2)}) collective-permute-start(f32[4,256,128]{2,1,0:T(8,128)S(1)} %get-tuple-element.207.refs_1_), channel_id=1, source_target_pairs={{0,8},{1,9},{2,10},{3,11},{4,12},{5,13},{6,14},{7,15},{8,0},{9,1},... | collective-permute-start | bytes 1572872 | tf_op jit(solution)/shard_map/ppermute | solution.py:353
  172.7 19.0 %collective-permute-start.39 = (f32[8,256,128]{2,1,0:T(8,128)S(1)}, f32[8,256,128]{2,1,0:T(8,128)S(1)}, u32[]{:S(2)}, u32[]{:S(2)}) collective-permute-start(f32[8,256,128]{2,1,0:T(8,128)S(1)} %get-tuple-element.211.refs_7_.refs_3_), channel_id=1, source_target_pairs={{0,2},{1,5},{2,0},{3,7},{4,6},{5,1},{6,4},{7,3},{8,10},{9,13},{10,... | collective-permute-start | bytes 3145736 | tf_op jit(solution)/shard_map/ppermute | solution.py:353
  180.8 30.2 %collective-permute-start.41 = (f32[8,256,128]{2,1,0:T(8,128)S(1)}, f32[8,256,128]{2,1,0:T(8,128)S(1)}, u32[]{:S(2)}, u32[]{:S(2)}) collective-permute-start(f32[8,256,128]{2,1,0:T(8,128)S(1)} %get-tuple-element.214.refs_5_.refs_3_), channel_id=1, source_target_pairs={{0,2},{1,5},{2,0},{3,7},{4,6},{5,1},{6,4},{7,3},{8,10},{9,13},{10,... | collective-permute-start | bytes 3145736 | tf_op jit(solution)/shard_map/ppermute | solution.py:353
  190.3 34.2 %collective-permute-start.42 = (f32[8,128,128]{2,1,0:T(8,128)S(1)}, f32[8,128,128]{2,1,0:T(8,128)S(1)}, u32[]{:S(2)}, u32[]{:S(2)}) collective-permute-start(f32[8,128,128]{2,1,0:T(8,128)S(1)} %get-tuple-element.217.refs_5_), channel_id=1, source_target_pairs={{0,2},{1,5},{2,0},{3,7},{4,6},{5,1},{6,4},{7,3},{8,10},{9,13},{10,... | collective-permute-start | bytes 1572872 | tf_op jit(solution)/shard_map/ppermute | solution.py:353
  (15 other events, 114.4 us)

commit v5 on v4

--- a/solution.py
+++ b/solution.py
@@ -21,22 +21,21 @@
 )
 GRAM_GROUP = 1
 CALLS = ((0,), (1,), (2,), (3, 4))
-UPDATES = ((0, 1), (2,), (3,))
 ORDER = (
-    ["p0", "g", "p1", "k1.0", "p2", "k2.0", "p3", "k1.1", "k1.2", "k2.1", "k1.3", "k1.4", "k3.0", "k2.2", "k3.1"]
-    + ["k3.2", "k2.3", "k2.4", "k4.0", "k3.3", "k4.1", "k3.4", "k4.2", "k5.0", "k4.3", "k6.0", "k5.1", "k4.4"]
-    + ["k6.1", "k5.2", "k7.0", "k5.3", "k5.4", "k6.2", "f.0", "k7.1", "k6.3", "k6.4", "k7.2", "f.1", "x", "k7.3"]
-    + ["k7.4", "f.2", "u0", "f.3", "u1", "f.4", "u2"]
+    ["p0", "g", "p1", "k1.0", "p2", "k2.0", "k1.1", "p3", "k1.2", "k2.1", "k3.0", "k1.3", "k1.4", "k2.2", "k3.1"]
+    + ["k3.2", "k2.3", "k4.0", "k2.4", "k3.3", "k4.1", "k3.4", "k4.2", "k5.0", "k4.3", "k6.0", "k5.1", "k4.4"]
+    + ["k5.2", "k6.1", "k7.0", "k5.3", "k6.2", "k5.4", "f.0", "k7.1", "k6.4", "k6.3", "u0a", "k7.2", "k7.4", "f.1"]
+    + ["x", "u0b", "u1a", "f.2", "k7.3", "u1b", "f.4", "u2a", "u3a", "f.3", "u2b", "u3b"]
 )
 
 
-def schedule(steps):
+def schedule(steps, panels):
     if steps == 7:
         return ORDER
     groups = range(len(GROUPS))
     order = ["p0", "g"] + [f"p{call}" for call in range(1, len(CALLS))]
     order += [f"k{step}.{group}" for step in range(1, steps + 1) for group in groups]
-    return order + ["x"] + [f"u{update}" for update in range(len(UPDATES))]
+    return order + ["x"] + [f"u{panel}{half}" for panel in range(panels) for half in "ab"]
 
 
 def rows_of(chunk):
@@ -82,7 +81,7 @@
 ANY = pl.BlockSpec(memory_space=pl.ANY)
 SMEM = pl.BlockSpec(memory_space=pltpu.SMEM)
 
-COST = pl.CostEstimate(flops=1, bytes_accessed=1, transcendentals=0)
+COST = pl.CostEstimate(flops=10**12, bytes_accessed=100, transcendentals=0)
 
 
 def params():
@@ -236,104 +235,108 @@
     outs[0][half:] = ins[1][...]
 
 
-def update_kernel(panels, parts, carried, left_over, skip, groups, place, *refs):
-    count = len(panels)
-    factor_ref, refs = refs[skip], refs[skip + 1 :]
-    summed = {group: refs[2 * at : 2 * at + 2] for at, group in enumerate(groups)}
-    refs = refs[2 * len(groups) :]
-    gram_refs, refs = refs[:parts], refs[parts:]
-    carry_ref, refs = (refs[0], refs[1:]) if carried else (None, refs)
-    blocks, slab_ref, out_ref = refs[: 2 * count], refs[2 * count], refs[2 * count + 1]
-    depth_ref, proj_ref = refs[-2:]
-    depth = count * SIZE
+def update_kernel(panel, counts, place, *refs):
+    refs = list(refs)
+    take = lambda count: [refs.pop(0) for _ in range(count)]
+    take(counts["after"])
+    (factor_ref,) = take(1)
+    summed = take(counts["groups"])
+    gram_refs, past_refs, carry_refs = take(counts["grams"]), take(counts["past"]), take(counts["carry"])
+    blocks, (slab_ref,) = take(2), take(1)
+    take(counts["target"])
+    (out_ref,), extra_out, (token_out,) = take(1), take(counts["extra"]), take(1)
+    depth_ref, proj_ref = refs
     columns = slab_ref.shape[1]
-    wide = columns // 4
+    wide = columns // 2
 
     def gram_block(panel, other):
         at = pl.ds((panel * (panel - 1) // 2 + other) * SIZE, SIZE)
         width = gram_refs[0].shape[0]
         rows = [ref[:, at] for ref in gram_refs]
-        return jnp.concatenate([pltpu.roll(part, step * width, 1) if step else part for step, part in enumerate(rows)])
+        return left_depth(
+            jnp.concatenate([pltpu.roll(part, step * width, 1) if step else part for step, part in enumerate(rows)])
+        )
 
     @pl.when(pl.program_id(0) == 0)
     def _():
-        for row, panel in enumerate(panels):
-            for at, group, first, tall in pieces_of(panel):
-                half = summed[group][0].shape[0]
-                for slot in range(2 * half):
-                    lanes = pl.ds(pl.multiple_of((place[0] ^ slot) * LANES, LANES), LANES)
-                    proj_ref[pl.ds(row * SIZE + at, tall), lanes] = summed[group][slot // half][
-                        slot % half, pl.ds(first, tall)
-                    ]
-        factor = [left_depth(factor_ref[row]) for row in range(count)]
-        later = [panels[-1] + 1 + more for more in range(left_over)]
-        grams = {
-            (panel, row): left_depth(gram_block(panel, panels[row]))
-            for panel in list(panels) + later
-            for row in range(count)
-            if panels[row] < panel
-        }
-        for quarter in range(4):
-            at = pl.ds(quarter * wide, wide)
-            past = []
-
-            def less(value, panel, sign):
-                for row, weights in enumerate(past):
-                    value = value + sign * dot(grams[panel, row], weights)
-                return value
-
-            for row in range(count):
-                proj = proj_ref[pl.ds(row * SIZE, SIZE), at]
-                if carried:
-                    proj = proj - carry_ref[pl.ds(row * SIZE, SIZE), at]
-                proj = less(proj, panels[row], -1.0)
-                high, low = halves(dot(factor[row], right_depth(proj)))
-                past.append(jnp.concatenate([high, high, low]))
-                for copy, value in enumerate([high, high, low]):
-                    depth_ref[pl.ds(copy * depth + row * SIZE, SIZE), at] = value
-            for more, panel in enumerate(later):
-                value = carry_ref[pl.ds((count + more) * SIZE, SIZE), at] if carried else jnp.zeros((SIZE, wide), F32)
-                refs[2 * count + 2][pl.ds(more * SIZE, SIZE), at] = less(value, panel, 1.0)
+        token_out[...] = jnp.zeros(TOKEN.shape, F32)
+        groups = groups_of(panel)
+        for at, group, first, tall in pieces_of(panel):
+            ref = summed[groups.index(group)]
+            half = ref.shape[0]
+            for slot in range(half):
+                lanes = pl.ds(pl.multiple_of(((place[0] ^ slot) & (half - 1)) * LANES, LANES), LANES)
+                proj_ref[pl.ds(at, tall), lanes] = ref[slot, pl.ds(first, tall)]
+        factor = left_depth(factor_ref[0])
+        before = [gram_block(panel, other) for other in range(counts["past"])]
+        later = list(range(panel + 1, panel + 1 + extra_out[0].shape[0] // SIZE)) if gram_refs else []
+        grams = {more: [gram_block(more, other) for other in range(panel - counts["past"], panel + 1)] for more in later}
+        for side in range(2):
+            at = pl.ds(side * wide, wide)
+            proj = proj_ref[:, at]
+            if carry_refs:
+                proj = proj - carry_refs[0][:SIZE, at]
+            for other, block in enumerate(before):
+                proj = proj - dot(block, past_refs[other][:, at])
+            high, low = halves(dot(factor, right_depth(proj)))
+            weights = jnp.concatenate([high, high, low])
+            depth_ref[:, at] = weights
+            if extra_out and not gram_refs:
+                extra_out[0][:, at] = weights
+            for row, more in enumerate(later):
+                terms = [ref[:, at] for ref in past_refs] + [weights]
+                value = sum(dot(block, term) for block, term in zip(grams[more], terms))
+                if carry_refs:
+                    value = value + carry_refs[0][pl.ds((row + 1) * SIZE, SIZE), at]
+                extra_out[0][pl.ds(row * SIZE, SIZE), at] = value
 
     left = left_depth(jnp.concatenate([ref[0] for ref in blocks], axis=1))
-    for quarter in range(4):
-        at = pl.ds(quarter * wide, wide)
+    for side in range(2):
+        at = pl.ds(side * wide, wide)
         out_ref[:, at] = slab_ref[:, at] - dot(left, depth_ref[:, at])
 
 
-def update(place, after, panels, left_over, sides, factors, slab, state, grams, carry):
-    rows, columns = slab.shape
+def groups_of(panel):
+    return sorted({piece[1] for piece in pieces_of(panel)})
+
+
+def update(place, after, panel, far, later, sides, factors, slab, target, pieces, grams, past, carry):
+    rows, columns = slab.shape[0], slab.shape[1] // 2
     steps = 4
     deep = rows // steps
-    first, count = panels[0], len(panels)
     size = factors.shape[-1]
-    groups = sorted({piece[1] for panel in panels for piece in pieces_of(panel)})
-    strip = pl.BlockSpec((deep, columns), lambda j: (j, 0))
-    specs, blocks = [], []
-    for panel in panels:
-        for side in range(2):
-            specs.append(pl.BlockSpec((1, deep, LANES), lambda j, panel=panel: (panel, j, 0)))
-            blocks.append(sides[side])
-    factor = pl.BlockSpec((count, size, size), lambda j: (first // count, 0, 0), pipeline_mode=pl.Buffered(1))
-    grams = grams if left_over or count > 1 else []
-    carries = [] if carry is None else [carry]
-    constant = [x for group in groups for x in state[group]] + list(grams) + carries
-    outs, out_specs = [shape(rows, columns)], [strip]
-    if left_over:
-        outs.append(shape(left_over * size, columns))
-        out_specs.append(pl.BlockSpec(outs[1].shape, lambda j: (0, 0)))
-    made = pl.pallas_call(
-        functools.partial(update_kernel, panels, len(grams), len(carries), left_over, len(after), groups),
-        grid=(steps,),
-        in_specs=[SMEM] + [ANY] * len(after) + [factor] + [whole(x) for x in constant] + specs + [strip],
-        out_specs=out_specs,
-        scratch_shapes=[pltpu.VMEM((3 * count * size, columns), jnp.bfloat16), pltpu.VMEM((count * size, columns), F32)],
+    strip = pl.BlockSpec((deep, columns), lambda j, place: (j, place[1] ^ far))
+    fixed = lambda x: pl.BlockSpec(x.shape, lambda j, place: (0,) * len(x.shape), pipeline_mode=pl.Buffered(1))
+    block = pl.BlockSpec((1, deep, LANES), lambda j, place: (panel, j, 0))
+    factor = pl.BlockSpec((1, size, size), lambda j, place: (panel, 0, 0), pipeline_mode=pl.Buffered(1))
+    constant = list(pieces) + list(grams) + list(past) + list(carry)
+    outs, out_specs = [shape(*slab.shape)], [strip]
+    if later:
+        extra = shape(later * size, columns) if grams else jax.ShapeDtypeStruct((3 * size, columns), jnp.bfloat16)
+        outs.append(extra)
+        out_specs.append(pl.BlockSpec(extra.shape, lambda j, place: (0, 0)))
+    outs.append(TOKEN)
+    out_specs.append(pl.BlockSpec(TOKEN.shape, lambda j, place: (0, 0)))
+    operands = [place, *after, factors, *constant, sides[0], sides[1], slab, *target]
+    counts = dict(
+        after=len(after), groups=len(pieces), grams=len(grams), past=len(past), carry=len(carry), target=len(target),
+        extra=len(outs) - 2,
+    )
+    return pl.pallas_call(
+        functools.partial(update_kernel, panel, counts),
+        grid_spec=pltpu.PrefetchScalarGridSpec(
+            num_scalar_prefetch=1,
+            grid=(steps,),
+            in_specs=[ANY] * len(after) + [factor] + [fixed(x) for x in constant] + [block, block, strip] + [ANY] * len(target),
+            out_specs=out_specs,
+            scratch_shapes=[pltpu.VMEM((3 * size, columns), jnp.bfloat16), pltpu.VMEM((size, columns), F32)],
+        ),
         out_shape=outs,
+        input_output_aliases={len(operands) - 1: 0} if panel or target else {},
         compiler_params=params(),
         cost_estimate=COST,
-        name="update_panels" + "".join(map(str, panels)),
-    )(place, *after, factors, *constant, *blocks, slab)
-    return made[0], made[1] if left_over else None
+        name=f"update_{panel}" + "ab"[far],
+    )(*operands)
 
 
 def order_of(kind, bits):
@@ -369,7 +372,8 @@
     own = [
         sum(((me >> bit) & 1) << (cuts - 1 - at) for at, bit in enumerate(order_of(kind, bits)[:cuts])) for kind in range(2)
     ]
-    place = jnp.stack([jnp.where(core % 2 == 0, own[0], own[1])]).astype(jnp.int32)
+    block = jnp.where(core % 2 == 0, own[0], own[1])
+    place = jnp.stack([block, block >> (cuts - 1)]).astype(jnp.int32)
 
     parts = [reflectors] + [shift(reflectors, step) for step in range(1, others)]
     join = lambda some: some[0] if len(some) == 1 else jnp.concatenate(some, axis=2)
@@ -378,7 +382,8 @@
     factors = lax.dynamic_slice_in_dim(jnp.concatenate([factor_rows, factor_rows], axis=2), core * width, size, axis=2)
 
     after = [jnp.zeros(TOKEN.shape, F32)]
-    state, grams, slab, carry = {}, [], eigvecs, None
+    state, grams, slab = {}, [], eigvecs
+    past, carry = [[], []], [[], []]
 
     def kernel(function, name, ins, outs):
         nonlocal after
@@ -386,7 +391,7 @@
         after = [token]
         return made
 
-    for event in schedule(bits + cuts - 1):
+    for event in schedule(bits + cuts - 1, panels):
         if event[0] == "p":
             call = CALLS[int(event[1:])]
             after = after + ([factors] if event == "p1" else [])
@@ -417,11 +422,16 @@
             (rows,) = kernel(gram_rows_kernel, "gram_own", state[GRAM_GROUP], [shape(width, wide)])
             grams = [rows] + [shift(rows, step) for step in range(1, others)]
         else:
-            some = UPDATES[int(event[1:])]
-            slab, carry = update(
-                place, after, some, panels - 1 - some[-1], sides, factors, slab, state, grams, carry
+            panel, far = int(event[1]), "ab".index(event[2])
+            later = panels - 1 - panel
+            pieces = [state[group][far] for group in groups_of(panel)]
+            source, target = (eigvecs, [slab] if far else []) if panel == 0 else (slab, [])
+            slab, *extra, token = update(
+                place, after, panel, far, later, sides, factors, source, target, pieces,
+                grams if panel and later else [], past[far] if panel == 1 else [], carry[far],
             )
-            after = [slab]
+            (carry if panel else past)[far] = extra
+            after = [token]
     return slab
 
 

time: 235 us -> 273 us (1.16)
  Pallas kernels: 79.4 us -> 177 us
  waiting for transfers between devices: 98.3 us -> 37.1 us
    pallas_call x36, Pallas kernels: 2.73 us -> 66.4 us  [small_call(): pl.pallas_call(run, in_specs=[SMEM] + [ANY] * len(after) + [pl.BlockSpec(...]
    ppermute x40, waiting for transfers between devices: 98.3 us -> 37.1 us  [swap(): return lax.ppermute(value, ('row', 'col'), pairs)]
    pallas_call x3 -> x8, Pallas kernels: 43.3 us -> 73 us  [update(): pl.pallas_call(functools.partial(update_kernel, panel, counts), grid_spec...]
    pallas_call x4, Pallas kernels: 29.9 us -> 33.4 us  [project(): pl.pallas_call(functools.partial(project_kernel, steps, call, blocks, len...]
  transfers between devices with their start and end apart: 43 -> 43, of which waited for: 24 -> 8; matrix products, arithmetic and copies ran while one was open for 1% -> 1% of each run, Pallas kernels for 29% -> 58%
where the time goes in v5:
time: 273 us; the launch traced here: 272 us
  Pallas kernels  177 us (65%)
  starting transfers between devices  51.3 us (19%)
  waiting for transfers between devices  37.1 us (14%)
  local copies, waits for them, and re-layouts  4.99 us (2%)
    pallas_call x8, Pallas kernels, update(): pl.pallas_call(functools.partial(update_kernel, panel, counts), grid_spec...  73 us
    pallas_call x36, Pallas kernels, small_call(): pl.pallas_call(run, in_specs=[SMEM] + [ANY] * len(after) + [pl.BlockSpec(...  66.4 us
    ppermute x40, starting transfers between devices, swap(): return lax.ppermute(value, ('row', 'col'), pairs)  50.8 us
    ppermute x40, waiting for transfers between devices, swap(): return lax.ppermute(value, ('row', 'col'), pairs)  37.1 us
    pallas_call x4, Pallas kernels, project(): pl.pallas_call(functools.partial(project_kernel, steps, call, blocks, len...  33.4 us
  transfers between devices with their start and end apart: 43, of which 8 were waited for; matrix products, arithmetic and copies ran while one was open for 1% of the time, Pallas kernels for 58%

profile of v5, /device:TPU:0, one launch (start us, length us, event | category | flops | bytes accessed | tf_op | source)
XLA Modules:
  0.0 271.6 jit_solution(12923541469769558556)
XLA Ops:
  0.6 3.4 %copy-done.2 = f32[1024,2048]{1,0:T(8,128)S(1)} copy-done((f32[1024,2048]{1,0:T(8,128)S(1)}, f32[1024,2048]{1,0:T(8,128)}, u32[]{:S(2)}) %copy-start.2) | copy-done | bytes 8388632
  5.6 6.1 %project_0.1 = (f32[8,192,128]{2,1,0:T(8,128)S(1)}, f32[8,192,128]{2,1,0:T(8,128)}, f32[8,128]{1,0:T(8,128)S(1)}) custom-call(s32[2]{0:T(128)S(1)} %pad_add_fusion.place.place_ref, f32[8,128]{1,0:T(8,128)S(1)} %broadcast_in_dim.3.refs_0_, f32[4,1024,128]{2,1,0:T(8,128)S(1)} %copy-done.3, f32[4,1024,128]{2,1,0:T(8,128)S(1)} %copy-done.3, ...), custom_call_target="tpu_custom_call" | custom-call | flops 999999995904 | bytes 100 | tf_op jit(solution)/shard_map/project_0/pallas_call | solution.py:161
  11.7 2.9 %collective-permute-start.2 = (f32[8,192,128]{2,1,0:T(8,128)}, f32[8,192,128]{2,1,0:T(8,128)}, u32[]{:S(2)}, u32[]{:S(2)}) collective-permute-start(f32[8,192,128]{2,1,0:T(8,128)} %get-tuple-element.134), channel_id=1, source_target_pairs={{0,2},{1,5},{2,0},{3,7},{4,6},{5,1},{6,4},{7,3},{8,10},{9,13},{10,... | collective-permute-start | bytes 2359304 | tf_op jit(solution)/shard_map/ppermute | solution.py:356
  15.9 3.9 %gram_rows.1 = (f32[16,96,128]{2,1,0:T(8,128)S(1)}, f32[8,128]{1,0:T(8,128)S(1)}) custom-call(s32[2]{0:T(128)S(1)} %pad_add_fusion.place.place_ref, f32[8,128]{1,0:T(8,128)S(1)} %get-tuple-element.129.refs_0_, f32[4,1024,128]{2,1,0:T(8,128)S(1)} %copy-done.4, f32[4,1024,128]{2,1,0:T(8,128)S(1)} %copy-done.4, ...), custom_call_target="tpu_custom_call" | custom-call | flops 999999995904 | bytes 100 | tf_op jit(solution)/shard_map/gram_rows/pallas_call | solution.py:199
  19.8 7.9 %project_1.1 = (f32[8,288,128]{2,1,0:T(8,128)S(1)}, f32[8,288,128]{2,1,0:T(8,128)}, f32[8,128]{1,0:T(8,128)S(1)}) custom-call(s32[2]{0:T(128)S(1)} %pad_add_fusion.place.place_ref, f32[8,128]{1,0:T(8,128)S(1)} %get-tuple-element.130.refs_0_, f32[4,256,256]{2,1,0:T(8,128)S(1)} %fusion.1.refs_1_.refs_2_, ...), custom_call_target="tpu_custom_call" | custom-call | flops 999999995904 | bytes 100 | tf_op jit(solution)/shard_map/project_1/pallas_call | solution.py:161
  31.9 8.8 %project_2.1 = (f32[8,256,128]{2,1,0:T(8,128)S(1)}, f32[8,256,128]{2,1,0:T(8,128)}, f32[8,128]{1,0:T(8,128)S(1)}) custom-call(s32[2]{0:T(128)S(1)} %pad_add_fusion.place.place_ref, f32[8,128]{1,0:T(8,128)S(1)} %get-tuple-element.135.refs_0_, f32[4,1024,128]{2,1,0:T(8,128)S(1)} %copy-done.4, ...), custom_call_target="tpu_custom_call" | custom-call | flops 999999995904 | bytes 100 | tf_op jit(solution)/shard_map/project_2/pallas_call | solution.py:161
  45.3 4.6 %collective-permute-done.4.refs_2_ = f32[8,288,128]{2,1,0:T(8,128)} collective-permute-done((f32[8,288,128]{2,1,0:T(8,128)}, f32[8,288,128]{2,1,0:T(8,128)}, u32[]{:S(2)}, u32[]{:S(2)}) %collective-permute-start.4) | collective-permute-done | bytes 1179680 | tf_op jit(solution)/shard_map/ppermute | solution.py:356
  49.9 2.3 halve1_1.1
  52.2 10.7 %project_34.1 = (f32[8,256,128]{2,1,0:T(8,128)S(1)}, f32[8,256,128]{2,1,0:T(8,128)}, f32[8,128,128]{2,1,0:T(8,128)S(1)}, f32[8,128,128]{2,1,0:T(8,128)}, f32[8,128]{1,0:T(8,128)S(1)}) custom-call(s32[2]{0:T(128)S(1)} %pad_add_fusion.place.place_ref, f32[8,128]{1,0:T(8,128)S(1)} %get-tuple-element.142.refs_0_, ...), custom_call_target="tpu_custom_call" | custom-call | flops 999999995904 | bytes 100 | tf_op jit(solution)/shard_map/project_34/pallas_call | solution.py:161
  64.9 2.2 halve1_2.1
  74.1 2.6 collective-permute-start.14
  76.7 4.5 %collective-permute-done.8.refs_2_ = f32[8,256,128]{2,1,0:T(8,128)} collective-permute-done((f32[8,256,128]{2,1,0:T(8,128)}, f32[8,256,128]{2,1,0:T(8,128)}, u32[]{:S(2)}, u32[]{:S(2)}) %collective-permute-start.8) | collective-permute-done | bytes 1048608 | tf_op jit(solution)/shard_map/ppermute | solution.py:356
  81.2 2.2 halve1_3.1
  83.4 3.5 %collective-permute-done.9.refs_2_ = f32[8,128,128]{2,1,0:T(8,128)} collective-permute-done((f32[8,128,128]{2,1,0:T(8,128)}, f32[8,128,128]{2,1,0:T(8,128)}, u32[]{:S(2)}, u32[]{:S(2)}) %collective-permute-start.9) | collective-permute-done | bytes 524320 | tf_op jit(solution)/shard_map/ppermute | solution.py:356
  96.1 2.6 collective-permute-start.17
  101.4 9.0 %collective-permute-done.13.refs_2_ = f32[4,256,128]{2,1,0:T(8,128)} collective-permute-done((f32[4,256,128]{2,1,0:T(8,128)}, f32[4,256,128]{2,1,0:T(8,128)}, u32[]{:S(2)}, u32[]{:S(2)}) %collective-permute-start.13) | collective-permute-done | bytes 524320 | tf_op jit(solution)/shard_map/ppermute | solution.py:356
  138.4 3.4 %collective-permute-done.23.refs_2_ = f32[1,288,128]{2,1,0:T(8,128)} collective-permute-done((f32[1,288,128]{2,1,0:T(8,128)}, f32[1,288,128]{2,1,0:T(8,128)}, u32[]{:S(2)}, u32[]{:S(2)}) %collective-permute-start.23) | collective-permute-done | bytes 147488 | tf_op jit(solution)/shard_map/ppermute | solution.py:356
  155.4 3.2 %collective-permute-done.27.refs_2_ = f32[4,192,128]{2,1,0:T(8,128)} collective-permute-done((f32[4,192,128]{2,1,0:T(8,128)}, f32[4,192,128]{2,1,0:T(8,128)}, u32[]{:S(2)}, u32[]{:S(2)}) %collective-permute-start.27) | collective-permute-done | bytes 393248 | tf_op jit(solution)/shard_map/ppermute | solution.py:356
  168.5 2.8 %collective-permute-done.32.refs_3_ = f32[4,288,128]{2,1,0:T(8,128)} collective-permute-done((f32[4,288,128]{2,1,0:T(8,128)}, f32[4,288,128]{2,1,0:T(8,128)}, u32[]{:S(2)}, u32[]{:S(2)}) %collective-permute-start.32) | collective-permute-done | bytes 589856 | tf_op jit(solution)/shard_map/ppermute | solution.py:356
  171.3 6.0 %collective-permute-done.31.refs_1_.refs_2_ = f32[8,192,128]{2,1,0:T(8,128)} collective-permute-done((f32[8,192,128]{2,1,0:T(8,128)}, f32[8,192,128]{2,1,0:T(8,128)}, u32[]{:S(2)}, u32[]{:S(2)}) %collective-permute-start.31) | collective-permute-done | bytes 786464 | tf_op jit(solution)/shard_map/ppermute | solution.py:356
  177.3 2.4 join7_1.1
  183.9 8.1 %update_0a.1 = (f32[1024,2048]{1,0:T(8,128)}, bf16[768,1024]{1,0:T(8,128)(2,1)S(1)}, f32[8,128]{1,0:T(8,128)S(1)}) custom-call(s32[2]{0:T(128)S(1)} %pad_add_fusion.place.place_ref, f32[8,128]{1,0:T(8,128)S(1)} %get-tuple-element.219.refs_0_, f32[4,256,256]{2,1,0:T(8,128)S(1)} %copy-done.1, f32[8,192,128]{2,1,0:T(8,128)} %get-tuple-element.213.refs_2_, ...), custom_call_target="tpu_custom_call" | custom-call | flops 999999995904 | bytes 100 | tf_op jit(solution)/shard_map/update_0a/pallas_call | solution.py:325
  192.0 2.3 join7_2.1
  200.2 2.6 gram_own.1
  202.8 8.0 %update_0b.1 = (f32[1024,2048]{1,0:T(8,128)}, bf16[768,1024]{1,0:T(8,128)(2,1)S(1)}, f32[8,128]{1,0:T(8,128)S(1)}) custom-call(s32[2]{0:T(128)S(1)} %pad_add_fusion.place.place_ref, f32[8,128]{1,0:T(8,128)S(1)} %get-tuple-element.226.refs_0_, f32[4,256,256]{2,1,0:T(8,128)S(1)} %copy-done.1, ...), custom_call_target="tpu_custom_call", output_to_operand_aliasing={{0}: (8, {})} | custom-call | flops 999999995904 | bytes 100 | tf_op jit(solution)/shard_map/update_0b/pallas_call | solution.py:325
  210.8 11.2 %update_1a.1 = (f32[1024,2048]{1,0:T(8,128)}, f32[512,1024]{1,0:T(8,128)S(1)}, f32[8,128]{1,0:T(8,128)S(1)}) custom-call(s32[2]{0:T(128)S(1)} %pad_add_fusion.place.place_ref, f32[8,128]{1,0:T(8,128)S(1)} %get-tuple-element.228.refs_0_, f32[4,256,256]{2,1,0:T(8,128)S(1)} %copy-done.1, ...), custom_call_target="tpu_custom_call", output_to_operand_aliasing={{0}: (11, {})} | custom-call | flops 999999995904 | bytes 100 | tf_op jit(solution)/shard_map/update_1a/pallas_call | solution.py:325
  222.1 2.3 join7_3.1
  225.9 11.5 %update_1b.1 = (f32[1024,2048]{1,0:T(8,128)}, f32[512,1024]{1,0:T(8,128)S(1)}, f32[8,128]{1,0:T(8,128)S(1)}) custom-call(s32[2]{0:T(128)S(1)} %pad_add_fusion.place.place_ref, f32[8,128]{1,0:T(8,128)S(1)} %get-tuple-element.235.refs_0_, f32[4,256,256]{2,1,0:T(8,128)S(1)} %copy-done.1, ...), custom_call_target="tpu_custom_call", output_to_operand_aliasing={{0}: (11, {})} | custom-call | flops 999999995904 | bytes 100 | tf_op jit(solution)/shard_map/update_1b/pallas_call | solution.py:325
  237.3 9.3 %update_2a.1 = (f32[1024,2048]{1,0:T(8,128)}, f32[256,1024]{1,0:T(8,128)S(1)}, f32[8,128]{1,0:T(8,128)S(1)}) custom-call(s32[2]{0:T(128)S(1)} %pad_add_fusion.place.place_ref, f32[8,128]{1,0:T(8,128)S(1)} %get-tuple-element.238.refs_0_, f32[8,128,128]{2,1,0:T(8,128)} %collective-permute-done.41.refs_1_.refs_3_, ...), custom_call_target="tpu_custom_call", output_to_operand_aliasing={{0}: (11, {})} | custom-call | flops 999999995904 | bytes 100 | tf_op jit(solution)/shard_map/update_2a/pallas_call | solution.py:325
  246.6 7.9 %update_3a.1 = (f32[1024,2048]{1,0:T(8,128)}, f32[8,128]{1,0:T(8,128)S(1)}) custom-call(s32[2]{0:T(128)S(1)} %pad_add_fusion.place.place_ref, f32[8,128]{1,0:T(8,128)S(1)} %get-tuple-element.243.refs_0_, f32[4,256,256]{2,1,0:T(8,128)S(1)} %copy-done.1, f32[8,256,128]{2,1,0:T(8,128)} %get-tuple-element.240.refs_4_.refs_2_, ...), custom_call_target="tpu_custom_call", output_to_operand_aliasing={{0}: (8, {})} | custom-call | flops 999999995904 | bytes 100 | tf_op jit(solution)/shard_map/update_3a/pallas_call | solution.py:325
  254.5 9.2 %update_2b.1 = (f32[1024,2048]{1,0:T(8,128)}, f32[256,1024]{1,0:T(8,128)S(1)}, f32[8,128]{1,0:T(8,128)S(1)}) custom-call(s32[2]{0:T(128)S(1)} %pad_add_fusion.place.place_ref, f32[8,128]{1,0:T(8,128)S(1)} %get-tuple-element.246.refs_0_, f32[8,256,128]{2,1,0:T(8,128)} %collective-permute-done.42.refs_1_.refs_4_.refs_2_, ...), custom_call_target="tpu_custom_call", output_to_operand_aliasing={{0}: (11, {})} | custom-call | flops 999999995904 | bytes 100 | tf_op jit(solution)/shard_map/update_2b/pallas_call | solution.py:325
  263.7 7.9 %update_3b.1 = (f32[1024,2048]{1,0:T(8,128)}, f32[8,128]{1,0:T(8,128)}) custom-call(s32[2]{0:T(128)S(1)} %pad_add_fusion.place.place_ref, f32[8,128]{1,0:T(8,128)S(1)} %get-tuple-element.249.refs_0_, f32[4,256,256]{2,1,0:T(8,128)S(1)} %copy-done.1, f32[8,256,128]{2,1,0:T(8,128)} %collective-permute-done.42.refs_1_.refs_4_.refs_2_, ...), custom_call_target="tpu_custom_call", output_to_operand_aliasing={{0}: (8, {})} | custom-call | flops 999999995904 | bytes 100 | tf_op jit(solution)/shard_map/update_3b/pallas_call | solution.py:325
  (118 shorter events, 96.5 us)
Async XLA Ops:
  0.0 15.9 %collective-permute-start = (f32[4,1024,128]{2,1,0:T(8,128)}, f32[4,1024,128]{2,1,0:T(8,128)}, u32[]{:S(2)}, u32[]{:S(2)}) collective-permute-start(f32[4,1024,128]{2,1,0:T(8,128)} %refs_5_.3), channel_id=1, source_target_pairs={{1,0},{0,1},{3,2},{2,3},{5,4},{4,5},{7,6},{6,7},{9,8},{8,9},{11,10... | collective-permute-start | bytes 6291464 | tf_op jit(solution)/shard_map/ppermute | solution.py:361
  0.5 14.2 %collective-permute-start.1 = (f32[4,128,256]{2,1,0:T(8,128)}, f32[4,128,256]{2,1,0:T(8,128)}, u32[]{:S(2)}, u32[]{:S(2)}) collective-permute-start(f32[4,128,256]{2,1,0:T(8,128)} %param.5), channel_id=1, source_target_pairs={{1,0},{0,1},{3,2},{2,3},{5,4},{4,5},{7,6},{6,7},{9,8},{8,9},{11,10... | collective-permute-start | bytes 1572872 | tf_op jit(solution)/shard_map/ppermute | solution.py:361
  11.7 16.0 %collective-permute-start.2 = (f32[8,192,128]{2,1,0:T(8,128)}, f32[8,192,128]{2,1,0:T(8,128)}, u32[]{:S(2)}, u32[]{:S(2)}) collective-permute-start(f32[8,192,128]{2,1,0:T(8,128)} %get-tuple-element.134), channel_id=1, source_target_pairs={{0,2},{1,5},{2,0},{3,7},{4,6},{5,1},{6,4},{7,3},{8,10},{9,13},{10,... | collective-permute-start | bytes 2359304 | tf_op jit(solution)/shard_map/ppermute | solution.py:356
  31.3 18.6 %collective-permute-start.4 = (f32[8,288,128]{2,1,0:T(8,128)}, f32[8,288,128]{2,1,0:T(8,128)}, u32[]{:S(2)}, u32[]{:S(2)}) collective-permute-start(f32[8,288,128]{2,1,0:T(8,128)} %get-tuple-element.141), channel_id=1, source_target_pairs={{0,2},{1,5},{2,0},{3,7},{4,6},{5,1},{6,4},{7,3},{8,10},{9,13},{10,... | collective-permute-start | bytes 3538952 | tf_op jit(solution)/shard_map/ppermute | solution.py:356
  40.7 24.3 %collective-permute-start.5 = (f32[8,256,128]{2,1,0:T(8,128)}, f32[8,256,128]{2,1,0:T(8,128)}, u32[]{:S(2)}, u32[]{:S(2)}) collective-permute-start(f32[8,256,128]{2,1,0:T(8,128)} %get-tuple-element.145), channel_id=1, source_target_pairs={{0,2},{1,5},{2,0},{3,7},{4,6},{5,1},{6,4},{7,3},{8,10},{9,13},{10,... | collective-permute-start | bytes 3145736 | tf_op jit(solution)/shard_map/ppermute | solution.py:356
  43.8 28.8 %collective-permute-start.7 = (f32[2,192,128]{2,1,0:T(8,128)}, f32[2,192,128]{2,1,0:T(8,128)}, u32[]{:S(2)}, u32[]{:S(2)}) collective-permute-start(f32[2,192,128]{2,1,0:T(8,128)} %get-tuple-element.151), channel_id=1, source_target_pairs={{0,4},{1,3},{2,6},{3,1},{4,0},{5,7},{6,2},{7,5},{8,12},{9,11},{10,... | collective-permute-start | bytes 589832 | tf_op jit(solution)/shard_map/ppermute | solution.py:356
  52.2 16.9 %collective-permute-start.6 = (f32[4,288,128]{2,1,0:T(8,128)}, f32[4,288,128]{2,1,0:T(8,128)}, u32[]{:S(2)}, u32[]{:S(2)}) collective-permute-start(f32[4,288,128]{2,1,0:T(8,128)} %get-tuple-element.148), channel_id=1, source_target_pairs={{0,8},{1,9},{2,10},{3,11},{4,12},{5,13},{6,14},{7,15},{8,0},{9,1},... | collective-permute-start | bytes 1769480 | tf_op jit(solution)/shard_map/ppermute | solution.py:356
  62.9 18.3 %collective-permute-start.8 = (f32[8,256,128]{2,1,0:T(8,128)}, f32[8,256,128]{2,1,0:T(8,128)}, u32[]{:S(2)}, u32[]{:S(2)}) collective-permute-start(f32[8,256,128]{2,1,0:T(8,128)} %get-tuple-element.154), channel_id=1, source_target_pairs={{0,2},{1,5},{2,0},{3,7},{4,6},{5,1},{6,4},{7,3},{8,10},{9,13},{10,... | collective-permute-start | bytes 3145736 | tf_op jit(solution)/shard_map/ppermute | solution.py:356
  62.9 23.9 %collective-permute-start.9 = (f32[8,128,128]{2,1,0:T(8,128)}, f32[8,128,128]{2,1,0:T(8,128)}, u32[]{:S(2)}, u32[]{:S(2)}) collective-permute-start(f32[8,128,128]{2,1,0:T(8,128)} %get-tuple-element.157), channel_id=1, source_target_pairs={{0,2},{1,5},{2,0},{3,7},{4,6},{5,1},{6,4},{7,3},{8,10},{9,13},{10,... | collective-permute-start | bytes 1572872 | tf_op jit(solution)/shard_map/ppermute | solution.py:356
  67.1 21.5 %collective-permute-start.10 = (f32[4,256,128]{2,1,0:T(8,128)}, f32[4,256,128]{2,1,0:T(8,128)}, u32[]{:S(2)}, u32[]{:S(2)}) collective-permute-start(f32[4,256,128]{2,1,0:T(8,128)} %get-tuple-element.160), channel_id=1, source_target_pairs={{0,8},{1,9},{2,10},{3,11},{4,12},{5,13},{6,14},{7,15},{8,0},{9,1},... | collective-permute-start | bytes 1572872 | tf_op jit(solution)/shard_map/ppermute | solution.py:356
  71.0 23.4 %collective-permute-start.11 = (f32[2,288,128]{2,1,0:T(8,128)}, f32[2,288,128]{2,1,0:T(8,128)}, u32[]{:S(2)}, u32[]{:S(2)}) collective-permute-start(f32[2,288,128]{2,1,0:T(8,128)} %get-tuple-element.163), channel_id=1, source_target_pairs={{0,4},{1,3},{2,6},{3,1},{4,0},{5,7},{6,2},{7,5},{8,12},{9,11},{10,... | collective-permute-start | bytes 884744 | tf_op jit(solution)/shard_map/ppermute | solution.py:356
  74.1 38.7 %collective-permute-start.14 = (f32[1,192,128]{2,1,0:T(8,128)}, f32[1,192,128]{2,1,0:T(8,128)}, u32[]{:S(2)}, u32[]{:S(2)}) collective-permute-start(f32[1,192,128]{2,1,0:T(8,128)} %get-tuple-element.172), channel_id=1, source_target_pairs={{0,16},{1,17},{2,18},{3,19},{4,20},{5,21},{6,22},{7,23},{8,24},{9,... | collective-permute-start | bytes 294920 | tf_op jit(solution)/shard_map/ppermute | solution.py:356
  92.4 18.0 %collective-permute-start.13 = (f32[4,256,128]{2,1,0:T(8,128)}, f32[4,256,128]{2,1,0:T(8,128)}, u32[]{:S(2)}, u32[]{:S(2)}) collective-permute-start(f32[4,256,128]{2,1,0:T(8,128)} %get-tuple-element.169), channel_id=1, source_target_pairs={{0,8},{1,9},{2,10},{3,11},{4,12},{5,13},{6,14},{7,15},{8,0},{9,1},... | collective-permute-start | bytes 1572872 | tf_op jit(solution)/shard_map/ppermute | solution.py:356
  93.9 20.5 %collective-permute-start.15 = (f32[4,128,128]{2,1,0:T(8,128)}, f32[4,128,128]{2,1,0:T(8,128)}, u32[]{:S(2)}, u32[]{:S(2)}) collective-permute-start(f32[4,128,128]{2,1,0:T(8,128)} %get-tuple-element.175), channel_id=1, source_target_pairs={{0,8},{1,9},{2,10},{3,11},{4,12},{5,13},{6,14},{7,15},{8,0},{9,1},... | collective-permute-start | bytes 786440 | tf_op jit(solution)/shard_map/ppermute | solution.py:356
  96.1 26.1 %collective-permute-start.17 = (f32[1,288,128]{2,1,0:T(8,128)}, f32[1,288,128]{2,1,0:T(8,128)}, u32[]{:S(2)}, u32[]{:S(2)}) collective-permute-start(f32[1,288,128]{2,1,0:T(8,128)} %get-tuple-element.181), channel_id=1, source_target_pairs={{0,16},{1,17},{2,18},{3,19},{4,20},{5,21},{6,22},{7,23},{8,24},{9,... | collective-permute-start | bytes 442376 | tf_op jit(solution)/shard_map/ppermute | solution.py:356
  100.4 25.0 %collective-permute-start.19 = (f32[1,256,128]{2,1,0:T(8,128)}, f32[1,256,128]{2,1,0:T(8,128)}, u32[]{:S(2)}, u32[]{:S(2)}) collective-permute-start(f32[1,256,128]{2,1,0:T(8,128)} %get-tuple-element.187), channel_id=1, source_target_pairs={{0,16},{1,17},{2,18},{3,19},{4,20},{5,21},{6,22},{7,23},{8,24},{9,... | collective-permute-start | bytes 393224 | tf_op jit(solution)/shard_map/ppermute | solution.py:356
  130.6 15.8 %collective-permute-start.24 = (f32[1,128,128]{2,1,0:T(8,128)}, f32[1,128,128]{2,1,0:T(8,128)}, u32[]{:S(2)}, u32[]{:S(2)}) collective-permute-start(f32[1,128,128]{2,1,0:T(8,128)} %get-tuple-element.199), channel_id=1, source_target_pairs={{0,16},{1,17},{2,18},{3,19},{4,20},{5,21},{6,22},{7,23},{8,24},{9,... | collective-permute-start | bytes 196616 | tf_op jit(solution)/shard_map/ppermute | solution.py:356
  132.1 15.9 %collective-permute-start.25 = (f32[1,256,128]{2,1,0:T(8,128)}, f32[1,256,128]{2,1,0:T(8,128)}, u32[]{:S(2)}, u32[]{:S(2)}) collective-permute-start(f32[1,256,128]{2,1,0:T(8,128)} %get-tuple-element.201.refs_1_), channel_id=1, source_target_pairs={{0,16},{1,17},{2,18},{3,19},{4,20},{5,21},{6,22},{7,23},{8,24},{9,... | collective-permute-start | bytes 393224 | tf_op jit(solution)/shard_map/ppermute | solution.py:356
  135.2 26.2 %collective-permute-start.28 = (f32[1,256,128]{2,1,0:T(8,128)}, f32[1,256,128]{2,1,0:T(8,128)}, u32[]{:S(2)}, u32[]{:S(2)}) collective-permute-start(f32[1,256,128]{2,1,0:T(8,128)} %get-tuple-element.207.refs_1_), channel_id=1, source_target_pairs={{0,16},{1,17},{2,18},{3,19},{4,20},{5,21},{6,22},{7,23},{8,24},{9,... | collective-permute-start | bytes 393224 | tf_op jit(solution)/shard_map/ppermute | solution.py:356
  144.4 14.3 %collective-permute-start.27 = (f32[4,192,128]{2,1,0:T(8,128)}, f32[4,192,128]{2,1,0:T(8,128)}, u32[]{:S(2)}, u32[]{:S(2)}) collective-permute-start(f32[4,192,128]{2,1,0:T(8,128)} %get-tuple-element.205.refs_1_), channel_id=1, source_target_pairs={{0,8},{1,9},{2,10},{3,11},{4,12},{5,13},{6,14},{7,15},{8,0},{9,1},... | collective-permute-start | bytes 1179656 | tf_op jit(solution)/shard_map/ppermute | solution.py:356
  149.6 13.4 %collective-permute-start.29 = (f32[2,256,128]{2,1,0:T(8,128)}, f32[2,256,128]{2,1,0:T(8,128)}, u32[]{:S(2)}, u32[]{:S(2)}) collective-permute-start(f32[2,256,128]{2,1,0:T(8,128)} %get-tuple-element.209.refs_1_), channel_id=1, source_target_pairs={{0,4},{1,3},{2,6},{3,1},{4,0},{5,7},{6,2},{7,5},{8,12},{9,11},{10,... | collective-permute-start | bytes 786440 | tf_op jit(solution)/shard_map/ppermute | solution.py:356
  151.7 13.2 %collective-permute-start.30 = (f32[1,128,128]{2,1,0:T(8,128)}, f32[1,128,128]{2,1,0:T(8,128)}, u32[]{:S(2)}, u32[]{:S(2)}) collective-permute-start(f32[1,128,128]{2,1,0:T(8,128)} %get-tuple-element.211.refs_1_), channel_id=1, source_target_pairs={{0,16},{1,17},{2,18},{3,19},{4,20},{5,21},{6,22},{7,23},{8,24},{9,... | collective-permute-start | bytes 196616 | tf_op jit(solution)/shard_map/ppermute | solution.py:356
  154.7 16.6 %collective-permute-start.32 = (f32[4,288,128]{2,1,0:T(8,128)}, f32[4,288,128]{2,1,0:T(8,128)}, u32[]{:S(2)}, u32[]{:S(2)}) collective-permute-start(f32[4,288,128]{2,1,0:T(8,128)} %get-tuple-element.214.refs_2_), channel_id=1, source_target_pairs={{0,8},{1,9},{2,10},{3,11},{4,12},{5,13},{6,14},{7,15},{8,0},{9,1},... | collective-permute-start | bytes 1769480 | tf_op jit(solution)/shard_map/ppermute | solution.py:356
  160.8 16.5 %collective-permute-start.31 = (f32[8,192,128]{2,1,0:T(8,128)}, f32[8,192,128]{2,1,0:T(8,128)}, u32[]{:S(2)}, u32[]{:S(2)}) collective-permute-start(f32[8,192,128]{2,1,0:T(8,128)} %get-tuple-element.213.refs_2_), channel_id=1, source_target_pairs={{0,2},{1,5},{2,0},{3,7},{4,6},{5,1},{6,4},{7,3},{8,10},{9,13},{10,... | collective-permute-start | bytes 2359304 | tf_op jit(solution)/shard_map/ppermute | solution.py:356
  166.5 15.5 %collective-permute-start.34 = (f32[2,256,128]{2,1,0:T(8,128)}, f32[2,256,128]{2,1,0:T(8,128)}, u32[]{:S(2)}, u32[]{:S(2)}) collective-permute-start(f32[2,256,128]{2,1,0:T(8,128)} %get-tuple-element.218.refs_1_), channel_id=1, source_target_pairs={{0,4},{1,3},{2,6},{3,1},{4,0},{5,7},{6,2},{7,5},{8,12},{9,11},{10,... | collective-permute-start | bytes 786440 | tf_op jit(solution)/shard_map/ppermute | solution.py:356
  168.5 23.5 %collective-permute-start.35 = (f32[4,256,128]{2,1,0:T(8,128)}, f32[4,256,128]{2,1,0:T(8,128)}, u32[]{:S(2)}, u32[]{:S(2)}) collective-permute-start(f32[4,256,128]{2,1,0:T(8,128)} %get-tuple-element.222.refs_1_), channel_id=1, source_target_pairs={{0,8},{1,9},{2,10},{3,11},{4,12},{5,13},{6,14},{7,15},{8,0},{9,1},... | collective-permute-start | bytes 1572872 | tf_op jit(solution)/shard_map/ppermute | solution.py:356
  181.4 16.3 %collective-permute-start.36 = (f32[4,128,128]{2,1,0:T(8,128)}, f32[4,128,128]{2,1,0:T(8,128)}, u32[]{:S(2)}, u32[]{:S(2)}) collective-permute-start(f32[4,128,128]{2,1,0:T(8,128)} %get-tuple-element.224.refs_1_), channel_id=1, source_target_pairs={{0,8},{1,9},{2,10},{3,11},{4,12},{5,13},{6,14},{7,15},{8,0},{9,1},... | collective-permute-start | bytes 786440 | tf_op jit(solution)/shard_map/ppermute | solution.py:356
  181.4 18.8 %collective-permute-start.37 = (f32[8,288,128]{2,1,0:T(8,128)}, f32[8,288,128]{2,1,0:T(8,128)}, u32[]{:S(2)}, u32[]{:S(2)}) collective-permute-start(f32[8,288,128]{2,1,0:T(8,128)} %get-tuple-element.220.refs_3_.refs_2_), channel_id=1, source_target_pairs={{0,2},{1,5},{2,0},{3,7},{4,6},{5,1},{6,4},{7,3},{8,10},{9,13},{10,... | collective-permute-start | bytes 3538952 | tf_op jit(solution)/shard_map/ppermute | solution.py:356
  194.2 27.8 %collective-permute-start.39 = (f32[8,256,128]{2,1,0:T(8,128)}, f32[8,256,128]{2,1,0:T(8,128)}, u32[]{:S(2)}, u32[]{:S(2)}) collective-permute-start(f32[8,256,128]{2,1,0:T(8,128)} %get-tuple-element.229.refs_4_.refs_3_), channel_id=1, source_target_pairs={{0,2},{1,5},{2,0},{3,7},{4,6},{5,1},{6,4},{7,3},{8,10},{9,13},{10,... | collective-permute-start | bytes 3145736 | tf_op jit(solution)/shard_map/ppermute | solution.py:356
  195.7 26.3 %collective-permute-start.40 = (f32[4,256,128]{2,1,0:T(8,128)}, f32[4,256,128]{2,1,0:T(8,128)}, u32[]{:S(2)}, u32[]{:S(2)}) collective-permute-start(f32[4,256,128]{2,1,0:T(8,128)} %get-tuple-element.234.refs_2_), channel_id=1, source_target_pairs={{0,8},{1,9},{2,10},{3,11},{4,12},{5,13},{6,14},{7,15},{8,0},{9,1},... | collective-permute-start | bytes 1572872 | tf_op jit(solution)/shard_map/ppermute | solution.py:356
  199.7 37.7 %collective-permute-start.41 = (f32[8,128,128]{2,1,0:T(8,128)}, f32[8,128,128]{2,1,0:T(8,128)}, u32[]{:S(2)}, u32[]{:S(2)}) collective-permute-start(f32[8,128,128]{2,1,0:T(8,128)} %get-tuple-element.239.refs_3_), channel_id=1, source_target_pairs={{0,2},{1,5},{2,0},{3,7},{4,6},{5,1},{6,4},{7,3},{8,10},{9,13},{10,... | collective-permute-start | bytes 1572872 | tf_op jit(solution)/shard_map/ppermute | solution.py:356
  224.4 30.1 %collective-permute-start.42 = (f32[8,256,128]{2,1,0:T(8,128)}, f32[8,256,128]{2,1,0:T(8,128)}, u32[]{:S(2)}, u32[]{:S(2)}) collective-permute-start(f32[8,256,128]{2,1,0:T(8,128)} %get-tuple-element.240.refs_4_.refs_2_), channel_id=1, source_target_pairs={{0,2},{1,5},{2,0},{3,7},{4,6},{5,1},{6,4},{7,3},{8,10},{9,13},{10,... | collective-permute-start | bytes 3145736 | tf_op jit(solution)/shard_map/ppermute | solution.py:356
  (17 other events, 133.0 us)

commit v6 on v4

--- a/solution.py
+++ b/solution.py
@@ -10,23 +10,22 @@
 LANES = 128
 SIZE = 2 * LANES
 VMEM_LIMIT = 40 * 1024 * 1024
+FIRST_LIMIT = 58 * 1024 * 1024
 F32 = jnp.float32
 
 GROUPS = (
-    ((0, 0, 0, 128), (1, 0, 0, 64)),
-    ((0, 1, 0, 128), (1, 1, 0, 64)),
-    ((1, 0, 64, 128), (1, 1, 64, 128), (2, 0, 0, 128)),
-    ((2, 1, 0, 128), (3, 0, 0, 128)),
-    ((3, 1, 0, 128),),
+    ((0, 0, 0, 128), (1, 0, 0, 128)),
+    ((0, 1, 0, 128), (1, 1, 0, 128)),
+    ((2, 0, 0, 128), (2, 1, 0, 128)),
+    ((3, 0, 0, 128), (3, 1, 0, 128)),
 )
 GRAM_GROUP = 1
-CALLS = ((0,), (1,), (2,), (3, 4))
+CALLS = ((0,), (1,), (2,), (3,))
 UPDATES = ((0, 1), (2,), (3,))
 ORDER = (
-    ["p0", "g", "p1", "k1.0", "p2", "k2.0", "p3", "k1.1", "k1.2", "k2.1", "k1.3", "k1.4", "k3.0", "k2.2", "k3.1"]
-    + ["k3.2", "k2.3", "k2.4", "k4.0", "k3.3", "k4.1", "k3.4", "k4.2", "k5.0", "k4.3", "k6.0", "k5.1", "k4.4"]
-    + ["k6.1", "k5.2", "k7.0", "k5.3", "k5.4", "k6.2", "f.0", "k7.1", "k6.3", "k6.4", "k7.2", "f.1", "x", "k7.3"]
-    + ["k7.4", "f.2", "u0", "f.3", "u1", "f.4", "u2"]
+    ["p0", "g", "p1", "k1.0", "p2", "k2.0", "k1.1", "p3", "k2.1", "k3.0", "k1.2", "k1.3", "k3.1", "k4.0", "k2.2"]
+    + ["k4.1", "k3.2", "k5.0", "k2.3", "k6.0", "k5.1", "k4.2", "k3.3", "k6.1", "k4.3", "k5.2", "k7.0", "k6.2", "k5.3"]
+    + ["k7.1", "f.0", "k6.3", "k7.2", "f.1", "x", "k7.3", "u0", "f.2", "u1", "f.3", "u2"]
 )
 
 
@@ -85,8 +84,8 @@
 COST = pl.CostEstimate(flops=1, bytes_accessed=1, transcendentals=0)
 
 
-def params():
-    return pltpu.CompilerParams(vmem_limit_bytes=VMEM_LIMIT)
+def params(limit=VMEM_LIMIT):
+    return pltpu.CompilerParams(vmem_limit_bytes=limit)
 
 
 def whole(array):
@@ -167,7 +166,7 @@
         + [pl.BlockSpec(TOKEN.shape, lambda j: (0, 0))],
         scratch_shapes=[pltpu.VMEM((above, columns), F32)],
         out_shape=halves_of + [TOKEN],
-        compiler_params=params(),
+        compiler_params=params(FIRST_LIMIT if call == CALLS[0] else VMEM_LIMIT),
         cost_estimate=COST,
         name="project_" + "".join(map(str, call)),
     )(place, *after, *[sides[side] for _, side in blocks], slab, *grams)

time: 235 us -> 229 us (0.974)
  local copies, waits for them, and re-layouts: 4.98 us -> 0.6 us
  starting transfers between devices: 50.8 us -> 47.5 us
    unnamed x8 -> x6, local copies, waits for them, and re-layouts: 4.98 us -> 0.01 us
    ppermute x40 -> x32, starting transfers between devices: 50.3 us -> 47 us  [swap(): return lax.ppermute(value, ('row', 'col'), pairs)]
    ppermute x40 -> x32, waiting for transfers between devices: 98.3 us -> 96.6 us  [swap(): return lax.ppermute(value, ('row', 'col'), pairs)]
  transfers between devices with their start and end apart: 43 -> 35, of which waited for: 24 -> 20; matrix products, arithmetic and copies ran while one was open for 1% -> 1% of each run, Pallas kernels for 29% -> 30%
where the time goes in v6:
time: 229 us
  waiting for transfers between devices  98.9 us (43%)
  Pallas kernels  80.2 us (35%)
  starting transfers between devices  47.5 us (21%)
    ppermute x32, waiting for transfers between devices, swap(): return lax.ppermute(value, ('row', 'col'), pairs)  96.6 us
    ppermute x32, starting transfers between devices, swap(): return lax.ppermute(value, ('row', 'col'), pairs)  47 us
    pallas_call x3, Pallas kernels, update(): pl.pallas_call(functools.partial(update_kernel, panels, len(grams), len(c...  43.2 us
    pallas_call x4, Pallas kernels, project(): pl.pallas_call(functools.partial(project_kernel, steps, call, blocks, len...  32 us
  transfers between devices with their start and end apart: 35, of which 20 were waited for; matrix products, arithmetic and copies ran while one was open for 1% of the time, Pallas kernels for 30%

profile of v6, /device:TPU:0, one launch (start us, length us, event | category | flops | bytes accessed | tf_op | source)
XLA Modules:
  0.0 228.9 jit_solution(11863658846938967637)
XLA Ops:
  1.1 8.9 %project_0.1 = (f32[8,256,128]{2,1,0:T(8,128)}, f32[8,256,128]{2,1,0:T(8,128)}, f32[8,128]{1,0:T(8,128)}) custom-call(s32[1]{0:T(128)} %bitcast.place.place_ref, f32[8,128]{1,0:T(8,128)} %broadcast_in_dim.3.refs_0_, f32[4,1024,128]{2,1,0:T(8,128)} %refs_6_.1, f32[4,1024,128]{2,1,0:T(8,128)} %refs_6_.1, f32[1024,2048]{1,0:T(8,128)} %refs_12_.1), custom_call_target="tpu_custom_call" | custom-call | flops 1 | bytes 1 | tf_op jit(solution)/shard_map/project_0/pallas_call | solution.py:161
  10.0 3.0 %collective-permute-start.2 = (f32[8,256,128]{2,1,0:T(8,128)}, f32[8,256,128]{2,1,0:T(8,128)S(1)}, u32[]{:S(2)}, u32[]{:S(2)}) collective-permute-start(f32[8,256,128]{2,1,0:T(8,128)} %get-tuple-element.98), channel_id=1, source_target_pairs={{0,2},{1,5},{2,0},{3,7},{4,6},{5,1},{6,4},{7,3},{8,10},{9,13},{10,... | collective-permute-start | bytes 3145736 | tf_op jit(solution)/shard_map/ppermute | solution.py:352
  14.5 3.5 %gram_rows.1 = (f32[16,96,128]{2,1,0:T(8,128)S(1)}, f32[8,128]{1,0:T(8,128)S(1)}) custom-call(s32[1]{0:T(128)} %bitcast.place.place_ref, f32[8,128]{1,0:T(8,128)S(1)} %copy-done.2, f32[4,1024,128]{2,1,0:T(8,128)S(1)} %copy-done, f32[4,1024,128]{2,1,0:T(8,128)S(1)} %copy-done, f32[4,1024,128]{2,1,0:T(8,128)} %collective-permute-done.refs_3_.refs_2_.refs_9_.refs_11_.refs_7_), custom_call_target="tpu_custom_call" | custom-call | flops 1 | bytes 1 | tf_op jit(solution)/shard_map/gram_rows/pallas_call | solution.py:199
  18.0 7.8 %project_1.1 = (f32[8,352,128]{2,1,0:T(8,128)S(1)}, f32[8,352,128]{2,1,0:T(8,128)S(1)}, f32[8,128]{1,0:T(8,128)S(1)}) custom-call(s32[1]{0:T(128)} %bitcast.place.place_ref, f32[8,128]{1,0:T(8,128)S(1)} %get-tuple-element.94.refs_0_, f32[4,256,256]{2,1,0:T(8,128)S(1)} %fusion.1.refs_1_.refs_2_, ...), custom_call_target="tpu_custom_call" | custom-call | flops 1 | bytes 1 | tf_op jit(solution)/shard_map/project_1/pallas_call | solution.py:161
  28.3 7.6 %project_2.1 = (f32[8,256,128]{2,1,0:T(8,128)S(1)}, f32[8,256,128]{2,1,0:T(8,128)S(1)}, f32[8,128]{1,0:T(8,128)S(1)}) custom-call(s32[1]{0:T(128)} %bitcast.place.place_ref, f32[8,128]{1,0:T(8,128)S(1)} %get-tuple-element.99.refs_0_, f32[4,1024,128]{2,1,0:T(8,128)S(1)} %copy-done, ...), custom_call_target="tpu_custom_call" | custom-call | flops 1 | bytes 1 | tf_op jit(solution)/shard_map/project_2/pallas_call | solution.py:161
  37.4 2.6 %collective-permute-done.3.refs_2_ = f32[4,256,128]{2,1,0:T(8,128)S(1)} collective-permute-done((f32[4,256,128]{2,1,0:T(8,128)S(1)}, f32[4,256,128]{2,1,0:T(8,128)S(1)}, u32[]{:S(2)}, u32[]{:S(2)}) %collective-permute-start.3) | collective-permute-done | bytes 524320 | tf_op jit(solution)/shard_map/ppermute | solution.py:352
  40.1 4.8 %collective-permute-done.4.refs_2_ = f32[8,352,128]{2,1,0:T(8,128)S(1)} collective-permute-done((f32[8,352,128]{2,1,0:T(8,128)S(1)}, f32[8,352,128]{2,1,0:T(8,128)S(1)}, u32[]{:S(2)}, u32[]{:S(2)}) %collective-permute-start.4) | collective-permute-done | bytes 1441824 | tf_op jit(solution)/shard_map/ppermute | solution.py:352
  46.6 7.7 %project_3.1 = (f32[8,256,128]{2,1,0:T(8,128)S(1)}, f32[8,256,128]{2,1,0:T(8,128)S(1)}, f32[8,128]{1,0:T(8,128)S(1)}) custom-call(s32[1]{0:T(128)} %bitcast.place.place_ref, f32[8,128]{1,0:T(8,128)S(1)} %get-tuple-element.106.refs_0_, f32[4,1024,128]{2,1,0:T(8,128)S(1)} %copy-done, ...), custom_call_target="tpu_custom_call" | custom-call | flops 1 | bytes 1 | tf_op jit(solution)/shard_map/project_3/pallas_call | solution.py:161
  56.5 5.5 %collective-permute-done.5.refs_2_ = f32[4,352,128]{2,1,0:T(8,128)S(1)} collective-permute-done((f32[4,352,128]{2,1,0:T(8,128)S(1)}, f32[4,352,128]{2,1,0:T(8,128)S(1)}, u32[]{:S(2)}, u32[]{:S(2)}) %collective-permute-start.5) | collective-permute-done | bytes 720928 | tf_op jit(solution)/shard_map/ppermute | solution.py:352
  62.1 2.2 collective-permute-done.6.refs_2_
  66.4 2.6 %collective-permute-start.10 = (f32[1,256,128]{2,1,0:T(8,128)S(1)}, f32[1,256,128]{2,1,0:T(8,128)S(1)}, u32[]{:S(2)}, u32[]{:S(2)}) collective-permute-start(f32[1,256,128]{2,1,0:T(8,128)S(1)} %get-tuple-element.124), channel_id=1, source_target_pairs={{0,16},{1,17},{2,18},{3,19},{4,20},{5,21},{6,22},{7,23},{8,24},{9,... | collective-permute-start | bytes 393224 | tf_op jit(solution)/shard_map/ppermute | solution.py:352
  69.0 5.0 %collective-permute-done.8.refs_2_ = f32[8,256,128]{2,1,0:T(8,128)S(1)} collective-permute-done((f32[8,256,128]{2,1,0:T(8,128)S(1)}, f32[8,256,128]{2,1,0:T(8,128)S(1)}, u32[]{:S(2)}, u32[]{:S(2)}) %collective-permute-start.8) | collective-permute-done | bytes 1048608 | tf_op jit(solution)/shard_map/ppermute | solution.py:352
  74.2 2.5 %collective-permute-done.10.refs_2_ = f32[1,256,128]{2,1,0:T(8,128)S(1)} collective-permute-done((f32[1,256,128]{2,1,0:T(8,128)S(1)}, f32[1,256,128]{2,1,0:T(8,128)S(1)}, u32[]{:S(2)}, u32[]{:S(2)}) %collective-permute-start.10) | collective-permute-done | bytes 131104 | tf_op jit(solution)/shard_map/ppermute | solution.py:352
  78.9 2.6 %collective-permute-start.15 = (f32[4,256,128]{2,1,0:T(8,128)S(1)}, f32[4,256,128]{2,1,0:T(8,128)S(1)}, u32[]{:S(2)}, u32[]{:S(2)}) collective-permute-start(f32[4,256,128]{2,1,0:T(8,128)S(1)} %get-tuple-element.138), channel_id=1, source_target_pairs={{0,8},{1,9},{2,10},{3,11},{4,12},{5,13},{6,14},{7,15},{8,0},{9,1},... | collective-permute-start | bytes 1572872 | tf_op jit(solution)/shard_map/ppermute | solution.py:352
  84.5 9.8 %collective-permute-done.12.refs_2_ = f32[1,352,128]{2,1,0:T(8,128)S(1)} collective-permute-done((f32[1,352,128]{2,1,0:T(8,128)S(1)}, f32[1,352,128]{2,1,0:T(8,128)S(1)}, u32[]{:S(2)}, u32[]{:S(2)}) %collective-permute-start.12) | collective-permute-done | bytes 180256 | tf_op jit(solution)/shard_map/ppermute | solution.py:352
  94.3 2.7 %collective-permute-done.14.refs_2_ = f32[1,256,128]{2,1,0:T(8,128)S(1)} collective-permute-done((f32[1,256,128]{2,1,0:T(8,128)S(1)}, f32[1,256,128]{2,1,0:T(8,128)S(1)}, u32[]{:S(2)}, u32[]{:S(2)}) %collective-permute-start.14) | collective-permute-done | bytes 131104 | tf_op jit(solution)/shard_map/ppermute | solution.py:352
  97.8 3.4 %collective-permute-start.17 = (f32[1,352,128]{2,1,0:T(8,128)S(1)}, f32[1,352,128]{2,1,0:T(8,128)S(1)}, u32[]{:S(2)}, u32[]{:S(2)}) collective-permute-start(f32[1,352,128]{2,1,0:T(8,128)S(1)} %get-tuple-element.142.refs_1_), channel_id=1, source_target_pairs={{0,16},{1,17},{2,18},{3,19},{4,20},{5,21},{6,22},{7,23},{8,24},{9,... | collective-permute-start | bytes 540680 | tf_op jit(solution)/shard_map/ppermute | solution.py:352
  101.3 2.2 collective-permute-done.16.refs_2_
  103.5 3.8 %collective-permute-done.17.refs_2_ = f32[1,352,128]{2,1,0:T(8,128)S(1)} collective-permute-done((f32[1,352,128]{2,1,0:T(8,128)S(1)}, f32[1,352,128]{2,1,0:T(8,128)S(1)}, u32[]{:S(2)}, u32[]{:S(2)}) %collective-permute-start.17) | collective-permute-done | bytes 180256 | tf_op jit(solution)/shard_map/ppermute | solution.py:352
  111.1 5.0 %collective-permute-done.18.refs_2_ = f32[1,256,128]{2,1,0:T(8,128)S(1)} collective-permute-done((f32[1,256,128]{2,1,0:T(8,128)S(1)}, f32[1,256,128]{2,1,0:T(8,128)S(1)}, u32[]{:S(2)}, u32[]{:S(2)}) %collective-permute-start.18) | collective-permute-done | bytes 131104 | tf_op jit(solution)/shard_map/ppermute | solution.py:352
  122.8 21.8 %collective-permute-done.21.refs_2_ = f32[1,256,128]{2,1,0:T(8,128)S(1)} collective-permute-done((f32[1,256,128]{2,1,0:T(8,128)S(1)}, f32[1,256,128]{2,1,0:T(8,128)S(1)}, u32[]{:S(2)}, u32[]{:S(2)}) %collective-permute-start.21) | collective-permute-done | bytes 131104 | tf_op jit(solution)/shard_map/ppermute | solution.py:352
  144.6 2.7 %collective-permute-done.22.refs_2_ = f32[1,256,128]{2,1,0:T(8,128)S(1)} collective-permute-done((f32[1,256,128]{2,1,0:T(8,128)S(1)}, f32[1,256,128]{2,1,0:T(8,128)S(1)}, u32[]{:S(2)}, u32[]{:S(2)}) %collective-permute-start.22) | collective-permute-done | bytes 131104 | tf_op jit(solution)/shard_map/ppermute | solution.py:352
  147.7 3.4 %collective-permute-start.25 = (f32[1,256,128]{2,1,0:T(8,128)S(1)}, f32[1,256,128]{2,1,0:T(8,128)S(1)}, u32[]{:S(2)}, u32[]{:S(2)}) collective-permute-start(f32[1,256,128]{2,1,0:T(8,128)S(1)} %get-tuple-element.161.refs_1_), channel_id=1, source_target_pairs={{0,16},{1,17},{2,18},{3,19},{4,20},{5,21},{6,22},{7,23},{8,24},{9,... | collective-permute-start | bytes 393224 | tf_op jit(solution)/shard_map/ppermute | solution.py:352
  152.5 4.1 %collective-permute-done.24.refs_2_ = f32[2,256,128]{2,1,0:T(8,128)S(1)} collective-permute-done((f32[2,256,128]{2,1,0:T(8,128)S(1)}, f32[2,256,128]{2,1,0:T(8,128)S(1)}, u32[]{:S(2)}, u32[]{:S(2)}) %collective-permute-start.24) | collective-permute-done | bytes 262176 | tf_op jit(solution)/shard_map/ppermute | solution.py:352
  160.4 7.2 %collective-permute-done.28.refs_3_ = f32[2,256,128]{2,1,0:T(8,128)S(1)} collective-permute-done((f32[2,256,128]{2,1,0:T(8,128)S(1)}, f32[2,256,128]{2,1,0:T(8,128)S(1)}, u32[]{:S(2)}, u32[]{:S(2)}) %collective-permute-start.28) | collective-permute-done | bytes 262176 | tf_op jit(solution)/shard_map/ppermute | solution.py:352
  167.7 2.1 collective-permute-start.31
  169.8 2.7 %collective-permute-done.29.refs_2_ = f32[4,256,128]{2,1,0:T(8,128)S(1)} collective-permute-done((f32[4,256,128]{2,1,0:T(8,128)S(1)}, f32[4,256,128]{2,1,0:T(8,128)S(1)}, u32[]{:S(2)}, u32[]{:S(2)}) %collective-permute-start.29) | collective-permute-done | bytes 524320 | tf_op jit(solution)/shard_map/ppermute | solution.py:352
  172.6 9.9 %collective-permute-done.30.refs_1_.refs_3_.refs_5_ = f32[8,352,128]{2,1,0:T(8,128)S(1)} collective-permute-done((f32[8,352,128]{2,1,0:T(8,128)S(1)}, f32[8,352,128]{2,1,0:T(8,128)S(1)}, u32[]{:S(2)}, u32[]{:S(2)}) %collective-permute-start.30) | collective-permute-done | bytes 1441824 | tf_op jit(solution)/shard_map/ppermute | solution.py:352
  183.4 2.3 collective-permute-done.32.refs_7_.refs_6_
  185.7 19.3 %update_panels01.1 = (f32[1024,2048]{1,0:T(8,128)}, f32[512,2048]{1,0:T(8,128)}) custom-call(s32[1]{0:T(128)} %bitcast.place.place_ref, f32[8,128]{1,0:T(8,128)S(1)} %get-tuple-element.173.refs_0_, f32[4,256,256]{2,1,0:T(8,128)S(1)} %fusion.1.refs_1_.refs_2_, f32[8,256,128]{2,1,0:T(8,128)S(1)} %get-tuple-element.165.refs_2_, ...), custom_call_target="tpu_custom_call" | custom-call | flops 1 | bytes 1 | tf_op jit(solution)/shard_map/update_panels01/pallas_call | solution.py:324
  205.0 13.4 %update_panels2.1 = (f32[1024,2048]{1,0:T(8,128)}, f32[256,2048]{1,0:T(8,128)S(1)}) custom-call(s32[1]{0:T(128)} %bitcast.place.place_ref, f32[1024,2048]{1,0:T(8,128)} %get-tuple-element.175.refs_0_.refs_10_, f32[8,256,128]{2,1,0:T(8,128)S(1)} %collective-permute-done.33.refs_1_.refs_4_, f32[4,256,256]{2,1,0:T(8,128)S(1)} %fusion.1.refs_1_.refs_2_, ...), custom_call_target="tpu_custom_call" | custom-call | flops 1 | bytes 1 | tf_op jit(solution)/shard_map/update_panels2/pallas_call | solution.py:324
  218.4 10.5 %update_panels3.1 = f32[1024,2048]{1,0:T(8,128)} custom-call(s32[1]{0:T(128)} %bitcast.place.place_ref, f32[1024,2048]{1,0:T(8,128)} %get-tuple-element.178.refs_0_.refs_8_, f32[8,256,128]{2,1,0:T(8,128)S(1)} %collective-permute-done.34.refs_1_.refs_4_, f32[4,256,256]{2,1,0:T(8,128)S(1)} %fusion.1.refs_1_.refs_2_, ...), custom_call_target="tpu_custom_call" | custom-call | flops 1 | bytes 1 | tf_op jit(solution)/shard_map/update_panels3/pallas_call | solution.py:324
  (83 shorter events, 36.2 us)
Async XLA Ops:
  0.0 14.5 %collective-permute-start = (f32[4,1024,128]{2,1,0:T(8,128)}, f32[4,1024,128]{2,1,0:T(8,128)}, u32[]{:S(2)}, u32[]{:S(2)}) collective-permute-start(f32[4,1024,128]{2,1,0:T(8,128)} %refs_6_.1), channel_id=1, source_target_pairs={{1,0},{0,1},{3,2},{2,3},{5,4},{4,5},{7,6},{6,7},{9,8},{8,9},{11,10... | collective-permute-start | bytes 6291464 | tf_op jit(solution)/shard_map/ppermute | solution.py:357
  0.5 12.6 %collective-permute-start.1 = (f32[4,128,256]{2,1,0:T(8,128)}, f32[4,128,256]{2,1,0:T(8,128)}, u32[]{:S(2)}, u32[]{:S(2)}) collective-permute-start(f32[4,128,256]{2,1,0:T(8,128)} %param.5), channel_id=1, source_target_pairs={{1,0},{0,1},{3,2},{2,3},{5,4},{4,5},{7,6},{6,7},{9,8},{8,9},{11,10... | collective-permute-start | bytes 1572872 | tf_op jit(solution)/shard_map/ppermute | solution.py:357
  10.0 16.2 %collective-permute-start.2 = (f32[8,256,128]{2,1,0:T(8,128)}, f32[8,256,128]{2,1,0:T(8,128)S(1)}, u32[]{:S(2)}, u32[]{:S(2)}) collective-permute-start(f32[8,256,128]{2,1,0:T(8,128)} %get-tuple-element.98), channel_id=1, source_target_pairs={{0,2},{1,5},{2,0},{3,7},{4,6},{5,1},{6,4},{7,3},{8,10},{9,13},{10,... | collective-permute-start | bytes 3145736 | tf_op jit(solution)/shard_map/ppermute | solution.py:352
  25.8 19.1 %collective-permute-start.4 = (f32[8,352,128]{2,1,0:T(8,128)S(1)}, f32[8,352,128]{2,1,0:T(8,128)S(1)}, u32[]{:S(2)}, u32[]{:S(2)}) collective-permute-start(f32[8,352,128]{2,1,0:T(8,128)S(1)} %get-tuple-element.105), channel_id=1, source_target_pairs={{0,2},{1,5},{2,0},{3,7},{4,6},{5,1},{6,4},{7,3},{8,10},{9,13},{10,... | collective-permute-start | bytes 4325384 | tf_op jit(solution)/shard_map/ppermute | solution.py:352
  26.3 13.7 %collective-permute-start.3 = (f32[4,256,128]{2,1,0:T(8,128)S(1)}, f32[4,256,128]{2,1,0:T(8,128)S(1)}, u32[]{:S(2)}, u32[]{:S(2)}) collective-permute-start(f32[4,256,128]{2,1,0:T(8,128)S(1)} %get-tuple-element.102), channel_id=1, source_target_pairs={{0,8},{1,9},{2,10},{3,11},{4,12},{5,13},{6,14},{7,15},{8,0},{9,1},... | collective-permute-start | bytes 1572872 | tf_op jit(solution)/shard_map/ppermute | solution.py:352
  35.9 28.4 %collective-permute-start.7 = (f32[8,256,128]{2,1,0:T(8,128)S(1)}, f32[8,256,128]{2,1,0:T(8,128)S(1)}, u32[]{:S(2)}, u32[]{:S(2)}) collective-permute-start(f32[8,256,128]{2,1,0:T(8,128)S(1)} %get-tuple-element.115), channel_id=1, source_target_pairs={{0,2},{1,5},{2,0},{3,7},{4,6},{5,1},{6,4},{7,3},{8,10},{9,13},{10,... | collective-permute-start | bytes 3145736 | tf_op jit(solution)/shard_map/ppermute | solution.py:352
  45.0 17.0 %collective-permute-start.5 = (f32[4,352,128]{2,1,0:T(8,128)S(1)}, f32[4,352,128]{2,1,0:T(8,128)S(1)}, u32[]{:S(2)}, u32[]{:S(2)}) collective-permute-start(f32[4,352,128]{2,1,0:T(8,128)S(1)} %get-tuple-element.109), channel_id=1, source_target_pairs={{0,8},{1,9},{2,10},{3,11},{4,12},{5,13},{6,14},{7,15},{8,0},{9,1},... | collective-permute-start | bytes 2162696 | tf_op jit(solution)/shard_map/ppermute | solution.py:352
  54.4 19.6 %collective-permute-start.8 = (f32[8,256,128]{2,1,0:T(8,128)S(1)}, f32[8,256,128]{2,1,0:T(8,128)S(1)}, u32[]{:S(2)}, u32[]{:S(2)}) collective-permute-start(f32[8,256,128]{2,1,0:T(8,128)S(1)} %get-tuple-element.118), channel_id=1, source_target_pairs={{0,2},{1,5},{2,0},{3,7},{4,6},{5,1},{6,4},{7,3},{8,10},{9,13},{10,... | collective-permute-start | bytes 3145736 | tf_op jit(solution)/shard_map/ppermute | solution.py:352
  55.0 9.2 %collective-permute-start.6 = (f32[2,256,128]{2,1,0:T(8,128)S(1)}, f32[2,256,128]{2,1,0:T(8,128)S(1)}, u32[]{:S(2)}, u32[]{:S(2)}) collective-permute-start(f32[2,256,128]{2,1,0:T(8,128)S(1)} %get-tuple-element.112), channel_id=1, source_target_pairs={{0,4},{1,3},{2,6},{3,1},{4,0},{5,7},{6,2},{7,5},{8,12},{9,11},{10,... | collective-permute-start | bytes 786440 | tf_op jit(solution)/shard_map/ppermute | solution.py:352
  64.4 13.0 %collective-permute-start.11 = (f32[4,256,128]{2,1,0:T(8,128)S(1)}, f32[4,256,128]{2,1,0:T(8,128)S(1)}, u32[]{:S(2)}, u32[]{:S(2)}) collective-permute-start(f32[4,256,128]{2,1,0:T(8,128)S(1)} %get-tuple-element.127), channel_id=1, source_target_pairs={{0,8},{1,9},{2,10},{3,11},{4,12},{5,13},{6,14},{7,15},{8,0},{9,1},... | collective-permute-start | bytes 1572872 | tf_op jit(solution)/shard_map/ppermute | solution.py:352
  64.7 9.4 %collective-permute-start.9 = (f32[2,352,128]{2,1,0:T(8,128)S(1)}, f32[2,352,128]{2,1,0:T(8,128)S(1)}, u32[]{:S(2)}, u32[]{:S(2)}) collective-permute-start(f32[2,352,128]{2,1,0:T(8,128)S(1)} %get-tuple-element.121), channel_id=1, source_target_pairs={{0,4},{1,3},{2,6},{3,1},{4,0},{5,7},{6,2},{7,5},{8,12},{9,11},{10,... | collective-permute-start | bytes 1081352 | tf_op jit(solution)/shard_map/ppermute | solution.py:352
  66.4 10.2 %collective-permute-start.10 = (f32[1,256,128]{2,1,0:T(8,128)S(1)}, f32[1,256,128]{2,1,0:T(8,128)S(1)}, u32[]{:S(2)}, u32[]{:S(2)}) collective-permute-start(f32[1,256,128]{2,1,0:T(8,128)S(1)} %get-tuple-element.124), channel_id=1, source_target_pairs={{0,16},{1,17},{2,18},{3,19},{4,20},{5,21},{6,22},{7,23},{8,24},{9,... | collective-permute-start | bytes 393224 | tf_op jit(solution)/shard_map/ppermute | solution.py:352
  77.5 16.8 %collective-permute-start.13 = (f32[2,256,128]{2,1,0:T(8,128)S(1)}, f32[2,256,128]{2,1,0:T(8,128)S(1)}, u32[]{:S(2)}, u32[]{:S(2)}) collective-permute-start(f32[2,256,128]{2,1,0:T(8,128)S(1)} %get-tuple-element.133), channel_id=1, source_target_pairs={{0,4},{1,3},{2,6},{3,1},{4,0},{5,7},{6,2},{7,5},{8,12},{9,11},{10,... | collective-permute-start | bytes 786440 | tf_op jit(solution)/shard_map/ppermute | solution.py:352
  78.9 22.4 %collective-permute-start.15 = (f32[4,256,128]{2,1,0:T(8,128)S(1)}, f32[4,256,128]{2,1,0:T(8,128)S(1)}, u32[]{:S(2)}, u32[]{:S(2)}) collective-permute-start(f32[4,256,128]{2,1,0:T(8,128)S(1)} %get-tuple-element.138), channel_id=1, source_target_pairs={{0,8},{1,9},{2,10},{3,11},{4,12},{5,13},{6,14},{7,15},{8,0},{9,1},... | collective-permute-start | bytes 1572872 | tf_op jit(solution)/shard_map/ppermute | solution.py:352
  81.5 12.7 %collective-permute-start.12 = (f32[1,352,128]{2,1,0:T(8,128)S(1)}, f32[1,352,128]{2,1,0:T(8,128)S(1)}, u32[]{:S(2)}, u32[]{:S(2)}) collective-permute-start(f32[1,352,128]{2,1,0:T(8,128)S(1)} %get-tuple-element.130), channel_id=1, source_target_pairs={{0,16},{1,17},{2,18},{3,19},{4,20},{5,21},{6,22},{7,23},{8,24},{9,... | collective-permute-start | bytes 540680 | tf_op jit(solution)/shard_map/ppermute | solution.py:352
  83.2 13.8 %collective-permute-start.14 = (f32[1,256,128]{2,1,0:T(8,128)S(1)}, f32[1,256,128]{2,1,0:T(8,128)S(1)}, u32[]{:S(2)}, u32[]{:S(2)}) collective-permute-start(f32[1,256,128]{2,1,0:T(8,128)S(1)} %get-tuple-element.135.refs_1_), channel_id=1, source_target_pairs={{0,16},{1,17},{2,18},{3,19},{4,20},{5,21},{6,22},{7,23},{8,24},{9,... | collective-permute-start | bytes 393224 | tf_op jit(solution)/shard_map/ppermute | solution.py:352
  97.8 9.5 %collective-permute-start.17 = (f32[1,352,128]{2,1,0:T(8,128)S(1)}, f32[1,352,128]{2,1,0:T(8,128)S(1)}, u32[]{:S(2)}, u32[]{:S(2)}) collective-permute-start(f32[1,352,128]{2,1,0:T(8,128)S(1)} %get-tuple-element.142.refs_1_), channel_id=1, source_target_pairs={{0,16},{1,17},{2,18},{3,19},{4,20},{5,21},{6,22},{7,23},{8,24},{9,... | collective-permute-start | bytes 540680 | tf_op jit(solution)/shard_map/ppermute | solution.py:352
  107.4 10.3 %collective-permute-start.20 = (f32[2,352,128]{2,1,0:T(8,128)S(1)}, f32[2,352,128]{2,1,0:T(8,128)S(1)}, u32[]{:S(2)}, u32[]{:S(2)}) collective-permute-start(f32[2,352,128]{2,1,0:T(8,128)S(1)} %get-tuple-element.150.refs_1_), channel_id=1, source_target_pairs={{0,4},{1,3},{2,6},{3,1},{4,0},{5,7},{6,2},{7,5},{8,12},{9,11},{10,... | collective-permute-start | bytes 1081352 | tf_op jit(solution)/shard_map/ppermute | solution.py:352
  107.5 10.2 %collective-permute-start.19 = (f32[2,256,128]{2,1,0:T(8,128)S(1)}, f32[2,256,128]{2,1,0:T(8,128)S(1)}, u32[]{:S(2)}, u32[]{:S(2)}) collective-permute-start(f32[2,256,128]{2,1,0:T(8,128)S(1)} %get-tuple-element.148), channel_id=1, source_target_pairs={{0,4},{1,3},{2,6},{3,1},{4,0},{5,7},{6,2},{7,5},{8,12},{9,11},{10,... | collective-permute-start | bytes 786440 | tf_op jit(solution)/shard_map/ppermute | solution.py:352
  117.8 38.9 %collective-permute-start.26 = (f32[4,352,128]{2,1,0:T(8,128)S(1)}, f32[4,352,128]{2,1,0:T(8,128)S(1)}, u32[]{:S(2)}, u32[]{:S(2)}) collective-permute-start(f32[4,352,128]{2,1,0:T(8,128)S(1)} %get-tuple-element.163.refs_1_), channel_id=1, source_target_pairs={{0,8},{1,9},{2,10},{3,11},{4,12},{5,13},{6,14},{7,15},{8,0},{9,1},... | collective-permute-start | bytes 2162696 | tf_op jit(solution)/shard_map/ppermute | solution.py:352
  119.0 32.1 %collective-permute-start.23 = (f32[4,256,128]{2,1,0:T(8,128)S(1)}, f32[4,256,128]{2,1,0:T(8,128)S(1)}, u32[]{:S(2)}, u32[]{:S(2)}) collective-permute-start(f32[4,256,128]{2,1,0:T(8,128)S(1)} %get-tuple-element.157.refs_1_), channel_id=1, source_target_pairs={{0,8},{1,9},{2,10},{3,11},{4,12},{5,13},{6,14},{7,15},{8,0},{9,1},... | collective-permute-start | bytes 1572872 | tf_op jit(solution)/shard_map/ppermute | solution.py:352
  119.9 24.7 %collective-permute-start.21 = (f32[1,256,128]{2,1,0:T(8,128)S(1)}, f32[1,256,128]{2,1,0:T(8,128)S(1)}, u32[]{:S(2)}, u32[]{:S(2)}) collective-permute-start(f32[1,256,128]{2,1,0:T(8,128)S(1)} %get-tuple-element.153), channel_id=1, source_target_pairs={{0,16},{1,17},{2,18},{3,19},{4,20},{5,21},{6,22},{7,23},{8,24},{9,... | collective-permute-start | bytes 393224 | tf_op jit(solution)/shard_map/ppermute | solution.py:352
  121.8 25.5 %collective-permute-start.22 = (f32[1,256,128]{2,1,0:T(8,128)S(1)}, f32[1,256,128]{2,1,0:T(8,128)S(1)}, u32[]{:S(2)}, u32[]{:S(2)}) collective-permute-start(f32[1,256,128]{2,1,0:T(8,128)S(1)} %get-tuple-element.155.refs_1_), channel_id=1, source_target_pairs={{0,16},{1,17},{2,18},{3,19},{4,20},{5,21},{6,22},{7,23},{8,24},{9,... | collective-permute-start | bytes 393224 | tf_op jit(solution)/shard_map/ppermute | solution.py:352
  147.3 9.3 %collective-permute-start.24 = (f32[2,256,128]{2,1,0:T(8,128)S(1)}, f32[2,256,128]{2,1,0:T(8,128)S(1)}, u32[]{:S(2)}, u32[]{:S(2)}) collective-permute-start(f32[2,256,128]{2,1,0:T(8,128)S(1)} %get-tuple-element.159.refs_1_), channel_id=1, source_target_pairs={{0,4},{1,3},{2,6},{3,1},{4,0},{5,7},{6,2},{7,5},{8,12},{9,11},{10,... | collective-permute-start | bytes 786440 | tf_op jit(solution)/shard_map/ppermute | solution.py:352
  147.7 8.9 %collective-permute-start.25 = (f32[1,256,128]{2,1,0:T(8,128)S(1)}, f32[1,256,128]{2,1,0:T(8,128)S(1)}, u32[]{:S(2)}, u32[]{:S(2)}) collective-permute-start(f32[1,256,128]{2,1,0:T(8,128)S(1)} %get-tuple-element.161.refs_1_), channel_id=1, source_target_pairs={{0,16},{1,17},{2,18},{3,19},{4,20},{5,21},{6,22},{7,23},{8,24},{9,... | collective-permute-start | bytes 393224 | tf_op jit(solution)/shard_map/ppermute | solution.py:352
  151.2 16.5 %collective-permute-start.27 = (f32[8,256,128]{2,1,0:T(8,128)S(1)}, f32[8,256,128]{2,1,0:T(8,128)S(1)}, u32[]{:S(2)}, u32[]{:S(2)}) collective-permute-start(f32[8,256,128]{2,1,0:T(8,128)S(1)} %get-tuple-element.165.refs_2_), channel_id=1, source_target_pairs={{0,2},{1,5},{2,0},{3,7},{4,6},{5,1},{6,4},{7,3},{8,10},{9,13},{10,... | collective-permute-start | bytes 3145736 | tf_op jit(solution)/shard_map/ppermute | solution.py:352
  156.8 25.7 %collective-permute-start.30 = (f32[8,352,128]{2,1,0:T(8,128)S(1)}, f32[8,352,128]{2,1,0:T(8,128)S(1)}, u32[]{:S(2)}, u32[]{:S(2)}) collective-permute-start(f32[8,352,128]{2,1,0:T(8,128)S(1)} %get-tuple-element.170.refs_2_.refs_4_), channel_id=1, source_target_pairs={{0,2},{1,5},{2,0},{3,7},{4,6},{5,1},{6,4},{7,3},{8,10},{9,13},{10,... | collective-permute-start | bytes 4325384 | tf_op jit(solution)/shard_map/ppermute | solution.py:352
  158.4 9.2 %collective-permute-start.28 = (f32[2,256,128]{2,1,0:T(8,128)S(1)}, f32[2,256,128]{2,1,0:T(8,128)S(1)}, u32[]{:S(2)}, u32[]{:S(2)}) collective-permute-start(f32[2,256,128]{2,1,0:T(8,128)S(1)} %get-tuple-element.166.refs_2_), channel_id=1, source_target_pairs={{0,4},{1,3},{2,6},{3,1},{4,0},{5,7},{6,2},{7,5},{8,12},{9,11},{10,... | collective-permute-start | bytes 786440 | tf_op jit(solution)/shard_map/ppermute | solution.py:352
  158.4 14.1 %collective-permute-start.29 = (f32[4,256,128]{2,1,0:T(8,128)S(1)}, f32[4,256,128]{2,1,0:T(8,128)S(1)}, u32[]{:S(2)}, u32[]{:S(2)}) collective-permute-start(f32[4,256,128]{2,1,0:T(8,128)S(1)} %get-tuple-element.168.refs_1_), channel_id=1, source_target_pairs={{0,8},{1,9},{2,10},{3,11},{4,12},{5,13},{6,14},{7,15},{8,0},{9,1},... | collective-permute-start | bytes 1572872 | tf_op jit(solution)/shard_map/ppermute | solution.py:352
  167.7 14.9 %collective-permute-start.31 = (f32[4,256,128]{2,1,0:T(8,128)S(1)}, f32[4,256,128]{2,1,0:T(8,128)S(1)}, u32[]{:S(2)}, u32[]{:S(2)}) collective-permute-start(f32[4,256,128]{2,1,0:T(8,128)S(1)} %get-tuple-element.172.refs_1_), channel_id=1, source_target_pairs={{0,8},{1,9},{2,10},{3,11},{4,12},{5,13},{6,14},{7,15},{8,0},{9,1},... | collective-permute-start | bytes 1572872 | tf_op jit(solution)/shard_map/ppermute | solution.py:352
  172.5 32.5 %collective-permute-start.33 = (f32[8,256,128]{2,1,0:T(8,128)S(1)}, f32[8,256,128]{2,1,0:T(8,128)S(1)}, u32[]{:S(2)}, u32[]{:S(2)}) collective-permute-start(f32[8,256,128]{2,1,0:T(8,128)S(1)} %get-tuple-element.176.refs_3_), channel_id=1, source_target_pairs={{0,2},{1,5},{2,0},{3,7},{4,6},{5,1},{6,4},{7,3},{8,10},{9,13},{10,... | collective-permute-start | bytes 3145736 | tf_op jit(solution)/shard_map/ppermute | solution.py:352
  182.6 35.8 %collective-permute-start.34 = (f32[8,256,128]{2,1,0:T(8,128)S(1)}, f32[8,256,128]{2,1,0:T(8,128)S(1)}, u32[]{:S(2)}, u32[]{:S(2)}) collective-permute-start(f32[8,256,128]{2,1,0:T(8,128)S(1)} %get-tuple-element.179.refs_3_), channel_id=1, source_target_pairs={{0,2},{1,5},{2,0},{3,7},{4,6},{5,1},{6,4},{7,3},{8,10},{9,13},{10,... | collective-permute-start | bytes 3145736 | tf_op jit(solution)/shard_map/ppermute | solution.py:352
  (6 other events, 32.5 us)

commit v7 on v6

--- a/solution.py
+++ b/solution.py
@@ -23,9 +23,9 @@
 CALLS = ((0,), (1,), (2,), (3,))
 UPDATES = ((0, 1), (2,), (3,))
 ORDER = (
-    ["p0", "g", "p1", "k1.0", "p2", "k2.0", "k1.1", "p3", "k2.1", "k3.0", "k1.2", "k1.3", "k3.1", "k4.0", "k2.2"]
-    + ["k4.1", "k3.2", "k5.0", "k2.3", "k6.0", "k5.1", "k4.2", "k3.3", "k6.1", "k4.3", "k5.2", "k7.0", "k6.2", "k5.3"]
-    + ["k7.1", "f.0", "k6.3", "k7.2", "f.1", "x", "k7.3", "u0", "f.2", "u1", "f.3", "u2"]
+    ["p0", "g", "p1", "k1.0", "p2", "k2.0", "k1.1", "p3", "k1.2", "k2.1", "k3.0", "k3.1", "k2.2", "k1.3", "k4.0"]
+    + ["k3.2", "k4.1", "k5.0", "k2.3", "k6.0", "k4.2", "k5.1", "k3.3", "k6.1", "k5.2", "k4.3", "k7.0", "k6.2", "k5.3"]
+    + ["k7.1", "f.0", "k6.3", "k7.2", "k7.3", "f.1", "x", "u0", "f.2", "u1", "f.3", "u2"]
 )
 
 
@@ -81,7 +81,7 @@
 ANY = pl.BlockSpec(memory_space=pl.ANY)
 SMEM = pl.BlockSpec(memory_space=pltpu.SMEM)
 
-COST = pl.CostEstimate(flops=1, bytes_accessed=1, transcendentals=0)
+COST = pl.CostEstimate(flops=10**10, bytes_accessed=100, transcendentals=0)
 
 
 def params(limit=VMEM_LIMIT):
@@ -302,7 +302,7 @@
 
 def update(place, after, panels, left_over, sides, factors, slab, state, grams, carry):
     rows, columns = slab.shape
-    steps = 4
+    steps = 4 if len(panels) > 1 else 2
     deep = rows // steps
     first, count = panels[0], len(panels)
     size = factors.shape[-1]

time: 229 us -> 217 us (0.948)
  waiting for transfers between devices: 98.9 us -> 91.9 us
  starting transfers between devices: 47.5 us -> 43.7 us
    ppermute x32, waiting for transfers between devices: 96.6 us -> 91.7 us  [swap(): return lax.ppermute(value, ('row', 'col'), pairs)]
    ppermute x32, starting transfers between devices: 47 us -> 43.1 us  [swap(): return lax.ppermute(value, ('row', 'col'), pairs)]
    pallas_call x3, Pallas kernels: 43.2 us -> 40.7 us  [update(): pl.pallas_call(functools.partial(update_kernel, panels, len(grams), len(c...]
  transfers between devices with their start and end apart: 35 -> 35, of which waited for: 20 -> 20; matrix products, arithmetic and copies ran while one was open for 1% -> 1% of each run, Pallas kernels for 30% -> 32%
where the time goes in v7:
time: 217 us; the launch traced here: 216 us
  waiting for transfers between devices  91.9 us (42%)
  Pallas kernels  78.1 us (36%)
  starting transfers between devices  43.7 us (20%)
    ppermute x32, waiting for transfers between devices, swap(): return lax.ppermute(value, ('row', 'col'), pairs)  91.7 us
    ppermute x32, starting transfers between devices, swap(): return lax.ppermute(value, ('row', 'col'), pairs)  43.1 us
    pallas_call x3, Pallas kernels, update(): pl.pallas_call(functools.partial(update_kernel, panels, len(grams), len(c...  40.7 us
    pallas_call x4, Pallas kernels, project(): pl.pallas_call(functools.partial(project_kernel, steps, call, blocks, len...  32 us
  transfers between devices with their start and end apart: 35, of which 20 were waited for; matrix products, arithmetic and copies ran while one was open for 1% of the time, Pallas kernels for 32%

profile of v7, /device:TPU:0, one launch (start us, length us, event | category | flops | bytes accessed | tf_op | source)
XLA Modules:
  0.0 215.9 jit_solution(15773061110329022267)
XLA Ops:
  1.1 8.9 %project_0.1 = (f32[8,256,128]{2,1,0:T(8,128)}, f32[8,256,128]{2,1,0:T(8,128)}, f32[8,128]{1,0:T(8,128)}) custom-call(s32[1]{0:T(128)} %bitcast.place.place_ref, f32[8,128]{1,0:T(8,128)} %broadcast_in_dim.3.refs_0_, f32[4,1024,128]{2,1,0:T(8,128)} %refs_6_.1, f32[4,1024,128]{2,1,0:T(8,128)} %refs_6_.1, f32[1024,2048]{1,0:T(8,128)} %refs_12_.1), custom_call_target="tpu_custom_call" | custom-call | flops 10000000000 | bytes 100 | tf_op jit(solution)/shard_map/project_0/pallas_call | solution.py:161
  10.0 3.0 %collective-permute-start.2 = (f32[8,256,128]{2,1,0:T(8,128)}, f32[8,256,128]{2,1,0:T(8,128)S(1)}, u32[]{:S(2)}, u32[]{:S(2)}) collective-permute-start(f32[8,256,128]{2,1,0:T(8,128)} %get-tuple-element.98), channel_id=1, source_target_pairs={{0,2},{1,5},{2,0},{3,7},{4,6},{5,1},{6,4},{7,3},{8,10},{9,13},{10,... | collective-permute-start | bytes 3145736 | tf_op jit(solution)/shard_map/ppermute | solution.py:352
  14.5 3.8 %gram_rows.1 = (f32[16,96,128]{2,1,0:T(8,128)S(1)}, f32[8,128]{1,0:T(8,128)S(1)}) custom-call(s32[1]{0:T(128)} %bitcast.place.place_ref, f32[8,128]{1,0:T(8,128)S(1)} %copy-done.4, f32[4,1024,128]{2,1,0:T(8,128)S(1)} %copy-done.2, f32[4,1024,128]{2,1,0:T(8,128)S(1)} %copy-done.2, f32[4,1024,128]{2,1,0:T(8,128)} %collective-permute-done.refs_3_.refs_2_.refs_9_.refs_11_.refs_7_), custom_call_target="tpu_custom_call" | custom-call | flops 10000000000 | bytes 100 | tf_op jit(solution)/shard_map/gram_rows/pallas_call | solution.py:199
  18.4 7.8 %project_1.1 = (f32[8,352,128]{2,1,0:T(8,128)S(1)}, f32[8,352,128]{2,1,0:T(8,128)S(1)}, f32[8,128]{1,0:T(8,128)S(1)}) custom-call(s32[1]{0:T(128)} %bitcast.place.place_ref, f32[8,128]{1,0:T(8,128)S(1)} %get-tuple-element.94.refs_0_, f32[4,256,256]{2,1,0:T(8,128)S(1)} %fusion.1.refs_1_.refs_2_, ...), custom_call_target="tpu_custom_call" | custom-call | flops 10000000000 | bytes 100 | tf_op jit(solution)/shard_map/project_1/pallas_call | solution.py:161
  26.3 2.0 collective-permute-start.3
  29.8 7.6 %project_2.1 = (f32[8,256,128]{2,1,0:T(8,128)S(1)}, f32[8,256,128]{2,1,0:T(8,128)S(1)}, f32[8,128]{1,0:T(8,128)S(1)}) custom-call(s32[1]{0:T(128)} %bitcast.place.place_ref, f32[8,128]{1,0:T(8,128)S(1)} %get-tuple-element.99.refs_0_, f32[4,1024,128]{2,1,0:T(8,128)S(1)} %copy-done.2, ...), custom_call_target="tpu_custom_call" | custom-call | flops 10000000000 | bytes 100 | tf_op jit(solution)/shard_map/project_2/pallas_call | solution.py:161
  38.0 2.0 collective-permute-done.3.refs_2_
  41.4 8.8 %collective-permute-done.4.refs_2_ = f32[8,352,128]{2,1,0:T(8,128)S(1)} collective-permute-done((f32[8,352,128]{2,1,0:T(8,128)S(1)}, f32[8,352,128]{2,1,0:T(8,128)S(1)}, u32[]{:S(2)}, u32[]{:S(2)}) %collective-permute-start.4) | collective-permute-done | bytes 1441824 | tf_op jit(solution)/shard_map/ppermute | solution.py:352
  50.4 7.7 %project_3.1 = (f32[8,256,128]{2,1,0:T(8,128)S(1)}, f32[8,256,128]{2,1,0:T(8,128)S(1)}, f32[8,128]{1,0:T(8,128)S(1)}) custom-call(s32[1]{0:T(128)} %bitcast.place.place_ref, f32[8,128]{1,0:T(8,128)S(1)} %get-tuple-element.106.refs_0_, f32[4,1024,128]{2,1,0:T(8,128)S(1)} %copy-done.2, ...), custom_call_target="tpu_custom_call" | custom-call | flops 10000000000 | bytes 100 | tf_op jit(solution)/shard_map/project_3/pallas_call | solution.py:161
  58.2 3.2 %collective-permute-done.5.refs_2_ = f32[8,256,128]{2,1,0:T(8,128)S(1)} collective-permute-done((f32[8,256,128]{2,1,0:T(8,128)S(1)}, f32[8,256,128]{2,1,0:T(8,128)S(1)}, u32[]{:S(2)}, u32[]{:S(2)}) %collective-permute-start.5) | collective-permute-done | bytes 1048608 | tf_op jit(solution)/shard_map/ppermute | solution.py:352
  61.6 1.9 collective-permute-start.10
  63.5 6.5 %collective-permute-done.6.refs_2_ = f32[4,352,128]{2,1,0:T(8,128)S(1)} collective-permute-done((f32[4,352,128]{2,1,0:T(8,128)S(1)}, f32[4,352,128]{2,1,0:T(8,128)S(1)}, u32[]{:S(2)}, u32[]{:S(2)}) %collective-permute-start.6) | collective-permute-done | bytes 720928 | tf_op jit(solution)/shard_map/ppermute | solution.py:352
  72.8 4.8 %collective-permute-done.8.refs_2_ = f32[2,352,128]{2,1,0:T(8,128)S(1)} collective-permute-done((f32[2,352,128]{2,1,0:T(8,128)S(1)}, f32[2,352,128]{2,1,0:T(8,128)S(1)}, u32[]{:S(2)}, u32[]{:S(2)}) %collective-permute-start.8) | collective-permute-done | bytes 360480 | tf_op jit(solution)/shard_map/ppermute | solution.py:352
  82.7 2.6 %collective-permute-start.14 = (f32[1,256,128]{2,1,0:T(8,128)S(1)}, f32[1,256,128]{2,1,0:T(8,128)S(1)}, u32[]{:S(2)}, u32[]{:S(2)}) collective-permute-start(f32[1,256,128]{2,1,0:T(8,128)S(1)} %get-tuple-element.135.refs_1_), channel_id=1, source_target_pairs={{0,16},{1,17},{2,18},{3,19},{4,20},{5,21},{6,22},{7,23},{8,24},{9,... | collective-permute-start | bytes 393224 | tf_op jit(solution)/shard_map/ppermute | solution.py:352
  86.1 6.5 %collective-permute-done.13.refs_2_ = f32[1,352,128]{2,1,0:T(8,128)S(1)} collective-permute-done((f32[1,352,128]{2,1,0:T(8,128)S(1)}, f32[1,352,128]{2,1,0:T(8,128)S(1)}, u32[]{:S(2)}, u32[]{:S(2)}) %collective-permute-start.13) | collective-permute-done | bytes 180256 | tf_op jit(solution)/shard_map/ppermute | solution.py:352
  92.6 2.2 %collective-permute-done.14.refs_2_ = f32[1,256,128]{2,1,0:T(8,128)S(1)} collective-permute-done((f32[1,256,128]{2,1,0:T(8,128)S(1)}, f32[1,256,128]{2,1,0:T(8,128)S(1)}, u32[]{:S(2)}, u32[]{:S(2)}) %collective-permute-start.14) | collective-permute-done | bytes 131104 | tf_op jit(solution)/shard_map/ppermute | solution.py:352
  96.2 2.9 %collective-permute-start.18 = (f32[1,352,128]{2,1,0:T(8,128)S(1)}, f32[1,352,128]{2,1,0:T(8,128)S(1)}, u32[]{:S(2)}, u32[]{:S(2)}) collective-permute-start(f32[1,352,128]{2,1,0:T(8,128)S(1)} %get-tuple-element.145.refs_1_), channel_id=1, source_target_pairs={{0,16},{1,17},{2,18},{3,19},{4,20},{5,21},{6,22},{7,23},{8,24},{9,... | collective-permute-start | bytes 540680 | tf_op jit(solution)/shard_map/ppermute | solution.py:352
  101.9 7.6 %collective-permute-done.17.refs_2_ = f32[1,256,128]{2,1,0:T(8,128)S(1)} collective-permute-done((f32[1,256,128]{2,1,0:T(8,128)S(1)}, f32[1,256,128]{2,1,0:T(8,128)S(1)}, u32[]{:S(2)}, u32[]{:S(2)}) %collective-permute-start.17) | collective-permute-done | bytes 131104 | tf_op jit(solution)/shard_map/ppermute | solution.py:352
  109.5 2.4 %collective-permute-done.18.refs_2_ = f32[1,352,128]{2,1,0:T(8,128)S(1)} collective-permute-done((f32[1,352,128]{2,1,0:T(8,128)S(1)}, f32[1,352,128]{2,1,0:T(8,128)S(1)}, u32[]{:S(2)}, u32[]{:S(2)}) %collective-permute-start.18) | collective-permute-done | bytes 180256 | tf_op jit(solution)/shard_map/ppermute | solution.py:352
  113.7 3.0 %collective-permute-start.22 = (f32[1,256,128]{2,1,0:T(8,128)S(1)}, f32[1,256,128]{2,1,0:T(8,128)S(1)}, u32[]{:S(2)}, u32[]{:S(2)}) collective-permute-start(f32[1,256,128]{2,1,0:T(8,128)S(1)} %get-tuple-element.155), channel_id=1, source_target_pairs={{0,16},{1,17},{2,18},{3,19},{4,20},{5,21},{6,22},{7,23},{8,24},{9,... | collective-permute-start | bytes 393224 | tf_op jit(solution)/shard_map/ppermute | solution.py:352
  116.7 2.7 %collective-permute-done.20.refs_2_ = f32[2,352,128]{2,1,0:T(8,128)S(1)} collective-permute-done((f32[2,352,128]{2,1,0:T(8,128)S(1)}, f32[2,352,128]{2,1,0:T(8,128)S(1)}, u32[]{:S(2)}, u32[]{:S(2)}) %collective-permute-start.20) | collective-permute-done | bytes 360480 | tf_op jit(solution)/shard_map/ppermute | solution.py:352
  121.4 10.2 %collective-permute-done.22.refs_2_ = f32[1,256,128]{2,1,0:T(8,128)S(1)} collective-permute-done((f32[1,256,128]{2,1,0:T(8,128)S(1)}, f32[1,256,128]{2,1,0:T(8,128)S(1)}, u32[]{:S(2)}, u32[]{:S(2)}) %collective-permute-start.22) | collective-permute-done | bytes 131104 | tf_op jit(solution)/shard_map/ppermute | solution.py:352
  131.7 3.4 %collective-permute-start.25 = (f32[1,256,128]{2,1,0:T(8,128)S(1)}, f32[1,256,128]{2,1,0:T(8,128)S(1)}, u32[]{:S(2)}, u32[]{:S(2)}) collective-permute-start(f32[1,256,128]{2,1,0:T(8,128)S(1)} %get-tuple-element.161.refs_1_), channel_id=1, source_target_pairs={{0,16},{1,17},{2,18},{3,19},{4,20},{5,21},{6,22},{7,23},{8,24},{9,... | collective-permute-start | bytes 393224 | tf_op jit(solution)/shard_map/ppermute | solution.py:352
  136.5 11.9 %collective-permute-done.25.refs_2_ = f32[1,256,128]{2,1,0:T(8,128)S(1)} collective-permute-done((f32[1,256,128]{2,1,0:T(8,128)S(1)}, f32[1,256,128]{2,1,0:T(8,128)S(1)}, u32[]{:S(2)}, u32[]{:S(2)}) %collective-permute-start.25) | collective-permute-done | bytes 131104 | tf_op jit(solution)/shard_map/ppermute | solution.py:352
  149.9 2.0 collective-permute-start.29
  152.5 4.7 %collective-permute-done.28.refs_3_ = f32[2,256,128]{2,1,0:T(8,128)S(1)} collective-permute-done((f32[2,256,128]{2,1,0:T(8,128)S(1)}, f32[2,256,128]{2,1,0:T(8,128)S(1)}, u32[]{:S(2)}, u32[]{:S(2)}) %collective-permute-start.28) | collective-permute-done | bytes 262176 | tf_op jit(solution)/shard_map/ppermute | solution.py:352
  157.2 2.1 collective-permute-start.30
  159.4 5.4 %collective-permute-done.29.refs_2_ = f32[4,256,128]{2,1,0:T(8,128)S(1)} collective-permute-done((f32[4,256,128]{2,1,0:T(8,128)S(1)}, f32[4,256,128]{2,1,0:T(8,128)S(1)}, u32[]{:S(2)}, u32[]{:S(2)}) %collective-permute-start.29) | collective-permute-done | bytes 524320 | tf_op jit(solution)/shard_map/ppermute | solution.py:352
  164.9 7.8 %collective-permute-done.30.refs_2_ = f32[4,256,128]{2,1,0:T(8,128)S(1)} collective-permute-done((f32[4,256,128]{2,1,0:T(8,128)S(1)}, f32[4,256,128]{2,1,0:T(8,128)S(1)}, u32[]{:S(2)}, u32[]{:S(2)}) %collective-permute-start.30) | collective-permute-done | bytes 524320 | tf_op jit(solution)/shard_map/ppermute | solution.py:352
  175.2 19.3 %update_panels01.1 = (f32[1024,2048]{1,0:T(8,128)}, f32[512,2048]{1,0:T(8,128)}) custom-call(s32[1]{0:T(128)} %bitcast.place.place_ref, f32[8,128]{1,0:T(8,128)S(1)} %get-tuple-element.173.refs_0_, f32[4,256,256]{2,1,0:T(8,128)S(1)} %copy-done.1, f32[8,256,128]{2,1,0:T(8,128)S(1)} %get-tuple-element.165.refs_2_, ...), custom_call_target="tpu_custom_call" | custom-call | flops 10000000000 | bytes 100 | tf_op jit(solution)/shard_map/update_panels01/pallas_call | solution.py:324
  194.5 12.2 %update_panels2.1 = (f32[1024,2048]{1,0:T(8,128)}, f32[256,2048]{1,0:T(8,128)S(1)}) custom-call(s32[1]{0:T(128)} %bitcast.place.place_ref, f32[1024,2048]{1,0:T(8,128)} %get-tuple-element.175.refs_0_.refs_10_, f32[8,256,128]{2,1,0:T(8,128)S(1)} %collective-permute-done.33.refs_1_.refs_4_, f32[4,256,256]{2,1,0:T(8,128)S(1)} %copy-done.1, ...), custom_call_target="tpu_custom_call" | custom-call | flops 10000000000 | bytes 100 | tf_op jit(solution)/shard_map/update_panels2/pallas_call | solution.py:324
  206.7 9.2 %update_panels3.1 = f32[1024,2048]{1,0:T(8,128)} custom-call(s32[1]{0:T(128)} %bitcast.place.place_ref, f32[1024,2048]{1,0:T(8,128)} %get-tuple-element.178.refs_0_.refs_8_, f32[8,256,128]{2,1,0:T(8,128)S(1)} %collective-permute-done.34.refs_1_.refs_4_, f32[4,256,256]{2,1,0:T(8,128)S(1)} %copy-done.1, f32[8,256,128]{2,1,0:T(8,128)S(1)} %get-tuple-element.179.refs_3_, ...), custom_call_target="tpu_custom_call" | custom-call | flops 10000000000 | bytes 100 | tf_op jit(solution)/shard_map/update_panels3/pallas_call | solution.py:324
  (87 shorter events, 29.4 us)
Async XLA Ops:
  0.0 14.5 %collective-permute-start = (f32[4,1024,128]{2,1,0:T(8,128)}, f32[4,1024,128]{2,1,0:T(8,128)}, u32[]{:S(2)}, u32[]{:S(2)}) collective-permute-start(f32[4,1024,128]{2,1,0:T(8,128)} %refs_6_.1), channel_id=1, source_target_pairs={{1,0},{0,1},{3,2},{2,3},{5,4},{4,5},{7,6},{6,7},{9,8},{8,9},{11,10... | collective-permute-start | bytes 6291464 | tf_op jit(solution)/shard_map/ppermute | solution.py:357
  0.5 12.6 %collective-permute-start.1 = (f32[4,128,256]{2,1,0:T(8,128)}, f32[4,128,256]{2,1,0:T(8,128)}, u32[]{:S(2)}, u32[]{:S(2)}) collective-permute-start(f32[4,128,256]{2,1,0:T(8,128)} %param.5), channel_id=1, source_target_pairs={{1,0},{0,1},{3,2},{2,3},{5,4},{4,5},{7,6},{6,7},{9,8},{8,9},{11,10... | collective-permute-start | bytes 1572872 | tf_op jit(solution)/shard_map/ppermute | solution.py:357
  10.0 16.1 %collective-permute-start.2 = (f32[8,256,128]{2,1,0:T(8,128)}, f32[8,256,128]{2,1,0:T(8,128)S(1)}, u32[]{:S(2)}, u32[]{:S(2)}) collective-permute-start(f32[8,256,128]{2,1,0:T(8,128)} %get-tuple-element.98), channel_id=1, source_target_pairs={{0,2},{1,5},{2,0},{3,7},{4,6},{5,1},{6,4},{7,3},{8,10},{9,13},{10,... | collective-permute-start | bytes 3145736 | tf_op jit(solution)/shard_map/ppermute | solution.py:352
  26.3 13.7 %collective-permute-start.3 = (f32[4,256,128]{2,1,0:T(8,128)S(1)}, f32[4,256,128]{2,1,0:T(8,128)S(1)}, u32[]{:S(2)}, u32[]{:S(2)}) collective-permute-start(f32[4,256,128]{2,1,0:T(8,128)S(1)} %get-tuple-element.102), channel_id=1, source_target_pairs={{0,8},{1,9},{2,10},{3,11},{4,12},{5,13},{6,14},{7,15},{8,0},{9,1},... | collective-permute-start | bytes 1572872 | tf_op jit(solution)/shard_map/ppermute | solution.py:352
  28.3 21.8 %collective-permute-start.4 = (f32[8,352,128]{2,1,0:T(8,128)S(1)}, f32[8,352,128]{2,1,0:T(8,128)S(1)}, u32[]{:S(2)}, u32[]{:S(2)}) collective-permute-start(f32[8,352,128]{2,1,0:T(8,128)S(1)} %get-tuple-element.105), channel_id=1, source_target_pairs={{0,2},{1,5},{2,0},{3,7},{4,6},{5,1},{6,4},{7,3},{8,10},{9,13},{10,... | collective-permute-start | bytes 4325384 | tf_op jit(solution)/shard_map/ppermute | solution.py:352
  37.4 24.0 %collective-permute-start.5 = (f32[8,256,128]{2,1,0:T(8,128)S(1)}, f32[8,256,128]{2,1,0:T(8,128)S(1)}, u32[]{:S(2)}, u32[]{:S(2)}) collective-permute-start(f32[8,256,128]{2,1,0:T(8,128)S(1)} %get-tuple-element.109), channel_id=1, source_target_pairs={{0,2},{1,5},{2,0},{3,7},{4,6},{5,1},{6,4},{7,3},{8,10},{9,13},{10,... | collective-permute-start | bytes 3145736 | tf_op jit(solution)/shard_map/ppermute | solution.py:352
  40.0 31.5 %collective-permute-start.7 = (f32[2,256,128]{2,1,0:T(8,128)S(1)}, f32[2,256,128]{2,1,0:T(8,128)S(1)}, u32[]{:S(2)}, u32[]{:S(2)}) collective-permute-start(f32[2,256,128]{2,1,0:T(8,128)S(1)} %get-tuple-element.115), channel_id=1, source_target_pairs={{0,4},{1,3},{2,6},{3,1},{4,0},{5,7},{6,2},{7,5},{8,12},{9,11},{10,... | collective-permute-start | bytes 786440 | tf_op jit(solution)/shard_map/ppermute | solution.py:352
  50.3 19.8 %collective-permute-start.6 = (f32[4,352,128]{2,1,0:T(8,128)S(1)}, f32[4,352,128]{2,1,0:T(8,128)S(1)}, u32[]{:S(2)}, u32[]{:S(2)}) collective-permute-start(f32[4,352,128]{2,1,0:T(8,128)S(1)} %get-tuple-element.112), channel_id=1, source_target_pairs={{0,8},{1,9},{2,10},{3,11},{4,12},{5,13},{6,14},{7,15},{8,0},{9,1},... | collective-permute-start | bytes 2162696 | tf_op jit(solution)/shard_map/ppermute | solution.py:352
  61.5 18.1 %collective-permute-start.9 = (f32[4,256,128]{2,1,0:T(8,128)S(1)}, f32[4,256,128]{2,1,0:T(8,128)S(1)}, u32[]{:S(2)}, u32[]{:S(2)}) collective-permute-start(f32[4,256,128]{2,1,0:T(8,128)S(1)} %get-tuple-element.121), channel_id=1, source_target_pairs={{0,8},{1,9},{2,10},{3,11},{4,12},{5,13},{6,14},{7,15},{8,0},{9,1},... | collective-permute-start | bytes 1572872 | tf_op jit(solution)/shard_map/ppermute | solution.py:352
  61.6 20.9 %collective-permute-start.10 = (f32[8,256,128]{2,1,0:T(8,128)S(1)}, f32[8,256,128]{2,1,0:T(8,128)S(1)}, u32[]{:S(2)}, u32[]{:S(2)}) collective-permute-start(f32[8,256,128]{2,1,0:T(8,128)S(1)} %get-tuple-element.124), channel_id=1, source_target_pairs={{0,2},{1,5},{2,0},{3,7},{4,6},{5,1},{6,4},{7,3},{8,10},{9,13},{10,... | collective-permute-start | bytes 3145736 | tf_op jit(solution)/shard_map/ppermute | solution.py:352
  70.1 7.5 %collective-permute-start.8 = (f32[2,352,128]{2,1,0:T(8,128)S(1)}, f32[2,352,128]{2,1,0:T(8,128)S(1)}, u32[]{:S(2)}, u32[]{:S(2)}) collective-permute-start(f32[2,352,128]{2,1,0:T(8,128)S(1)} %get-tuple-element.118), channel_id=1, source_target_pairs={{0,4},{1,3},{2,6},{3,1},{4,0},{5,7},{6,2},{7,5},{8,12},{9,11},{10,... | collective-permute-start | bytes 1081352 | tf_op jit(solution)/shard_map/ppermute | solution.py:352
  71.5 11.1 %collective-permute-start.11 = (f32[1,256,128]{2,1,0:T(8,128)S(1)}, f32[1,256,128]{2,1,0:T(8,128)S(1)}, u32[]{:S(2)}, u32[]{:S(2)}) collective-permute-start(f32[1,256,128]{2,1,0:T(8,128)S(1)} %get-tuple-element.127), channel_id=1, source_target_pairs={{0,16},{1,17},{2,18},{3,19},{4,20},{5,21},{6,22},{7,23},{8,24},{9,... | collective-permute-start | bytes 393224 | tf_op jit(solution)/shard_map/ppermute | solution.py:352
  81.0 11.6 %collective-permute-start.13 = (f32[1,352,128]{2,1,0:T(8,128)S(1)}, f32[1,352,128]{2,1,0:T(8,128)S(1)}, u32[]{:S(2)}, u32[]{:S(2)}) collective-permute-start(f32[1,352,128]{2,1,0:T(8,128)S(1)} %get-tuple-element.133), channel_id=1, source_target_pairs={{0,16},{1,17},{2,18},{3,19},{4,20},{5,21},{6,22},{7,23},{8,24},{9,... | collective-permute-start | bytes 540680 | tf_op jit(solution)/shard_map/ppermute | solution.py:352
  82.7 12.1 %collective-permute-start.14 = (f32[1,256,128]{2,1,0:T(8,128)S(1)}, f32[1,256,128]{2,1,0:T(8,128)S(1)}, u32[]{:S(2)}, u32[]{:S(2)}) collective-permute-start(f32[1,256,128]{2,1,0:T(8,128)S(1)} %get-tuple-element.135.refs_1_), channel_id=1, source_target_pairs={{0,16},{1,17},{2,18},{3,19},{4,20},{5,21},{6,22},{7,23},{8,24},{9,... | collective-permute-start | bytes 393224 | tf_op jit(solution)/shard_map/ppermute | solution.py:352
  85.2 15.3 %collective-permute-start.15 = (f32[4,256,128]{2,1,0:T(8,128)S(1)}, f32[4,256,128]{2,1,0:T(8,128)S(1)}, u32[]{:S(2)}, u32[]{:S(2)}) collective-permute-start(f32[4,256,128]{2,1,0:T(8,128)S(1)} %get-tuple-element.138), channel_id=1, source_target_pairs={{0,8},{1,9},{2,10},{3,11},{4,12},{5,13},{6,14},{7,15},{8,0},{9,1},... | collective-permute-start | bytes 1572872 | tf_op jit(solution)/shard_map/ppermute | solution.py:352
  94.9 7.0 %collective-permute-start.16 = (f32[2,256,128]{2,1,0:T(8,128)S(1)}, f32[2,256,128]{2,1,0:T(8,128)S(1)}, u32[]{:S(2)}, u32[]{:S(2)}) collective-permute-start(f32[2,256,128]{2,1,0:T(8,128)S(1)} %get-tuple-element.140.refs_1_), channel_id=1, source_target_pairs={{0,4},{1,3},{2,6},{3,1},{4,0},{5,7},{6,2},{7,5},{8,12},{9,11},{10,... | collective-permute-start | bytes 786440 | tf_op jit(solution)/shard_map/ppermute | solution.py:352
  96.2 13.2 %collective-permute-start.17 = (f32[1,256,128]{2,1,0:T(8,128)S(1)}, f32[1,256,128]{2,1,0:T(8,128)S(1)}, u32[]{:S(2)}, u32[]{:S(2)}) collective-permute-start(f32[1,256,128]{2,1,0:T(8,128)S(1)} %get-tuple-element.143), channel_id=1, source_target_pairs={{0,16},{1,17},{2,18},{3,19},{4,20},{5,21},{6,22},{7,23},{8,24},{9,... | collective-permute-start | bytes 393224 | tf_op jit(solution)/shard_map/ppermute | solution.py:352
  96.2 15.7 %collective-permute-start.18 = (f32[1,352,128]{2,1,0:T(8,128)S(1)}, f32[1,352,128]{2,1,0:T(8,128)S(1)}, u32[]{:S(2)}, u32[]{:S(2)}) collective-permute-start(f32[1,352,128]{2,1,0:T(8,128)S(1)} %get-tuple-element.145.refs_1_), channel_id=1, source_target_pairs={{0,16},{1,17},{2,18},{3,19},{4,20},{5,21},{6,22},{7,23},{8,24},{9,... | collective-permute-start | bytes 540680 | tf_op jit(solution)/shard_map/ppermute | solution.py:352
  100.6 13.1 %collective-permute-start.19 = (f32[2,256,128]{2,1,0:T(8,128)S(1)}, f32[2,256,128]{2,1,0:T(8,128)S(1)}, u32[]{:S(2)}, u32[]{:S(2)}) collective-permute-start(f32[2,256,128]{2,1,0:T(8,128)S(1)} %get-tuple-element.148), channel_id=1, source_target_pairs={{0,4},{1,3},{2,6},{3,1},{4,0},{5,7},{6,2},{7,5},{8,12},{9,11},{10,... | collective-permute-start | bytes 786440 | tf_op jit(solution)/shard_map/ppermute | solution.py:352
  111.9 7.5 %collective-permute-start.20 = (f32[2,352,128]{2,1,0:T(8,128)S(1)}, f32[2,352,128]{2,1,0:T(8,128)S(1)}, u32[]{:S(2)}, u32[]{:S(2)}) collective-permute-start(f32[2,352,128]{2,1,0:T(8,128)S(1)} %get-tuple-element.150.refs_1_), channel_id=1, source_target_pairs={{0,4},{1,3},{2,6},{3,1},{4,0},{5,7},{6,2},{7,5},{8,12},{9,11},{10,... | collective-permute-start | bytes 1081352 | tf_op jit(solution)/shard_map/ppermute | solution.py:352
  113.7 21.5 %collective-permute-start.23 = (f32[4,256,128]{2,1,0:T(8,128)S(1)}, f32[4,256,128]{2,1,0:T(8,128)S(1)}, u32[]{:S(2)}, u32[]{:S(2)}) collective-permute-start(f32[4,256,128]{2,1,0:T(8,128)S(1)} %get-tuple-element.157.refs_1_), channel_id=1, source_target_pairs={{0,8},{1,9},{2,10},{3,11},{4,12},{5,13},{6,14},{7,15},{8,0},{9,1},... | collective-permute-start | bytes 1572872 | tf_op jit(solution)/shard_map/ppermute | solution.py:352
  113.7 17.9 %collective-permute-start.22 = (f32[1,256,128]{2,1,0:T(8,128)S(1)}, f32[1,256,128]{2,1,0:T(8,128)S(1)}, u32[]{:S(2)}, u32[]{:S(2)}) collective-permute-start(f32[1,256,128]{2,1,0:T(8,128)S(1)} %get-tuple-element.155), channel_id=1, source_target_pairs={{0,16},{1,17},{2,18},{3,19},{4,20},{5,21},{6,22},{7,23},{8,24},{9,... | collective-permute-start | bytes 393224 | tf_op jit(solution)/shard_map/ppermute | solution.py:352
  120.3 16.2 %collective-permute-start.24 = (f32[2,256,128]{2,1,0:T(8,128)S(1)}, f32[2,256,128]{2,1,0:T(8,128)S(1)}, u32[]{:S(2)}, u32[]{:S(2)}) collective-permute-start(f32[2,256,128]{2,1,0:T(8,128)S(1)} %get-tuple-element.159.refs_1_), channel_id=1, source_target_pairs={{0,4},{1,3},{2,6},{3,1},{4,0},{5,7},{6,2},{7,5},{8,12},{9,11},{10,... | collective-permute-start | bytes 786440 | tf_op jit(solution)/shard_map/ppermute | solution.py:352
  121.4 30.5 %collective-permute-start.26 = (f32[4,352,128]{2,1,0:T(8,128)S(1)}, f32[4,352,128]{2,1,0:T(8,128)S(1)}, u32[]{:S(2)}, u32[]{:S(2)}) collective-permute-start(f32[4,352,128]{2,1,0:T(8,128)S(1)} %get-tuple-element.163.refs_1_), channel_id=1, source_target_pairs={{0,8},{1,9},{2,10},{3,11},{4,12},{5,13},{6,14},{7,15},{8,0},{9,1},... | collective-permute-start | bytes 2162696 | tf_op jit(solution)/shard_map/ppermute | solution.py:352
  131.7 16.7 %collective-permute-start.25 = (f32[1,256,128]{2,1,0:T(8,128)S(1)}, f32[1,256,128]{2,1,0:T(8,128)S(1)}, u32[]{:S(2)}, u32[]{:S(2)}) collective-permute-start(f32[1,256,128]{2,1,0:T(8,128)S(1)} %get-tuple-element.161.refs_1_), channel_id=1, source_target_pairs={{0,16},{1,17},{2,18},{3,19},{4,20},{5,21},{6,22},{7,23},{8,24},{9,... | collective-permute-start | bytes 393224 | tf_op jit(solution)/shard_map/ppermute | solution.py:352
  135.2 22.0 %collective-permute-start.27 = (f32[8,256,128]{2,1,0:T(8,128)S(1)}, f32[8,256,128]{2,1,0:T(8,128)S(1)}, u32[]{:S(2)}, u32[]{:S(2)}) collective-permute-start(f32[8,256,128]{2,1,0:T(8,128)S(1)} %get-tuple-element.165.refs_2_), channel_id=1, source_target_pairs={{0,2},{1,5},{2,0},{3,7},{4,6},{5,1},{6,4},{7,3},{8,10},{9,13},{10,... | collective-permute-start | bytes 3145736 | tf_op jit(solution)/shard_map/ppermute | solution.py:352
  148.4 8.8 %collective-permute-start.28 = (f32[2,256,128]{2,1,0:T(8,128)S(1)}, f32[2,256,128]{2,1,0:T(8,128)S(1)}, u32[]{:S(2)}, u32[]{:S(2)}) collective-permute-start(f32[2,256,128]{2,1,0:T(8,128)S(1)} %get-tuple-element.166.refs_2_), channel_id=1, source_target_pairs={{0,4},{1,3},{2,6},{3,1},{4,0},{5,7},{6,2},{7,5},{8,12},{9,11},{10,... | collective-permute-start | bytes 786440 | tf_op jit(solution)/shard_map/ppermute | solution.py:352
  149.9 14.9 %collective-permute-start.29 = (f32[4,256,128]{2,1,0:T(8,128)S(1)}, f32[4,256,128]{2,1,0:T(8,128)S(1)}, u32[]{:S(2)}, u32[]{:S(2)}) collective-permute-start(f32[4,256,128]{2,1,0:T(8,128)S(1)} %get-tuple-element.168.refs_1_), channel_id=1, source_target_pairs={{0,8},{1,9},{2,10},{3,11},{4,12},{5,13},{6,14},{7,15},{8,0},{9,1},... | collective-permute-start | bytes 1572872 | tf_op jit(solution)/shard_map/ppermute | solution.py:352
  152.0 20.7 %collective-permute-start.31 = (f32[8,352,128]{2,1,0:T(8,128)S(1)}, f32[8,352,128]{2,1,0:T(8,128)S(1)}, u32[]{:S(2)}, u32[]{:S(2)}) collective-permute-start(f32[8,352,128]{2,1,0:T(8,128)S(1)} %get-tuple-element.172.refs_2_.refs_4_), channel_id=1, source_target_pairs={{0,2},{1,5},{2,0},{3,7},{4,6},{5,1},{6,4},{7,3},{8,10},{9,13},{10,... | collective-permute-start | bytes 4325384 | tf_op jit(solution)/shard_map/ppermute | solution.py:352
  157.2 15.4 %collective-permute-start.30 = (f32[4,256,128]{2,1,0:T(8,128)S(1)}, f32[4,256,128]{2,1,0:T(8,128)S(1)}, u32[]{:S(2)}, u32[]{:S(2)}) collective-permute-start(f32[4,256,128]{2,1,0:T(8,128)S(1)} %get-tuple-element.170.refs_1_), channel_id=1, source_target_pairs={{0,8},{1,9},{2,10},{3,11},{4,12},{5,13},{6,14},{7,15},{8,0},{9,1},... | collective-permute-start | bytes 1572872 | tf_op jit(solution)/shard_map/ppermute | solution.py:352
  172.9 21.6 %collective-permute-start.33 = (f32[8,256,128]{2,1,0:T(8,128)S(1)}, f32[8,256,128]{2,1,0:T(8,128)S(1)}, u32[]{:S(2)}, u32[]{:S(2)}) collective-permute-start(f32[8,256,128]{2,1,0:T(8,128)S(1)} %get-tuple-element.176.refs_3_), channel_id=1, source_target_pairs={{0,2},{1,5},{2,0},{3,7},{4,6},{5,1},{6,4},{7,3},{8,10},{9,13},{10,... | collective-permute-start | bytes 3145736 | tf_op jit(solution)/shard_map/ppermute | solution.py:352
  173.4 33.2 %collective-permute-start.34 = (f32[8,256,128]{2,1,0:T(8,128)S(1)}, f32[8,256,128]{2,1,0:T(8,128)S(1)}, u32[]{:S(2)}, u32[]{:S(2)}) collective-permute-start(f32[8,256,128]{2,1,0:T(8,128)S(1)} %get-tuple-element.179.refs_3_), channel_id=1, source_target_pairs={{0,2},{1,5},{2,0},{3,7},{4,6},{5,1},{6,4},{7,3},{8,10},{9,13},{10,... | collective-permute-start | bytes 3145736 | tf_op jit(solution)/shard_map/ppermute | solution.py:352
  (8 other events, 38.4 us)

commit v8 on v7

--- a/solution.py
+++ b/solution.py
@@ -23,8 +23,8 @@
 CALLS = ((0,), (1,), (2,), (3,))
 UPDATES = ((0, 1), (2,), (3,))
 ORDER = (
-    ["p0", "g", "p1", "k1.0", "p2", "k2.0", "k1.1", "p3", "k1.2", "k2.1", "k3.0", "k3.1", "k2.2", "k1.3", "k4.0"]
-    + ["k3.2", "k4.1", "k5.0", "k2.3", "k6.0", "k4.2", "k5.1", "k3.3", "k6.1", "k5.2", "k4.3", "k7.0", "k6.2", "k5.3"]
+    ["p0", "g", "p1", "k1.0", "p2", "k2.0", "p3", "k1.1", "k3.0", "k1.2", "k2.1", "k1.3", "k4.0", "k3.1", "k2.2"]
+    + ["k5.0", "k3.2", "k4.1", "k6.0", "k2.3", "k5.1", "k4.2", "k3.3", "k6.1", "k5.2", "k4.3", "k7.0", "k6.2", "k5.3"]
     + ["k7.1", "f.0", "k6.3", "k7.2", "k7.3", "f.1", "x", "u0", "f.2", "u1", "f.3", "u2"]
 )
 
@@ -266,33 +266,33 @@
                     ]
         factor = [left_depth(factor_ref[row]) for row in range(count)]
         later = [panels[-1] + 1 + more for more in range(left_over)]
-        grams = {
-            (panel, row): left_depth(gram_block(panel, panels[row]))
-            for panel in list(panels) + later
+        ahead = list(panels) + later
+        grams = [
+            left_depth(jnp.concatenate([gram_block(panel, panels[row]) for panel in ahead[row + 1 :]]))
+            if ahead[row + 1 :]
+            else None
             for row in range(count)
-            if panels[row] < panel
-        }
+        ]
         for quarter in range(4):
             at = pl.ds(quarter * wide, wide)
-            past = []
-
-            def less(value, panel, sign):
-                for row, weights in enumerate(past):
-                    value = value + sign * dot(grams[panel, row], weights)
-                return value
-
+            taken = [None] * len(ahead)
+            if carried:
+                taken = [carry_ref[pl.ds(row * SIZE, SIZE), at] for row in range(len(ahead))]
             for row in range(count):
                 proj = proj_ref[pl.ds(row * SIZE, SIZE), at]
-                if carried:
-                    proj = proj - carry_ref[pl.ds(row * SIZE, SIZE), at]
-                proj = less(proj, panels[row], -1.0)
+                if taken[row] is not None:
+                    proj = proj - taken[row]
                 high, low = halves(dot(factor[row], right_depth(proj)))
-                past.append(jnp.concatenate([high, high, low]))
+                weights = jnp.concatenate([high, high, low])
                 for copy, value in enumerate([high, high, low]):
                     depth_ref[pl.ds(copy * depth + row * SIZE, SIZE), at] = value
-            for more, panel in enumerate(later):
-                value = carry_ref[pl.ds((count + more) * SIZE, SIZE), at] if carried else jnp.zeros((SIZE, wide), F32)
-                refs[2 * count + 2][pl.ds(more * SIZE, SIZE), at] = less(value, panel, 1.0)
+                if grams[row] is not None:
+                    made = dot(grams[row], weights)
+                    for more in range(row + 1, len(ahead)):
+                        term = made[(more - row - 1) * SIZE : (more - row) * SIZE]
+                        taken[more] = term if taken[more] is None else taken[more] + term
+            for more in range(left_over):
+                refs[2 * count + 2][pl.ds(more * SIZE, SIZE), at] = taken[count + more]
 
     left = left_depth(jnp.concatenate([ref[0] for ref in blocks], axis=1))
     for quarter in range(4):
@@ -302,7 +302,7 @@
 
 def update(place, after, panels, left_over, sides, factors, slab, state, grams, carry):
     rows, columns = slab.shape
-    steps = 4 if len(panels) > 1 else 2
+    steps = 2
     deep = rows // steps
     first, count = panels[0], len(panels)
     size = factors.shape[-1]
@@ -328,7 +328,7 @@
         out_specs=out_specs,
         scratch_shapes=[pltpu.VMEM((3 * count * size, columns), jnp.bfloat16), pltpu.VMEM((count * size, columns), F32)],
         out_shape=outs,
-        compiler_params=params(),
+        compiler_params=params(FIRST_LIMIT if count > 1 else VMEM_LIMIT),
         cost_estimate=COST,
         name="update_panels" + "".join(map(str, panels)),
     )(place, *after, factors, *constant, *blocks, slab)

time: 217 us -> 222 us (1.023)
  local copies, waits for them, and re-layouts: 0.61 us -> 5.27 us
  Pallas kernels: 78.1 us -> 82.4 us
  starting transfers between devices: 43.7 us -> 40.3 us
    unnamed x10 -> x30, local copies, waits for them, and re-layouts: 0.02 us -> 4.68 us
    ppermute x32, starting transfers between devices: 43.1 us -> 39.8 us  [swap(): return lax.ppermute(value, ('row', 'col'), pairs)]
    pallas_call x3, Pallas kernels: 40.7 us -> 43.1 us  [update(): pl.pallas_call(functools.partial(update_kernel, panels, len(grams), len(c...]
  transfers between devices with their start and end apart: 35 -> 35, of which waited for: 20 -> 19; matrix products, arithmetic and copies ran while one was open for 1% -> 1% of each run, Pallas kernels for 32% -> 33%
where the time goes in v8:
time: 222 us
  waiting for transfers between devices  91.9 us (41%)
  Pallas kernels  82.4 us (37%)
  starting transfers between devices  40.3 us (18%)
  local copies, waits for them, and re-layouts  5.27 us (2%)
    ppermute x32, waiting for transfers between devices, swap(): return lax.ppermute(value, ('row', 'col'), pairs)  91.6 us
    pallas_call x3, Pallas kernels, update(): pl.pallas_call(functools.partial(update_kernel, panels, len(grams), len(c...  43.1 us
    ppermute x32, starting transfers between devices, swap(): return lax.ppermute(value, ('row', 'col'), pairs)  39.8 us
    pallas_call x4, Pallas kernels, project(): pl.pallas_call(functools.partial(project_kernel, steps, call, blocks, len...  32 us
    unnamed x30, local copies, waits for them, and re-layouts  4.68 us
  transfers between devices with their start and end apart: 35, of which 19 were waited for; matrix products, arithmetic and copies ran while one was open for 1% of the time, Pallas kernels for 33%

profile of v8, /device:TPU:0, one launch (start us, length us, event | category | flops | bytes accessed | tf_op | source)
XLA Modules:
  0.0 221.7 jit_solution(3505191314054157269)
XLA Ops:
  1.1 8.9 %project_0.1 = (f32[8,256,128]{2,1,0:T(8,128)}, f32[8,256,128]{2,1,0:T(8,128)}, f32[8,128]{1,0:T(8,128)}) custom-call(s32[1]{0:T(128)} %bitcast.place.place_ref, f32[8,128]{1,0:T(8,128)} %broadcast_in_dim.3.refs_0_, f32[4,1024,128]{2,1,0:T(8,128)} %refs_6_.1, f32[4,1024,128]{2,1,0:T(8,128)} %refs_6_.1, f32[1024,2048]{1,0:T(8,128)} %refs_12_.1), custom_call_target="tpu_custom_call" | custom-call | flops 10000000000 | bytes 100 | tf_op jit(solution)/shard_map/project_0/pallas_call | solution.py:161
  10.0 3.0 %collective-permute-start.2 = (f32[8,256,128]{2,1,0:T(8,128)}, f32[8,256,128]{2,1,0:T(8,128)S(1)}, u32[]{:S(2)}, u32[]{:S(2)}) collective-permute-start(f32[8,256,128]{2,1,0:T(8,128)} %get-tuple-element.98), channel_id=1, source_target_pairs={{0,2},{1,5},{2,0},{3,7},{4,6},{5,1},{6,4},{7,3},{8,10},{9,13},{10,... | collective-permute-start | bytes 3145736 | tf_op jit(solution)/shard_map/ppermute | solution.py:352
  14.5 3.8 %gram_rows.1 = (f32[16,96,128]{2,1,0:T(8,128)S(1)}, f32[8,128]{1,0:T(8,128)S(1)}) custom-call(s32[1]{0:T(128)} %bitcast.place.place_ref, f32[8,128]{1,0:T(8,128)S(1)} %copy-done.14, f32[4,1024,128]{2,1,0:T(8,128)S(1)} %copy-done.2, f32[4,1024,128]{2,1,0:T(8,128)S(1)} %copy-done.2, f32[4,1024,128]{2,1,0:T(8,128)} %collective-permute-done.refs_3_.refs_2_.refs_9_.refs_11_.refs_7_), custom_call_target="tpu_custom_call" | custom-call | flops 10000000000 | bytes 100 | tf_op jit(solution)/shard_map/gram_rows/pallas_call | solution.py:199
  18.4 7.8 %project_1.1 = (f32[8,352,128]{2,1,0:T(8,128)S(1)}, f32[8,352,128]{2,1,0:T(8,128)S(1)}, f32[8,128]{1,0:T(8,128)S(1)}) custom-call(s32[1]{0:T(128)} %bitcast.place.place_ref, f32[8,128]{1,0:T(8,128)S(1)} %get-tuple-element.94.refs_0_, f32[4,256,256]{2,1,0:T(8,128)S(1)} %fusion.1.refs_1_.refs_2_, ...), custom_call_target="tpu_custom_call" | custom-call | flops 10000000000 | bytes 100 | tf_op jit(solution)/shard_map/project_1/pallas_call | solution.py:161
  26.3 2.0 collective-permute-start.3
  29.8 7.6 %project_2.1 = (f32[8,256,128]{2,1,0:T(8,128)S(1)}, f32[8,256,128]{2,1,0:T(8,128)S(1)}, f32[8,128]{1,0:T(8,128)S(1)}) custom-call(s32[1]{0:T(128)} %bitcast.place.place_ref, f32[8,128]{1,0:T(8,128)S(1)} %get-tuple-element.99.refs_0_, f32[4,1024,128]{2,1,0:T(8,128)S(1)} %copy-done.2, ...), custom_call_target="tpu_custom_call" | custom-call | flops 10000000000 | bytes 100 | tf_op jit(solution)/shard_map/project_2/pallas_call | solution.py:161
  38.0 2.0 collective-permute-done.3.refs_2_
  41.4 7.7 %project_3.1 = (f32[8,256,128]{2,1,0:T(8,128)S(1)}, f32[8,256,128]{2,1,0:T(8,128)S(1)}, f32[8,128]{1,0:T(8,128)S(1)}) custom-call(s32[1]{0:T(128)} %bitcast.place.place_ref, f32[8,128]{1,0:T(8,128)S(1)} %get-tuple-element.103.refs_0_, f32[4,1024,128]{2,1,0:T(8,128)S(1)} %copy-done.2, ...), custom_call_target="tpu_custom_call" | custom-call | flops 10000000000 | bytes 100 | tf_op jit(solution)/shard_map/project_3/pallas_call | solution.py:161
  50.8 1.6 collective-permute-start.7
  52.5 2.6 %collective-permute-start.9 = (f32[1,256,128]{2,1,0:T(8,128)S(1)}, f32[1,256,128]{2,1,0:T(8,128)S(1)}, u32[]{:S(2)}, u32[]{:S(2)}) collective-permute-start(f32[1,256,128]{2,1,0:T(8,128)S(1)} %get-tuple-element.121), channel_id=1, source_target_pairs={{0,16},{1,17},{2,18},{3,19},{4,20},{5,21},{6,22},{7,23},{8,24},{9,... | collective-permute-start | bytes 393224 | tf_op jit(solution)/shard_map/ppermute | solution.py:352
  55.1 6.2 %collective-permute-done.6.refs_2_ = f32[8,256,128]{2,1,0:T(8,128)S(1)} collective-permute-done((f32[8,256,128]{2,1,0:T(8,128)S(1)}, f32[8,256,128]{2,1,0:T(8,128)S(1)}, u32[]{:S(2)}, u32[]{:S(2)}) %collective-permute-start.6) | collective-permute-done | bytes 1048608 | tf_op jit(solution)/shard_map/ppermute | solution.py:352
  61.6 10.2 %collective-permute-done.7.refs_2_ = f32[4,352,128]{2,1,0:T(8,128)S(1)} collective-permute-done((f32[4,352,128]{2,1,0:T(8,128)S(1)}, f32[4,352,128]{2,1,0:T(8,128)S(1)}, u32[]{:S(2)}, u32[]{:S(2)}) %collective-permute-start.7) | collective-permute-done | bytes 720928 | tf_op jit(solution)/shard_map/ppermute | solution.py:352
  72.9 2.4 %collective-permute-done.8.refs_2_ = f32[8,256,128]{2,1,0:T(8,128)S(1)} collective-permute-done((f32[8,256,128]{2,1,0:T(8,128)S(1)}, f32[8,256,128]{2,1,0:T(8,128)S(1)}, u32[]{:S(2)}, u32[]{:S(2)}) %collective-permute-start.8) | collective-permute-done | bytes 1048608 | tf_op jit(solution)/shard_map/ppermute | solution.py:352
  75.5 3.1 %collective-permute-start.12 = (f32[1,256,128]{2,1,0:T(8,128)S(1)}, f32[1,256,128]{2,1,0:T(8,128)S(1)}, u32[]{:S(2)}, u32[]{:S(2)}) collective-permute-start(f32[1,256,128]{2,1,0:T(8,128)S(1)} %get-tuple-element.129.refs_1_), channel_id=1, source_target_pairs={{0,16},{1,17},{2,18},{3,19},{4,20},{5,21},{6,22},{7,23},{8,24},{9,... | collective-permute-start | bytes 393224 | tf_op jit(solution)/shard_map/ppermute | solution.py:352
  79.5 8.4 %collective-permute-done.11.refs_2_ = f32[4,256,128]{2,1,0:T(8,128)S(1)} collective-permute-done((f32[4,256,128]{2,1,0:T(8,128)S(1)}, f32[4,256,128]{2,1,0:T(8,128)S(1)}, u32[]{:S(2)}, u32[]{:S(2)}) %collective-permute-start.11) | collective-permute-done | bytes 524320 | tf_op jit(solution)/shard_map/ppermute | solution.py:352
  90.1 4.3 %collective-permute-done.13.refs_2_ = f32[2,256,128]{2,1,0:T(8,128)S(1)} collective-permute-done((f32[2,256,128]{2,1,0:T(8,128)S(1)}, f32[2,256,128]{2,1,0:T(8,128)S(1)}, u32[]{:S(2)}, u32[]{:S(2)}) %collective-permute-start.13) | collective-permute-done | bytes 262176 | tf_op jit(solution)/shard_map/ppermute | solution.py:352
  94.4 3.3 %collective-permute-done.14.refs_2_ = f32[1,352,128]{2,1,0:T(8,128)S(1)} collective-permute-done((f32[1,352,128]{2,1,0:T(8,128)S(1)}, f32[1,352,128]{2,1,0:T(8,128)S(1)}, u32[]{:S(2)}, u32[]{:S(2)}) %collective-permute-start.14) | collective-permute-done | bytes 180256 | tf_op jit(solution)/shard_map/ppermute | solution.py:352
  97.7 3.5 %collective-permute-start.17 = (f32[1,352,128]{2,1,0:T(8,128)S(1)}, f32[1,352,128]{2,1,0:T(8,128)S(1)}, u32[]{:S(2)}, u32[]{:S(2)}) collective-permute-start(f32[1,352,128]{2,1,0:T(8,128)S(1)} %get-tuple-element.142.refs_1_), channel_id=1, source_target_pairs={{0,16},{1,17},{2,18},{3,19},{4,20},{5,21},{6,22},{7,23},{8,24},{9,... | collective-permute-start | bytes 540680 | tf_op jit(solution)/shard_map/ppermute | solution.py:352
  102.4 2.9 %collective-permute-start.23 = (f32[4,256,128]{2,1,0:T(8,128)S(1)}, f32[4,256,128]{2,1,0:T(8,128)S(1)}, u32[]{:S(2)}, u32[]{:S(2)}) collective-permute-start(f32[4,256,128]{2,1,0:T(8,128)S(1)} %get-tuple-element.157.refs_1_), channel_id=1, source_target_pairs={{0,8},{1,9},{2,10},{3,11},{4,12},{5,13},{6,14},{7,15},{8,0},{9,1},... | collective-permute-start | bytes 1572872 | tf_op jit(solution)/shard_map/ppermute | solution.py:352
  105.4 5.2 %collective-permute-done.17.refs_2_ = f32[1,352,128]{2,1,0:T(8,128)S(1)} collective-permute-done((f32[1,352,128]{2,1,0:T(8,128)S(1)}, f32[1,352,128]{2,1,0:T(8,128)S(1)}, u32[]{:S(2)}, u32[]{:S(2)}) %collective-permute-start.17) | collective-permute-done | bytes 180256 | tf_op jit(solution)/shard_map/ppermute | solution.py:352
  111.5 2.3 %collective-permute-done.18.refs_2_ = f32[1,256,128]{2,1,0:T(8,128)S(1)} collective-permute-done((f32[1,256,128]{2,1,0:T(8,128)S(1)}, f32[1,256,128]{2,1,0:T(8,128)S(1)}, u32[]{:S(2)}, u32[]{:S(2)}) %collective-permute-start.18) | collective-permute-done | bytes 131104 | tf_op jit(solution)/shard_map/ppermute | solution.py:352
  113.9 3.0 %collective-permute-start.22 = (f32[1,256,128]{2,1,0:T(8,128)S(1)}, f32[1,256,128]{2,1,0:T(8,128)S(1)}, u32[]{:S(2)}, u32[]{:S(2)}) collective-permute-start(f32[1,256,128]{2,1,0:T(8,128)S(1)} %get-tuple-element.155), channel_id=1, source_target_pairs={{0,16},{1,17},{2,18},{3,19},{4,20},{5,21},{6,22},{7,23},{8,24},{9,... | collective-permute-start | bytes 393224 | tf_op jit(solution)/shard_map/ppermute | solution.py:352
  118.1 7.7 %collective-permute-done.21.refs_2_ = f32[1,256,128]{2,1,0:T(8,128)S(1)} collective-permute-done((f32[1,256,128]{2,1,0:T(8,128)S(1)}, f32[1,256,128]{2,1,0:T(8,128)S(1)}, u32[]{:S(2)}, u32[]{:S(2)}) %collective-permute-start.21) | collective-permute-done | bytes 131104 | tf_op jit(solution)/shard_map/ppermute | solution.py:352
  128.0 2.5 %collective-permute-start.26 = (f32[4,352,128]{2,1,0:T(8,128)S(1)}, f32[4,352,128]{2,1,0:T(8,128)S(1)}, u32[]{:S(2)}, u32[]{:S(2)}) collective-permute-start(f32[4,352,128]{2,1,0:T(8,128)S(1)} %get-tuple-element.163.refs_1_), channel_id=1, source_target_pairs={{0,8},{1,9},{2,10},{3,11},{4,12},{5,13},{6,14},{7,15},{8,0},{9,1},... | collective-permute-start | bytes 2162696 | tf_op jit(solution)/shard_map/ppermute | solution.py:352
  132.3 3.8 %collective-permute-done.25.refs_2_ = f32[1,256,128]{2,1,0:T(8,128)S(1)} collective-permute-done((f32[1,256,128]{2,1,0:T(8,128)S(1)}, f32[1,256,128]{2,1,0:T(8,128)S(1)}, u32[]{:S(2)}, u32[]{:S(2)}) %collective-permute-start.25) | collective-permute-done | bytes 131104 | tf_op jit(solution)/shard_map/ppermute | solution.py:352
  137.2 13.1 %collective-permute-done.26.refs_2_ = f32[4,352,128]{2,1,0:T(8,128)S(1)} collective-permute-done((f32[4,352,128]{2,1,0:T(8,128)S(1)}, f32[4,352,128]{2,1,0:T(8,128)S(1)}, u32[]{:S(2)}, u32[]{:S(2)}) %collective-permute-start.26) | collective-permute-done | bytes 720928 | tf_op jit(solution)/shard_map/ppermute | solution.py:352
  151.8 9.7 %collective-permute-done.29.refs_2_ = f32[4,256,128]{2,1,0:T(8,128)S(1)} collective-permute-done((f32[4,256,128]{2,1,0:T(8,128)S(1)}, f32[4,256,128]{2,1,0:T(8,128)S(1)}, u32[]{:S(2)}, u32[]{:S(2)}) %collective-permute-start.29) | collective-permute-done | bytes 524320 | tf_op jit(solution)/shard_map/ppermute | solution.py:352
  162.5 8.9 %collective-permute-done.30.refs_2_ = f32[4,256,128]{2,1,0:T(8,128)S(1)} collective-permute-done((f32[4,256,128]{2,1,0:T(8,128)S(1)}, f32[4,256,128]{2,1,0:T(8,128)S(1)}, u32[]{:S(2)}, u32[]{:S(2)}) %collective-permute-start.30) | collective-permute-done | bytes 524320 | tf_op jit(solution)/shard_map/ppermute | solution.py:352
  174.3 1.9 collective-permute-start.34
  177.4 21.3 %update_panels01.1 = (f32[1024,2048]{1,0:T(8,128)}, f32[512,2048]{1,0:T(8,128)}) custom-call(s32[1]{0:T(128)} %bitcast.place.place_ref, f32[8,128]{1,0:T(8,128)} %copy-done.13, f32[4,256,256]{2,1,0:T(8,128)} %copy-done, f32[8,256,128]{2,1,0:T(8,128)} %copy-done.6, f32[8,256,128]{2,1,0:T(8,128)} %copy-done.7, f32[8,352,128]{2,1,0:T(8,128)} %copy-done.4, ...), custom_call_target="tpu_custom_call" | custom-call | flops 10000000000 | bytes 100 | tf_op jit(solution)/shard_map/update_panels01/pallas_call | solution.py:324
  199.9 12.3 %update_panels2.1 = (f32[1024,2048]{1,0:T(8,128)}, f32[256,2048]{1,0:T(8,128)S(1)}) custom-call(s32[1]{0:T(128)} %bitcast.place.place_ref, f32[1024,2048]{1,0:T(8,128)} %get-tuple-element.175.refs_0_.refs_10_, f32[8,256,128]{2,1,0:T(8,128)S(1)} %collective-permute-done.33.refs_1_.refs_4_, f32[4,256,256]{2,1,0:T(8,128)S(1)} %copy-done.1, ...), custom_call_target="tpu_custom_call" | custom-call | flops 10000000000 | bytes 100 | tf_op jit(solution)/shard_map/update_panels2/pallas_call | solution.py:324
  212.1 9.6 %update_panels3.1 = f32[1024,2048]{1,0:T(8,128)} custom-call(s32[1]{0:T(128)} %bitcast.place.place_ref, f32[1024,2048]{1,0:T(8,128)} %get-tuple-element.178.refs_0_.refs_8_, f32[8,256,128]{2,1,0:T(8,128)S(1)} %collective-permute-done.34.refs_1_.refs_4_, f32[4,256,256]{2,1,0:T(8,128)S(1)} %copy-done.1, f32[8,256,128]{2,1,0:T(8,128)} %get-tuple-element.179.refs_3_, ...), custom_call_target="tpu_custom_call" | custom-call | flops 10000000000 | bytes 100 | tf_op jit(solution)/shard_map/update_panels3/pallas_call | solution.py:324
  (107 shorter events, 28.9 us)
Async XLA Ops:
  0.0 14.5 %collective-permute-start = (f32[4,1024,128]{2,1,0:T(8,128)}, f32[4,1024,128]{2,1,0:T(8,128)}, u32[]{:S(2)}, u32[]{:S(2)}) collective-permute-start(f32[4,1024,128]{2,1,0:T(8,128)} %refs_6_.1), channel_id=1, source_target_pairs={{1,0},{0,1},{3,2},{2,3},{5,4},{4,5},{7,6},{6,7},{9,8},{8,9},{11,10... | collective-permute-start | bytes 6291464 | tf_op jit(solution)/shard_map/ppermute | solution.py:357
  0.5 12.6 %collective-permute-start.1 = (f32[4,128,256]{2,1,0:T(8,128)}, f32[4,128,256]{2,1,0:T(8,128)}, u32[]{:S(2)}, u32[]{:S(2)}) collective-permute-start(f32[4,128,256]{2,1,0:T(8,128)} %param.5), channel_id=1, source_target_pairs={{1,0},{0,1},{3,2},{2,3},{5,4},{4,5},{7,6},{6,7},{9,8},{8,9},{11,10... | collective-permute-start | bytes 1572872 | tf_op jit(solution)/shard_map/ppermute | solution.py:357
  10.0 16.1 %collective-permute-start.2 = (f32[8,256,128]{2,1,0:T(8,128)}, f32[8,256,128]{2,1,0:T(8,128)S(1)}, u32[]{:S(2)}, u32[]{:S(2)}) collective-permute-start(f32[8,256,128]{2,1,0:T(8,128)} %get-tuple-element.98), channel_id=1, source_target_pairs={{0,2},{1,5},{2,0},{3,7},{4,6},{5,1},{6,4},{7,3},{8,10},{9,13},{10,... | collective-permute-start | bytes 3145736 | tf_op jit(solution)/shard_map/ppermute | solution.py:352
  26.3 13.7 %collective-permute-start.3 = (f32[4,256,128]{2,1,0:T(8,128)S(1)}, f32[4,256,128]{2,1,0:T(8,128)S(1)}, u32[]{:S(2)}, u32[]{:S(2)}) collective-permute-start(f32[4,256,128]{2,1,0:T(8,128)S(1)} %get-tuple-element.102), channel_id=1, source_target_pairs={{0,8},{1,9},{2,10},{3,11},{4,12},{5,13},{6,14},{7,15},{8,0},{9,1},... | collective-permute-start | bytes 1572872 | tf_op jit(solution)/shard_map/ppermute | solution.py:352
  28.3 22.3 %collective-permute-start.4 = (f32[8,352,128]{2,1,0:T(8,128)S(1)}, f32[8,352,128]{2,1,0:T(8,128)S(1)}, u32[]{:S(2)}, u32[]{:S(2)}) collective-permute-start(f32[8,352,128]{2,1,0:T(8,128)S(1)} %get-tuple-element.106), channel_id=1, source_target_pairs={{0,2},{1,5},{2,0},{3,7},{4,6},{5,1},{6,4},{7,3},{8,10},{9,13},{10,... | collective-permute-start | bytes 4325384 | tf_op jit(solution)/shard_map/ppermute | solution.py:352
  37.4 24.0 %collective-permute-start.6 = (f32[8,256,128]{2,1,0:T(8,128)S(1)}, f32[8,256,128]{2,1,0:T(8,128)S(1)}, u32[]{:S(2)}, u32[]{:S(2)}) collective-permute-start(f32[8,256,128]{2,1,0:T(8,128)S(1)} %get-tuple-element.112), channel_id=1, source_target_pairs={{0,2},{1,5},{2,0},{3,7},{4,6},{5,1},{6,4},{7,3},{8,10},{9,13},{10,... | collective-permute-start | bytes 3145736 | tf_op jit(solution)/shard_map/ppermute | solution.py:352
  40.0 12.5 %collective-permute-start.5 = (f32[2,256,128]{2,1,0:T(8,128)S(1)}, f32[2,256,128]{2,1,0:T(8,128)S(1)}, u32[]{:S(2)}, u32[]{:S(2)}) collective-permute-start(f32[2,256,128]{2,1,0:T(8,128)S(1)} %get-tuple-element.109), channel_id=1, source_target_pairs={{0,4},{1,3},{2,6},{3,1},{4,0},{5,7},{6,2},{7,5},{8,12},{9,11},{10,... | collective-permute-start | bytes 786440 | tf_op jit(solution)/shard_map/ppermute | solution.py:352
  49.1 26.2 %collective-permute-start.8 = (f32[8,256,128]{2,1,0:T(8,128)S(1)}, f32[8,256,128]{2,1,0:T(8,128)S(1)}, u32[]{:S(2)}, u32[]{:S(2)}) collective-permute-start(f32[8,256,128]{2,1,0:T(8,128)S(1)} %get-tuple-element.118), channel_id=1, source_target_pairs={{0,2},{1,5},{2,0},{3,7},{4,6},{5,1},{6,4},{7,3},{8,10},{9,13},{10,... | collective-permute-start | bytes 3145736 | tf_op jit(solution)/shard_map/ppermute | solution.py:352
  50.8 21.0 %collective-permute-start.7 = (f32[4,352,128]{2,1,0:T(8,128)S(1)}, f32[4,352,128]{2,1,0:T(8,128)S(1)}, u32[]{:S(2)}, u32[]{:S(2)}) collective-permute-start(f32[4,352,128]{2,1,0:T(8,128)S(1)} %get-tuple-element.115), channel_id=1, source_target_pairs={{0,8},{1,9},{2,10},{3,11},{4,12},{5,13},{6,14},{7,15},{8,0},{9,1},... | collective-permute-start | bytes 2162696 | tf_op jit(solution)/shard_map/ppermute | solution.py:352
  52.5 22.9 %collective-permute-start.9 = (f32[1,256,128]{2,1,0:T(8,128)S(1)}, f32[1,256,128]{2,1,0:T(8,128)S(1)}, u32[]{:S(2)}, u32[]{:S(2)}) collective-permute-start(f32[1,256,128]{2,1,0:T(8,128)S(1)} %get-tuple-element.121), channel_id=1, source_target_pairs={{0,16},{1,17},{2,18},{3,19},{4,20},{5,21},{6,22},{7,23},{8,24},{9,... | collective-permute-start | bytes 393224 | tf_op jit(solution)/shard_map/ppermute | solution.py:352
  61.5 26.3 %collective-permute-start.11 = (f32[4,256,128]{2,1,0:T(8,128)S(1)}, f32[4,256,128]{2,1,0:T(8,128)S(1)}, u32[]{:S(2)}, u32[]{:S(2)}) collective-permute-start(f32[4,256,128]{2,1,0:T(8,128)S(1)} %get-tuple-element.127), channel_id=1, source_target_pairs={{0,8},{1,9},{2,10},{3,11},{4,12},{5,13},{6,14},{7,15},{8,0},{9,1},... | collective-permute-start | bytes 1572872 | tf_op jit(solution)/shard_map/ppermute | solution.py:352
  71.9 7.5 %collective-permute-start.10 = (f32[2,352,128]{2,1,0:T(8,128)S(1)}, f32[2,352,128]{2,1,0:T(8,128)S(1)}, u32[]{:S(2)}, u32[]{:S(2)}) collective-permute-start(f32[2,352,128]{2,1,0:T(8,128)S(1)} %get-tuple-element.124), channel_id=1, source_target_pairs={{0,4},{1,3},{2,6},{3,1},{4,0},{5,7},{6,2},{7,5},{8,12},{9,11},{10,... | collective-permute-start | bytes 1081352 | tf_op jit(solution)/shard_map/ppermute | solution.py:352
  75.5 13.4 %collective-permute-start.12 = (f32[1,256,128]{2,1,0:T(8,128)S(1)}, f32[1,256,128]{2,1,0:T(8,128)S(1)}, u32[]{:S(2)}, u32[]{:S(2)}) collective-permute-start(f32[1,256,128]{2,1,0:T(8,128)S(1)} %get-tuple-element.129.refs_1_), channel_id=1, source_target_pairs={{0,16},{1,17},{2,18},{3,19},{4,20},{5,21},{6,22},{7,23},{8,24},{9,... | collective-permute-start | bytes 393224 | tf_op jit(solution)/shard_map/ppermute | solution.py:352
  78.6 22.8 %collective-permute-start.16 = (f32[4,256,128]{2,1,0:T(8,128)S(1)}, f32[4,256,128]{2,1,0:T(8,128)S(1)}, u32[]{:S(2)}, u32[]{:S(2)}) collective-permute-start(f32[4,256,128]{2,1,0:T(8,128)S(1)} %get-tuple-element.140), channel_id=1, source_target_pairs={{0,8},{1,9},{2,10},{3,11},{4,12},{5,13},{6,14},{7,15},{8,0},{9,1},... | collective-permute-start | bytes 1572872 | tf_op jit(solution)/shard_map/ppermute | solution.py:352
  88.9 8.7 %collective-permute-start.14 = (f32[1,352,128]{2,1,0:T(8,128)S(1)}, f32[1,352,128]{2,1,0:T(8,128)S(1)}, u32[]{:S(2)}, u32[]{:S(2)}) collective-permute-start(f32[1,352,128]{2,1,0:T(8,128)S(1)} %get-tuple-element.135), channel_id=1, source_target_pairs={{0,16},{1,17},{2,18},{3,19},{4,20},{5,21},{6,22},{7,23},{8,24},{9,... | collective-permute-start | bytes 540680 | tf_op jit(solution)/shard_map/ppermute | solution.py:352
  88.9 12.4 %collective-permute-start.15 = (f32[2,256,128]{2,1,0:T(8,128)S(1)}, f32[2,256,128]{2,1,0:T(8,128)S(1)}, u32[]{:S(2)}, u32[]{:S(2)}) collective-permute-start(f32[2,256,128]{2,1,0:T(8,128)S(1)} %get-tuple-element.137.refs_1_), channel_id=1, source_target_pairs={{0,4},{1,3},{2,6},{3,1},{4,0},{5,7},{6,2},{7,5},{8,12},{9,11},{10,... | collective-permute-start | bytes 786440 | tf_op jit(solution)/shard_map/ppermute | solution.py:352
  97.7 12.9 %collective-permute-start.17 = (f32[1,352,128]{2,1,0:T(8,128)S(1)}, f32[1,352,128]{2,1,0:T(8,128)S(1)}, u32[]{:S(2)}, u32[]{:S(2)}) collective-permute-start(f32[1,352,128]{2,1,0:T(8,128)S(1)} %get-tuple-element.142.refs_1_), channel_id=1, source_target_pairs={{0,16},{1,17},{2,18},{3,19},{4,20},{5,21},{6,22},{7,23},{8,24},{9,... | collective-permute-start | bytes 540680 | tf_op jit(solution)/shard_map/ppermute | solution.py:352
  101.2 12.6 %collective-permute-start.18 = (f32[1,256,128]{2,1,0:T(8,128)S(1)}, f32[1,256,128]{2,1,0:T(8,128)S(1)}, u32[]{:S(2)}, u32[]{:S(2)}) collective-permute-start(f32[1,256,128]{2,1,0:T(8,128)S(1)} %get-tuple-element.145), channel_id=1, source_target_pairs={{0,16},{1,17},{2,18},{3,19},{4,20},{5,21},{6,22},{7,23},{8,24},{9,... | collective-permute-start | bytes 393224 | tf_op jit(solution)/shard_map/ppermute | solution.py:352
  101.4 12.5 %collective-permute-start.19 = (f32[2,256,128]{2,1,0:T(8,128)S(1)}, f32[2,256,128]{2,1,0:T(8,128)S(1)}, u32[]{:S(2)}, u32[]{:S(2)}) collective-permute-start(f32[2,256,128]{2,1,0:T(8,128)S(1)} %get-tuple-element.148), channel_id=1, source_target_pairs={{0,4},{1,3},{2,6},{3,1},{4,0},{5,7},{6,2},{7,5},{8,12},{9,11},{10,... | collective-permute-start | bytes 786440 | tf_op jit(solution)/shard_map/ppermute | solution.py:352
  102.4 28.1 %collective-permute-start.23 = (f32[4,256,128]{2,1,0:T(8,128)S(1)}, f32[4,256,128]{2,1,0:T(8,128)S(1)}, u32[]{:S(2)}, u32[]{:S(2)}) collective-permute-start(f32[4,256,128]{2,1,0:T(8,128)S(1)} %get-tuple-element.157.refs_1_), channel_id=1, source_target_pairs={{0,8},{1,9},{2,10},{3,11},{4,12},{5,13},{6,14},{7,15},{8,0},{9,1},... | collective-permute-start | bytes 1572872 | tf_op jit(solution)/shard_map/ppermute | solution.py:352
  110.5 7.5 %collective-permute-start.20 = (f32[2,352,128]{2,1,0:T(8,128)S(1)}, f32[2,352,128]{2,1,0:T(8,128)S(1)}, u32[]{:S(2)}, u32[]{:S(2)}) collective-permute-start(f32[2,352,128]{2,1,0:T(8,128)S(1)} %get-tuple-element.150.refs_1_), channel_id=1, source_target_pairs={{0,4},{1,3},{2,6},{3,1},{4,0},{5,7},{6,2},{7,5},{8,12},{9,11},{10,... | collective-permute-start | bytes 1081352 | tf_op jit(solution)/shard_map/ppermute | solution.py:352
  113.8 12.0 %collective-permute-start.21 = (f32[1,256,128]{2,1,0:T(8,128)S(1)}, f32[1,256,128]{2,1,0:T(8,128)S(1)}, u32[]{:S(2)}, u32[]{:S(2)}) collective-permute-start(f32[1,256,128]{2,1,0:T(8,128)S(1)} %get-tuple-element.152.refs_1_), channel_id=1, source_target_pairs={{0,16},{1,17},{2,18},{3,19},{4,20},{5,21},{6,22},{7,23},{8,24},{9,... | collective-permute-start | bytes 393224 | tf_op jit(solution)/shard_map/ppermute | solution.py:352
  113.9 14.0 %collective-permute-start.22 = (f32[1,256,128]{2,1,0:T(8,128)S(1)}, f32[1,256,128]{2,1,0:T(8,128)S(1)}, u32[]{:S(2)}, u32[]{:S(2)}) collective-permute-start(f32[1,256,128]{2,1,0:T(8,128)S(1)} %get-tuple-element.155), channel_id=1, source_target_pairs={{0,16},{1,17},{2,18},{3,19},{4,20},{5,21},{6,22},{7,23},{8,24},{9,... | collective-permute-start | bytes 393224 | tf_op jit(solution)/shard_map/ppermute | solution.py:352
  128.0 8.2 %collective-permute-start.25 = (f32[1,256,128]{2,1,0:T(8,128)S(1)}, f32[1,256,128]{2,1,0:T(8,128)S(1)}, u32[]{:S(2)}, u32[]{:S(2)}) collective-permute-start(f32[1,256,128]{2,1,0:T(8,128)S(1)} %get-tuple-element.161.refs_1_), channel_id=1, source_target_pairs={{0,16},{1,17},{2,18},{3,19},{4,20},{5,21},{6,22},{7,23},{8,24},{9,... | collective-permute-start | bytes 393224 | tf_op jit(solution)/shard_map/ppermute | solution.py:352
  128.0 22.2 %collective-permute-start.26 = (f32[4,352,128]{2,1,0:T(8,128)S(1)}, f32[4,352,128]{2,1,0:T(8,128)S(1)}, u32[]{:S(2)}, u32[]{:S(2)}) collective-permute-start(f32[4,352,128]{2,1,0:T(8,128)S(1)} %get-tuple-element.163.refs_1_), channel_id=1, source_target_pairs={{0,8},{1,9},{2,10},{3,11},{4,12},{5,13},{6,14},{7,15},{8,0},{9,1},... | collective-permute-start | bytes 2162696 | tf_op jit(solution)/shard_map/ppermute | solution.py:352
  130.6 20.2 %collective-permute-start.27 = (f32[8,256,128]{2,1,0:T(8,128)S(1)}, f32[8,256,128]{2,1,0:T(8,128)S(1)}, u32[]{:S(2)}, u32[]{:S(2)}) collective-permute-start(f32[8,256,128]{2,1,0:T(8,128)S(1)} %get-tuple-element.165.refs_2_), channel_id=1, source_target_pairs={{0,2},{1,5},{2,0},{3,7},{4,6},{5,1},{6,4},{7,3},{8,10},{9,13},{10,... | collective-permute-start | bytes 3145736 | tf_op jit(solution)/shard_map/ppermute | solution.py:352
  136.1 14.7 %collective-permute-start.28 = (f32[2,256,128]{2,1,0:T(8,128)S(1)}, f32[2,256,128]{2,1,0:T(8,128)S(1)}, u32[]{:S(2)}, u32[]{:S(2)}) collective-permute-start(f32[2,256,128]{2,1,0:T(8,128)S(1)} %get-tuple-element.166.refs_2_), channel_id=1, source_target_pairs={{0,4},{1,3},{2,6},{3,1},{4,0},{5,7},{6,2},{7,5},{8,12},{9,11},{10,... | collective-permute-start | bytes 786440 | tf_op jit(solution)/shard_map/ppermute | solution.py:352
  137.2 24.3 %collective-permute-start.29 = (f32[4,256,128]{2,1,0:T(8,128)S(1)}, f32[4,256,128]{2,1,0:T(8,128)S(1)}, u32[]{:S(2)}, u32[]{:S(2)}) collective-permute-start(f32[4,256,128]{2,1,0:T(8,128)S(1)} %get-tuple-element.168.refs_1_), channel_id=1, source_target_pairs={{0,8},{1,9},{2,10},{3,11},{4,12},{5,13},{6,14},{7,15},{8,0},{9,1},... | collective-permute-start | bytes 1572872 | tf_op jit(solution)/shard_map/ppermute | solution.py:352
  150.4 22.1 %collective-permute-start.31 = (f32[8,352,128]{2,1,0:T(8,128)S(1)}, f32[8,352,128]{2,1,0:T(8,128)S(1)}, u32[]{:S(2)}, u32[]{:S(2)}) collective-permute-start(f32[8,352,128]{2,1,0:T(8,128)S(1)} %get-tuple-element.172.refs_2_.refs_4_), channel_id=1, source_target_pairs={{0,2},{1,5},{2,0},{3,7},{4,6},{5,1},{6,4},{7,3},{8,10},{9,13},{10,... | collective-permute-start | bytes 4325384 | tf_op jit(solution)/shard_map/ppermute | solution.py:352
  151.8 19.6 %collective-permute-start.30 = (f32[4,256,128]{2,1,0:T(8,128)S(1)}, f32[4,256,128]{2,1,0:T(8,128)S(1)}, u32[]{:S(2)}, u32[]{:S(2)}) collective-permute-start(f32[4,256,128]{2,1,0:T(8,128)S(1)} %get-tuple-element.170.refs_1_), channel_id=1, source_target_pairs={{0,8},{1,9},{2,10},{3,11},{4,12},{5,13},{6,14},{7,15},{8,0},{9,1},... | collective-permute-start | bytes 1572872 | tf_op jit(solution)/shard_map/ppermute | solution.py:352
  174.2 24.5 %collective-permute-start.33 = (f32[8,256,128]{2,1,0:T(8,128)}, f32[8,256,128]{2,1,0:T(8,128)S(1)}, u32[]{:S(2)}, u32[]{:S(2)}) collective-permute-start(f32[8,256,128]{2,1,0:T(8,128)} %get-tuple-element.176.refs_3_), channel_id=1, source_target_pairs={{0,2},{1,5},{2,0},{3,7},{4,6},{5,1},{6,4},{7,3},{8,10},{9,13},{10,... | collective-permute-start | bytes 3145736 | tf_op jit(solution)/shard_map/ppermute | solution.py:352
  174.3 37.8 %collective-permute-start.34 = (f32[8,256,128]{2,1,0:T(8,128)}, f32[8,256,128]{2,1,0:T(8,128)S(1)}, u32[]{:S(2)}, u32[]{:S(2)}) collective-permute-start(f32[8,256,128]{2,1,0:T(8,128)} %get-tuple-element.179.refs_3_), channel_id=1, source_target_pairs={{0,2},{1,5},{2,0},{3,7},{4,6},{5,1},{6,4},{7,3},{8,10},{9,13},{10,... | collective-permute-start | bytes 3145736 | tf_op jit(solution)/shard_map/ppermute | solution.py:352
  (18 other events, 130.5 us)

commit v9 on v7

--- a/solution.py
+++ b/solution.py
@@ -23,9 +23,8 @@
 CALLS = ((0,), (1,), (2,), (3,))
 UPDATES = ((0, 1), (2,), (3,))
 ORDER = (
-    ["p0", "g", "p1", "k1.0", "p2", "k2.0", "k1.1", "p3", "k1.2", "k2.1", "k3.0", "k3.1", "k2.2", "k1.3", "k4.0"]
-    + ["k3.2", "k4.1", "k5.0", "k2.3", "k6.0", "k4.2", "k5.1", "k3.3", "k6.1", "k5.2", "k4.3", "k7.0", "k6.2", "k5.3"]
-    + ["k7.1", "f.0", "k6.3", "k7.2", "k7.3", "f.1", "x", "u0", "f.2", "u1", "f.3", "u2"]
+    ["p0", "g", "p1", "k1.0", "p2", "k2.0", "p3", "k1.1", "k3.0", "k1.2", "k2.1", "k1.3", "k4.0", "k3.1", "k2.2", "k5.0", "k3.2", "k4.1", "k6.0", "k2.3", "k5.1", "k4.2", "k3.3", "k6.1", "k5.2"]
+    + ["k4.3", "k7.0", "k7.1", "k6.2", "k5.3", "f.0", "k6.3", "k7.2", "k7.3", "f.1", "x", "u0", "f.2", "u1", "f.3", "u2"]
 )
 
 
@@ -81,7 +80,7 @@
 ANY = pl.BlockSpec(memory_space=pl.ANY)
 SMEM = pl.BlockSpec(memory_space=pltpu.SMEM)
 
-COST = pl.CostEstimate(flops=10**10, bytes_accessed=100, transcendentals=0)
+COST = pl.CostEstimate(flops=3*10**9, bytes_accessed=100, transcendentals=0)
 
 
 def params(limit=VMEM_LIMIT):

time: 217 us -> 211 us (0.972)
  starting transfers between devices: 43.7 us -> 39 us
  Pallas kernels: 78.1 us -> 75.7 us
    ppermute x32, starting transfers between devices: 43.1 us -> 38.5 us  [swap(): return lax.ppermute(value, ('row', 'col'), pairs)]
  transfers between devices with their start and end apart: 35 -> 35, of which waited for: 20 -> 18; matrix products, arithmetic and copies ran while one was open for 1% -> 1% of each run, Pallas kernels for 32% -> 32%
where the time goes in v9:
time: 211 us
  waiting for transfers between devices  93.2 us (44%)
  Pallas kernels  75.7 us (36%)
  starting transfers between devices  39 us (18%)
    ppermute x32, waiting for transfers between devices, swap(): return lax.ppermute(value, ('row', 'col'), pairs)  93 us
    pallas_call x3, Pallas kernels, update(): pl.pallas_call(functools.partial(update_kernel, panels, len(grams), len(c...  40.4 us
    ppermute x32, starting transfers between devices, swap(): return lax.ppermute(value, ('row', 'col'), pairs)  38.5 us
    pallas_call x4, Pallas kernels, project(): pl.pallas_call(functools.partial(project_kernel, steps, call, blocks, len...  31.6 us
  transfers between devices with their start and end apart: 35, of which 18 were waited for; matrix products, arithmetic and copies ran while one was open for 1% of the time, Pallas kernels for 32%

profile of v9, /device:TPU:0, one launch (start us, length us, event | category | flops | bytes accessed | tf_op | source)
XLA Modules:
  0.0 210.7 jit_solution(15080718724339705169)
XLA Ops:
  1.1 8.9 %project_0.1 = (f32[8,256,128]{2,1,0:T(8,128)}, f32[8,256,128]{2,1,0:T(8,128)}, f32[8,128]{1,0:T(8,128)}) custom-call(s32[1]{0:T(128)} %bitcast.place.place_ref, f32[8,128]{1,0:T(8,128)} %broadcast_in_dim.3.refs_0_, f32[4,1024,128]{2,1,0:T(8,128)} %refs_6_.1, f32[4,1024,128]{2,1,0:T(8,128)} %refs_6_.1, f32[1024,2048]{1,0:T(8,128)} %refs_12_.1), custom_call_target="tpu_custom_call" | custom-call | flops 3000000000 | bytes 100 | tf_op jit(solution)/shard_map/project_0/pallas_call | solution.py:160
  10.0 3.0 %collective-permute-start.2 = (f32[8,256,128]{2,1,0:T(8,128)}, f32[8,256,128]{2,1,0:T(8,128)S(1)}, u32[]{:S(2)}, u32[]{:S(2)}) collective-permute-start(f32[8,256,128]{2,1,0:T(8,128)} %get-tuple-element.98), channel_id=1, source_target_pairs={{0,2},{1,5},{2,0},{3,7},{4,6},{5,1},{6,4},{7,3},{8,10},{9,13},{10,... | collective-permute-start | bytes 3145736 | tf_op jit(solution)/shard_map/ppermute | solution.py:351
  14.9 2.0 gram_rows.1
  16.9 7.6 %project_1.1 = (f32[8,352,128]{2,1,0:T(8,128)S(1)}, f32[8,352,128]{2,1,0:T(8,128)S(1)}, f32[8,128]{1,0:T(8,128)S(1)}) custom-call(s32[1]{0:T(128)} %bitcast.place.place_ref, f32[8,128]{1,0:T(8,128)S(1)} %get-tuple-element.94.refs_0_, f32[4,256,256]{2,1,0:T(8,128)S(1)} %fusion.1.refs_1_.refs_2_, ...), custom_call_target="tpu_custom_call" | custom-call | flops 3000000000 | bytes 100 | tf_op jit(solution)/shard_map/project_1/pallas_call | solution.py:160
  26.1 2.2 %collective-permute-start.3 = (f32[4,256,128]{2,1,0:T(8,128)S(1)}, f32[4,256,128]{2,1,0:T(8,128)S(1)}, u32[]{:S(2)}, u32[]{:S(2)}) collective-permute-start(f32[4,256,128]{2,1,0:T(8,128)S(1)} %get-tuple-element.102), channel_id=1, source_target_pairs={{0,8},{1,9},{2,10},{3,11},{4,12},{5,13},{6,14},{7,15},{8,0},{9,1},... | collective-permute-start | bytes 1572872 | tf_op jit(solution)/shard_map/ppermute | solution.py:351
  28.2 7.5 %project_2.1 = (f32[8,256,128]{2,1,0:T(8,128)S(1)}, f32[8,256,128]{2,1,0:T(8,128)S(1)}, f32[8,128]{1,0:T(8,128)S(1)}) custom-call(s32[1]{0:T(128)} %bitcast.place.place_ref, f32[8,128]{1,0:T(8,128)S(1)} %get-tuple-element.99.refs_0_, f32[4,1024,128]{2,1,0:T(8,128)S(1)} %copy-done, ...), custom_call_target="tpu_custom_call" | custom-call | flops 3000000000 | bytes 100 | tf_op jit(solution)/shard_map/project_2/pallas_call | solution.py:160
  37.3 2.2 %collective-permute-done.3.refs_2_ = f32[4,256,128]{2,1,0:T(8,128)S(1)} collective-permute-done((f32[4,256,128]{2,1,0:T(8,128)S(1)}, f32[4,256,128]{2,1,0:T(8,128)S(1)}, u32[]{:S(2)}, u32[]{:S(2)}) %collective-permute-start.3) | collective-permute-done | bytes 524320 | tf_op jit(solution)/shard_map/ppermute | solution.py:351
  39.5 1.8 collective-permute-start.5
  41.3 7.6 %project_3.1 = (f32[8,256,128]{2,1,0:T(8,128)S(1)}, f32[8,256,128]{2,1,0:T(8,128)S(1)}, f32[8,128]{1,0:T(8,128)S(1)}) custom-call(s32[1]{0:T(128)} %bitcast.place.place_ref, f32[8,128]{1,0:T(8,128)S(1)} %get-tuple-element.103.refs_0_, f32[4,1024,128]{2,1,0:T(8,128)S(1)} %copy-done, ...), custom_call_target="tpu_custom_call" | custom-call | flops 3000000000 | bytes 100 | tf_op jit(solution)/shard_map/project_3/pallas_call | solution.py:160
  52.3 2.7 %collective-permute-start.9 = (f32[1,256,128]{2,1,0:T(8,128)S(1)}, f32[1,256,128]{2,1,0:T(8,128)S(1)}, u32[]{:S(2)}, u32[]{:S(2)}) collective-permute-start(f32[1,256,128]{2,1,0:T(8,128)S(1)} %get-tuple-element.121), channel_id=1, source_target_pairs={{0,16},{1,17},{2,18},{3,19},{4,20},{5,21},{6,22},{7,23},{8,24},{9,... | collective-permute-start | bytes 393224 | tf_op jit(solution)/shard_map/ppermute | solution.py:351
  55.0 2.7 %collective-permute-done.6.refs_2_ = f32[8,256,128]{2,1,0:T(8,128)S(1)} collective-permute-done((f32[8,256,128]{2,1,0:T(8,128)S(1)}, f32[8,256,128]{2,1,0:T(8,128)S(1)}, u32[]{:S(2)}, u32[]{:S(2)}) %collective-permute-start.6) | collective-permute-done | bytes 1048608 | tf_op jit(solution)/shard_map/ppermute | solution.py:351
  59.4 12.8 %collective-permute-done.7.refs_2_ = f32[4,352,128]{2,1,0:T(8,128)S(1)} collective-permute-done((f32[4,352,128]{2,1,0:T(8,128)S(1)}, f32[4,352,128]{2,1,0:T(8,128)S(1)}, u32[]{:S(2)}, u32[]{:S(2)}) %collective-permute-start.7) | collective-permute-done | bytes 720928 | tf_op jit(solution)/shard_map/ppermute | solution.py:351
  73.1 2.0 collective-permute-start.12
  76.3 3.4 %collective-permute-done.10.refs_2_ = f32[2,352,128]{2,1,0:T(8,128)S(1)} collective-permute-done((f32[2,352,128]{2,1,0:T(8,128)S(1)}, f32[2,352,128]{2,1,0:T(8,128)S(1)}, u32[]{:S(2)}, u32[]{:S(2)}) %collective-permute-start.10) | collective-permute-done | bytes 360480 | tf_op jit(solution)/shard_map/ppermute | solution.py:351
  79.8 7.8 %collective-permute-done.11.refs_2_ = f32[4,256,128]{2,1,0:T(8,128)S(1)} collective-permute-done((f32[4,256,128]{2,1,0:T(8,128)S(1)}, f32[4,256,128]{2,1,0:T(8,128)S(1)}, u32[]{:S(2)}, u32[]{:S(2)}) %collective-permute-start.11) | collective-permute-done | bytes 524320 | tf_op jit(solution)/shard_map/ppermute | solution.py:351
  88.0 1.8 collective-permute-start.15
  89.8 4.3 %collective-permute-done.13.refs_2_ = f32[2,256,128]{2,1,0:T(8,128)S(1)} collective-permute-done((f32[2,256,128]{2,1,0:T(8,128)S(1)}, f32[2,256,128]{2,1,0:T(8,128)S(1)}, u32[]{:S(2)}, u32[]{:S(2)}) %collective-permute-start.13) | collective-permute-done | bytes 262176 | tf_op jit(solution)/shard_map/ppermute | solution.py:351
  94.1 3.3 %collective-permute-done.14.refs_2_ = f32[1,352,128]{2,1,0:T(8,128)S(1)} collective-permute-done((f32[1,352,128]{2,1,0:T(8,128)S(1)}, f32[1,352,128]{2,1,0:T(8,128)S(1)}, u32[]{:S(2)}, u32[]{:S(2)}) %collective-permute-start.14) | collective-permute-done | bytes 180256 | tf_op jit(solution)/shard_map/ppermute | solution.py:351
  97.5 3.5 %collective-permute-start.17 = (f32[1,352,128]{2,1,0:T(8,128)S(1)}, f32[1,352,128]{2,1,0:T(8,128)S(1)}, u32[]{:S(2)}, u32[]{:S(2)}) collective-permute-start(f32[1,352,128]{2,1,0:T(8,128)S(1)} %get-tuple-element.142.refs_1_), channel_id=1, source_target_pairs={{0,16},{1,17},{2,18},{3,19},{4,20},{5,21},{6,22},{7,23},{8,24},{9,... | collective-permute-start | bytes 540680 | tf_op jit(solution)/shard_map/ppermute | solution.py:351
  101.8 3.0 %collective-permute-start.23 = (f32[4,256,128]{2,1,0:T(8,128)S(1)}, f32[4,256,128]{2,1,0:T(8,128)S(1)}, u32[]{:S(2)}, u32[]{:S(2)}) collective-permute-start(f32[4,256,128]{2,1,0:T(8,128)S(1)} %get-tuple-element.157.refs_1_), channel_id=1, source_target_pairs={{0,8},{1,9},{2,10},{3,11},{4,12},{5,13},{6,14},{7,15},{8,0},{9,1},... | collective-permute-start | bytes 1572872 | tf_op jit(solution)/shard_map/ppermute | solution.py:351
  104.8 5.7 %collective-permute-done.17.refs_2_ = f32[1,352,128]{2,1,0:T(8,128)S(1)} collective-permute-done((f32[1,352,128]{2,1,0:T(8,128)S(1)}, f32[1,352,128]{2,1,0:T(8,128)S(1)}, u32[]{:S(2)}, u32[]{:S(2)}) %collective-permute-start.17) | collective-permute-done | bytes 180256 | tf_op jit(solution)/shard_map/ppermute | solution.py:351
  111.0 2.6 %collective-permute-done.18.refs_2_ = f32[1,256,128]{2,1,0:T(8,128)S(1)} collective-permute-done((f32[1,256,128]{2,1,0:T(8,128)S(1)}, f32[1,256,128]{2,1,0:T(8,128)S(1)}, u32[]{:S(2)}, u32[]{:S(2)}) %collective-permute-start.18) | collective-permute-done | bytes 131104 | tf_op jit(solution)/shard_map/ppermute | solution.py:351
  113.7 3.0 %collective-permute-start.22 = (f32[1,256,128]{2,1,0:T(8,128)S(1)}, f32[1,256,128]{2,1,0:T(8,128)S(1)}, u32[]{:S(2)}, u32[]{:S(2)}) collective-permute-start(f32[1,256,128]{2,1,0:T(8,128)S(1)} %get-tuple-element.155), channel_id=1, source_target_pairs={{0,16},{1,17},{2,18},{3,19},{4,20},{5,21},{6,22},{7,23},{8,24},{9,... | collective-permute-start | bytes 393224 | tf_op jit(solution)/shard_map/ppermute | solution.py:351
  118.2 6.8 %collective-permute-done.21.refs_2_ = f32[1,256,128]{2,1,0:T(8,128)S(1)} collective-permute-done((f32[1,256,128]{2,1,0:T(8,128)S(1)}, f32[1,256,128]{2,1,0:T(8,128)S(1)}, u32[]{:S(2)}, u32[]{:S(2)}) %collective-permute-start.21) | collective-permute-done | bytes 131104 | tf_op jit(solution)/shard_map/ppermute | solution.py:351
  125.6 2.2 %collective-permute-done.22.refs_2_ = f32[1,256,128]{2,1,0:T(8,128)S(1)} collective-permute-done((f32[1,256,128]{2,1,0:T(8,128)S(1)}, f32[1,256,128]{2,1,0:T(8,128)S(1)}, u32[]{:S(2)}, u32[]{:S(2)}) %collective-permute-start.22) | collective-permute-done | bytes 131104 | tf_op jit(solution)/shard_map/ppermute | solution.py:351
  128.7 13.9 %collective-permute-done.24.refs_2_ = f32[4,352,128]{2,1,0:T(8,128)S(1)} collective-permute-done((f32[4,352,128]{2,1,0:T(8,128)S(1)}, f32[4,352,128]{2,1,0:T(8,128)S(1)}, u32[]{:S(2)}, u32[]{:S(2)}) %collective-permute-start.24) | collective-permute-done | bytes 720928 | tf_op jit(solution)/shard_map/ppermute | solution.py:351
  145.0 8.8 %collective-permute-done.28.refs_3_ = f32[2,256,128]{2,1,0:T(8,128)S(1)} collective-permute-done((f32[2,256,128]{2,1,0:T(8,128)S(1)}, f32[2,256,128]{2,1,0:T(8,128)S(1)}, u32[]{:S(2)}, u32[]{:S(2)}) %collective-permute-start.28) | collective-permute-done | bytes 262176 | tf_op jit(solution)/shard_map/ppermute | solution.py:351
  153.9 6.0 %collective-permute-done.29.refs_2_ = f32[4,256,128]{2,1,0:T(8,128)S(1)} collective-permute-done((f32[4,256,128]{2,1,0:T(8,128)S(1)}, f32[4,256,128]{2,1,0:T(8,128)S(1)}, u32[]{:S(2)}, u32[]{:S(2)}) %collective-permute-start.29) | collective-permute-done | bytes 524320 | tf_op jit(solution)/shard_map/ppermute | solution.py:351
  159.9 7.8 %collective-permute-done.30.refs_2_ = f32[4,256,128]{2,1,0:T(8,128)S(1)} collective-permute-done((f32[4,256,128]{2,1,0:T(8,128)S(1)}, f32[4,256,128]{2,1,0:T(8,128)S(1)}, u32[]{:S(2)}, u32[]{:S(2)}) %collective-permute-start.30) | collective-permute-done | bytes 524320 | tf_op jit(solution)/shard_map/ppermute | solution.py:351
  170.2 19.1 %update_panels01.1 = (f32[1024,2048]{1,0:T(8,128)}, f32[512,2048]{1,0:T(8,128)}) custom-call(s32[1]{0:T(128)} %bitcast.place.place_ref, f32[8,128]{1,0:T(8,128)S(1)} %get-tuple-element.173.refs_0_, f32[4,256,256]{2,1,0:T(8,128)S(1)} %fusion.1.refs_1_.refs_2_, f32[8,256,128]{2,1,0:T(8,128)S(1)} %get-tuple-element.165.refs_2_, ...), custom_call_target="tpu_custom_call" | custom-call | flops 3000000000 | bytes 100 | tf_op jit(solution)/shard_map/update_panels01/pallas_call | solution.py:323
  189.3 12.1 %update_panels2.1 = (f32[1024,2048]{1,0:T(8,128)}, f32[256,2048]{1,0:T(8,128)S(1)}) custom-call(s32[1]{0:T(128)} %bitcast.place.place_ref, f32[1024,2048]{1,0:T(8,128)} %get-tuple-element.175.refs_0_.refs_10_, f32[8,256,128]{2,1,0:T(8,128)S(1)} %collective-permute-done.33.refs_1_.refs_4_, f32[4,256,256]{2,1,0:T(8,128)S(1)} %fusion.1.refs_1_.refs_2_, ...), custom_call_target="tpu_custom_call" | custom-call | flops 3000000000 | bytes 100 | tf_op jit(solution)/shard_map/update_panels2/pallas_call | solution.py:323
  201.4 9.2 %update_panels3.1 = f32[1024,2048]{1,0:T(8,128)} custom-call(s32[1]{0:T(128)} %bitcast.place.place_ref, f32[1024,2048]{1,0:T(8,128)} %get-tuple-element.178.refs_0_.refs_8_, f32[8,256,128]{2,1,0:T(8,128)S(1)} %collective-permute-done.34.refs_1_.refs_4_, f32[4,256,256]{2,1,0:T(8,128)S(1)} %fusion.1.refs_1_.refs_2_, ...), custom_call_target="tpu_custom_call" | custom-call | flops 3000000000 | bytes 100 | tf_op jit(solution)/shard_map/update_panels3/pallas_call | solution.py:323
  (83 shorter events, 23.2 us)
Async XLA Ops:
  0.0 14.6 %collective-permute-start = (f32[4,1024,128]{2,1,0:T(8,128)}, f32[4,1024,128]{2,1,0:T(8,128)S(1)}, u32[]{:S(2)}, u32[]{:S(2)}) collective-permute-start(f32[4,1024,128]{2,1,0:T(8,128)} %refs_6_.1), channel_id=1, source_target_pairs={{1,0},{0,1},{3,2},{2,3},{5,4},{4,5},{7,6},{6,7},{9,8},{8,9},{11,10... | collective-permute-start | bytes 6291464 | tf_op jit(solution)/shard_map/ppermute | solution.py:356
  0.5 12.5 %collective-permute-start.1 = (f32[4,128,256]{2,1,0:T(8,128)}, f32[4,128,256]{2,1,0:T(8,128)}, u32[]{:S(2)}, u32[]{:S(2)}) collective-permute-start(f32[4,128,256]{2,1,0:T(8,128)} %param.5), channel_id=1, source_target_pairs={{1,0},{0,1},{3,2},{2,3},{5,4},{4,5},{7,6},{6,7},{9,8},{8,9},{11,10... | collective-permute-start | bytes 1572872 | tf_op jit(solution)/shard_map/ppermute | solution.py:356
  10.0 15.9 %collective-permute-start.2 = (f32[8,256,128]{2,1,0:T(8,128)}, f32[8,256,128]{2,1,0:T(8,128)S(1)}, u32[]{:S(2)}, u32[]{:S(2)}) collective-permute-start(f32[8,256,128]{2,1,0:T(8,128)} %get-tuple-element.98), channel_id=1, source_target_pairs={{0,2},{1,5},{2,0},{3,7},{4,6},{5,1},{6,4},{7,3},{8,10},{9,13},{10,... | collective-permute-start | bytes 3145736 | tf_op jit(solution)/shard_map/ppermute | solution.py:351
  24.5 25.9 %collective-permute-start.4 = (f32[8,352,128]{2,1,0:T(8,128)S(1)}, f32[8,352,128]{2,1,0:T(8,128)S(1)}, u32[]{:S(2)}, u32[]{:S(2)}) collective-permute-start(f32[8,352,128]{2,1,0:T(8,128)S(1)} %get-tuple-element.106), channel_id=1, source_target_pairs={{0,2},{1,5},{2,0},{3,7},{4,6},{5,1},{6,4},{7,3},{8,10},{9,13},{10,... | collective-permute-start | bytes 4325384 | tf_op jit(solution)/shard_map/ppermute | solution.py:351
  26.1 13.4 %collective-permute-start.3 = (f32[4,256,128]{2,1,0:T(8,128)S(1)}, f32[4,256,128]{2,1,0:T(8,128)S(1)}, u32[]{:S(2)}, u32[]{:S(2)}) collective-permute-start(f32[4,256,128]{2,1,0:T(8,128)S(1)} %get-tuple-element.102), channel_id=1, source_target_pairs={{0,8},{1,9},{2,10},{3,11},{4,12},{5,13},{6,14},{7,15},{8,0},{9,1},... | collective-permute-start | bytes 1572872 | tf_op jit(solution)/shard_map/ppermute | solution.py:351
  35.7 21.9 %collective-permute-start.6 = (f32[8,256,128]{2,1,0:T(8,128)S(1)}, f32[8,256,128]{2,1,0:T(8,128)S(1)}, u32[]{:S(2)}, u32[]{:S(2)}) collective-permute-start(f32[8,256,128]{2,1,0:T(8,128)S(1)} %get-tuple-element.112), channel_id=1, source_target_pairs={{0,2},{1,5},{2,0},{3,7},{4,6},{5,1},{6,4},{7,3},{8,10},{9,13},{10,... | collective-permute-start | bytes 3145736 | tf_op jit(solution)/shard_map/ppermute | solution.py:351
  39.5 12.8 %collective-permute-start.5 = (f32[2,256,128]{2,1,0:T(8,128)S(1)}, f32[2,256,128]{2,1,0:T(8,128)S(1)}, u32[]{:S(2)}, u32[]{:S(2)}) collective-permute-start(f32[2,256,128]{2,1,0:T(8,128)S(1)} %get-tuple-element.109), channel_id=1, source_target_pairs={{0,4},{1,3},{2,6},{3,1},{4,0},{5,7},{6,2},{7,5},{8,12},{9,11},{10,... | collective-permute-start | bytes 786440 | tf_op jit(solution)/shard_map/ppermute | solution.py:351
  48.9 24.0 %collective-permute-start.8 = (f32[8,256,128]{2,1,0:T(8,128)S(1)}, f32[8,256,128]{2,1,0:T(8,128)S(1)}, u32[]{:S(2)}, u32[]{:S(2)}) collective-permute-start(f32[8,256,128]{2,1,0:T(8,128)S(1)} %get-tuple-element.118), channel_id=1, source_target_pairs={{0,2},{1,5},{2,0},{3,7},{4,6},{5,1},{6,4},{7,3},{8,10},{9,13},{10,... | collective-permute-start | bytes 3145736 | tf_op jit(solution)/shard_map/ppermute | solution.py:351
  50.6 21.5 %collective-permute-start.7 = (f32[4,352,128]{2,1,0:T(8,128)S(1)}, f32[4,352,128]{2,1,0:T(8,128)S(1)}, u32[]{:S(2)}, u32[]{:S(2)}) collective-permute-start(f32[4,352,128]{2,1,0:T(8,128)S(1)} %get-tuple-element.115), channel_id=1, source_target_pairs={{0,8},{1,9},{2,10},{3,11},{4,12},{5,13},{6,14},{7,15},{8,0},{9,1},... | collective-permute-start | bytes 2162696 | tf_op jit(solution)/shard_map/ppermute | solution.py:351
  52.3 20.8 %collective-permute-start.9 = (f32[1,256,128]{2,1,0:T(8,128)S(1)}, f32[1,256,128]{2,1,0:T(8,128)S(1)}, u32[]{:S(2)}, u32[]{:S(2)}) collective-permute-start(f32[1,256,128]{2,1,0:T(8,128)S(1)} %get-tuple-element.121), channel_id=1, source_target_pairs={{0,16},{1,17},{2,18},{3,19},{4,20},{5,21},{6,22},{7,23},{8,24},{9,... | collective-permute-start | bytes 393224 | tf_op jit(solution)/shard_map/ppermute | solution.py:351
  57.8 29.8 %collective-permute-start.11 = (f32[4,256,128]{2,1,0:T(8,128)S(1)}, f32[4,256,128]{2,1,0:T(8,128)S(1)}, u32[]{:S(2)}, u32[]{:S(2)}) collective-permute-start(f32[4,256,128]{2,1,0:T(8,128)S(1)} %get-tuple-element.127), channel_id=1, source_target_pairs={{0,8},{1,9},{2,10},{3,11},{4,12},{5,13},{6,14},{7,15},{8,0},{9,1},... | collective-permute-start | bytes 1572872 | tf_op jit(solution)/shard_map/ppermute | solution.py:351
  72.2 7.5 %collective-permute-start.10 = (f32[2,352,128]{2,1,0:T(8,128)S(1)}, f32[2,352,128]{2,1,0:T(8,128)S(1)}, u32[]{:S(2)}, u32[]{:S(2)}) collective-permute-start(f32[2,352,128]{2,1,0:T(8,128)S(1)} %get-tuple-element.124), channel_id=1, source_target_pairs={{0,4},{1,3},{2,6},{3,1},{4,0},{5,7},{6,2},{7,5},{8,12},{9,11},{10,... | collective-permute-start | bytes 1081352 | tf_op jit(solution)/shard_map/ppermute | solution.py:351
  73.1 14.8 %collective-permute-start.12 = (f32[1,256,128]{2,1,0:T(8,128)S(1)}, f32[1,256,128]{2,1,0:T(8,128)S(1)}, u32[]{:S(2)}, u32[]{:S(2)}) collective-permute-start(f32[1,256,128]{2,1,0:T(8,128)S(1)} %get-tuple-element.129.refs_1_), channel_id=1, source_target_pairs={{0,16},{1,17},{2,18},{3,19},{4,20},{5,21},{6,22},{7,23},{8,24},{9,... | collective-permute-start | bytes 393224 | tf_op jit(solution)/shard_map/ppermute | solution.py:351
  75.2 26.0 %collective-permute-start.16 = (f32[4,256,128]{2,1,0:T(8,128)S(1)}, f32[4,256,128]{2,1,0:T(8,128)S(1)}, u32[]{:S(2)}, u32[]{:S(2)}) collective-permute-start(f32[4,256,128]{2,1,0:T(8,128)S(1)} %get-tuple-element.140), channel_id=1, source_target_pairs={{0,8},{1,9},{2,10},{3,11},{4,12},{5,13},{6,14},{7,15},{8,0},{9,1},... | collective-permute-start | bytes 1572872 | tf_op jit(solution)/shard_map/ppermute | solution.py:351
  88.0 9.5 %collective-permute-start.14 = (f32[1,352,128]{2,1,0:T(8,128)S(1)}, f32[1,352,128]{2,1,0:T(8,128)S(1)}, u32[]{:S(2)}, u32[]{:S(2)}) collective-permute-start(f32[1,352,128]{2,1,0:T(8,128)S(1)} %get-tuple-element.135), channel_id=1, source_target_pairs={{0,16},{1,17},{2,18},{3,19},{4,20},{5,21},{6,22},{7,23},{8,24},{9,... | collective-permute-start | bytes 540680 | tf_op jit(solution)/shard_map/ppermute | solution.py:351
  88.0 13.1 %collective-permute-start.15 = (f32[2,256,128]{2,1,0:T(8,128)S(1)}, f32[2,256,128]{2,1,0:T(8,128)S(1)}, u32[]{:S(2)}, u32[]{:S(2)}) collective-permute-start(f32[2,256,128]{2,1,0:T(8,128)S(1)} %get-tuple-element.137.refs_1_), channel_id=1, source_target_pairs={{0,4},{1,3},{2,6},{3,1},{4,0},{5,7},{6,2},{7,5},{8,12},{9,11},{10,... | collective-permute-start | bytes 786440 | tf_op jit(solution)/shard_map/ppermute | solution.py:351
  97.5 13.0 %collective-permute-start.17 = (f32[1,352,128]{2,1,0:T(8,128)S(1)}, f32[1,352,128]{2,1,0:T(8,128)S(1)}, u32[]{:S(2)}, u32[]{:S(2)}) collective-permute-start(f32[1,352,128]{2,1,0:T(8,128)S(1)} %get-tuple-element.142.refs_1_), channel_id=1, source_target_pairs={{0,16},{1,17},{2,18},{3,19},{4,20},{5,21},{6,22},{7,23},{8,24},{9,... | collective-permute-start | bytes 540680 | tf_op jit(solution)/shard_map/ppermute | solution.py:351
  101.0 12.6 %collective-permute-start.18 = (f32[1,256,128]{2,1,0:T(8,128)S(1)}, f32[1,256,128]{2,1,0:T(8,128)S(1)}, u32[]{:S(2)}, u32[]{:S(2)}) collective-permute-start(f32[1,256,128]{2,1,0:T(8,128)S(1)} %get-tuple-element.145), channel_id=1, source_target_pairs={{0,16},{1,17},{2,18},{3,19},{4,20},{5,21},{6,22},{7,23},{8,24},{9,... | collective-permute-start | bytes 393224 | tf_op jit(solution)/shard_map/ppermute | solution.py:351
  101.2 12.5 %collective-permute-start.19 = (f32[2,256,128]{2,1,0:T(8,128)S(1)}, f32[2,256,128]{2,1,0:T(8,128)S(1)}, u32[]{:S(2)}, u32[]{:S(2)}) collective-permute-start(f32[2,256,128]{2,1,0:T(8,128)S(1)} %get-tuple-element.148), channel_id=1, source_target_pairs={{0,4},{1,3},{2,6},{3,1},{4,0},{5,7},{6,2},{7,5},{8,12},{9,11},{10,... | collective-permute-start | bytes 786440 | tf_op jit(solution)/shard_map/ppermute | solution.py:351
  101.8 26.1 %collective-permute-start.23 = (f32[4,256,128]{2,1,0:T(8,128)S(1)}, f32[4,256,128]{2,1,0:T(8,128)S(1)}, u32[]{:S(2)}, u32[]{:S(2)}) collective-permute-start(f32[4,256,128]{2,1,0:T(8,128)S(1)} %get-tuple-element.157.refs_1_), channel_id=1, source_target_pairs={{0,8},{1,9},{2,10},{3,11},{4,12},{5,13},{6,14},{7,15},{8,0},{9,1},... | collective-permute-start | bytes 1572872 | tf_op jit(solution)/shard_map/ppermute | solution.py:351
  113.6 11.4 %collective-permute-start.21 = (f32[1,256,128]{2,1,0:T(8,128)S(1)}, f32[1,256,128]{2,1,0:T(8,128)S(1)}, u32[]{:S(2)}, u32[]{:S(2)}) collective-permute-start(f32[1,256,128]{2,1,0:T(8,128)S(1)} %get-tuple-element.152.refs_1_), channel_id=1, source_target_pairs={{0,16},{1,17},{2,18},{3,19},{4,20},{5,21},{6,22},{7,23},{8,24},{9,... | collective-permute-start | bytes 393224 | tf_op jit(solution)/shard_map/ppermute | solution.py:351
  113.7 14.1 %collective-permute-start.22 = (f32[1,256,128]{2,1,0:T(8,128)S(1)}, f32[1,256,128]{2,1,0:T(8,128)S(1)}, u32[]{:S(2)}, u32[]{:S(2)}) collective-permute-start(f32[1,256,128]{2,1,0:T(8,128)S(1)} %get-tuple-element.155), channel_id=1, source_target_pairs={{0,16},{1,17},{2,18},{3,19},{4,20},{5,21},{6,22},{7,23},{8,24},{9,... | collective-permute-start | bytes 393224 | tf_op jit(solution)/shard_map/ppermute | solution.py:351
  118.1 24.5 %collective-permute-start.24 = (f32[4,352,128]{2,1,0:T(8,128)S(1)}, f32[4,352,128]{2,1,0:T(8,128)S(1)}, u32[]{:S(2)}, u32[]{:S(2)}) collective-permute-start(f32[4,352,128]{2,1,0:T(8,128)S(1)} %get-tuple-element.159.refs_1_), channel_id=1, source_target_pairs={{0,8},{1,9},{2,10},{3,11},{4,12},{5,13},{6,14},{7,15},{8,0},{9,1},... | collective-permute-start | bytes 2162696 | tf_op jit(solution)/shard_map/ppermute | solution.py:351
  125.0 19.4 %collective-permute-start.25 = (f32[2,256,128]{2,1,0:T(8,128)S(1)}, f32[2,256,128]{2,1,0:T(8,128)S(1)}, u32[]{:S(2)}, u32[]{:S(2)}) collective-permute-start(f32[2,256,128]{2,1,0:T(8,128)S(1)} %get-tuple-element.161.refs_1_), channel_id=1, source_target_pairs={{0,4},{1,3},{2,6},{3,1},{4,0},{5,7},{6,2},{7,5},{8,12},{9,11},{10,... | collective-permute-start | bytes 786440 | tf_op jit(solution)/shard_map/ppermute | solution.py:351
  127.8 16.6 %collective-permute-start.26 = (f32[1,256,128]{2,1,0:T(8,128)S(1)}, f32[1,256,128]{2,1,0:T(8,128)S(1)}, u32[]{:S(2)}, u32[]{:S(2)}) collective-permute-start(f32[1,256,128]{2,1,0:T(8,128)S(1)} %get-tuple-element.163.refs_1_), channel_id=1, source_target_pairs={{0,16},{1,17},{2,18},{3,19},{4,20},{5,21},{6,22},{7,23},{8,24},{9,... | collective-permute-start | bytes 393224 | tf_op jit(solution)/shard_map/ppermute | solution.py:351
  128.0 25.7 %collective-permute-start.27 = (f32[8,256,128]{2,1,0:T(8,128)S(1)}, f32[8,256,128]{2,1,0:T(8,128)S(1)}, u32[]{:S(2)}, u32[]{:S(2)}) collective-permute-start(f32[8,256,128]{2,1,0:T(8,128)S(1)} %get-tuple-element.165.refs_2_), channel_id=1, source_target_pairs={{0,2},{1,5},{2,0},{3,7},{4,6},{5,1},{6,4},{7,3},{8,10},{9,13},{10,... | collective-permute-start | bytes 3145736 | tf_op jit(solution)/shard_map/ppermute | solution.py:351
  142.7 25.1 %collective-permute-start.31 = (f32[8,352,128]{2,1,0:T(8,128)S(1)}, f32[8,352,128]{2,1,0:T(8,128)S(1)}, u32[]{:S(2)}, u32[]{:S(2)}) collective-permute-start(f32[8,352,128]{2,1,0:T(8,128)S(1)} %get-tuple-element.172.refs_2_.refs_4_), channel_id=1, source_target_pairs={{0,2},{1,5},{2,0},{3,7},{4,6},{5,1},{6,4},{7,3},{8,10},{9,13},{10,... | collective-permute-start | bytes 4325384 | tf_op jit(solution)/shard_map/ppermute | solution.py:351
  144.4 9.3 %collective-permute-start.28 = (f32[2,256,128]{2,1,0:T(8,128)S(1)}, f32[2,256,128]{2,1,0:T(8,128)S(1)}, u32[]{:S(2)}, u32[]{:S(2)}) collective-permute-start(f32[2,256,128]{2,1,0:T(8,128)S(1)} %get-tuple-element.166.refs_2_), channel_id=1, source_target_pairs={{0,4},{1,3},{2,6},{3,1},{4,0},{5,7},{6,2},{7,5},{8,12},{9,11},{10,... | collective-permute-start | bytes 786440 | tf_op jit(solution)/shard_map/ppermute | solution.py:351
  145.0 14.9 %collective-permute-start.29 = (f32[4,256,128]{2,1,0:T(8,128)S(1)}, f32[4,256,128]{2,1,0:T(8,128)S(1)}, u32[]{:S(2)}, u32[]{:S(2)}) collective-permute-start(f32[4,256,128]{2,1,0:T(8,128)S(1)} %get-tuple-element.168.refs_1_), channel_id=1, source_target_pairs={{0,8},{1,9},{2,10},{3,11},{4,12},{5,13},{6,14},{7,15},{8,0},{9,1},... | collective-permute-start | bytes 1572872 | tf_op jit(solution)/shard_map/ppermute | solution.py:351
  153.8 13.9 %collective-permute-start.30 = (f32[4,256,128]{2,1,0:T(8,128)S(1)}, f32[4,256,128]{2,1,0:T(8,128)S(1)}, u32[]{:S(2)}, u32[]{:S(2)}) collective-permute-start(f32[4,256,128]{2,1,0:T(8,128)S(1)} %get-tuple-element.170.refs_1_), channel_id=1, source_target_pairs={{0,8},{1,9},{2,10},{3,11},{4,12},{5,13},{6,14},{7,15},{8,0},{9,1},... | collective-permute-start | bytes 1572872 | tf_op jit(solution)/shard_map/ppermute | solution.py:351
  167.9 21.4 %collective-permute-start.33 = (f32[8,256,128]{2,1,0:T(8,128)S(1)}, f32[8,256,128]{2,1,0:T(8,128)S(1)}, u32[]{:S(2)}, u32[]{:S(2)}) collective-permute-start(f32[8,256,128]{2,1,0:T(8,128)S(1)} %get-tuple-element.176.refs_3_), channel_id=1, source_target_pairs={{0,2},{1,5},{2,0},{3,7},{4,6},{5,1},{6,4},{7,3},{8,10},{9,13},{10,... | collective-permute-start | bytes 3145736 | tf_op jit(solution)/shard_map/ppermute | solution.py:351
  169.4 32.0 %collective-permute-start.34 = (f32[8,256,128]{2,1,0:T(8,128)S(1)}, f32[8,256,128]{2,1,0:T(8,128)S(1)}, u32[]{:S(2)}, u32[]{:S(2)}) collective-permute-start(f32[8,256,128]{2,1,0:T(8,128)S(1)} %get-tuple-element.179.refs_3_), channel_id=1, source_target_pairs={{0,2},{1,5},{2,0},{3,7},{4,6},{5,1},{6,4},{7,3},{8,10},{9,13},{10,... | collective-permute-start | bytes 3145736 | tf_op jit(solution)/shard_map/ppermute | solution.py:351
  (6 other events, 31.8 us)

commit v10 on v9

--- a/solution.py
+++ b/solution.py
@@ -11,6 +11,7 @@
 SIZE = 2 * LANES
 VMEM_LIMIT = 40 * 1024 * 1024
 FIRST_LIMIT = 58 * 1024 * 1024
+PAIR_LIMIT = 48 * 1024 * 1024
 F32 = jnp.float32
 
 GROUPS = (
@@ -301,7 +302,7 @@
 
 def update(place, after, panels, left_over, sides, factors, slab, state, grams, carry):
     rows, columns = slab.shape
-    steps = 4 if len(panels) > 1 else 2
+    steps = 2
     deep = rows // steps
     first, count = panels[0], len(panels)
     size = factors.shape[-1]
@@ -327,7 +328,7 @@
         out_specs=out_specs,
         scratch_shapes=[pltpu.VMEM((3 * count * size, columns), jnp.bfloat16), pltpu.VMEM((count * size, columns), F32)],
         out_shape=outs,
-        compiler_params=params(),
+        compiler_params=params(PAIR_LIMIT if count > 1 else VMEM_LIMIT),
         cost_estimate=COST,
         name="update_panels" + "".join(map(str, panels)),
     )(place, *after, factors, *constant, *blocks, slab)

time: 211 us -> 213 us (level)
  Pallas kernels: 75.7 us -> 78 us
where the time goes in v10:
time: 213 us
  waiting for transfers between devices  92.9 us (44%)
  Pallas kernels  78 us (37%)
  starting transfers between devices  38.5 us (18%)
    ppermute x32, waiting for transfers between devices, swap(): return lax.ppermute(value, ('row', 'col'), pairs)  92.6 us
    pallas_call x3, Pallas kernels, update(): pl.pallas_call(functools.partial(update_kernel, panels, len(grams), len(c...  42 us
    ppermute x32, starting transfers between devices, swap(): return lax.ppermute(value, ('row', 'col'), pairs)  38 us
    pallas_call x4, Pallas kernels, project(): pl.pallas_call(functools.partial(project_kernel, steps, call, blocks, len...  31.6 us
  transfers between devices with their start and end apart: 35, of which 18 were waited for; matrix products, arithmetic and copies ran while one was open for 1% of the time, Pallas kernels for 32%

profile of v10, /device:TPU:0, one launch (start us, length us, event | category | flops | bytes accessed | tf_op | source)
XLA Modules:
  0.0 213.3 jit_solution(16217905061926652854)
XLA Ops:
  1.1 8.9 %project_0.1 = (f32[8,256,128]{2,1,0:T(8,128)}, f32[8,256,128]{2,1,0:T(8,128)}, f32[8,128]{1,0:T(8,128)}) custom-call(s32[1]{0:T(128)} %bitcast.place.place_ref, f32[8,128]{1,0:T(8,128)} %broadcast_in_dim.3.refs_0_, f32[4,1024,128]{2,1,0:T(8,128)} %refs_6_.1, f32[4,1024,128]{2,1,0:T(8,128)} %refs_6_.1, f32[1024,2048]{1,0:T(8,128)} %refs_12_.1), custom_call_target="tpu_custom_call" | custom-call | flops 3000000000 | bytes 100 | tf_op jit(solution)/shard_map/project_0/pallas_call | solution.py:161
  10.0 2.9 %collective-permute-start.2 = (f32[8,256,128]{2,1,0:T(8,128)}, f32[8,256,128]{2,1,0:T(8,128)S(1)}, u32[]{:S(2)}, u32[]{:S(2)}) collective-permute-start(f32[8,256,128]{2,1,0:T(8,128)} %get-tuple-element.98), channel_id=1, source_target_pairs={{0,2},{1,5},{2,0},{3,7},{4,6},{5,1},{6,4},{7,3},{8,10},{9,13},{10,... | collective-permute-start | bytes 3145736 | tf_op jit(solution)/shard_map/ppermute | solution.py:352
  14.9 1.9 gram_rows.1
  16.8 7.6 %project_1.1 = (f32[8,352,128]{2,1,0:T(8,128)S(1)}, f32[8,352,128]{2,1,0:T(8,128)S(1)}, f32[8,128]{1,0:T(8,128)S(1)}) custom-call(s32[1]{0:T(128)} %bitcast.place.place_ref, f32[8,128]{1,0:T(8,128)S(1)} %get-tuple-element.94.refs_0_, f32[4,256,256]{2,1,0:T(8,128)S(1)} %fusion.1.refs_1_.refs_2_, ...), custom_call_target="tpu_custom_call" | custom-call | flops 3000000000 | bytes 100 | tf_op jit(solution)/shard_map/project_1/pallas_call | solution.py:161
  26.1 2.2 %collective-permute-start.3 = (f32[4,256,128]{2,1,0:T(8,128)S(1)}, f32[4,256,128]{2,1,0:T(8,128)S(1)}, u32[]{:S(2)}, u32[]{:S(2)}) collective-permute-start(f32[4,256,128]{2,1,0:T(8,128)S(1)} %get-tuple-element.102), channel_id=1, source_target_pairs={{0,8},{1,9},{2,10},{3,11},{4,12},{5,13},{6,14},{7,15},{8,0},{9,1},... | collective-permute-start | bytes 1572872 | tf_op jit(solution)/shard_map/ppermute | solution.py:352
  28.3 7.5 %project_2.1 = (f32[8,256,128]{2,1,0:T(8,128)S(1)}, f32[8,256,128]{2,1,0:T(8,128)S(1)}, f32[8,128]{1,0:T(8,128)S(1)}) custom-call(s32[1]{0:T(128)} %bitcast.place.place_ref, f32[8,128]{1,0:T(8,128)S(1)} %get-tuple-element.99.refs_0_, f32[4,1024,128]{2,1,0:T(8,128)S(1)} %copy-done.2, ...), custom_call_target="tpu_custom_call" | custom-call | flops 3000000000 | bytes 100 | tf_op jit(solution)/shard_map/project_2/pallas_call | solution.py:161
  37.3 2.2 %collective-permute-done.3.refs_2_ = f32[4,256,128]{2,1,0:T(8,128)S(1)} collective-permute-done((f32[4,256,128]{2,1,0:T(8,128)S(1)}, f32[4,256,128]{2,1,0:T(8,128)S(1)}, u32[]{:S(2)}, u32[]{:S(2)}) %collective-permute-start.3) | collective-permute-done | bytes 524320 | tf_op jit(solution)/shard_map/ppermute | solution.py:352
  39.6 1.7 collective-permute-start.5
  41.3 7.6 %project_3.1 = (f32[8,256,128]{2,1,0:T(8,128)S(1)}, f32[8,256,128]{2,1,0:T(8,128)S(1)}, f32[8,128]{1,0:T(8,128)S(1)}) custom-call(s32[1]{0:T(128)} %bitcast.place.place_ref, f32[8,128]{1,0:T(8,128)S(1)} %get-tuple-element.103.refs_0_, f32[4,1024,128]{2,1,0:T(8,128)S(1)} %copy-done.2, ...), custom_call_target="tpu_custom_call" | custom-call | flops 3000000000 | bytes 100 | tf_op jit(solution)/shard_map/project_3/pallas_call | solution.py:161
  52.3 2.6 %collective-permute-start.9 = (f32[1,256,128]{2,1,0:T(8,128)S(1)}, f32[1,256,128]{2,1,0:T(8,128)S(1)}, u32[]{:S(2)}, u32[]{:S(2)}) collective-permute-start(f32[1,256,128]{2,1,0:T(8,128)S(1)} %get-tuple-element.121), channel_id=1, source_target_pairs={{0,16},{1,17},{2,18},{3,19},{4,20},{5,21},{6,22},{7,23},{8,24},{9,... | collective-permute-start | bytes 393224 | tf_op jit(solution)/shard_map/ppermute | solution.py:352
  55.0 2.5 %collective-permute-done.6.refs_2_ = f32[8,256,128]{2,1,0:T(8,128)S(1)} collective-permute-done((f32[8,256,128]{2,1,0:T(8,128)S(1)}, f32[8,256,128]{2,1,0:T(8,128)S(1)}, u32[]{:S(2)}, u32[]{:S(2)}) %collective-permute-start.6) | collective-permute-done | bytes 1048608 | tf_op jit(solution)/shard_map/ppermute | solution.py:352
  59.3 13.2 %collective-permute-done.7.refs_2_ = f32[4,352,128]{2,1,0:T(8,128)S(1)} collective-permute-done((f32[4,352,128]{2,1,0:T(8,128)S(1)}, f32[4,352,128]{2,1,0:T(8,128)S(1)}, u32[]{:S(2)}, u32[]{:S(2)}) %collective-permute-start.7) | collective-permute-done | bytes 720928 | tf_op jit(solution)/shard_map/ppermute | solution.py:352
  73.3 1.8 collective-permute-start.12
  76.2 3.8 %collective-permute-done.10.refs_2_ = f32[2,352,128]{2,1,0:T(8,128)S(1)} collective-permute-done((f32[2,352,128]{2,1,0:T(8,128)S(1)}, f32[2,352,128]{2,1,0:T(8,128)S(1)}, u32[]{:S(2)}, u32[]{:S(2)}) %collective-permute-start.10) | collective-permute-done | bytes 360480 | tf_op jit(solution)/shard_map/ppermute | solution.py:352
  80.1 7.6 %collective-permute-done.11.refs_2_ = f32[4,256,128]{2,1,0:T(8,128)S(1)} collective-permute-done((f32[4,256,128]{2,1,0:T(8,128)S(1)}, f32[4,256,128]{2,1,0:T(8,128)S(1)}, u32[]{:S(2)}, u32[]{:S(2)}) %collective-permute-start.11) | collective-permute-done | bytes 524320 | tf_op jit(solution)/shard_map/ppermute | solution.py:352
  88.0 1.9 collective-permute-start.15
  89.9 4.3 %collective-permute-done.13.refs_2_ = f32[2,256,128]{2,1,0:T(8,128)S(1)} collective-permute-done((f32[2,256,128]{2,1,0:T(8,128)S(1)}, f32[2,256,128]{2,1,0:T(8,128)S(1)}, u32[]{:S(2)}, u32[]{:S(2)}) %collective-permute-start.13) | collective-permute-done | bytes 262176 | tf_op jit(solution)/shard_map/ppermute | solution.py:352
  94.2 3.3 %collective-permute-done.14.refs_2_ = f32[1,352,128]{2,1,0:T(8,128)S(1)} collective-permute-done((f32[1,352,128]{2,1,0:T(8,128)S(1)}, f32[1,352,128]{2,1,0:T(8,128)S(1)}, u32[]{:S(2)}, u32[]{:S(2)}) %collective-permute-start.14) | collective-permute-done | bytes 180256 | tf_op jit(solution)/shard_map/ppermute | solution.py:352
  97.5 3.5 %collective-permute-start.17 = (f32[1,352,128]{2,1,0:T(8,128)S(1)}, f32[1,352,128]{2,1,0:T(8,128)S(1)}, u32[]{:S(2)}, u32[]{:S(2)}) collective-permute-start(f32[1,352,128]{2,1,0:T(8,128)S(1)} %get-tuple-element.142.refs_1_), channel_id=1, source_target_pairs={{0,16},{1,17},{2,18},{3,19},{4,20},{5,21},{6,22},{7,23},{8,24},{9,... | collective-permute-start | bytes 540680 | tf_op jit(solution)/shard_map/ppermute | solution.py:352
  101.8 3.0 %collective-permute-start.23 = (f32[4,256,128]{2,1,0:T(8,128)S(1)}, f32[4,256,128]{2,1,0:T(8,128)S(1)}, u32[]{:S(2)}, u32[]{:S(2)}) collective-permute-start(f32[4,256,128]{2,1,0:T(8,128)S(1)} %get-tuple-element.157.refs_1_), channel_id=1, source_target_pairs={{0,8},{1,9},{2,10},{3,11},{4,12},{5,13},{6,14},{7,15},{8,0},{9,1},... | collective-permute-start | bytes 1572872 | tf_op jit(solution)/shard_map/ppermute | solution.py:352
  104.8 5.7 %collective-permute-done.17.refs_2_ = f32[1,352,128]{2,1,0:T(8,128)S(1)} collective-permute-done((f32[1,352,128]{2,1,0:T(8,128)S(1)}, f32[1,352,128]{2,1,0:T(8,128)S(1)}, u32[]{:S(2)}, u32[]{:S(2)}) %collective-permute-start.17) | collective-permute-done | bytes 180256 | tf_op jit(solution)/shard_map/ppermute | solution.py:352
  111.0 2.6 %collective-permute-done.18.refs_2_ = f32[1,256,128]{2,1,0:T(8,128)S(1)} collective-permute-done((f32[1,256,128]{2,1,0:T(8,128)S(1)}, f32[1,256,128]{2,1,0:T(8,128)S(1)}, u32[]{:S(2)}, u32[]{:S(2)}) %collective-permute-start.18) | collective-permute-done | bytes 131104 | tf_op jit(solution)/shard_map/ppermute | solution.py:352
  113.7 3.0 %collective-permute-start.22 = (f32[1,256,128]{2,1,0:T(8,128)S(1)}, f32[1,256,128]{2,1,0:T(8,128)S(1)}, u32[]{:S(2)}, u32[]{:S(2)}) collective-permute-start(f32[1,256,128]{2,1,0:T(8,128)S(1)} %get-tuple-element.155), channel_id=1, source_target_pairs={{0,16},{1,17},{2,18},{3,19},{4,20},{5,21},{6,22},{7,23},{8,24},{9,... | collective-permute-start | bytes 393224 | tf_op jit(solution)/shard_map/ppermute | solution.py:352
  118.1 6.8 %collective-permute-done.21.refs_2_ = f32[1,256,128]{2,1,0:T(8,128)S(1)} collective-permute-done((f32[1,256,128]{2,1,0:T(8,128)S(1)}, f32[1,256,128]{2,1,0:T(8,128)S(1)}, u32[]{:S(2)}, u32[]{:S(2)}) %collective-permute-start.21) | collective-permute-done | bytes 131104 | tf_op jit(solution)/shard_map/ppermute | solution.py:352
  125.6 2.2 %collective-permute-done.22.refs_2_ = f32[1,256,128]{2,1,0:T(8,128)S(1)} collective-permute-done((f32[1,256,128]{2,1,0:T(8,128)S(1)}, f32[1,256,128]{2,1,0:T(8,128)S(1)}, u32[]{:S(2)}, u32[]{:S(2)}) %collective-permute-start.22) | collective-permute-done | bytes 131104 | tf_op jit(solution)/shard_map/ppermute | solution.py:352
  128.7 13.9 %collective-permute-done.24.refs_2_ = f32[4,352,128]{2,1,0:T(8,128)S(1)} collective-permute-done((f32[4,352,128]{2,1,0:T(8,128)S(1)}, f32[4,352,128]{2,1,0:T(8,128)S(1)}, u32[]{:S(2)}, u32[]{:S(2)}) %collective-permute-start.24) | collective-permute-done | bytes 720928 | tf_op jit(solution)/shard_map/ppermute | solution.py:352
  144.9 8.8 %collective-permute-done.28.refs_3_ = f32[2,256,128]{2,1,0:T(8,128)S(1)} collective-permute-done((f32[2,256,128]{2,1,0:T(8,128)S(1)}, f32[2,256,128]{2,1,0:T(8,128)S(1)}, u32[]{:S(2)}, u32[]{:S(2)}) %collective-permute-start.28) | collective-permute-done | bytes 262176 | tf_op jit(solution)/shard_map/ppermute | solution.py:352
  153.8 6.0 %collective-permute-done.29.refs_2_ = f32[4,256,128]{2,1,0:T(8,128)S(1)} collective-permute-done((f32[4,256,128]{2,1,0:T(8,128)S(1)}, f32[4,256,128]{2,1,0:T(8,128)S(1)}, u32[]{:S(2)}, u32[]{:S(2)}) %collective-permute-start.29) | collective-permute-done | bytes 524320 | tf_op jit(solution)/shard_map/ppermute | solution.py:352
  160.8 6.9 %collective-permute-done.30.refs_2_ = f32[4,256,128]{2,1,0:T(8,128)S(1)} collective-permute-done((f32[4,256,128]{2,1,0:T(8,128)S(1)}, f32[4,256,128]{2,1,0:T(8,128)S(1)}, u32[]{:S(2)}, u32[]{:S(2)}) %collective-permute-start.30) | collective-permute-done | bytes 524320 | tf_op jit(solution)/shard_map/ppermute | solution.py:352
  171.2 20.4 %update_panels01.1 = (f32[1024,2048]{1,0:T(8,128)}, f32[512,2048]{1,0:T(8,128)}) custom-call(s32[1]{0:T(128)} %bitcast.place.place_ref, f32[8,128]{1,0:T(8,128)S(1)} %get-tuple-element.173.refs_0_, f32[4,256,256]{2,1,0:T(8,128)S(1)} %fusion.1.refs_1_.refs_2_, f32[8,256,128]{2,1,0:T(8,128)S(1)} %get-tuple-element.165.refs_2_, ...), custom_call_target="tpu_custom_call" | custom-call | flops 3000000000 | bytes 100 | tf_op jit(solution)/shard_map/update_panels01/pallas_call | solution.py:324
  191.6 12.5 %update_panels2.1 = (f32[1024,2048]{1,0:T(8,128)}, f32[256,2048]{1,0:T(8,128)S(1)}) custom-call(s32[1]{0:T(128)} %bitcast.place.place_ref, f32[1024,2048]{1,0:T(8,128)} %get-tuple-element.175.refs_0_.refs_10_, f32[8,256,128]{2,1,0:T(8,128)S(1)} %collective-permute-done.33.refs_1_.refs_4_, f32[4,256,256]{2,1,0:T(8,128)S(1)} %fusion.1.refs_1_.refs_2_, ...), custom_call_target="tpu_custom_call" | custom-call | flops 3000000000 | bytes 100 | tf_op jit(solution)/shard_map/update_panels2/pallas_call | solution.py:324
  204.1 9.2 %update_panels3.1 = f32[1024,2048]{1,0:T(8,128)} custom-call(s32[1]{0:T(128)} %bitcast.place.place_ref, f32[1024,2048]{1,0:T(8,128)} %get-tuple-element.178.refs_0_.refs_8_, f32[8,256,128]{2,1,0:T(8,128)S(1)} %collective-permute-done.34.refs_1_.refs_4_, f32[4,256,256]{2,1,0:T(8,128)S(1)} %fusion.1.refs_1_.refs_2_, ...), custom_call_target="tpu_custom_call" | custom-call | flops 3000000000 | bytes 100 | tf_op jit(solution)/shard_map/update_panels3/pallas_call | solution.py:324
  (91 shorter events, 24.9 us)
Async XLA Ops:
  0.0 14.6 %collective-permute-start = (f32[4,1024,128]{2,1,0:T(8,128)}, f32[4,1024,128]{2,1,0:T(8,128)S(1)}, u32[]{:S(2)}, u32[]{:S(2)}) collective-permute-start(f32[4,1024,128]{2,1,0:T(8,128)} %refs_6_.1), channel_id=1, source_target_pairs={{1,0},{0,1},{3,2},{2,3},{5,4},{4,5},{7,6},{6,7},{9,8},{8,9},{11,10... | collective-permute-start | bytes 6291464 | tf_op jit(solution)/shard_map/ppermute | solution.py:357
  0.5 12.5 %collective-permute-start.1 = (f32[4,128,256]{2,1,0:T(8,128)}, f32[4,128,256]{2,1,0:T(8,128)}, u32[]{:S(2)}, u32[]{:S(2)}) collective-permute-start(f32[4,128,256]{2,1,0:T(8,128)} %param.5), channel_id=1, source_target_pairs={{1,0},{0,1},{3,2},{2,3},{5,4},{4,5},{7,6},{6,7},{9,8},{8,9},{11,10... | collective-permute-start | bytes 1572872 | tf_op jit(solution)/shard_map/ppermute | solution.py:357
  10.0 15.9 %collective-permute-start.2 = (f32[8,256,128]{2,1,0:T(8,128)}, f32[8,256,128]{2,1,0:T(8,128)S(1)}, u32[]{:S(2)}, u32[]{:S(2)}) collective-permute-start(f32[8,256,128]{2,1,0:T(8,128)} %get-tuple-element.98), channel_id=1, source_target_pairs={{0,2},{1,5},{2,0},{3,7},{4,6},{5,1},{6,4},{7,3},{8,10},{9,13},{10,... | collective-permute-start | bytes 3145736 | tf_op jit(solution)/shard_map/ppermute | solution.py:352
  24.4 26.1 %collective-permute-start.4 = (f32[8,352,128]{2,1,0:T(8,128)S(1)}, f32[8,352,128]{2,1,0:T(8,128)S(1)}, u32[]{:S(2)}, u32[]{:S(2)}) collective-permute-start(f32[8,352,128]{2,1,0:T(8,128)S(1)} %get-tuple-element.106), channel_id=1, source_target_pairs={{0,2},{1,5},{2,0},{3,7},{4,6},{5,1},{6,4},{7,3},{8,10},{9,13},{10,... | collective-permute-start | bytes 4325384 | tf_op jit(solution)/shard_map/ppermute | solution.py:352
  26.1 13.4 %collective-permute-start.3 = (f32[4,256,128]{2,1,0:T(8,128)S(1)}, f32[4,256,128]{2,1,0:T(8,128)S(1)}, u32[]{:S(2)}, u32[]{:S(2)}) collective-permute-start(f32[4,256,128]{2,1,0:T(8,128)S(1)} %get-tuple-element.102), channel_id=1, source_target_pairs={{0,8},{1,9},{2,10},{3,11},{4,12},{5,13},{6,14},{7,15},{8,0},{9,1},... | collective-permute-start | bytes 1572872 | tf_op jit(solution)/shard_map/ppermute | solution.py:352
  35.7 21.8 %collective-permute-start.6 = (f32[8,256,128]{2,1,0:T(8,128)S(1)}, f32[8,256,128]{2,1,0:T(8,128)S(1)}, u32[]{:S(2)}, u32[]{:S(2)}) collective-permute-start(f32[8,256,128]{2,1,0:T(8,128)S(1)} %get-tuple-element.112), channel_id=1, source_target_pairs={{0,2},{1,5},{2,0},{3,7},{4,6},{5,1},{6,4},{7,3},{8,10},{9,13},{10,... | collective-permute-start | bytes 3145736 | tf_op jit(solution)/shard_map/ppermute | solution.py:352
  39.6 12.8 %collective-permute-start.5 = (f32[2,256,128]{2,1,0:T(8,128)S(1)}, f32[2,256,128]{2,1,0:T(8,128)S(1)}, u32[]{:S(2)}, u32[]{:S(2)}) collective-permute-start(f32[2,256,128]{2,1,0:T(8,128)S(1)} %get-tuple-element.109), channel_id=1, source_target_pairs={{0,4},{1,3},{2,6},{3,1},{4,0},{5,7},{6,2},{7,5},{8,12},{9,11},{10,... | collective-permute-start | bytes 786440 | tf_op jit(solution)/shard_map/ppermute | solution.py:352
  48.9 24.3 %collective-permute-start.8 = (f32[8,256,128]{2,1,0:T(8,128)S(1)}, f32[8,256,128]{2,1,0:T(8,128)S(1)}, u32[]{:S(2)}, u32[]{:S(2)}) collective-permute-start(f32[8,256,128]{2,1,0:T(8,128)S(1)} %get-tuple-element.118), channel_id=1, source_target_pairs={{0,2},{1,5},{2,0},{3,7},{4,6},{5,1},{6,4},{7,3},{8,10},{9,13},{10,... | collective-permute-start | bytes 3145736 | tf_op jit(solution)/shard_map/ppermute | solution.py:352
  50.7 21.8 %collective-permute-start.7 = (f32[4,352,128]{2,1,0:T(8,128)S(1)}, f32[4,352,128]{2,1,0:T(8,128)S(1)}, u32[]{:S(2)}, u32[]{:S(2)}) collective-permute-start(f32[4,352,128]{2,1,0:T(8,128)S(1)} %get-tuple-element.115), channel_id=1, source_target_pairs={{0,8},{1,9},{2,10},{3,11},{4,12},{5,13},{6,14},{7,15},{8,0},{9,1},... | collective-permute-start | bytes 2162696 | tf_op jit(solution)/shard_map/ppermute | solution.py:352
  52.3 21.0 %collective-permute-start.9 = (f32[1,256,128]{2,1,0:T(8,128)S(1)}, f32[1,256,128]{2,1,0:T(8,128)S(1)}, u32[]{:S(2)}, u32[]{:S(2)}) collective-permute-start(f32[1,256,128]{2,1,0:T(8,128)S(1)} %get-tuple-element.121), channel_id=1, source_target_pairs={{0,16},{1,17},{2,18},{3,19},{4,20},{5,21},{6,22},{7,23},{8,24},{9,... | collective-permute-start | bytes 393224 | tf_op jit(solution)/shard_map/ppermute | solution.py:352
  57.6 30.0 %collective-permute-start.11 = (f32[4,256,128]{2,1,0:T(8,128)S(1)}, f32[4,256,128]{2,1,0:T(8,128)S(1)}, u32[]{:S(2)}, u32[]{:S(2)}) collective-permute-start(f32[4,256,128]{2,1,0:T(8,128)S(1)} %get-tuple-element.127), channel_id=1, source_target_pairs={{0,8},{1,9},{2,10},{3,11},{4,12},{5,13},{6,14},{7,15},{8,0},{9,1},... | collective-permute-start | bytes 1572872 | tf_op jit(solution)/shard_map/ppermute | solution.py:352
  72.6 7.5 %collective-permute-start.10 = (f32[2,352,128]{2,1,0:T(8,128)S(1)}, f32[2,352,128]{2,1,0:T(8,128)S(1)}, u32[]{:S(2)}, u32[]{:S(2)}) collective-permute-start(f32[2,352,128]{2,1,0:T(8,128)S(1)} %get-tuple-element.124), channel_id=1, source_target_pairs={{0,4},{1,3},{2,6},{3,1},{4,0},{5,7},{6,2},{7,5},{8,12},{9,11},{10,... | collective-permute-start | bytes 1081352 | tf_op jit(solution)/shard_map/ppermute | solution.py:352
  73.3 14.6 %collective-permute-start.12 = (f32[1,256,128]{2,1,0:T(8,128)S(1)}, f32[1,256,128]{2,1,0:T(8,128)S(1)}, u32[]{:S(2)}, u32[]{:S(2)}) collective-permute-start(f32[1,256,128]{2,1,0:T(8,128)S(1)} %get-tuple-element.129.refs_1_), channel_id=1, source_target_pairs={{0,16},{1,17},{2,18},{3,19},{4,20},{5,21},{6,22},{7,23},{8,24},{9,... | collective-permute-start | bytes 393224 | tf_op jit(solution)/shard_map/ppermute | solution.py:352
  75.2 26.0 %collective-permute-start.16 = (f32[4,256,128]{2,1,0:T(8,128)S(1)}, f32[4,256,128]{2,1,0:T(8,128)S(1)}, u32[]{:S(2)}, u32[]{:S(2)}) collective-permute-start(f32[4,256,128]{2,1,0:T(8,128)S(1)} %get-tuple-element.140), channel_id=1, source_target_pairs={{0,8},{1,9},{2,10},{3,11},{4,12},{5,13},{6,14},{7,15},{8,0},{9,1},... | collective-permute-start | bytes 1572872 | tf_op jit(solution)/shard_map/ppermute | solution.py:352
  87.9 9.5 %collective-permute-start.14 = (f32[1,352,128]{2,1,0:T(8,128)S(1)}, f32[1,352,128]{2,1,0:T(8,128)S(1)}, u32[]{:S(2)}, u32[]{:S(2)}) collective-permute-start(f32[1,352,128]{2,1,0:T(8,128)S(1)} %get-tuple-element.135), channel_id=1, source_target_pairs={{0,16},{1,17},{2,18},{3,19},{4,20},{5,21},{6,22},{7,23},{8,24},{9,... | collective-permute-start | bytes 540680 | tf_op jit(solution)/shard_map/ppermute | solution.py:352
  88.0 13.2 %collective-permute-start.15 = (f32[2,256,128]{2,1,0:T(8,128)S(1)}, f32[2,256,128]{2,1,0:T(8,128)S(1)}, u32[]{:S(2)}, u32[]{:S(2)}) collective-permute-start(f32[2,256,128]{2,1,0:T(8,128)S(1)} %get-tuple-element.137.refs_1_), channel_id=1, source_target_pairs={{0,4},{1,3},{2,6},{3,1},{4,0},{5,7},{6,2},{7,5},{8,12},{9,11},{10,... | collective-permute-start | bytes 786440 | tf_op jit(solution)/shard_map/ppermute | solution.py:352
  97.5 13.0 %collective-permute-start.17 = (f32[1,352,128]{2,1,0:T(8,128)S(1)}, f32[1,352,128]{2,1,0:T(8,128)S(1)}, u32[]{:S(2)}, u32[]{:S(2)}) collective-permute-start(f32[1,352,128]{2,1,0:T(8,128)S(1)} %get-tuple-element.142.refs_1_), channel_id=1, source_target_pairs={{0,16},{1,17},{2,18},{3,19},{4,20},{5,21},{6,22},{7,23},{8,24},{9,... | collective-permute-start | bytes 540680 | tf_op jit(solution)/shard_map/ppermute | solution.py:352
  101.0 12.6 %collective-permute-start.18 = (f32[1,256,128]{2,1,0:T(8,128)S(1)}, f32[1,256,128]{2,1,0:T(8,128)S(1)}, u32[]{:S(2)}, u32[]{:S(2)}) collective-permute-start(f32[1,256,128]{2,1,0:T(8,128)S(1)} %get-tuple-element.145), channel_id=1, source_target_pairs={{0,16},{1,17},{2,18},{3,19},{4,20},{5,21},{6,22},{7,23},{8,24},{9,... | collective-permute-start | bytes 393224 | tf_op jit(solution)/shard_map/ppermute | solution.py:352
  101.2 12.5 %collective-permute-start.19 = (f32[2,256,128]{2,1,0:T(8,128)S(1)}, f32[2,256,128]{2,1,0:T(8,128)S(1)}, u32[]{:S(2)}, u32[]{:S(2)}) collective-permute-start(f32[2,256,128]{2,1,0:T(8,128)S(1)} %get-tuple-element.148), channel_id=1, source_target_pairs={{0,4},{1,3},{2,6},{3,1},{4,0},{5,7},{6,2},{7,5},{8,12},{9,11},{10,... | collective-permute-start | bytes 786440 | tf_op jit(solution)/shard_map/ppermute | solution.py:352
  101.8 26.1 %collective-permute-start.23 = (f32[4,256,128]{2,1,0:T(8,128)S(1)}, f32[4,256,128]{2,1,0:T(8,128)S(1)}, u32[]{:S(2)}, u32[]{:S(2)}) collective-permute-start(f32[4,256,128]{2,1,0:T(8,128)S(1)} %get-tuple-element.157.refs_1_), channel_id=1, source_target_pairs={{0,8},{1,9},{2,10},{3,11},{4,12},{5,13},{6,14},{7,15},{8,0},{9,1},... | collective-permute-start | bytes 1572872 | tf_op jit(solution)/shard_map/ppermute | solution.py:352
  113.6 11.4 %collective-permute-start.21 = (f32[1,256,128]{2,1,0:T(8,128)S(1)}, f32[1,256,128]{2,1,0:T(8,128)S(1)}, u32[]{:S(2)}, u32[]{:S(2)}) collective-permute-start(f32[1,256,128]{2,1,0:T(8,128)S(1)} %get-tuple-element.152.refs_1_), channel_id=1, source_target_pairs={{0,16},{1,17},{2,18},{3,19},{4,20},{5,21},{6,22},{7,23},{8,24},{9,... | collective-permute-start | bytes 393224 | tf_op jit(solution)/shard_map/ppermute | solution.py:352
  113.7 14.1 %collective-permute-start.22 = (f32[1,256,128]{2,1,0:T(8,128)S(1)}, f32[1,256,128]{2,1,0:T(8,128)S(1)}, u32[]{:S(2)}, u32[]{:S(2)}) collective-permute-start(f32[1,256,128]{2,1,0:T(8,128)S(1)} %get-tuple-element.155), channel_id=1, source_target_pairs={{0,16},{1,17},{2,18},{3,19},{4,20},{5,21},{6,22},{7,23},{8,24},{9,... | collective-permute-start | bytes 393224 | tf_op jit(solution)/shard_map/ppermute | solution.py:352
  118.1 24.5 %collective-permute-start.24 = (f32[4,352,128]{2,1,0:T(8,128)S(1)}, f32[4,352,128]{2,1,0:T(8,128)S(1)}, u32[]{:S(2)}, u32[]{:S(2)}) collective-permute-start(f32[4,352,128]{2,1,0:T(8,128)S(1)} %get-tuple-element.159.refs_1_), channel_id=1, source_target_pairs={{0,8},{1,9},{2,10},{3,11},{4,12},{5,13},{6,14},{7,15},{8,0},{9,1},... | collective-permute-start | bytes 2162696 | tf_op jit(solution)/shard_map/ppermute | solution.py:352
  125.0 19.3 %collective-permute-start.25 = (f32[2,256,128]{2,1,0:T(8,128)S(1)}, f32[2,256,128]{2,1,0:T(8,128)S(1)}, u32[]{:S(2)}, u32[]{:S(2)}) collective-permute-start(f32[2,256,128]{2,1,0:T(8,128)S(1)} %get-tuple-element.161.refs_1_), channel_id=1, source_target_pairs={{0,4},{1,3},{2,6},{3,1},{4,0},{5,7},{6,2},{7,5},{8,12},{9,11},{10,... | collective-permute-start | bytes 786440 | tf_op jit(solution)/shard_map/ppermute | solution.py:352
  127.8 16.5 %collective-permute-start.26 = (f32[1,256,128]{2,1,0:T(8,128)S(1)}, f32[1,256,128]{2,1,0:T(8,128)S(1)}, u32[]{:S(2)}, u32[]{:S(2)}) collective-permute-start(f32[1,256,128]{2,1,0:T(8,128)S(1)} %get-tuple-element.163.refs_1_), channel_id=1, source_target_pairs={{0,16},{1,17},{2,18},{3,19},{4,20},{5,21},{6,22},{7,23},{8,24},{9,... | collective-permute-start | bytes 393224 | tf_op jit(solution)/shard_map/ppermute | solution.py:352
  128.0 25.7 %collective-permute-start.27 = (f32[8,256,128]{2,1,0:T(8,128)S(1)}, f32[8,256,128]{2,1,0:T(8,128)S(1)}, u32[]{:S(2)}, u32[]{:S(2)}) collective-permute-start(f32[8,256,128]{2,1,0:T(8,128)S(1)} %get-tuple-element.165.refs_2_), channel_id=1, source_target_pairs={{0,2},{1,5},{2,0},{3,7},{4,6},{5,1},{6,4},{7,3},{8,10},{9,13},{10,... | collective-permute-start | bytes 3145736 | tf_op jit(solution)/shard_map/ppermute | solution.py:352
  142.7 25.1 %collective-permute-start.31 = (f32[8,352,128]{2,1,0:T(8,128)S(1)}, f32[8,352,128]{2,1,0:T(8,128)S(1)}, u32[]{:S(2)}, u32[]{:S(2)}) collective-permute-start(f32[8,352,128]{2,1,0:T(8,128)S(1)} %get-tuple-element.172.refs_2_.refs_4_), channel_id=1, source_target_pairs={{0,2},{1,5},{2,0},{3,7},{4,6},{5,1},{6,4},{7,3},{8,10},{9,13},{10,... | collective-permute-start | bytes 4325384 | tf_op jit(solution)/shard_map/ppermute | solution.py:352
  144.4 9.3 %collective-permute-start.28 = (f32[2,256,128]{2,1,0:T(8,128)S(1)}, f32[2,256,128]{2,1,0:T(8,128)S(1)}, u32[]{:S(2)}, u32[]{:S(2)}) collective-permute-start(f32[2,256,128]{2,1,0:T(8,128)S(1)} %get-tuple-element.166.refs_2_), channel_id=1, source_target_pairs={{0,4},{1,3},{2,6},{3,1},{4,0},{5,7},{6,2},{7,5},{8,12},{9,11},{10,... | collective-permute-start | bytes 786440 | tf_op jit(solution)/shard_map/ppermute | solution.py:352
  144.9 14.9 %collective-permute-start.29 = (f32[4,256,128]{2,1,0:T(8,128)S(1)}, f32[4,256,128]{2,1,0:T(8,128)S(1)}, u32[]{:S(2)}, u32[]{:S(2)}) collective-permute-start(f32[4,256,128]{2,1,0:T(8,128)S(1)} %get-tuple-element.168.refs_1_), channel_id=1, source_target_pairs={{0,8},{1,9},{2,10},{3,11},{4,12},{5,13},{6,14},{7,15},{8,0},{9,1},... | collective-permute-start | bytes 1572872 | tf_op jit(solution)/shard_map/ppermute | solution.py:352
  153.7 14.0 %collective-permute-start.30 = (f32[4,256,128]{2,1,0:T(8,128)S(1)}, f32[4,256,128]{2,1,0:T(8,128)S(1)}, u32[]{:S(2)}, u32[]{:S(2)}) collective-permute-start(f32[4,256,128]{2,1,0:T(8,128)S(1)} %get-tuple-element.170.refs_1_), channel_id=1, source_target_pairs={{0,8},{1,9},{2,10},{3,11},{4,12},{5,13},{6,14},{7,15},{8,0},{9,1},... | collective-permute-start | bytes 1572872 | tf_op jit(solution)/shard_map/ppermute | solution.py:352
  168.9 22.7 %collective-permute-start.33 = (f32[8,256,128]{2,1,0:T(8,128)}, f32[8,256,128]{2,1,0:T(8,128)S(1)}, u32[]{:S(2)}, u32[]{:S(2)}) collective-permute-start(f32[8,256,128]{2,1,0:T(8,128)} %get-tuple-element.176.refs_3_), channel_id=1, source_target_pairs={{0,2},{1,5},{2,0},{3,7},{4,6},{5,1},{6,4},{7,3},{8,10},{9,13},{10,... | collective-permute-start | bytes 3145736 | tf_op jit(solution)/shard_map/ppermute | solution.py:352
  170.4 33.7 %collective-permute-start.34 = (f32[8,256,128]{2,1,0:T(8,128)S(1)}, f32[8,256,128]{2,1,0:T(8,128)S(1)}, u32[]{:S(2)}, u32[]{:S(2)}) collective-permute-start(f32[8,256,128]{2,1,0:T(8,128)S(1)} %get-tuple-element.179.refs_3_), channel_id=1, source_target_pairs={{0,2},{1,5},{2,0},{3,7},{4,6},{5,1},{6,4},{7,3},{8,10},{9,13},{10,... | collective-permute-start | bytes 3145736 | tf_op jit(solution)/shard_map/ppermute | solution.py:352
  (10 other events, 100.5 us)

commit v11 on v9

--- a/solution.py
+++ b/solution.py
@@ -147,7 +147,7 @@
 
 def project(place, after, sides, call, slab, grams, slots):
     rows, columns = slab.shape
-    steps = 2
+    steps = 4 if call == CALLS[0] else 2
     deep = rows // steps
     above = sum(rows_of(GROUPS[group]) for group in call)
     halves_of = []

time: 211 us -> 212 us (level)
  no operation moved by 1% of the time
where the time goes in v11:
time: 212 us
  waiting for transfers between devices  92.1 us (43%)
  Pallas kernels  77.1 us (36%)
  starting transfers between devices  40 us (19%)
    ppermute x32, waiting for transfers between devices, swap(): return lax.ppermute(value, ('row', 'col'), pairs)  91.9 us
    pallas_call x3, Pallas kernels, update(): pl.pallas_call(functools.partial(update_kernel, panels, len(grams), len(c...  40.4 us
    ppermute x32, starting transfers between devices, swap(): return lax.ppermute(value, ('row', 'col'), pairs)  39.4 us
    pallas_call x4, Pallas kernels, project(): pl.pallas_call(functools.partial(project_kernel, steps, call, blocks, len...  33 us
  transfers between devices with their start and end apart: 35, of which 18 were waited for; matrix products, arithmetic and copies ran while one was open for 1% of the time, Pallas kernels for 32%

profile of v11, /device:TPU:0, one launch (start us, length us, event | category | flops | bytes accessed | tf_op | source)
XLA Modules:
  0.0 211.9 jit_solution(15430760700024435138)
XLA Ops:
  1.1 10.3 %project_0.1 = (f32[8,256,128]{2,1,0:T(8,128)}, f32[8,256,128]{2,1,0:T(8,128)}, f32[8,128]{1,0:T(8,128)}) custom-call(s32[1]{0:T(128)} %bitcast.place.place_ref, f32[8,128]{1,0:T(8,128)} %broadcast_in_dim.3.refs_0_, f32[4,1024,128]{2,1,0:T(8,128)} %refs_6_.1, f32[4,1024,128]{2,1,0:T(8,128)} %refs_6_.1, f32[1024,2048]{1,0:T(8,128)} %refs_12_.1), custom_call_target="tpu_custom_call" | custom-call | flops 3000000000 | bytes 100 | tf_op jit(solution)/shard_map/project_0/pallas_call | solution.py:160
  11.4 2.9 %collective-permute-start.2 = (f32[8,256,128]{2,1,0:T(8,128)}, f32[8,256,128]{2,1,0:T(8,128)S(1)}, u32[]{:S(2)}, u32[]{:S(2)}) collective-permute-start(f32[8,256,128]{2,1,0:T(8,128)} %get-tuple-element.98), channel_id=1, source_target_pairs={{0,2},{1,5},{2,0},{3,7},{4,6},{5,1},{6,4},{7,3},{8,10},{9,13},{10,... | collective-permute-start | bytes 3145736 | tf_op jit(solution)/shard_map/ppermute | solution.py:351
  16.3 2.0 gram_rows.1
  18.3 7.6 %project_1.1 = (f32[8,352,128]{2,1,0:T(8,128)S(1)}, f32[8,352,128]{2,1,0:T(8,128)S(1)}, f32[8,128]{1,0:T(8,128)S(1)}) custom-call(s32[1]{0:T(128)} %bitcast.place.place_ref, f32[8,128]{1,0:T(8,128)S(1)} %get-tuple-element.94.refs_0_, f32[4,256,256]{2,1,0:T(8,128)S(1)} %fusion.1.refs_1_.refs_2_, ...), custom_call_target="tpu_custom_call" | custom-call | flops 3000000000 | bytes 100 | tf_op jit(solution)/shard_map/project_1/pallas_call | solution.py:160
  27.5 2.2 %collective-permute-start.3 = (f32[4,256,128]{2,1,0:T(8,128)S(1)}, f32[4,256,128]{2,1,0:T(8,128)S(1)}, u32[]{:S(2)}, u32[]{:S(2)}) collective-permute-start(f32[4,256,128]{2,1,0:T(8,128)S(1)} %get-tuple-element.102), channel_id=1, source_target_pairs={{0,8},{1,9},{2,10},{3,11},{4,12},{5,13},{6,14},{7,15},{8,0},{9,1},... | collective-permute-start | bytes 1572872 | tf_op jit(solution)/shard_map/ppermute | solution.py:351
  29.6 7.5 %project_2.1 = (f32[8,256,128]{2,1,0:T(8,128)S(1)}, f32[8,256,128]{2,1,0:T(8,128)S(1)}, f32[8,128]{1,0:T(8,128)S(1)}) custom-call(s32[1]{0:T(128)} %bitcast.place.place_ref, f32[8,128]{1,0:T(8,128)S(1)} %get-tuple-element.99.refs_0_, f32[4,1024,128]{2,1,0:T(8,128)S(1)} %copy-done, ...), custom_call_target="tpu_custom_call" | custom-call | flops 3000000000 | bytes 100 | tf_op jit(solution)/shard_map/project_2/pallas_call | solution.py:160
  38.7 2.2 %collective-permute-done.3.refs_2_ = f32[4,256,128]{2,1,0:T(8,128)S(1)} collective-permute-done((f32[4,256,128]{2,1,0:T(8,128)S(1)}, f32[4,256,128]{2,1,0:T(8,128)S(1)}, u32[]{:S(2)}, u32[]{:S(2)}) %collective-permute-start.3) | collective-permute-done | bytes 524320 | tf_op jit(solution)/shard_map/ppermute | solution.py:351
  42.7 7.6 %project_3.1 = (f32[8,256,128]{2,1,0:T(8,128)S(1)}, f32[8,256,128]{2,1,0:T(8,128)S(1)}, f32[8,128]{1,0:T(8,128)S(1)}) custom-call(s32[1]{0:T(128)} %bitcast.place.place_ref, f32[8,128]{1,0:T(8,128)S(1)} %get-tuple-element.103.refs_0_, f32[4,1024,128]{2,1,0:T(8,128)S(1)} %copy-done, ...), custom_call_target="tpu_custom_call" | custom-call | flops 3000000000 | bytes 100 | tf_op jit(solution)/shard_map/project_3/pallas_call | solution.py:160
  53.6 2.7 %collective-permute-start.9 = (f32[1,256,128]{2,1,0:T(8,128)S(1)}, f32[1,256,128]{2,1,0:T(8,128)S(1)}, u32[]{:S(2)}, u32[]{:S(2)}) collective-permute-start(f32[1,256,128]{2,1,0:T(8,128)S(1)} %get-tuple-element.121), channel_id=1, source_target_pairs={{0,16},{1,17},{2,18},{3,19},{4,20},{5,21},{6,22},{7,23},{8,24},{9,... | collective-permute-start | bytes 393224 | tf_op jit(solution)/shard_map/ppermute | solution.py:351
  56.4 2.7 %collective-permute-done.6.refs_2_ = f32[8,256,128]{2,1,0:T(8,128)S(1)} collective-permute-done((f32[8,256,128]{2,1,0:T(8,128)S(1)}, f32[8,256,128]{2,1,0:T(8,128)S(1)}, u32[]{:S(2)}, u32[]{:S(2)}) %collective-permute-start.6) | collective-permute-done | bytes 1048608 | tf_op jit(solution)/shard_map/ppermute | solution.py:351
  60.8 12.7 %collective-permute-done.7.refs_2_ = f32[4,352,128]{2,1,0:T(8,128)S(1)} collective-permute-done((f32[4,352,128]{2,1,0:T(8,128)S(1)}, f32[4,352,128]{2,1,0:T(8,128)S(1)}, u32[]{:S(2)}, u32[]{:S(2)}) %collective-permute-start.7) | collective-permute-done | bytes 720928 | tf_op jit(solution)/shard_map/ppermute | solution.py:351
  74.5 2.0 collective-permute-start.12
  77.6 3.4 %collective-permute-done.10.refs_2_ = f32[2,352,128]{2,1,0:T(8,128)S(1)} collective-permute-done((f32[2,352,128]{2,1,0:T(8,128)S(1)}, f32[2,352,128]{2,1,0:T(8,128)S(1)}, u32[]{:S(2)}, u32[]{:S(2)}) %collective-permute-start.10) | collective-permute-done | bytes 360480 | tf_op jit(solution)/shard_map/ppermute | solution.py:351
  81.1 7.9 %collective-permute-done.11.refs_2_ = f32[4,256,128]{2,1,0:T(8,128)S(1)} collective-permute-done((f32[4,256,128]{2,1,0:T(8,128)S(1)}, f32[4,256,128]{2,1,0:T(8,128)S(1)}, u32[]{:S(2)}, u32[]{:S(2)}) %collective-permute-start.11) | collective-permute-done | bytes 524320 | tf_op jit(solution)/shard_map/ppermute | solution.py:351
  89.4 1.9 collective-permute-start.15
  91.3 4.3 %collective-permute-done.13.refs_2_ = f32[2,256,128]{2,1,0:T(8,128)S(1)} collective-permute-done((f32[2,256,128]{2,1,0:T(8,128)S(1)}, f32[2,256,128]{2,1,0:T(8,128)S(1)}, u32[]{:S(2)}, u32[]{:S(2)}) %collective-permute-start.13) | collective-permute-done | bytes 262176 | tf_op jit(solution)/shard_map/ppermute | solution.py:351
  95.6 3.2 %collective-permute-done.14.refs_2_ = f32[1,352,128]{2,1,0:T(8,128)S(1)} collective-permute-done((f32[1,352,128]{2,1,0:T(8,128)S(1)}, f32[1,352,128]{2,1,0:T(8,128)S(1)}, u32[]{:S(2)}, u32[]{:S(2)}) %collective-permute-start.14) | collective-permute-done | bytes 180256 | tf_op jit(solution)/shard_map/ppermute | solution.py:351
  98.8 3.5 %collective-permute-start.17 = (f32[1,352,128]{2,1,0:T(8,128)S(1)}, f32[1,352,128]{2,1,0:T(8,128)S(1)}, u32[]{:S(2)}, u32[]{:S(2)}) collective-permute-start(f32[1,352,128]{2,1,0:T(8,128)S(1)} %get-tuple-element.142.refs_1_), channel_id=1, source_target_pairs={{0,16},{1,17},{2,18},{3,19},{4,20},{5,21},{6,22},{7,23},{8,24},{9,... | collective-permute-start | bytes 540680 | tf_op jit(solution)/shard_map/ppermute | solution.py:351
  103.2 3.0 %collective-permute-start.23 = (f32[4,256,128]{2,1,0:T(8,128)S(1)}, f32[4,256,128]{2,1,0:T(8,128)S(1)}, u32[]{:S(2)}, u32[]{:S(2)}) collective-permute-start(f32[4,256,128]{2,1,0:T(8,128)S(1)} %get-tuple-element.157.refs_1_), channel_id=1, source_target_pairs={{0,8},{1,9},{2,10},{3,11},{4,12},{5,13},{6,14},{7,15},{8,0},{9,1},... | collective-permute-start | bytes 1572872 | tf_op jit(solution)/shard_map/ppermute | solution.py:351
  106.2 5.7 %collective-permute-done.17.refs_2_ = f32[1,352,128]{2,1,0:T(8,128)S(1)} collective-permute-done((f32[1,352,128]{2,1,0:T(8,128)S(1)}, f32[1,352,128]{2,1,0:T(8,128)S(1)}, u32[]{:S(2)}, u32[]{:S(2)}) %collective-permute-start.17) | collective-permute-done | bytes 180256 | tf_op jit(solution)/shard_map/ppermute | solution.py:351
  112.5 2.3 %collective-permute-done.18.refs_2_ = f32[1,256,128]{2,1,0:T(8,128)S(1)} collective-permute-done((f32[1,256,128]{2,1,0:T(8,128)S(1)}, f32[1,256,128]{2,1,0:T(8,128)S(1)}, u32[]{:S(2)}, u32[]{:S(2)}) %collective-permute-start.18) | collective-permute-done | bytes 131104 | tf_op jit(solution)/shard_map/ppermute | solution.py:351
  115.0 3.0 %collective-permute-start.22 = (f32[1,256,128]{2,1,0:T(8,128)S(1)}, f32[1,256,128]{2,1,0:T(8,128)S(1)}, u32[]{:S(2)}, u32[]{:S(2)}) collective-permute-start(f32[1,256,128]{2,1,0:T(8,128)S(1)} %get-tuple-element.155), channel_id=1, source_target_pairs={{0,16},{1,17},{2,18},{3,19},{4,20},{5,21},{6,22},{7,23},{8,24},{9,... | collective-permute-start | bytes 393224 | tf_op jit(solution)/shard_map/ppermute | solution.py:351
  119.5 6.6 %collective-permute-done.21.refs_2_ = f32[1,256,128]{2,1,0:T(8,128)S(1)} collective-permute-done((f32[1,256,128]{2,1,0:T(8,128)S(1)}, f32[1,256,128]{2,1,0:T(8,128)S(1)}, u32[]{:S(2)}, u32[]{:S(2)}) %collective-permute-start.21) | collective-permute-done | bytes 131104 | tf_op jit(solution)/shard_map/ppermute | solution.py:351
  126.9 2.1 collective-permute-done.22.refs_2_
  130.1 13.7 %collective-permute-done.24.refs_2_ = f32[4,352,128]{2,1,0:T(8,128)S(1)} collective-permute-done((f32[4,352,128]{2,1,0:T(8,128)S(1)}, f32[4,352,128]{2,1,0:T(8,128)S(1)}, u32[]{:S(2)}, u32[]{:S(2)}) %collective-permute-start.24) | collective-permute-done | bytes 720928 | tf_op jit(solution)/shard_map/ppermute | solution.py:351
  143.9 1.8 collective-permute-start.31
  146.3 8.7 %collective-permute-done.28.refs_3_ = f32[2,256,128]{2,1,0:T(8,128)S(1)} collective-permute-done((f32[2,256,128]{2,1,0:T(8,128)S(1)}, f32[2,256,128]{2,1,0:T(8,128)S(1)}, u32[]{:S(2)}, u32[]{:S(2)}) %collective-permute-start.28) | collective-permute-done | bytes 262176 | tf_op jit(solution)/shard_map/ppermute | solution.py:351
  155.2 6.0 %collective-permute-done.29.refs_2_ = f32[4,256,128]{2,1,0:T(8,128)S(1)} collective-permute-done((f32[4,256,128]{2,1,0:T(8,128)S(1)}, f32[4,256,128]{2,1,0:T(8,128)S(1)}, u32[]{:S(2)}, u32[]{:S(2)}) %collective-permute-start.29) | collective-permute-done | bytes 524320 | tf_op jit(solution)/shard_map/ppermute | solution.py:351
  161.3 7.7 %collective-permute-done.30.refs_2_ = f32[4,256,128]{2,1,0:T(8,128)S(1)} collective-permute-done((f32[4,256,128]{2,1,0:T(8,128)S(1)}, f32[4,256,128]{2,1,0:T(8,128)S(1)}, u32[]{:S(2)}, u32[]{:S(2)}) %collective-permute-start.30) | collective-permute-done | bytes 524320 | tf_op jit(solution)/shard_map/ppermute | solution.py:351
  171.5 19.1 %update_panels01.1 = (f32[1024,2048]{1,0:T(8,128)}, f32[512,2048]{1,0:T(8,128)}) custom-call(s32[1]{0:T(128)} %bitcast.place.place_ref, f32[8,128]{1,0:T(8,128)S(1)} %get-tuple-element.173.refs_0_, f32[4,256,256]{2,1,0:T(8,128)S(1)} %fusion.1.refs_1_.refs_2_, f32[8,256,128]{2,1,0:T(8,128)S(1)} %get-tuple-element.165.refs_2_, ...), custom_call_target="tpu_custom_call" | custom-call | flops 3000000000 | bytes 100 | tf_op jit(solution)/shard_map/update_panels01/pallas_call | solution.py:323
  190.6 12.1 %update_panels2.1 = (f32[1024,2048]{1,0:T(8,128)}, f32[256,2048]{1,0:T(8,128)S(1)}) custom-call(s32[1]{0:T(128)} %bitcast.place.place_ref, f32[1024,2048]{1,0:T(8,128)} %get-tuple-element.175.refs_0_.refs_10_, f32[8,256,128]{2,1,0:T(8,128)S(1)} %collective-permute-done.33.refs_1_.refs_4_, f32[4,256,256]{2,1,0:T(8,128)S(1)} %fusion.1.refs_1_.refs_2_, ...), custom_call_target="tpu_custom_call" | custom-call | flops 3000000000 | bytes 100 | tf_op jit(solution)/shard_map/update_panels2/pallas_call | solution.py:323
  202.7 9.2 %update_panels3.1 = f32[1024,2048]{1,0:T(8,128)} custom-call(s32[1]{0:T(128)} %bitcast.place.place_ref, f32[1024,2048]{1,0:T(8,128)} %get-tuple-element.178.refs_0_.refs_8_, f32[8,256,128]{2,1,0:T(8,128)S(1)} %collective-permute-done.34.refs_1_.refs_4_, f32[4,256,256]{2,1,0:T(8,128)S(1)} %fusion.1.refs_1_.refs_2_, ...), custom_call_target="tpu_custom_call" | custom-call | flops 3000000000 | bytes 100 | tf_op jit(solution)/shard_map/update_panels3/pallas_call | solution.py:323
  (83 shorter events, 24.2 us)
Async XLA Ops:
  0.0 15.9 %collective-permute-start = (f32[4,1024,128]{2,1,0:T(8,128)}, f32[4,1024,128]{2,1,0:T(8,128)S(1)}, u32[]{:S(2)}, u32[]{:S(2)}) collective-permute-start(f32[4,1024,128]{2,1,0:T(8,128)} %refs_6_.1), channel_id=1, source_target_pairs={{1,0},{0,1},{3,2},{2,3},{5,4},{4,5},{7,6},{6,7},{9,8},{8,9},{11,10... | collective-permute-start | bytes 6291464 | tf_op jit(solution)/shard_map/ppermute | solution.py:356
  0.5 13.9 %collective-permute-start.1 = (f32[4,128,256]{2,1,0:T(8,128)}, f32[4,128,256]{2,1,0:T(8,128)}, u32[]{:S(2)}, u32[]{:S(2)}) collective-permute-start(f32[4,128,256]{2,1,0:T(8,128)} %param.5), channel_id=1, source_target_pairs={{1,0},{0,1},{3,2},{2,3},{5,4},{4,5},{7,6},{6,7},{9,8},{8,9},{11,10... | collective-permute-start | bytes 1572872 | tf_op jit(solution)/shard_map/ppermute | solution.py:356
  11.4 15.9 %collective-permute-start.2 = (f32[8,256,128]{2,1,0:T(8,128)}, f32[8,256,128]{2,1,0:T(8,128)S(1)}, u32[]{:S(2)}, u32[]{:S(2)}) collective-permute-start(f32[8,256,128]{2,1,0:T(8,128)} %get-tuple-element.98), channel_id=1, source_target_pairs={{0,2},{1,5},{2,0},{3,7},{4,6},{5,1},{6,4},{7,3},{8,10},{9,13},{10,... | collective-permute-start | bytes 3145736 | tf_op jit(solution)/shard_map/ppermute | solution.py:351
  25.9 25.9 %collective-permute-start.4 = (f32[8,352,128]{2,1,0:T(8,128)S(1)}, f32[8,352,128]{2,1,0:T(8,128)S(1)}, u32[]{:S(2)}, u32[]{:S(2)}) collective-permute-start(f32[8,352,128]{2,1,0:T(8,128)S(1)} %get-tuple-element.106), channel_id=1, source_target_pairs={{0,2},{1,5},{2,0},{3,7},{4,6},{5,1},{6,4},{7,3},{8,10},{9,13},{10,... | collective-permute-start | bytes 4325384 | tf_op jit(solution)/shard_map/ppermute | solution.py:351
  27.5 13.4 %collective-permute-start.3 = (f32[4,256,128]{2,1,0:T(8,128)S(1)}, f32[4,256,128]{2,1,0:T(8,128)S(1)}, u32[]{:S(2)}, u32[]{:S(2)}) collective-permute-start(f32[4,256,128]{2,1,0:T(8,128)S(1)} %get-tuple-element.102), channel_id=1, source_target_pairs={{0,8},{1,9},{2,10},{3,11},{4,12},{5,13},{6,14},{7,15},{8,0},{9,1},... | collective-permute-start | bytes 1572872 | tf_op jit(solution)/shard_map/ppermute | solution.py:351
  37.1 21.9 %collective-permute-start.6 = (f32[8,256,128]{2,1,0:T(8,128)S(1)}, f32[8,256,128]{2,1,0:T(8,128)S(1)}, u32[]{:S(2)}, u32[]{:S(2)}) collective-permute-start(f32[8,256,128]{2,1,0:T(8,128)S(1)} %get-tuple-element.112), channel_id=1, source_target_pairs={{0,2},{1,5},{2,0},{3,7},{4,6},{5,1},{6,4},{7,3},{8,10},{9,13},{10,... | collective-permute-start | bytes 3145736 | tf_op jit(solution)/shard_map/ppermute | solution.py:351
  40.9 12.7 %collective-permute-start.5 = (f32[2,256,128]{2,1,0:T(8,128)S(1)}, f32[2,256,128]{2,1,0:T(8,128)S(1)}, u32[]{:S(2)}, u32[]{:S(2)}) collective-permute-start(f32[2,256,128]{2,1,0:T(8,128)S(1)} %get-tuple-element.109), channel_id=1, source_target_pairs={{0,4},{1,3},{2,6},{3,1},{4,0},{5,7},{6,2},{7,5},{8,12},{9,11},{10,... | collective-permute-start | bytes 786440 | tf_op jit(solution)/shard_map/ppermute | solution.py:351
  50.3 24.0 %collective-permute-start.8 = (f32[8,256,128]{2,1,0:T(8,128)S(1)}, f32[8,256,128]{2,1,0:T(8,128)S(1)}, u32[]{:S(2)}, u32[]{:S(2)}) collective-permute-start(f32[8,256,128]{2,1,0:T(8,128)S(1)} %get-tuple-element.118), channel_id=1, source_target_pairs={{0,2},{1,5},{2,0},{3,7},{4,6},{5,1},{6,4},{7,3},{8,10},{9,13},{10,... | collective-permute-start | bytes 3145736 | tf_op jit(solution)/shard_map/ppermute | solution.py:351
  52.0 21.5 %collective-permute-start.7 = (f32[4,352,128]{2,1,0:T(8,128)S(1)}, f32[4,352,128]{2,1,0:T(8,128)S(1)}, u32[]{:S(2)}, u32[]{:S(2)}) collective-permute-start(f32[4,352,128]{2,1,0:T(8,128)S(1)} %get-tuple-element.115), channel_id=1, source_target_pairs={{0,8},{1,9},{2,10},{3,11},{4,12},{5,13},{6,14},{7,15},{8,0},{9,1},... | collective-permute-start | bytes 2162696 | tf_op jit(solution)/shard_map/ppermute | solution.py:351
  53.6 20.8 %collective-permute-start.9 = (f32[1,256,128]{2,1,0:T(8,128)S(1)}, f32[1,256,128]{2,1,0:T(8,128)S(1)}, u32[]{:S(2)}, u32[]{:S(2)}) collective-permute-start(f32[1,256,128]{2,1,0:T(8,128)S(1)} %get-tuple-element.121), channel_id=1, source_target_pairs={{0,16},{1,17},{2,18},{3,19},{4,20},{5,21},{6,22},{7,23},{8,24},{9,... | collective-permute-start | bytes 393224 | tf_op jit(solution)/shard_map/ppermute | solution.py:351
  59.1 29.9 %collective-permute-start.11 = (f32[4,256,128]{2,1,0:T(8,128)S(1)}, f32[4,256,128]{2,1,0:T(8,128)S(1)}, u32[]{:S(2)}, u32[]{:S(2)}) collective-permute-start(f32[4,256,128]{2,1,0:T(8,128)S(1)} %get-tuple-element.127), channel_id=1, source_target_pairs={{0,8},{1,9},{2,10},{3,11},{4,12},{5,13},{6,14},{7,15},{8,0},{9,1},... | collective-permute-start | bytes 1572872 | tf_op jit(solution)/shard_map/ppermute | solution.py:351
  73.5 7.5 %collective-permute-start.10 = (f32[2,352,128]{2,1,0:T(8,128)S(1)}, f32[2,352,128]{2,1,0:T(8,128)S(1)}, u32[]{:S(2)}, u32[]{:S(2)}) collective-permute-start(f32[2,352,128]{2,1,0:T(8,128)S(1)} %get-tuple-element.124), channel_id=1, source_target_pairs={{0,4},{1,3},{2,6},{3,1},{4,0},{5,7},{6,2},{7,5},{8,12},{9,11},{10,... | collective-permute-start | bytes 1081352 | tf_op jit(solution)/shard_map/ppermute | solution.py:351
  74.5 14.9 %collective-permute-start.12 = (f32[1,256,128]{2,1,0:T(8,128)S(1)}, f32[1,256,128]{2,1,0:T(8,128)S(1)}, u32[]{:S(2)}, u32[]{:S(2)}) collective-permute-start(f32[1,256,128]{2,1,0:T(8,128)S(1)} %get-tuple-element.129.refs_1_), channel_id=1, source_target_pairs={{0,16},{1,17},{2,18},{3,19},{4,20},{5,21},{6,22},{7,23},{8,24},{9,... | collective-permute-start | bytes 393224 | tf_op jit(solution)/shard_map/ppermute | solution.py:351
  76.5 25.9 %collective-permute-start.16 = (f32[4,256,128]{2,1,0:T(8,128)S(1)}, f32[4,256,128]{2,1,0:T(8,128)S(1)}, u32[]{:S(2)}, u32[]{:S(2)}) collective-permute-start(f32[4,256,128]{2,1,0:T(8,128)S(1)} %get-tuple-element.140), channel_id=1, source_target_pairs={{0,8},{1,9},{2,10},{3,11},{4,12},{5,13},{6,14},{7,15},{8,0},{9,1},... | collective-permute-start | bytes 1572872 | tf_op jit(solution)/shard_map/ppermute | solution.py:351
  89.4 9.3 %collective-permute-start.14 = (f32[1,352,128]{2,1,0:T(8,128)S(1)}, f32[1,352,128]{2,1,0:T(8,128)S(1)}, u32[]{:S(2)}, u32[]{:S(2)}) collective-permute-start(f32[1,352,128]{2,1,0:T(8,128)S(1)} %get-tuple-element.135), channel_id=1, source_target_pairs={{0,16},{1,17},{2,18},{3,19},{4,20},{5,21},{6,22},{7,23},{8,24},{9,... | collective-permute-start | bytes 540680 | tf_op jit(solution)/shard_map/ppermute | solution.py:351
  89.4 13.0 %collective-permute-start.15 = (f32[2,256,128]{2,1,0:T(8,128)S(1)}, f32[2,256,128]{2,1,0:T(8,128)S(1)}, u32[]{:S(2)}, u32[]{:S(2)}) collective-permute-start(f32[2,256,128]{2,1,0:T(8,128)S(1)} %get-tuple-element.137.refs_1_), channel_id=1, source_target_pairs={{0,4},{1,3},{2,6},{3,1},{4,0},{5,7},{6,2},{7,5},{8,12},{9,11},{10,... | collective-permute-start | bytes 786440 | tf_op jit(solution)/shard_map/ppermute | solution.py:351
  98.8 13.1 %collective-permute-start.17 = (f32[1,352,128]{2,1,0:T(8,128)S(1)}, f32[1,352,128]{2,1,0:T(8,128)S(1)}, u32[]{:S(2)}, u32[]{:S(2)}) collective-permute-start(f32[1,352,128]{2,1,0:T(8,128)S(1)} %get-tuple-element.142.refs_1_), channel_id=1, source_target_pairs={{0,16},{1,17},{2,18},{3,19},{4,20},{5,21},{6,22},{7,23},{8,24},{9,... | collective-permute-start | bytes 540680 | tf_op jit(solution)/shard_map/ppermute | solution.py:351
  102.3 12.5 %collective-permute-start.18 = (f32[1,256,128]{2,1,0:T(8,128)S(1)}, f32[1,256,128]{2,1,0:T(8,128)S(1)}, u32[]{:S(2)}, u32[]{:S(2)}) collective-permute-start(f32[1,256,128]{2,1,0:T(8,128)S(1)} %get-tuple-element.145), channel_id=1, source_target_pairs={{0,16},{1,17},{2,18},{3,19},{4,20},{5,21},{6,22},{7,23},{8,24},{9,... | collective-permute-start | bytes 393224 | tf_op jit(solution)/shard_map/ppermute | solution.py:351
  102.5 12.4 %collective-permute-start.19 = (f32[2,256,128]{2,1,0:T(8,128)S(1)}, f32[2,256,128]{2,1,0:T(8,128)S(1)}, u32[]{:S(2)}, u32[]{:S(2)}) collective-permute-start(f32[2,256,128]{2,1,0:T(8,128)S(1)} %get-tuple-element.148), channel_id=1, source_target_pairs={{0,4},{1,3},{2,6},{3,1},{4,0},{5,7},{6,2},{7,5},{8,12},{9,11},{10,... | collective-permute-start | bytes 786440 | tf_op jit(solution)/shard_map/ppermute | solution.py:351
  103.2 25.9 %collective-permute-start.23 = (f32[4,256,128]{2,1,0:T(8,128)S(1)}, f32[4,256,128]{2,1,0:T(8,128)S(1)}, u32[]{:S(2)}, u32[]{:S(2)}) collective-permute-start(f32[4,256,128]{2,1,0:T(8,128)S(1)} %get-tuple-element.157.refs_1_), channel_id=1, source_target_pairs={{0,8},{1,9},{2,10},{3,11},{4,12},{5,13},{6,14},{7,15},{8,0},{9,1},... | collective-permute-start | bytes 1572872 | tf_op jit(solution)/shard_map/ppermute | solution.py:351
  114.8 11.2 %collective-permute-start.21 = (f32[1,256,128]{2,1,0:T(8,128)S(1)}, f32[1,256,128]{2,1,0:T(8,128)S(1)}, u32[]{:S(2)}, u32[]{:S(2)}) collective-permute-start(f32[1,256,128]{2,1,0:T(8,128)S(1)} %get-tuple-element.152.refs_1_), channel_id=1, source_target_pairs={{0,16},{1,17},{2,18},{3,19},{4,20},{5,21},{6,22},{7,23},{8,24},{9,... | collective-permute-start | bytes 393224 | tf_op jit(solution)/shard_map/ppermute | solution.py:351
  115.0 14.0 %collective-permute-start.22 = (f32[1,256,128]{2,1,0:T(8,128)S(1)}, f32[1,256,128]{2,1,0:T(8,128)S(1)}, u32[]{:S(2)}, u32[]{:S(2)}) collective-permute-start(f32[1,256,128]{2,1,0:T(8,128)S(1)} %get-tuple-element.155), channel_id=1, source_target_pairs={{0,16},{1,17},{2,18},{3,19},{4,20},{5,21},{6,22},{7,23},{8,24},{9,... | collective-permute-start | bytes 393224 | tf_op jit(solution)/shard_map/ppermute | solution.py:351
  119.4 24.4 %collective-permute-start.24 = (f32[4,352,128]{2,1,0:T(8,128)S(1)}, f32[4,352,128]{2,1,0:T(8,128)S(1)}, u32[]{:S(2)}, u32[]{:S(2)}) collective-permute-start(f32[4,352,128]{2,1,0:T(8,128)S(1)} %get-tuple-element.159.refs_1_), channel_id=1, source_target_pairs={{0,8},{1,9},{2,10},{3,11},{4,12},{5,13},{6,14},{7,15},{8,0},{9,1},... | collective-permute-start | bytes 2162696 | tf_op jit(solution)/shard_map/ppermute | solution.py:351
  126.1 19.6 %collective-permute-start.25 = (f32[2,256,128]{2,1,0:T(8,128)S(1)}, f32[2,256,128]{2,1,0:T(8,128)S(1)}, u32[]{:S(2)}, u32[]{:S(2)}) collective-permute-start(f32[2,256,128]{2,1,0:T(8,128)S(1)} %get-tuple-element.161.refs_1_), channel_id=1, source_target_pairs={{0,4},{1,3},{2,6},{3,1},{4,0},{5,7},{6,2},{7,5},{8,12},{9,11},{10,... | collective-permute-start | bytes 786440 | tf_op jit(solution)/shard_map/ppermute | solution.py:351
  129.0 16.7 %collective-permute-start.26 = (f32[1,256,128]{2,1,0:T(8,128)S(1)}, f32[1,256,128]{2,1,0:T(8,128)S(1)}, u32[]{:S(2)}, u32[]{:S(2)}) collective-permute-start(f32[1,256,128]{2,1,0:T(8,128)S(1)} %get-tuple-element.163.refs_1_), channel_id=1, source_target_pairs={{0,16},{1,17},{2,18},{3,19},{4,20},{5,21},{6,22},{7,23},{8,24},{9,... | collective-permute-start | bytes 393224 | tf_op jit(solution)/shard_map/ppermute | solution.py:351
  129.2 25.9 %collective-permute-start.27 = (f32[8,256,128]{2,1,0:T(8,128)S(1)}, f32[8,256,128]{2,1,0:T(8,128)S(1)}, u32[]{:S(2)}, u32[]{:S(2)}) collective-permute-start(f32[8,256,128]{2,1,0:T(8,128)S(1)} %get-tuple-element.165.refs_2_), channel_id=1, source_target_pairs={{0,2},{1,5},{2,0},{3,7},{4,6},{5,1},{6,4},{7,3},{8,10},{9,13},{10,... | collective-permute-start | bytes 3145736 | tf_op jit(solution)/shard_map/ppermute | solution.py:351
  143.9 25.2 %collective-permute-start.31 = (f32[8,352,128]{2,1,0:T(8,128)S(1)}, f32[8,352,128]{2,1,0:T(8,128)S(1)}, u32[]{:S(2)}, u32[]{:S(2)}) collective-permute-start(f32[8,352,128]{2,1,0:T(8,128)S(1)} %get-tuple-element.172.refs_2_.refs_4_), channel_id=1, source_target_pairs={{0,2},{1,5},{2,0},{3,7},{4,6},{5,1},{6,4},{7,3},{8,10},{9,13},{10,... | collective-permute-start | bytes 4325384 | tf_op jit(solution)/shard_map/ppermute | solution.py:351
  145.8 9.3 %collective-permute-start.28 = (f32[2,256,128]{2,1,0:T(8,128)S(1)}, f32[2,256,128]{2,1,0:T(8,128)S(1)}, u32[]{:S(2)}, u32[]{:S(2)}) collective-permute-start(f32[2,256,128]{2,1,0:T(8,128)S(1)} %get-tuple-element.166.refs_2_), channel_id=1, source_target_pairs={{0,4},{1,3},{2,6},{3,1},{4,0},{5,7},{6,2},{7,5},{8,12},{9,11},{10,... | collective-permute-start | bytes 786440 | tf_op jit(solution)/shard_map/ppermute | solution.py:351
  146.3 14.9 %collective-permute-start.29 = (f32[4,256,128]{2,1,0:T(8,128)S(1)}, f32[4,256,128]{2,1,0:T(8,128)S(1)}, u32[]{:S(2)}, u32[]{:S(2)}) collective-permute-start(f32[4,256,128]{2,1,0:T(8,128)S(1)} %get-tuple-element.168.refs_1_), channel_id=1, source_target_pairs={{0,8},{1,9},{2,10},{3,11},{4,12},{5,13},{6,14},{7,15},{8,0},{9,1},... | collective-permute-start | bytes 1572872 | tf_op jit(solution)/shard_map/ppermute | solution.py:351
  155.1 13.9 %collective-permute-start.30 = (f32[4,256,128]{2,1,0:T(8,128)S(1)}, f32[4,256,128]{2,1,0:T(8,128)S(1)}, u32[]{:S(2)}, u32[]{:S(2)}) collective-permute-start(f32[4,256,128]{2,1,0:T(8,128)S(1)} %get-tuple-element.170.refs_1_), channel_id=1, source_target_pairs={{0,8},{1,9},{2,10},{3,11},{4,12},{5,13},{6,14},{7,15},{8,0},{9,1},... | collective-permute-start | bytes 1572872 | tf_op jit(solution)/shard_map/ppermute | solution.py:351
  169.2 21.4 %collective-permute-start.33 = (f32[8,256,128]{2,1,0:T(8,128)S(1)}, f32[8,256,128]{2,1,0:T(8,128)S(1)}, u32[]{:S(2)}, u32[]{:S(2)}) collective-permute-start(f32[8,256,128]{2,1,0:T(8,128)S(1)} %get-tuple-element.176.refs_3_), channel_id=1, source_target_pairs={{0,2},{1,5},{2,0},{3,7},{4,6},{5,1},{6,4},{7,3},{8,10},{9,13},{10,... | collective-permute-start | bytes 3145736 | tf_op jit(solution)/shard_map/ppermute | solution.py:351
  170.5 32.2 %collective-permute-start.34 = (f32[8,256,128]{2,1,0:T(8,128)S(1)}, f32[8,256,128]{2,1,0:T(8,128)S(1)}, u32[]{:S(2)}, u32[]{:S(2)}) collective-permute-start(f32[8,256,128]{2,1,0:T(8,128)S(1)} %get-tuple-element.179.refs_3_), channel_id=1, source_target_pairs={{0,2},{1,5},{2,0},{3,7},{4,6},{5,1},{6,4},{7,3},{8,10},{9,13},{10,... | collective-permute-start | bytes 3145736 | tf_op jit(solution)/shard_map/ppermute | solution.py:351
  (6 other events, 31.8 us)
